TPU v7x, 32 devices: a whole 2x2x4 slice. The times are simulated.
32 devices in a mesh: pts: 16 (over z, y, x), slab: 2 (over core).
Axes of the slice: x: 2, y: 2, z: 4, core: 2. Of those that a mesh axis runs over, the one named last changes fastest.
Arguments:
- features: float32 [8192, 256], P(('slab', 'pts')), parts along dimension 0, may hold values from -25 to 25
- orders: int32 [2, 8192], P(None, ('slab', 'pts')), parts along dimension 1, may hold values from 0 to 4095, as said below
- norm_gains: float32 [2, 2, 256], replicated, may hold values from 0.1 to 1.9
- qkv_weight: bfloat16 [2, 256, 768], replicated, may hold values from -4 to 4
- proj_weight: bfloat16 [2, 256, 256], replicated, may hold values from -0.375 to 0.375
- fc1_weight: bfloat16 [2, 256, 1024], replicated, may hold values from -0.375 to 0.375
- fc2_weight: bfloat16 [2, 1024, 256], replicated, may hold values from -0.1875 to 0.1875
Outputs:
- output_features: float32 [8192, 256], P(('slab', 'pts')), parts along dimension 0
There are 2 independent parts, one for each index of `slab`. A program takes and returns all parts, laid end to end along the dimension named above; an argument that names none is the same for every part. Nothing has to cross between parts.
Inputs may be any that keep to these rules, and one draw needn't show every extreme that they name: `orders`: each row is a permutation of the 4096 storage rows. In each row the 256 serial positions of one device take exactly 8 or 24 of their points from the rows stored on each device, 24 from half of the devices.
All inputs are finite; a program needn't handle non-finite values.
Results may differ from a plain program's by a relative error of at most 0.013.
Values may be sent and summed in bfloat16 or wider, within the bound.
No kernel may reach another device: no remote copies, remote signals or barrier semaphores. Data moves between devices by JAX's collectives and lax.ppermute only.
A program may use at most 64 MiB of HBM per device.

v0:
```python
import jax
import jax.numpy as jnp
from jax import lax
from jax.sharding import PartitionSpec as P

HEADS = 16
PATCH = 1024


def from_partner(block, axis, bit):
    count = lax.axis_size(axis)
    route = []
    for low in range(count):
        high = low | 1 << bit
        if high != low and high < count:
            route += [(low, high), (high, low)]
    return lax.ppermute(block, axis, route)


def layer_norm(values, gain_row):
    center = values - jnp.mean(values, axis=1, keepdims=True)
    spread = jnp.mean(center * center, axis=1, keepdims=True)
    return center * lax.rsqrt(spread + 1e-05) * gain_row


def routing(order_row, row_count, peers, capacity):
    owner_dev = order_row // row_count
    within = order_row % row_count
    onehot = (owner_dev[:, None] == jnp.arange(peers, dtype=jnp.int32)[None, :]).astype(jnp.int32)
    earlier = jnp.cumsum(onehot, axis=0) - onehot
    rank_pos = jnp.sum(onehot * earlier, axis=1)
    slot_pos = owner_dev * capacity + rank_pos
    request = jnp.full((peers * capacity,), row_count, jnp.int32).at[slot_pos].set(within)
    received = lax.all_to_all(request, "pts", split_axis=0, concat_axis=0, tiled=True)
    return (slot_pos, received)


def feed_forward(attended, gain_row, first_weight, second_weight):
    normed_two = layer_norm(attended, gain_row).astype(jnp.bfloat16)
    expanded = jax.nn.gelu(
        jnp.dot(normed_two, first_weight, preferred_element_type=jnp.float32), approximate=False
    ).astype(jnp.bfloat16)
    return jnp.dot(expanded, second_weight, preferred_element_type=jnp.float32)


def mix_heads(normed, in_weight):
    row_count, model_width = normed.shape
    projected_all = jnp.dot(normed, in_weight, preferred_element_type=jnp.float32).astype(
        jnp.bfloat16
    )
    queries = projected_all[:, :model_width]
    paired = projected_all[:, model_width:]
    doublings = (PATCH // row_count).bit_length() - 1
    gathered = paired
    for bit_index in range(doublings):
        gathered = jnp.concatenate((gathered, from_partner(gathered, "pts", bit_index)), axis=0)
    keys_all = gathered[:, :model_width]
    values_all = gathered[:, model_width:]
    head_size = model_width // HEADS
    per_group = min(4, HEADS)
    groups = HEADS // per_group
    score_scale = head_size ** (-0.5)

    def split_heads(matrix):
        return matrix.reshape(matrix.shape[0], groups, per_group, head_size).transpose(1, 0, 2, 3)

    def one_group(operands):
        query_part, key_part, value_part = operands
        scores = (
            jnp.einsum("qhd,khd->hqk", query_part, key_part, preferred_element_type=jnp.float32)
            * score_scale
        )
        row_peak = jnp.max(scores, axis=2, keepdims=True)
        weights = jnp.exp(scores - row_peak)
        probabilities = (weights / jnp.sum(weights, axis=2, keepdims=True)).astype(jnp.bfloat16)
        return jnp.einsum(
            "hqk,khd->qhd", probabilities, value_part, preferred_element_type=jnp.float32
        )

    mixed_heads = lax.map(
        one_group, (split_heads(queries), split_heads(keys_all), split_heads(values_all))
    )
    return mixed_heads.transpose(1, 0, 2, 3).reshape(row_count, model_width).astype(jnp.bfloat16)


def local(features, orders, norm_gains, qkv_weight, proj_weight, fc1_weight, fc2_weight):
    row_count, model_width = features.shape
    peers = lax.axis_size("pts")
    capacity = 3 * row_count // (2 * peers)
    state_rows = features
    for block_index in range(orders.shape[0]):
        slot_pos, received = routing(orders[block_index], row_count, peers, capacity)
        source_rows = jnp.minimum(received, row_count - 1)
        normed_local = layer_norm(state_rows, norm_gains[block_index, 0]).astype(jnp.bfloat16)
        arrived = lax.all_to_all(
            normed_local[source_rows], "pts", split_axis=0, concat_axis=0, tiled=True
        )
        mixed_heads = mix_heads(arrived[slot_pos], qkv_weight[block_index])
        returning = (
            jnp.zeros((peers * capacity, model_width), jnp.bfloat16).at[slot_pos].set(mixed_heads)
        )
        landed = lax.all_to_all(returning, "pts", split_axis=0, concat_axis=0, tiled=True)
        stored_mixed = (
            jnp.zeros((row_count, model_width), jnp.bfloat16).at[received].set(landed, mode="drop")
        )
        attended = state_rows + jnp.dot(
            stored_mixed, proj_weight[block_index], preferred_element_type=jnp.float32
        )
        state_rows = attended + feed_forward(
            attended, norm_gains[block_index, 1], fc1_weight[block_index], fc2_weight[block_index]
        )
    return state_rows


def solution(mesh):
    placed = (P(("slab", "pts"), None), P(None, ("slab", "pts")), P(), P(), P(), P(), P())
    return jax.shard_map(
        local, mesh=mesh, in_specs=placed, out_specs=P(("slab", "pts"), None), check_vma=False
    )
```

profile of v0, /device:TPU:0, one launch (start us, length us, event | category | flops | bytes accessed | tf_op | source)
XLA Modules:
  0.0 154.5 jit_solution(12804735705842227755)
XLA Ops:
  0.0 0.8 fusion.361
  0.8 0.6 reduce-window.14
  1.6 0.6 reduce-window.16
  2.7 0.8 compare_select_fusion.4
  3.4 1.4 scatter_custom_fusion
  4.8 0.7 all_to_all.48
  5.5 8.3 %all-to-all-start = ((s32[16,24,1]{1,2,0:T(1,128)}), s32[16,24,1]{1,2,0:T(1,128)S(1)}, u32[]{:S(2)}, u32[]{:S(2)}) async-start(s32[16,24,1]{1,2,0:T(1,128)} %bitcast.16), calls=%async_computation | async-start | bytes 16384 | tf_op jit(solution)/shard_map/all_to_all | solution.py:34
  13.9 0.8 fusion.360
  14.6 1.1 reduce_sum.114
  15.7 1.1 multiply_reduce_fusion.5
  16.8 1.1 multiply_convert_fusion.3
  17.9 3.1 %all-to-all-done = s32[16,24,1]{1,2,0:T(1,128)S(1)} async-done(((s32[16,24,1]{1,2,0:T(1,128)}), s32[16,24,1]{1,2,0:T(1,128)S(1)}, u32[]{:S(2)}, u32[]{:S(2)}) %all-to-all-start) | async-done | bytes 1568 | tf_op jit(solution)/shard_map/all_to_all | solution.py:34
  21.1 0.5 broadcast.919
  21.6 0.7 reduce.18
  22.4 2.6 %gather_fusion = bf16[384,256]{1,0:T(8,128)(2,1)} fusion(bf16[256,256]{1,0:T(8,128)(2,1)S(1)} %multiply_convert_fusion.3, s32[1024]{0:T(1024)S(1)} %pad_clamp_fusion.3), kind=kCustom, calls=%fused_computation | custom fusion | bytes 394752 | tf_op jit(solution)/shard_map/gather | solution.py:96
  24.9 3.9 %all-to-all-start.1 = ((bf16[16,24,256]{2,1,0:T(8,128)(2,1)}), bf16[16,24,256]{2,1,0:T(8,128)(2,1)S(1)}, u32[]{:S(2)}, u32[]{:S(2)}) async-start(bf16[16,24,256]{2,1,0:T(8,128)(2,1)} %bitcast.18), calls=%async_computation.1 | async-start | bytes 393216 | tf_op jit(solution)/shard_map/all_to_all | solution.py:95
  28.9 8.1 %all-to-all-done.1 = bf16[16,24,256]{2,1,0:T(8,128)(2,1)S(1)} async-done(((bf16[16,24,256]{2,1,0:T(8,128)(2,1)}), bf16[16,24,256]{2,1,0:T(8,128)(2,1)S(1)}, u32[]{:S(2)}, u32[]{:S(2)}) %all-to-all-start.1) | async-done | bytes 196640 | tf_op jit(solution)/shard_map/all_to_all | solution.py:95
  37.0 1.2 gather_fusion.1
  38.1 0.3 convolution_convert_fusion.1
  38.4 1.4 collective-permute-start
  39.8 5.0 %collective-permute-done = bf16[256,512]{1,0:T(8,128)(2,1)S(1)} collective-permute-done((bf16[256,512]{1,0:T(8,128)(2,1)S(1)}, bf16[256,512]{1,0:T(8,128)(2,1)S(1)}, u32[]{:S(2)}, u32[]{:S(2)}) %collective-permute-start) | collective-permute-done | bytes 262176 | tf_op jit(solution)/shard_map/ppermute | solution.py:17
  44.9 0.9 collective-permute-start.1
  45.8 1.4 scatter_custom_fusion.3
  47.2 0.7 all_to_all.57
  47.9 4.3 %all-to-all-start.3 = ((s32[16,24,1]{1,2,0:T(1,128)}), s32[16,24,1]{1,2,0:T(1,128)S(1)}, u32[]{:S(2)}, u32[]{:S(2)}) async-start(s32[16,24,1]{1,2,0:T(1,128)} %all_to_all.57), calls=%async_computation.3 | async-start | bytes 16384 | tf_op jit(solution)/shard_map/all_to_all | solution.py:34
  52.3 3.3 %collective-permute-done.1 = bf16[512,512]{1,0:T(8,128)(2,1)S(1)} collective-permute-done((bf16[512,512]{1,0:T(8,128)(2,1)S(1)}, bf16[512,512]{1,0:T(8,128)(2,1)S(1)}, u32[]{:S(2)}, u32[]{:S(2)}) %collective-permute-start.1) | collective-permute-done | bytes 524320 | tf_op jit(solution)/shard_map/ppermute | solution.py:17
  56.2 12.0 %while.20 = (s32[]{:T(128)}, bf16[4,256,4,16]{1,3,2,0:T(8,128)(2,1)S(1)}, bf16[4,1024,4,16]{1,3,2,0:T(8,128)(2,1)S(1)}, bf16[4,256,4,16]{1,3,2,0:T(8,128)(2,1)S(...) while((s32[]{:T(128)}, bf16[4,256,4,16]{1,3,2,0:T(8,128)(2,1)S(1)}, ...), condition=%wide.region_9.10_spmd, body=%wide.region_6.9_spmd.sunk | while | flops 108006400 | bytes 535621 | solution.py:80
  56.2 1.4 fusion.393
  57.7 1.6 %fusion.394 = bf16[4,256,4,16]{1,3,2,0:T(8,128)(2,1)S(1)} fusion(bf16[4,256,4,16]{1,3,2,0:T(8,128)(2,1)S(1)} %get-tuple-element.176, s32[]{:T(128)} %get-tuple-element.175, f32[4,256]{1,0:T(4,128)S(1)} %fusion.393, bf16[4,1024,4,16]{1,3,2,0:T(8,128)(2,1)S(1)} %get-tuple-element.183, bf16[4,1024,4,16]{1,3,2,0:T(8,128)(2,1)S(1)} %get-tuple-element.185, ...), kind=kOutput, calls=%fused_computation.18.clone.1 | convolution fusion | flops 71305216 | bytes 366592 | tf_op jit(solution)/shard_map/while/body/eval_jaxpr/hqk,khd->qhd/dot_general | solution.py:76
  59.2 1.4 fusion.393
  60.7 1.6 %fusion.394 = bf16[4,256,4,16]{1,3,2,0:T(8,128)(2,1)S(1)} fusion(bf16[4,256,4,16]{1,3,2,0:T(8,128)(2,1)S(1)} %get-tuple-element.176, s32[]{:T(128)} %get-tuple-element.175, f32[4,256]{1,0:T(4,128)S(1)} %fusion.393, bf16[4,1024,4,16]{1,3,2,0:T(8,128)(2,1)S(1)} %get-tuple-element.183, bf16[4,1024,4,16]{1,3,2,0:T(8,128)(2,1)S(1)} %get-tuple-element.185, ...), kind=kOutput, calls=%fused_computation.18.clone.1 | convolution fusion | flops 71305216 | bytes 366592 | tf_op jit(solution)/shard_map/while/body/eval_jaxpr/hqk,khd->qhd/dot_general | solution.py:76
  62.2 1.4 fusion.393
  63.7 1.6 %fusion.394 = bf16[4,256,4,16]{1,3,2,0:T(8,128)(2,1)S(1)} fusion(bf16[4,256,4,16]{1,3,2,0:T(8,128)(2,1)S(1)} %get-tuple-element.176, s32[]{:T(128)} %get-tuple-element.175, f32[4,256]{1,0:T(4,128)S(1)} %fusion.393, bf16[4,1024,4,16]{1,3,2,0:T(8,128)(2,1)S(1)} %get-tuple-element.183, bf16[4,1024,4,16]{1,3,2,0:T(8,128)(2,1)S(1)} %get-tuple-element.185, ...), kind=kOutput, calls=%fused_computation.18.clone.1 | convolution fusion | flops 71305216 | bytes 366592 | tf_op jit(solution)/shard_map/while/body/eval_jaxpr/hqk,khd->qhd/dot_general | solution.py:76
  65.2 1.4 fusion.393
  66.7 1.6 %fusion.394 = bf16[4,256,4,16]{1,3,2,0:T(8,128)(2,1)S(1)} fusion(bf16[4,256,4,16]{1,3,2,0:T(8,128)(2,1)S(1)} %get-tuple-element.176, s32[]{:T(128)} %get-tuple-element.175, f32[4,256]{1,0:T(4,128)S(1)} %fusion.393, bf16[4,1024,4,16]{1,3,2,0:T(8,128)(2,1)S(1)} %get-tuple-element.183, bf16[4,1024,4,16]{1,3,2,0:T(8,128)(2,1)S(1)} %get-tuple-element.185, ...), kind=kOutput, calls=%fused_computation.18.clone.1 | convolution fusion | flops 71305216 | bytes 366592 | tf_op jit(solution)/shard_map/while/body/eval_jaxpr/hqk,khd->qhd/dot_general | solution.py:76
  68.4 2.1 %scatter_custom_fusion.1 = bf16[384,256]{1,0:T(8,128)(2,1)} fusion(s32[256]{0:T(256)S(1)} %bitcast.295, bf16[256,256]{1,0:T(8,128)(2,1)S(1)} %copy.37, bf16[]{:T(256)} %constant.75.clone.1), kind=kCustom, calls=%fused_computation.206 | custom fusion | bytes 196610 | tf_op jit(solution)/shard_map/scatter | solution.py:100
  70.5 6.3 %all-to-all-start.2 = ((bf16[16,24,256]{2,1,0:T(8,128)(2,1)}), bf16[16,24,256]{2,1,0:T(8,128)(2,1)S(1)}, u32[]{:S(2)}, u32[]{:S(2)}) async-start(bf16[16,24,256]{2,1,0:T(8,128)(2,1)} %bitcast.29), calls=%async_computation.2 | async-start | bytes 393216 | tf_op jit(solution)/shard_map/all_to_all | solution.py:102
  77.0 0.7 reduce.19
  77.8 7.1 %all-to-all-done.2 = bf16[16,24,256]{2,1,0:T(8,128)(2,1)S(1)} async-done(((bf16[16,24,256]{2,1,0:T(8,128)(2,1)}), bf16[16,24,256]{2,1,0:T(8,128)(2,1)S(1)}, u32[]{:S(2)}, u32[]{:S(2)}) %all-to-all-start.2) | async-done | bytes 196640 | tf_op jit(solution)/shard_map/all_to_all | solution.py:102
  84.9 2.1 %scatter_custom_fusion.2 = bf16[256,256]{1,0:T(8,128)(2,1)S(1)} fusion(s32[384]{0:T(512)S(1)} %get-tuple-element.64, bf16[384,256]{1,0:T(8,128)(2,1)S(1)} %bitcast.280, bf16[]{:T(256)} %constant.75.clone.1), kind=kCustom, calls=%fused_computation.210 | custom fusion | bytes 131074 | tf_op jit(solution)/shard_map/scatter | solution.py:104
  87.4 4.0 %fusion.363 = (f32[256]{0:T(256)S(1)}, f32[256,256]{0,1:T(8,128)S(1)}) fusion(f32[256,256]{0,1:T(8,128)S(1)} %get-tuple-element.102, bf16[2,1024,256]{2,1,0:T(8,128)(2,1)S(1)} %copy-done.3, bf16[2,256,1024]{2,1,0:T(8,128)(2,1)} %param.16, f32[256]{0:T(256)S(1)} %bitcast.299, f32[256]{0:T(256)S(1)} %add_rsqrt_fusion.2, f32[256]{0:T(256)S(1)} %broadcast_multiply_fusion.2), kind=kOutput, calls=%fused_computation.355 | convolution fusion | flops 285867776 | bytes 1839104 | tf_op jit(solution)/shard_map/dot_general | solution.py:43
  91.6 2.6 %gather_fusion.2 = bf16[384,256]{1,0:T(8,128)(2,1)} fusion(bf16[256,256]{1,0:T(8,128)(2,1)S(1)} %copy.40, s32[1024]{0:T(1024)S(1)} %pad_clamp_fusion.1), kind=kCustom, calls=%fused_computation.2 | custom fusion | bytes 394752 | tf_op jit(solution)/shard_map/gather | solution.py:96
  94.2 3.5 %all-to-all-start.4 = ((bf16[16,24,256]{2,1,0:T(8,128)(2,1)}), bf16[16,24,256]{2,1,0:T(8,128)(2,1)S(1)}, u32[]{:S(2)}, u32[]{:S(2)}) async-start(bf16[16,24,256]{2,1,0:T(8,128)(2,1)} %bitcast.42), calls=%async_computation.4 | async-start | bytes 393216 | tf_op jit(solution)/shard_map/all_to_all | solution.py:95
  97.7 8.1 %all-to-all-done.4 = bf16[16,24,256]{2,1,0:T(8,128)(2,1)S(1)} async-done(((bf16[16,24,256]{2,1,0:T(8,128)(2,1)}), bf16[16,24,256]{2,1,0:T(8,128)(2,1)S(1)}, u32[]{:S(2)}, u32[]{:S(2)}) %all-to-all-start.4) | async-done | bytes 196640 | tf_op jit(solution)/shard_map/all_to_all | solution.py:95
  105.9 1.2 gather_fusion.3
  107.0 0.3 convolution_convert_fusion
  107.3 1.3 collective-permute-start.2
  108.6 5.1 %collective-permute-done.2 = bf16[256,512]{1,0:T(8,128)(2,1)S(1)} collective-permute-done((bf16[256,512]{1,0:T(8,128)(2,1)S(1)}, bf16[256,512]{1,0:T(8,128)(2,1)S(1)}, u32[]{:S(2)}, u32[]{:S(2)}) %collective-permute-start.2) | collective-permute-done | bytes 262176 | tf_op jit(solution)/shard_map/ppermute | solution.py:17
  113.8 0.9 collective-permute-start.3
  114.8 8.2 %collective-permute-done.3 = bf16[512,512]{1,0:T(8,128)(2,1)S(1)} collective-permute-done((bf16[512,512]{1,0:T(8,128)(2,1)S(1)}, bf16[512,512]{1,0:T(8,128)(2,1)S(1)}, u32[]{:S(2)}, u32[]{:S(2)}) %collective-permute-start.3) | collective-permute-done | bytes 524320 | tf_op jit(solution)/shard_map/ppermute | solution.py:17
  123.6 12.0 %while.21 = (s32[]{:T(128)}, bf16[4,256,4,16]{1,3,2,0:T(8,128)(2,1)S(1)}, bf16[4,1024,4,16]{1,3,2,0:T(8,128)(2,1)S(1)}, bf16[4,256,4,16]{1,3,2,0:T(8,128)(2,1)S(...) while((s32[]{:T(128)}, bf16[4,256,4,16]{1,3,2,0:T(8,128)(2,1)S(1)}, ...), condition=%wide.region_23.24_spmd, body=%wide.region_20.23_spmd.sunk | while | flops 108006400 | bytes 535621 | solution.py:80
  123.6 1.4 fusion.401
  125.1 1.6 %fusion.402 = bf16[4,256,4,16]{1,3,2,0:T(8,128)(2,1)S(1)} fusion(bf16[4,256,4,16]{1,3,2,0:T(8,128)(2,1)S(1)} %get-tuple-element.194, s32[]{:T(128)} %get-tuple-element.193, f32[4,256]{1,0:T(4,128)S(1)} %fusion.401, bf16[4,1024,4,16]{1,3,2,0:T(8,128)(2,1)S(1)} %get-tuple-element.201, bf16[4,1024,4,16]{1,3,2,0:T(8,128)(2,1)S(1)} %get-tuple-element.203, ...), kind=kOutput, calls=%fused_computation.45.clone.1 | convolution fusion | flops 71305216 | bytes 366592 | tf_op jit(solution)/shard_map/while/body/eval_jaxpr/hqk,khd->qhd/dot_general | solution.py:76
  126.6 1.4 fusion.401
  128.1 1.6 %fusion.402 = bf16[4,256,4,16]{1,3,2,0:T(8,128)(2,1)S(1)} fusion(bf16[4,256,4,16]{1,3,2,0:T(8,128)(2,1)S(1)} %get-tuple-element.194, s32[]{:T(128)} %get-tuple-element.193, f32[4,256]{1,0:T(4,128)S(1)} %fusion.401, bf16[4,1024,4,16]{1,3,2,0:T(8,128)(2,1)S(1)} %get-tuple-element.201, bf16[4,1024,4,16]{1,3,2,0:T(8,128)(2,1)S(1)} %get-tuple-element.203, ...), kind=kOutput, calls=%fused_computation.45.clone.1 | convolution fusion | flops 71305216 | bytes 366592 | tf_op jit(solution)/shard_map/while/body/eval_jaxpr/hqk,khd->qhd/dot_general | solution.py:76
  129.6 1.4 fusion.401
  131.1 1.6 %fusion.402 = bf16[4,256,4,16]{1,3,2,0:T(8,128)(2,1)S(1)} fusion(bf16[4,256,4,16]{1,3,2,0:T(8,128)(2,1)S(1)} %get-tuple-element.194, s32[]{:T(128)} %get-tuple-element.193, f32[4,256]{1,0:T(4,128)S(1)} %fusion.401, bf16[4,1024,4,16]{1,3,2,0:T(8,128)(2,1)S(1)} %get-tuple-element.201, bf16[4,1024,4,16]{1,3,2,0:T(8,128)(2,1)S(1)} %get-tuple-element.203, ...), kind=kOutput, calls=%fused_computation.45.clone.1 | convolution fusion | flops 71305216 | bytes 366592 | tf_op jit(solution)/shard_map/while/body/eval_jaxpr/hqk,khd->qhd/dot_general | solution.py:76
  132.6 1.4 fusion.401
  134.0 1.6 %fusion.402 = bf16[4,256,4,16]{1,3,2,0:T(8,128)(2,1)S(1)} fusion(bf16[4,256,4,16]{1,3,2,0:T(8,128)(2,1)S(1)} %get-tuple-element.194, s32[]{:T(128)} %get-tuple-element.193, f32[4,256]{1,0:T(4,128)S(1)} %fusion.401, bf16[4,1024,4,16]{1,3,2,0:T(8,128)(2,1)S(1)} %get-tuple-element.201, bf16[4,1024,4,16]{1,3,2,0:T(8,128)(2,1)S(1)} %get-tuple-element.203, ...), kind=kOutput, calls=%fused_computation.45.clone.1 | convolution fusion | flops 71305216 | bytes 366592 | tf_op jit(solution)/shard_map/while/body/eval_jaxpr/hqk,khd->qhd/dot_general | solution.py:76
  135.7 1.5 scatter_custom_fusion.4
  137.3 11.0 %all_to_all.72 = bf16[16,24,256]{2,1,0:T(8,128)(2,1)S(1)} all-to-all(bf16[16,24,256]{2,1,0:T(8,128)(2,1)S(1)} %bitcast.273), channel_id=1, replica_groups=mesh['pts'=16,'slab'=2] {'pts'}, dimensions={0} | all-to-all | bytes 393216 | tf_op jit(solution)/shard_map/all_to_all | solution.py:102
  148.3 2.1 %scatter_custom_fusion.5 = bf16[256,256]{1,0:T(8,128)(2,1)S(1)} fusion(s32[384]{0:T(512)S(1)} %get-tuple-element.62, bf16[384,256]{1,0:T(8,128)(2,1)S(1)} %bitcast.281, bf16[]{:T(256)} %constant.75.clone.1), kind=kCustom, calls=%fused_computation.208 | custom fusion | bytes 131074 | tf_op jit(solution)/shard_map/scatter | solution.py:104
  150.7 2.9 %convolution_add_fusion.2 = f32[256,256]{0,1:T(8,128)S(1)} fusion(f32[256,256]{0,1:T(8,128)S(1)} %get-tuple-element.106, bf16[2,1024,256]{2,1,0:T(8,128)(2,1)S(1)} %copy-done.3, bf16[2,256,1024]{2,1,0:T(8,128)(2,1)S(1)} %copy-done.4, f32[256]{0:T(256)S(1)} %bitcast.298, f32[256]{0:T(256)S(1)} %add_rsqrt_fusion, f32[256]{0:T(256)S(1)} %broadcast_multiply_fusion), kind=kOutput, calls=%fused_computation.70 | convolution fusion | flops 285802496 | bytes 1838080 | tf_op jit(solution)/shard_map/dot_general | solution.py:43
  153.7 0.8 copy.46
  (69 shorter events, 3.7 us)
Async XLA Ops:
  5.5 15.5 %all-to-all-start = ((s32[16,24,1]{1,2,0:T(1,128)}), s32[16,24,1]{1,2,0:T(1,128)S(1)}, u32[]{:S(2)}, u32[]{:S(2)}) async-start(s32[16,24,1]{1,2,0:T(1,128)} %bitcast.16), calls=%async_computation | async-start | bytes 16384 | tf_op jit(solution)/shard_map/all_to_all | solution.py:34
  24.9 13.2 %copy-start.1 = (bf16[2,256,768]{2,1,0:T(8,128)(2,1)S(1)}, bf16[2,256,768]{2,1,0:T(8,128)(2,1)}, u32[]{:S(2)}) copy-start(bf16[2,256,768]{2,1,0:T(8,128)(2,1)} %param.14) | copy-start | bytes 2359300
  24.9 12.0 %all-to-all-start.1 = ((bf16[16,24,256]{2,1,0:T(8,128)(2,1)}), bf16[16,24,256]{2,1,0:T(8,128)(2,1)S(1)}, u32[]{:S(2)}, u32[]{:S(2)}) async-start(bf16[16,24,256]{2,1,0:T(8,128)(2,1)} %bitcast.18), calls=%async_computation.1 | async-start | bytes 393216 | tf_op jit(solution)/shard_map/all_to_all | solution.py:95
  38.4 6.4 %collective-permute-start = (bf16[256,512]{1,0:T(8,128)(2,1)S(1)}, bf16[256,512]{1,0:T(8,128)(2,1)S(1)}, u32[]{:S(2)}, u32[]{:S(2)}) collective-permute-start(bf16[256,512]{1,0:T(8,128)(2,1)S(1)} %slice.113), channel_id=1, source_target_pairs={{0,2},{2,0},{4,6},{6,4},{8,10},{10,8},{12,14},{14,12},{16,18},{18,... | collective-permute-start | bytes 786440 | tf_op jit(solution)/shard_map/ppermute | solution.py:17
  44.9 10.7 %collective-permute-start.1 = (bf16[512,512]{1,0:T(8,128)(2,1)S(1)}, bf16[512,512]{1,0:T(8,128)(2,1)S(1)}, u32[]{:S(2)}, u32[]{:S(2)}) collective-permute-start(bf16[512,512]{1,0:T(8,128)(2,1)S(1)} %pad_maximum_fusion.2), channel_id=1, source_target_pairs={{0,4},{4,0},{2,6},{6,2},{8,12},{12,8},{10,14},{14,10},{16,20},{20,... | collective-permute-start | bytes 1572872 | tf_op jit(solution)/shard_map/ppermute | solution.py:17
  47.9 22.6 %all-to-all-start.3 = ((s32[16,24,1]{1,2,0:T(1,128)}), s32[16,24,1]{1,2,0:T(1,128)S(1)}, u32[]{:S(2)}, u32[]{:S(2)}) async-start(s32[16,24,1]{1,2,0:T(1,128)} %all_to_all.57), calls=%async_computation.3 | async-start | bytes 16384 | tf_op jit(solution)/shard_map/all_to_all | solution.py:34
  56.2 20.6 %copy-start = (f32[256,256]{1,0:T(8,128)S(1)}, f32[256,256]{1,0:T(8,128)}, u32[]{:S(2)}) copy-start(f32[256,256]{1,0:T(8,128)} %param.11) | copy-start | bytes 786436
  68.2 18.8 %copy-start.2 = (bf16[2,256,256]{2,1,0:T(8,128)(2,1)S(1)}, bf16[2,256,256]{2,1,0:T(8,128)(2,1)}, u32[]{:S(2)}) copy-start(bf16[2,256,256]{2,1,0:T(8,128)(2,1)} %param.15) | copy-start | bytes 786436
  70.5 16.9 %copy-start.3 = (bf16[2,1024,256]{2,1,0:T(8,128)(2,1)S(1)}, bf16[2,1024,256]{2,1,0:T(8,128)(2,1)}, u32[]{:S(2)}) copy-start(bf16[2,1024,256]{2,1,0:T(8,128)(2,1)} %param.17) | copy-start | bytes 3145732
  70.5 14.4 %all-to-all-start.2 = ((bf16[16,24,256]{2,1,0:T(8,128)(2,1)}), bf16[16,24,256]{2,1,0:T(8,128)(2,1)S(1)}, u32[]{:S(2)}, u32[]{:S(2)}) async-start(bf16[16,24,256]{2,1,0:T(8,128)(2,1)} %bitcast.29), calls=%async_computation.2 | async-start | bytes 393216 | tf_op jit(solution)/shard_map/all_to_all | solution.py:102
  94.2 11.7 %all-to-all-start.4 = ((bf16[16,24,256]{2,1,0:T(8,128)(2,1)}), bf16[16,24,256]{2,1,0:T(8,128)(2,1)S(1)}, u32[]{:S(2)}, u32[]{:S(2)}) async-start(bf16[16,24,256]{2,1,0:T(8,128)(2,1)} %bitcast.42), calls=%async_computation.4 | async-start | bytes 393216 | tf_op jit(solution)/shard_map/all_to_all | solution.py:95
  107.3 6.4 %collective-permute-start.2 = (bf16[256,512]{1,0:T(8,128)(2,1)S(1)}, bf16[256,512]{1,0:T(8,128)(2,1)S(1)}, u32[]{:S(2)}, u32[]{:S(2)}) collective-permute-start(bf16[256,512]{1,0:T(8,128)(2,1)S(1)} %slice.118), channel_id=1, source_target_pairs={{0,2},{2,0},{4,6},{6,4},{8,10},{10,8},{12,14},{14,12},{16,18},{18,... | collective-permute-start | bytes 786440 | tf_op jit(solution)/shard_map/ppermute | solution.py:17
  113.8 9.2 %collective-permute-start.3 = (bf16[512,512]{1,0:T(8,128)(2,1)S(1)}, bf16[512,512]{1,0:T(8,128)(2,1)S(1)}, u32[]{:S(2)}, u32[]{:S(2)}) collective-permute-start(bf16[512,512]{1,0:T(8,128)(2,1)S(1)} %pad_maximum_fusion.3), channel_id=1, source_target_pairs={{0,4},{4,0},{2,6},{6,2},{8,12},{12,8},{10,14},{14,10},{16,20},{20,... | collective-permute-start | bytes 1572872 | tf_op jit(solution)/shard_map/ppermute | solution.py:17
  135.6 15.1 %copy-start.4 = (bf16[2,256,1024]{2,1,0:T(8,128)(2,1)S(1)}, bf16[2,256,1024]{2,1,0:T(8,128)(2,1)}, u32[]{:S(2)}) copy-start(bf16[2,256,1024]{2,1,0:T(8,128)(2,1)} %param.16) | copy-start | bytes 3145732
where the time goes:
time: 155 us
  waiting for transfers between devices  48.2 us (31%)
  matrix products  31.9 us (21%)
  starting transfers between devices  30.9 us (20%)
  local copies, waits for them, and re-layouts  24.6 us (16%)
  blocking collectives  11 us (7%)
  other arithmetic  7.47 us (5%)
    ppermute x4, waiting for transfers between devices, from_partner(): return lax.ppermute(block, axis, route)  21.7 us
    all_to_all x2, waiting for transfers between devices, local(): lax.all_to_all(normed_local[source_rows], 'pts', split_axis=0, concat_axi...  16.2 us
    dot_general x8, matrix products, one_group(): jnp.einsum('hqk,khd->qhd', probabilities, value_part, preferred_element_t...  12.6 us
    all_to_all x2, starting transfers between devices, routing(): lax.all_to_all(request, 'pts', split_axis=0, concat_axis=0, tiled=True)  12.6 us
    sub x8, matrix products, one_group(): weights = jnp.exp(scores - row_peak)  11.4 us
    all_to_all x1, blocking collectives, local(): lax.all_to_all(returning, 'pts', split_axis=0, concat_axis=0, tiled=True)  11 us
    all_to_all x2, starting transfers between devices, local(): lax.all_to_all(normed_local[source_rows], 'pts', split_axis=0, concat_axi...  7.46 us
    all_to_all x1, waiting for transfers between devices, local(): lax.all_to_all(returning, 'pts', split_axis=0, concat_axis=0, tiled=True)  7.14 us
  transfers between devices with their start and end apart: 9, of which 8 were waited for; matrix products, arithmetic and copies ran while one was open for 14% of the time, Pallas kernels for 0%

commit v1 on v0

--- a/solution.py
+++ b/solution.py
@@ -1,10 +1,319 @@
+import functools
+
 import jax
 import jax.numpy as jnp
 from jax import lax
+from jax.experimental import pallas as pl
+from jax.experimental.pallas import tpu as pltpu
 from jax.sharding import PartitionSpec as P
 
 HEADS = 16
 PATCH = 1024
+BF16, F32, I32 = jnp.bfloat16, jnp.float32, jnp.int32
+NT = (((1,), (1,)), ((), ()))
+TN = (((0,), (0,)), ((), ()))
+VMEM = pltpu.VMEM
+SMEM = pltpu.SMEM
+
+
+def layer_norm(values, gain_row):
+    center = values - jnp.mean(values, axis=1, keepdims=True)
+    spread = jnp.mean(center * center, axis=1, keepdims=True)
+    return center * lax.rsqrt(spread + 1e-05) * gain_row
+
+
+def matmul(a, b, dims=(((1,), (0,)), ((), ()))):
+    return lax.dot_general(a, b, dims, preferred_element_type=F32)
+
+
+def iota(shape, axis):
+    return lax.broadcasted_iota(I32, shape, axis)
+
+
+def ones_where(mask):
+    return jnp.where(mask, 1.0, 0.0).astype(BF16)
+
+
+def earlier_mask(count):
+    return ones_where(iota((count, count), 0) < iota((count, count), 1))
+
+
+def as_index(row):
+    return row.astype(I32)
+
+
+def slot_rows(members, ranks):
+    return jnp.where(members > 0.5, ranks, -1.0)
+
+
+class Plan:
+    def __init__(self, row_count, peers, width):
+        self.rows, self.peers, self.width = row_count, peers, width
+        self.group = PATCH // row_count
+        self.lines = peers // self.group
+        self.base = row_count // (2 * peers)
+        self.cap = 3 * self.base * self.group
+        self.held = self.cap * self.lines
+
+    def fits(self):
+        return (
+            self.group == 4
+            and self.lines == 4
+            and self.rows == self.width == 256
+            and self.base % 8 == 0
+        )
+
+
+def kernel_call(body, outs, in_specs, scratch=()):
+    return pl.pallas_call(
+        body,
+        out_shape=outs,
+        in_specs=in_specs,
+        out_specs=[pl.BlockSpec(memory_space=VMEM)] * len(outs),
+        scratch_shapes=list(scratch),
+        compiler_params=pltpu.CompilerParams(vmem_limit_bytes=40 * 2**20),
+    )
+
+
+def whole():
+    return pl.BlockSpec(memory_space=VMEM)
+
+
+def scalars():
+    return pl.BlockSpec(memory_space=SMEM)
+
+
+def open_body(plan, place, feature_ref, order_ref, gain_ref, normed_ref, *note_refs):
+    normed_ref[...] = layer_norm(feature_ref[...], gain_ref[0, 0:1, :]).astype(BF16)
+    line, column = place[0], place[1]
+    bits = plan.rows.bit_length() - 1
+    entry = iota((32, 1), 0)
+    notes = [None] * plan.group
+    for b in range(order_ref.shape[0]):
+        order_row = order_ref[b : b + 1, :]
+        owner = order_row >> bits
+        within = order_row & (plan.rows - 1)
+        inside = ones_where(iota((plan.rows, 1), 0) == within)
+        picks = []
+        for k in range(plan.group):
+            target = column ^ k
+            member = entry - 8 * b
+            stored = jnp.where(
+                (member >= 0) & (member < plan.lines), (member ^ line) * plan.group + target, -1
+            )
+            other = entry - 16
+            counted = ((other & 3) ^ line) * plan.group + (target ^ (other >> 2))
+            picks.append(ones_where(owner == jnp.where(other >= 0, counted, stored)))
+        pick = jnp.concatenate(picks, axis=0)
+        found = matmul(pick, inside, NT)
+        counts = jnp.sum(found, axis=1, keepdims=True)
+        lane = iota((1, plan.width), 1)
+        rowid = iota((32 * plan.group, 1), 0) & 31
+        mine = (lane >= 128 * b) & (lane < 128 * (b + 1))
+        part = jnp.where(rowid < 16, found, jnp.where(mine, counts, 0.0))
+        notes = part if b == 0 else notes + part
+    for k in range(plan.group):
+        note_refs[k][...] = notes[32 * k : 32 * (k + 1)].astype(BF16)
+
+
+def first_pack_body(plan, *refs):
+    row_refs, note_refs = refs[:4], refs[4:8]
+    packed_ref, count_ref, member_ref = refs[8:]
+    total = sum(r[...].astype(F32) for r in note_refs)
+    members = total[:16]
+    member_ref[...] = members.astype(BF16)
+    count_ref[...] = jnp.concatenate([total[16:, :64], total[16:, 128:192]], axis=1).astype(I32)
+    ranks = matmul(members.astype(BF16), earlier_mask(plan.rows))
+    slot = iota((plan.held, 1), 0).astype(F32)
+    offset = jnp.zeros((1, 1), F32)
+    out = jnp.zeros((plan.held, plan.width), F32)
+    for j in range(plan.lines):
+        row = members[j : j + 1]
+        where = jnp.where(row > 0.5, ranks[j : j + 1] + offset, -1.0)
+        out = out + matmul(ones_where(slot == where), row_refs[j][...])
+        offset = offset + jnp.sum(row, axis=1, keepdims=True)
+    packed_ref[...] = out.astype(BF16)
+
+
+def pack_body(plan, b, count_ref, *refs):
+    piece_refs, packed_ref, room = refs[:4], refs[4], refs[5]
+    room[...] = jnp.zeros(room.shape, room.dtype)
+    offset = 0
+    for j in range(plan.lines):
+        room[pl.ds(pl.multiple_of(offset, 16), plan.cap), :] = piece_refs[j][...]
+        offset = offset + count_ref[j, 64 * b]
+    packed_ref[...] = room[0 : plan.held]
+
+
+def attend_body(plan, b, with_notes, count_ref, *refs):
+    group, lines, held, cap, width = plan.group, plan.lines, plan.held, plan.cap, plan.width
+    part_refs, weight_ref = refs[:group], refs[group]
+    refs = refs[group + 1 :]
+    if with_notes:
+        member_ref, refs = refs[0], refs[1:]
+    out_refs, (all_rows, keys, values, queries, mixed) = refs[:lines], refs[lines:]
+    head_size = width // HEADS
+    offset = 0
+    for k in range(group):
+        all_rows[pl.ds(pl.multiple_of(offset, 16), held), :] = part_refs[k][...]
+        for j in range(lines):
+            offset = offset + count_ref[k * lines + j, 64 * b]
+    patch_rows = all_rows[0:PATCH]
+    keys[...] = matmul(patch_rows, weight_ref[b, :, width : 2 * width]).astype(BF16)
+    values[...] = matmul(patch_rows, weight_ref[b, :, 2 * width :]).astype(BF16)
+    scaled = matmul(part_refs[0][...], weight_ref[b, :, :width]).astype(BF16) * (head_size**-0.5)
+    queries[...] = scaled.astype(BF16)
+    mixed[...] = jnp.zeros(mixed.shape, mixed.dtype)
+    own = 0
+    offsets = []
+    for j in range(lines):
+        offsets.append(own)
+        own = own + count_ref[j, 64 * b]
+    head_mask = iota((HEADS, 1, width), 0) == iota((HEADS, 1, width), 2) // head_size
+
+    def sixteen(start):
+        block = queries[pl.ds(start, 16), :]
+        spread = jnp.where(head_mask, block[None], jnp.zeros((), BF16)).reshape(HEADS * 16, width)
+        scores = matmul(spread, keys[...], NT)
+        weights = jnp.exp(scores - jnp.max(scores, axis=1, keepdims=True))
+        total = jnp.sum(weights, axis=1, keepdims=True)
+        summed = matmul(weights.astype(BF16), values[...]) / total
+        kept = jnp.where(head_mask, summed.reshape(HEADS, 16, width), 0.0)
+        mixed[pl.ds(start, 16), :] = jnp.sum(kept, axis=0).astype(BF16)
+
+    def step(i, carry):
+        start = pl.multiple_of(i * 32, 32)
+        sixteen(start)
+        sixteen(pl.multiple_of(start + 16, 16))
+        return carry
+
+    lax.fori_loop(0, (own + 31) // 32, step, 0)
+    for j in range(lines):
+        out_refs[j][0:cap, :] = mixed[pl.ds(pl.multiple_of(offsets[j], 16), cap), :]
+        if with_notes:
+            entry = iota((16, 1), 0)
+            now = member_ref[j : j + 1, :].astype(F32)
+            later = member_ref[8 + j : 9 + j, :].astype(F32)
+            note = jnp.where(entry == 0, now, jnp.where(entry == 1, later, 0.0))
+            out_refs[j][cap : cap + 16, :] = note.astype(BF16)
+
+
+def store_body(plan, b, last, *refs):
+    lines, cap, rows = plan.lines, plan.cap, plan.rows
+    piece_refs, refs = refs[:lines], refs[lines:]
+    if b:
+        note_refs, refs = refs[:lines], refs[lines:]
+    else:
+        note_refs = piece_refs
+    state_ref, gain_ref, proj_ref, fc1_ref, fc2_ref = refs[:5]
+    refs = refs[5:]
+    state_out, send_refs = refs[0], refs[1:]
+    notes = [r[cap : cap + 16, :].astype(F32) for r in note_refs]
+    members = jnp.concatenate(notes, axis=0)
+    ranks = matmul(members.astype(BF16), earlier_mask(rows))
+    slot = iota((cap, 1), 0).astype(F32)
+
+    def places(j, block):
+        at = 16 * j + block
+        where = jnp.where(members[at : at + 1] > 0.5, ranks[at : at + 1], -1.0)
+        return ones_where(slot == where)
+
+    where_from = jnp.concatenate([places(j, b) for j in range(lines)], axis=0)
+    pieces = jnp.concatenate([r[0:cap, :] for r in piece_refs], axis=0)
+    mixed = matmul(where_from, pieces, TN).astype(BF16)
+    attended = state_ref[...] + matmul(mixed, proj_ref[b])
+    normed_two = layer_norm(attended, gain_ref[b, 1:2, :]).astype(BF16)
+    hidden = matmul(normed_two, fc1_ref[b])
+    expanded = (0.5 * hidden * (1.0 + lax.erf(hidden * (0.5**0.5)))).astype(BF16)
+    state = attended + matmul(expanded, fc2_ref[b])
+    state_out[...] = state
+    if not last:
+        normed = layer_norm(state, gain_ref[b + 1, 0:1, :]).astype(BF16)
+        for j in range(lines):
+            send_refs[j][...] = matmul(places(j, b + 1), normed).astype(BF16)
+
+
+def flip(block, count, bit):
+    return lax.ppermute(block, "pts", [(i, i ^ bit) for i in range(count)])
+
+
+def struct(shape, dtype):
+    return jax.ShapeDtypeStruct(shape, dtype)
+
+
+def by_lines(plan, features, orders, norm_gains, qkv_weight, proj_weight, fc1_weight, fc2_weight):
+    rows, width, peers = plan.rows, plan.width, plan.peers
+    group, lines, held, cap = plan.group, plan.lines, plan.held, plan.cap
+    blocks = orders.shape[0]
+    me = lax.axis_index("pts")
+    place = jnp.stack([me // group, me % group]).astype(I32)
+
+    def along_line(pieces):
+        return [pieces[0]] + [flip(pieces[j], peers, group * j) for j in range(1, lines)]
+
+    def in_group(piece):
+        return [piece] + [flip(piece, peers, k) for k in range(1, group)]
+
+    opened = kernel_call(
+        functools.partial(open_body, plan),
+        [struct((rows, width), BF16)] + [struct((32, width), BF16)] * group,
+        [scalars(), whole(), whole(), whole()],
+    )(place, features, orders, norm_gains)
+    normed, notes = opened[0], opened[1:]
+    line_rows = along_line([normed] * lines)
+    notes = [notes[0]] + [flip(notes[k], peers, k) for k in range(1, group)]
+    packed, counts, members = kernel_call(
+        functools.partial(first_pack_body, plan),
+        [struct((held, width), BF16), struct((16, 128), I32), struct((16, width), BF16)],
+        [whole()] * (lines + group),
+    )(*line_rows, *notes)
+    state = features
+    for b in range(blocks):
+        last = b == blocks - 1
+        tall = cap if b else cap + 16
+        parts = in_group(packed)
+        extra = [] if b else [members]
+        mixed = kernel_call(
+            functools.partial(attend_body, plan, b, b == 0),
+            [struct((tall, width), BF16)] * lines,
+            [scalars()] + [whole()] * (group + 1 + len(extra)),
+            [
+                pltpu.VMEM((PATCH + held, width), BF16),
+                pltpu.VMEM((PATCH, width), BF16),
+                pltpu.VMEM((PATCH, width), BF16),
+                pltpu.VMEM((held, width), BF16),
+                pltpu.VMEM((held + cap, width), BF16),
+            ],
+        )(counts, *parts, qkv_weight, *extra)
+        pieces = along_line(mixed)
+        if b == 0:
+            kept = pieces
+        outs = [struct((rows, width), F32)]
+        if not last:
+            outs += [struct((cap, width), BF16)] * lines
+        stored = kernel_call(
+            functools.partial(store_body, plan, b, last),
+            outs,
+            [whole()] * (lines * (2 if b else 1) + 5),
+        )(
+            *pieces,
+            *(kept if b else []),
+            state,
+            norm_gains,
+            proj_weight,
+            fc1_weight,
+            fc2_weight,
+        )
+        state = stored[0]
+        if not last:
+            arrived = along_line(stored[1:])
+            (packed,) = kernel_call(
+                functools.partial(pack_body, plan, b + 1),
+                [struct((held, width), BF16)],
+                [scalars()] + [whole()] * lines,
+                [pltpu.VMEM((held + cap, width), BF16)],
+            )(counts, *arrived)
+    return state
 
 
 def from_partner(block, axis, bit):
@@ -15,12 +324,6 @@
         if high != low and high < count:
             route += [(low, high), (high, low)]
     return lax.ppermute(block, axis, route)
-
-
-def layer_norm(values, gain_row):
-    center = values - jnp.mean(values, axis=1, keepdims=True)
-    spread = jnp.mean(center * center, axis=1, keepdims=True)
-    return center * lax.rsqrt(spread + 1e-05) * gain_row
 
 
 def routing(order_row, row_count, peers, capacity):
@@ -83,7 +386,7 @@
     return mixed_heads.transpose(1, 0, 2, 3).reshape(row_count, model_width).astype(jnp.bfloat16)
 
 
-def local(features, orders, norm_gains, qkv_weight, proj_weight, fc1_weight, fc2_weight):
+def by_request(features, orders, norm_gains, qkv_weight, proj_weight, fc1_weight, fc2_weight):
     row_count, model_width = features.shape
     peers = lax.axis_size("pts")
     capacity = 3 * row_count // (2 * peers)
@@ -112,6 +415,13 @@
     return state_rows
 
 
+def local(*arrays):
+    row_count, model_width = arrays[0].shape
+    peers = lax.axis_size("pts")
+    plan = Plan(row_count, peers, model_width)
+    return by_lines(plan, *arrays) if plan.fits() else by_request(*arrays)
+
+
 def solution(mesh):
     placed = (P(("slab", "pts"), None), P(None, ("slab", "pts")), P(), P(), P(), P(), P())
     return jax.shard_map(

time: 155 us -> 94.4 us (0.61)
  matrix products: 31.9 us -> 0 us
  Pallas kernels: 0 us -> 28.4 us
  local copies, waits for them, and re-layouts: 24.6 us -> 3.66 us
  waiting for transfers between devices: 48.2 us -> 29.9 us
  blocking collectives: 11 us -> 0 us
  other arithmetic: 7.47 us -> 0.07 us
    pallas_call x0 -> x7, Pallas kernels: none -> 28.4 us  [the longest x2 22.6 us: by_lines(): kernel_call(functools.partial(attend_body, plan, b, b == 0), [struct((tal...]
    ppermute x4 -> x21, starting transfers between devices: 4.47 us -> 31.9 us  [flip(): return lax.ppermute(block, 'pts', [(i, i ^ bit) for i in range(count)])]
    all_to_all x5 -> x0, waiting for transfers between devices: 26.4 us -> none  [the longest x2 16.2 us: local(): lax.all_to_all(normed_local[source_rows], 'pts', split_axis=0, concat_axi...]
    all_to_all x5 -> x0, starting transfers between devices: 26.4 us -> none  [the longest x2 12.6 us: routing(): lax.all_to_all(request, 'pts', split_axis=0, concat_axis=0, tiled=True)]
    dot_general x14 -> x0, matrix products: 20.5 us -> none  [the longest x8 12.6 us: one_group(): jnp.einsum('hqk,khd->qhd', probabilities, value_part, preferred_element_t...]
    sub x8 -> x0, matrix products: 11.4 us -> none  [one_group(): weights = jnp.exp(scores - row_peak)]
    all_to_all x1 -> x0, blocking collectives: 11 us -> none  [local(): lax.all_to_all(returning, 'pts', split_axis=0, concat_axis=0, tiled=True)]
    scatter x6 -> x0, local copies, waits for them, and re-layouts: 10.6 us -> none  [the longest x2 4.22 us: local(): jnp.zeros((row_count, model_width), jnp.bfloat16).at[received]]
  transfers between devices with their start and end apart: 9 -> 21, of which waited for: 8 -> 15; matrix products, arithmetic and copies ran while one was open for 14% -> 0% of each run, Pallas kernels for 0% -> 0%
where the time goes in v1:
time: 94.4 us; the launch traced here: 94.1 us
  starting transfers between devices  31.9 us (34%)
  waiting for transfers between devices  29.9 us (32%)
  Pallas kernels  28.4 us (30%)
  local copies, waits for them, and re-layouts  3.66 us (4%)
    ppermute x21, starting transfers between devices, flip(): return lax.ppermute(block, 'pts', [(i, i ^ bit) for i in range(count)])  31.9 us
    ppermute x21, waiting for transfers between devices, flip(): return lax.ppermute(block, 'pts', [(i, i ^ bit) for i in range(count)])  29.9 us
    pallas_call x2, Pallas kernels, by_lines(): kernel_call(functools.partial(attend_body, plan, b, b == 0), [struct((tal...  22.6 us
    unnamed x18, local copies, waits for them, and re-layouts  3.66 us
    pallas_call x2, Pallas kernels, by_lines(): kernel_call(functools.partial(store_body, plan, b, last), outs, [whole()]...  3.63 us
  transfers between devices with their start and end apart: 21, of which 15 were waited for; matrix products, arithmetic and copies ran while one was open for 0% of the time, Pallas kernels for 0%

profile of v1, /device:TPU:0, one launch (start us, length us, event | category | flops | bytes accessed | tf_op | source)
XLA Modules:
  0.0 94.1 jit_solution(15764450776899312838)
XLA Ops:
  0.0 0.0 copy-start.7
  0.0 0.0 copy-start.8
  0.0 0.1 pad_add_fusion.place
  0.1 0.6 copy-done.7
  0.7 0.0 copy-done.8
  0.7 0.0 copy-start.5
  0.7 0.9 %copy-done.5 = f32[256,256]{1,0:T(8,128)S(1)} copy-done((f32[256,256]{1,0:T(8,128)S(1)}, f32[256,256]{1,0:T(8,128)}, u32[]{:S(2)}) %copy-start.5) | copy-done | bytes 262168
  1.6 0.0 copy-start.4
  1.7 0.9 shard_map.73
  2.5 5.1 %collective-permute-start.2 = (bf16[256,256]{1,0:T(8,128)(2,1)S(1)}, bf16[256,256]{1,0:T(8,128)(2,1)S(1)}, u32[]{:S(2)}, u32[]{:S(2)}) collective-permute-start(bf16[256,256]{1,0:T(8,128)(2,1)S(1)} %get-tuple-element.26.refs_0_), channel_id=1, source_target_pairs={{0,24},{2,26},{4,28},{6,30},{8,16},{10,18},{12,20},{14,22},{16,8},... | collective-permute-start | bytes 393224 | tf_op jit(solution)/shard_map/ppermute | solution.py:237
  7.6 0.0 collective-permute-start.1
  7.7 0.6 collective-permute-start
  8.3 1.6 %collective-permute-start.3 = (bf16[32,256]{1,0:T(8,128)(2,1)S(1)}, bf16[32,256]{1,0:T(8,128)(2,1)S(1)}, u32[]{:S(2)}, u32[]{:S(2)}) collective-permute-start(bf16[32,256]{1,0:T(8,128)(2,1)S(1)} %get-tuple-element.28), channel_id=1, source_target_pairs={{0,2},{2,0},{4,6},{6,4},{8,10},{10,8},{12,14},{14,12},{16,18},{18,... | collective-permute-start | bytes 49160 | tf_op jit(solution)/shard_map/ppermute | solution.py:237
  9.9 1.5 %collective-permute-start.4 = (bf16[32,256]{1,0:T(8,128)(2,1)S(1)}, bf16[32,256]{1,0:T(8,128)(2,1)S(1)}, u32[]{:S(2)}, u32[]{:S(2)}) collective-permute-start(bf16[32,256]{1,0:T(8,128)(2,1)S(1)} %get-tuple-element.29), channel_id=1, source_target_pairs={{0,4},{2,6},{4,0},{6,2},{8,12},{10,14},{12,8},{14,10},{16,20},{18,... | collective-permute-start | bytes 49160 | tf_op jit(solution)/shard_map/ppermute | solution.py:237
  11.4 0.6 collective-permute-done.3.refs_5_
  12.0 2.6 %collective-permute-start.5 = (bf16[32,256]{1,0:T(8,128)(2,1)S(1)}, bf16[32,256]{1,0:T(8,128)(2,1)S(1)}, u32[]{:S(2)}, u32[]{:S(2)}) collective-permute-start(bf16[32,256]{1,0:T(8,128)(2,1)S(1)} %get-tuple-element.30), channel_id=1, source_target_pairs={{0,6},{2,4},{4,2},{6,0},{8,14},{10,12},{12,10},{14,8},{16,22},{18,... | collective-permute-start | bytes 49160 | tf_op jit(solution)/shard_map/ppermute | solution.py:237
  14.6 0.0 collective-permute-done.4.refs_6_
  14.6 2.0 %collective-permute-done.5.refs_7_ = bf16[32,256]{1,0:T(8,128)(2,1)S(1)} collective-permute-done((bf16[32,256]{1,0:T(8,128)(2,1)S(1)}, bf16[32,256]{1,0:T(8,128)(2,1)S(1)}, u32[]{:S(2)}, u32[]{:S(2)}) %collective-permute-start.5) | collective-permute-done | bytes 16416 | tf_op jit(solution)/shard_map/ppermute | solution.py:237
  16.7 0.0 collective-permute-done.2.refs_3_
  16.7 2.0 %collective-permute-done.1.refs_2_ = bf16[256,256]{1,0:T(8,128)(2,1)S(1)} collective-permute-done((bf16[256,256]{1,0:T(8,128)(2,1)S(1)}, bf16[256,256]{1,0:T(8,128)(2,1)S(1)}, u32[]{:S(2)}, u32[]{:S(2)}) %collective-permute-start.1) | collective-permute-done | bytes 131104 | tf_op jit(solution)/shard_map/ppermute | solution.py:237
  18.7 0.0 collective-permute-done.refs_1_
  18.7 0.5 shard_map.74
  19.3 2.5 %collective-permute-start.8 = (bf16[384,256]{1,0:T(8,128)(2,1)S(1)}, bf16[384,256]{1,0:T(8,128)(2,1)S(1)}, u32[]{:S(2)}, u32[]{:S(2)}) collective-permute-start(bf16[384,256]{1,0:T(8,128)(2,1)S(1)} %get-tuple-element.32.refs_0_), channel_id=1, source_target_pairs={{0,6},{2,4},{4,2},{6,0},{8,14},{10,12},{12,10},{14,8},{16,22},{18,... | collective-permute-start | bytes 589832 | tf_op jit(solution)/shard_map/ppermute | solution.py:237
  21.8 0.5 collective-permute-start.7
  22.3 0.5 collective-permute-start.6
  22.8 5.1 %collective-permute-done.8.refs_3_ = bf16[384,256]{1,0:T(8,128)(2,1)S(1)} collective-permute-done((bf16[384,256]{1,0:T(8,128)(2,1)S(1)}, bf16[384,256]{1,0:T(8,128)(2,1)S(1)}, u32[]{:S(2)}, u32[]{:S(2)}) %collective-permute-start.8) | collective-permute-done | bytes 196640 | tf_op jit(solution)/shard_map/ppermute | solution.py:237
  28.0 2.5 %collective-permute-done.7.refs_2_ = bf16[384,256]{1,0:T(8,128)(2,1)S(1)} collective-permute-done((bf16[384,256]{1,0:T(8,128)(2,1)S(1)}, bf16[384,256]{1,0:T(8,128)(2,1)S(1)}, u32[]{:S(2)}, u32[]{:S(2)}) %collective-permute-start.7) | collective-permute-done | bytes 196640 | tf_op jit(solution)/shard_map/ppermute | solution.py:237
  30.4 0.1 collective-permute-done.6.refs_1_
  30.5 1.1 %copy-done.2 = bf16[2,256,768]{2,1,0:T(8,128)(2,1)S(1)} copy-done((bf16[2,256,768]{2,1,0:T(8,128)(2,1)S(1)}, bf16[2,256,768]{2,1,0:T(8,128)(2,1)}, u32[]{:S(2)}) %copy-start.2) | copy-done | bytes 786456
  31.6 11.3 %shard_map.75 = (bf16[112,256]{1,0:T(8,128)(2,1)S(1)}, bf16[112,256]{1,0:T(8,128)(2,1)S(1)}, bf16[112,256]{1,0:T(8,128)(2,1)S(1)}, bf16[112,256]{1,0:T(8,128)(2,1)S(1)}) custom-call(s32[16,128]{1,0:T(8,128)S(1)} %get-tuple-element.31.count_ref, bf16[384,256]{1,0:T(8,128)(2,1)S(1)} %get-tuple-element.32.refs_0_, ...), custom_call_target="tpu_custom_call" | custom-call | tf_op jit(solution)/shard_map/pallas_call | solution.py:276
  43.0 0.1 collective-permute-start.9
  43.1 2.8 %collective-permute-start.10 = (bf16[112,256]{1,0:T(8,128)(2,1)S(1)}, bf16[112,256]{1,0:T(8,128)(2,1)S(1)}, u32[]{:S(2)}, u32[]{:S(2)}) collective-permute-start(bf16[112,256]{1,0:T(8,128)(2,1)S(1)} %get-tuple-element.36), channel_id=1, source_target_pairs={{0,16},{2,18},{4,20},{6,22},{8,24},{10,26},{12,28},{14,30},{16,0},... | collective-permute-start | bytes 172040 | tf_op jit(solution)/shard_map/ppermute | solution.py:237
  45.9 1.5 %collective-permute-start.11 = (bf16[112,256]{1,0:T(8,128)(2,1)S(1)}, bf16[112,256]{1,0:T(8,128)(2,1)S(1)}, u32[]{:S(2)}, u32[]{:S(2)}) collective-permute-start(bf16[112,256]{1,0:T(8,128)(2,1)S(1)} %get-tuple-element.37), channel_id=1, source_target_pairs={{0,24},{2,26},{4,28},{6,30},{8,16},{10,18},{12,20},{14,22},{16,8},... | collective-permute-start | bytes 172040 | tf_op jit(solution)/shard_map/ppermute | solution.py:237
  47.4 0.0 collective-permute-done.9.refs_1_.refs_5_
  47.4 1.5 %collective-permute-done.10.refs_2_.refs_6_ = bf16[112,256]{1,0:T(8,128)(2,1)S(1)} collective-permute-done((bf16[112,256]{1,0:T(8,128)(2,1)S(1)}, bf16[112,256]{1,0:T(8,128)(2,1)S(1)}, u32[]{:S(2)}, u32[]{:S(2)}) %collective-permute-start.10) | collective-permute-done | bytes 57376 | tf_op jit(solution)/shard_map/ppermute | solution.py:237
  49.0 2.9 %collective-permute-done.11.refs_3_.refs_7_ = bf16[112,256]{1,0:T(8,128)(2,1)S(1)} collective-permute-done((bf16[112,256]{1,0:T(8,128)(2,1)S(1)}, bf16[112,256]{1,0:T(8,128)(2,1)S(1)}, u32[]{:S(2)}, u32[]{:S(2)}) %collective-permute-start.11) | collective-permute-done | bytes 57376 | tf_op jit(solution)/shard_map/ppermute | solution.py:237
  51.9 0.0 copy-done.4
  51.9 0.0 copy-done
  51.9 0.0 copy-done.1
  51.9 0.0 copy-start.6
  51.9 0.9 copy-done.6
  52.8 1.7 %shard_map.76 = (f32[256,256]{1,0:T(8,128)S(1)}, bf16[96,256]{1,0:T(8,128)(2,1)S(1)}, bf16[96,256]{1,0:T(8,128)(2,1)S(1)}, bf16[96,256]{1,0:T(8,128)(2,1)S(1)}, bf16[96,256]{1,0:T(8,128)(2,1)S(1)}) custom-call(bf16[112,256]{1,0:T(8,128)(2,1)S(1)} %get-tuple-element.34.refs_0_.refs_4_, bf16[112,256]{1,0:T(8,128)(2,1)S(1)} %collective-permute-done.9.refs_1_.refs_5_, ...), custom_call_target="tpu_custom_call" | custom-call | tf_op jit(solution)/shard_map/pallas_call | solution.py:294
  54.5 0.1 collective-permute-start.12
  54.6 2.1 %collective-permute-start.13 = (bf16[96,256]{1,0:T(8,128)(2,1)S(1)}, bf16[96,256]{1,0:T(8,128)(2,1)S(1)}, u32[]{:S(2)}, u32[]{:S(2)}) collective-permute-start(bf16[96,256]{1,0:T(8,128)(2,1)S(1)} %get-tuple-element.40), channel_id=1, source_target_pairs={{0,16},{2,18},{4,20},{6,22},{8,24},{10,26},{12,28},{14,30},{16,0},... | collective-permute-start | bytes 147464 | tf_op jit(solution)/shard_map/ppermute | solution.py:237
  56.7 2.3 %collective-permute-start.14 = (bf16[96,256]{1,0:T(8,128)(2,1)S(1)}, bf16[96,256]{1,0:T(8,128)(2,1)S(1)}, u32[]{:S(2)}, u32[]{:S(2)}) collective-permute-start(bf16[96,256]{1,0:T(8,128)(2,1)S(1)} %get-tuple-element.41), channel_id=1, source_target_pairs={{0,24},{2,26},{4,28},{6,30},{8,16},{10,18},{12,20},{14,22},{16,8},... | collective-permute-start | bytes 147464 | tf_op jit(solution)/shard_map/ppermute | solution.py:237
  59.0 0.0 collective-permute-done.12.refs_1_
  59.0 0.8 collective-permute-done.13.refs_2_
  59.7 2.8 %collective-permute-done.14.refs_3_ = bf16[96,256]{1,0:T(8,128)(2,1)S(1)} collective-permute-done((bf16[96,256]{1,0:T(8,128)(2,1)S(1)}, bf16[96,256]{1,0:T(8,128)(2,1)S(1)}, u32[]{:S(2)}, u32[]{:S(2)}) %collective-permute-start.14) | collective-permute-done | bytes 49184 | tf_op jit(solution)/shard_map/ppermute | solution.py:237
  62.6 0.7 shard_map.77.refs_0_
  63.3 1.7 %collective-permute-start.17 = (bf16[384,256]{1,0:T(8,128)(2,1)S(1)}, bf16[384,256]{1,0:T(8,128)(2,1)S(1)}, u32[]{:S(2)}, u32[]{:S(2)}) collective-permute-start(bf16[384,256]{1,0:T(8,128)(2,1)S(1)} %shard_map.77.refs_0_), channel_id=1, source_target_pairs={{0,6},{2,4},{4,2},{6,0},{8,14},{10,12},{12,10},{14,8},{16,22},{18,... | collective-permute-start | bytes 589832 | tf_op jit(solution)/shard_map/ppermute | solution.py:237
  65.0 1.4 %collective-permute-start.16 = (bf16[384,256]{1,0:T(8,128)(2,1)S(1)}, bf16[384,256]{1,0:T(8,128)(2,1)S(1)}, u32[]{:S(2)}, u32[]{:S(2)}) collective-permute-start(bf16[384,256]{1,0:T(8,128)(2,1)S(1)} %shard_map.77.refs_0_), channel_id=1, source_target_pairs={{0,4},{2,6},{4,0},{6,2},{8,12},{10,14},{12,8},{14,10},{16,20},{18,... | collective-permute-start | bytes 589832 | tf_op jit(solution)/shard_map/ppermute | solution.py:237
  66.4 0.5 collective-permute-start.15
  66.8 3.2 %collective-permute-done.17.refs_3_ = bf16[384,256]{1,0:T(8,128)(2,1)S(1)} collective-permute-done((bf16[384,256]{1,0:T(8,128)(2,1)S(1)}, bf16[384,256]{1,0:T(8,128)(2,1)S(1)}, u32[]{:S(2)}, u32[]{:S(2)}) %collective-permute-start.17) | collective-permute-done | bytes 196640 | tf_op jit(solution)/shard_map/ppermute | solution.py:237
  70.0 2.0 %collective-permute-done.16.refs_2_ = bf16[384,256]{1,0:T(8,128)(2,1)S(1)} collective-permute-done((bf16[384,256]{1,0:T(8,128)(2,1)S(1)}, bf16[384,256]{1,0:T(8,128)(2,1)S(1)}, u32[]{:S(2)}, u32[]{:S(2)}) %collective-permute-start.16) | collective-permute-done | bytes 196640 | tf_op jit(solution)/shard_map/ppermute | solution.py:237
  72.0 0.7 collective-permute-done.15.refs_1_
  72.7 0.0 copy-done.3
  72.7 11.3 %shard_map.78 = (bf16[96,256]{1,0:T(8,128)(2,1)S(1)}, bf16[96,256]{1,0:T(8,128)(2,1)S(1)}, bf16[96,256]{1,0:T(8,128)(2,1)S(1)}, bf16[96,256]{1,0:T(8,128)(2,1)S(1)}) custom-call(s32[16,128]{1,0:T(8,128)S(1)} %get-tuple-element.31.count_ref, bf16[384,256]{1,0:T(8,128)(2,1)S(1)} %shard_map.77.refs_0_, bf16[384,256]{1,0:T(8,128)(2,1)S(1)} %collective-permute-done.15.refs_1_, ...), custom_call_target="tpu_custom_call" | custom-call | tf_op jit(solution)/shard_map/pallas_call | solution.py:276
  84.1 0.1 collective-permute-start.18
  84.1 2.1 %collective-permute-start.19 = (bf16[96,256]{1,0:T(8,128)(2,1)S(1)}, bf16[96,256]{1,0:T(8,128)(2,1)S(1)}, u32[]{:S(2)}, u32[]{:S(2)}) collective-permute-start(bf16[96,256]{1,0:T(8,128)(2,1)S(1)} %get-tuple-element.44), channel_id=1, source_target_pairs={{0,16},{2,18},{4,20},{6,22},{8,24},{10,26},{12,28},{14,30},{16,0},... | collective-permute-start | bytes 147464 | tf_op jit(solution)/shard_map/ppermute | solution.py:237
  86.3 2.2 %collective-permute-start.20 = (bf16[96,256]{1,0:T(8,128)(2,1)S(1)}, bf16[96,256]{1,0:T(8,128)(2,1)S(1)}, u32[]{:S(2)}, u32[]{:S(2)}) collective-permute-start(bf16[96,256]{1,0:T(8,128)(2,1)S(1)} %get-tuple-element.45), channel_id=1, source_target_pairs={{0,24},{2,26},{4,28},{6,30},{8,16},{10,18},{12,20},{14,22},{16,8},... | collective-permute-start | bytes 147464 | tf_op jit(solution)/shard_map/ppermute | solution.py:237
  88.5 0.0 collective-permute-done.18.refs_1_
  88.5 0.7 collective-permute-done.19.refs_2_
  89.2 3.0 %collective-permute-done.20.refs_3_ = bf16[96,256]{1,0:T(8,128)(2,1)S(1)} collective-permute-done((bf16[96,256]{1,0:T(8,128)(2,1)S(1)}, bf16[96,256]{1,0:T(8,128)(2,1)S(1)}, u32[]{:S(2)}, u32[]{:S(2)}) %collective-permute-start.20) | collective-permute-done | bytes 49184 | tf_op jit(solution)/shard_map/ppermute | solution.py:237
  92.2 1.9 %shard_map.79 = f32[256,256]{1,0:T(8,128)} custom-call(bf16[96,256]{1,0:T(8,128)(2,1)S(1)} %get-tuple-element.42.refs_0_, bf16[96,256]{1,0:T(8,128)(2,1)S(1)} %collective-permute-done.18.refs_1_, bf16[96,256]{1,0:T(8,128)(2,1)S(1)} %collective-permute-done.19.refs_2_, bf16[96,256]{1,0:T(8,128)(2,1)S(1)} %collective-permute-done.20.refs_3_, ...), custom_call_target="tpu_custom_call" | custom-call | tf_op jit(solution)/shard_map/pallas_call | solution.py:294
  (4 shorter events, 0.0 us)
Async XLA Ops:
  0.0 0.7 copy-start.7
  0.0 0.7 copy-start.8
  0.7 0.9 %copy-start.5 = (f32[256,256]{1,0:T(8,128)S(1)}, f32[256,256]{1,0:T(8,128)}, u32[]{:S(2)}) copy-start(f32[256,256]{1,0:T(8,128)} %refs_4_.4) | copy-start | bytes 786436
  1.6 50.2 %copy-start.4 = (bf16[2,256,256]{2,1,0:T(8,128)(2,1)S(1)}, bf16[2,256,256]{2,1,0:T(8,128)(2,1)}, u32[]{:S(2)}) copy-start(bf16[2,256,256]{2,1,0:T(8,128)(2,1)} %refs_10_.1) | copy-start | bytes 786436
  2.5 14.1 %collective-permute-start.2 = (bf16[256,256]{1,0:T(8,128)(2,1)S(1)}, bf16[256,256]{1,0:T(8,128)(2,1)S(1)}, u32[]{:S(2)}, u32[]{:S(2)}) collective-permute-start(bf16[256,256]{1,0:T(8,128)(2,1)S(1)} %get-tuple-element.26.refs_0_), channel_id=1, source_target_pairs={{0,24},{2,26},{4,28},{6,30},{8,16},{10,18},{12,20},{14,22},{16,8},... | collective-permute-start | bytes 393224 | tf_op jit(solution)/shard_map/ppermute | solution.py:237
  7.6 11.1 %collective-permute-start.1 = (bf16[256,256]{1,0:T(8,128)(2,1)S(1)}, bf16[256,256]{1,0:T(8,128)(2,1)S(1)}, u32[]{:S(2)}, u32[]{:S(2)}) collective-permute-start(bf16[256,256]{1,0:T(8,128)(2,1)S(1)} %get-tuple-element.26.refs_0_), channel_id=1, source_target_pairs={{0,16},{2,18},{4,20},{6,22},{8,24},{10,26},{12,28},{14,30},{16,0},... | collective-permute-start | bytes 393224 | tf_op jit(solution)/shard_map/ppermute | solution.py:237
  7.7 11.1 %collective-permute-start = (bf16[256,256]{1,0:T(8,128)(2,1)S(1)}, bf16[256,256]{1,0:T(8,128)(2,1)S(1)}, u32[]{:S(2)}, u32[]{:S(2)}) collective-permute-start(bf16[256,256]{1,0:T(8,128)(2,1)S(1)} %get-tuple-element.26.refs_0_), channel_id=1, source_target_pairs={{0,8},{2,10},{4,12},{6,14},{8,0},{10,2},{12,4},{14,6},{16,24},{18,... | collective-permute-start | bytes 393224 | tf_op jit(solution)/shard_map/ppermute | solution.py:237
  8.3 3.7 %collective-permute-start.3 = (bf16[32,256]{1,0:T(8,128)(2,1)S(1)}, bf16[32,256]{1,0:T(8,128)(2,1)S(1)}, u32[]{:S(2)}, u32[]{:S(2)}) collective-permute-start(bf16[32,256]{1,0:T(8,128)(2,1)S(1)} %get-tuple-element.28), channel_id=1, source_target_pairs={{0,2},{2,0},{4,6},{6,4},{8,10},{10,8},{12,14},{14,12},{16,18},{18,... | collective-permute-start | bytes 49160 | tf_op jit(solution)/shard_map/ppermute | solution.py:237
  9.9 4.7 %collective-permute-start.4 = (bf16[32,256]{1,0:T(8,128)(2,1)S(1)}, bf16[32,256]{1,0:T(8,128)(2,1)S(1)}, u32[]{:S(2)}, u32[]{:S(2)}) collective-permute-start(bf16[32,256]{1,0:T(8,128)(2,1)S(1)} %get-tuple-element.29), channel_id=1, source_target_pairs={{0,4},{2,6},{4,0},{6,2},{8,12},{10,14},{12,8},{14,10},{16,20},{18,... | collective-permute-start | bytes 49160 | tf_op jit(solution)/shard_map/ppermute | solution.py:237
  12.0 4.6 %collective-permute-start.5 = (bf16[32,256]{1,0:T(8,128)(2,1)S(1)}, bf16[32,256]{1,0:T(8,128)(2,1)S(1)}, u32[]{:S(2)}, u32[]{:S(2)}) collective-permute-start(bf16[32,256]{1,0:T(8,128)(2,1)S(1)} %get-tuple-element.30), channel_id=1, source_target_pairs={{0,6},{2,4},{4,2},{6,0},{8,14},{10,12},{12,10},{14,8},{16,22},{18,... | collective-permute-start | bytes 49160 | tf_op jit(solution)/shard_map/ppermute | solution.py:237
  18.7 33.2 %copy-start = (bf16[2,256,1024]{2,1,0:T(8,128)(2,1)S(1)}, bf16[2,256,1024]{2,1,0:T(8,128)(2,1)}, u32[]{:S(2)}) copy-start(bf16[2,256,1024]{2,1,0:T(8,128)(2,1)} %refs_11_.1) | copy-start | bytes 3145732
  18.7 33.2 %copy-start.1 = (bf16[2,1024,256]{2,1,0:T(8,128)(2,1)S(1)}, bf16[2,1024,256]{2,1,0:T(8,128)(2,1)}, u32[]{:S(2)}) copy-start(bf16[2,1024,256]{2,1,0:T(8,128)(2,1)} %refs_12_.1) | copy-start | bytes 3145732
  19.3 8.7 %collective-permute-start.8 = (bf16[384,256]{1,0:T(8,128)(2,1)S(1)}, bf16[384,256]{1,0:T(8,128)(2,1)S(1)}, u32[]{:S(2)}, u32[]{:S(2)}) collective-permute-start(bf16[384,256]{1,0:T(8,128)(2,1)S(1)} %get-tuple-element.32.refs_0_), channel_id=1, source_target_pairs={{0,6},{2,4},{4,2},{6,0},{8,14},{10,12},{12,10},{14,8},{16,22},{18,... | collective-permute-start | bytes 589832 | tf_op jit(solution)/shard_map/ppermute | solution.py:237
  21.8 8.6 %collective-permute-start.7 = (bf16[384,256]{1,0:T(8,128)(2,1)S(1)}, bf16[384,256]{1,0:T(8,128)(2,1)S(1)}, u32[]{:S(2)}, u32[]{:S(2)}) collective-permute-start(bf16[384,256]{1,0:T(8,128)(2,1)S(1)} %get-tuple-element.32.refs_0_), channel_id=1, source_target_pairs={{0,4},{2,6},{4,0},{6,2},{8,12},{10,14},{12,8},{14,10},{16,20},{18,... | collective-permute-start | bytes 589832 | tf_op jit(solution)/shard_map/ppermute | solution.py:237
  22.3 8.2 %collective-permute-start.6 = (bf16[384,256]{1,0:T(8,128)(2,1)S(1)}, bf16[384,256]{1,0:T(8,128)(2,1)S(1)}, u32[]{:S(2)}, u32[]{:S(2)}) collective-permute-start(bf16[384,256]{1,0:T(8,128)(2,1)S(1)} %get-tuple-element.32.refs_0_), channel_id=1, source_target_pairs={{0,2},{2,0},{4,6},{6,4},{8,10},{10,8},{12,14},{14,12},{16,18},{18,... | collective-permute-start | bytes 589832 | tf_op jit(solution)/shard_map/ppermute | solution.py:237
  30.5 1.1 %copy-start.2 = (bf16[2,256,768]{2,1,0:T(8,128)(2,1)S(1)}, bf16[2,256,768]{2,1,0:T(8,128)(2,1)}, u32[]{:S(2)}) copy-start(bf16[2,256,768]{2,1,0:T(8,128)(2,1)} %refs_4_.5) | copy-start | bytes 2359300
  43.0 4.5 %collective-permute-start.9 = (bf16[112,256]{1,0:T(8,128)(2,1)S(1)}, bf16[112,256]{1,0:T(8,128)(2,1)S(1)}, u32[]{:S(2)}, u32[]{:S(2)}) collective-permute-start(bf16[112,256]{1,0:T(8,128)(2,1)S(1)} %get-tuple-element.35), channel_id=1, source_target_pairs={{0,8},{2,10},{4,12},{6,14},{8,0},{10,2},{12,4},{14,6},{16,24},{18,... | collective-permute-start | bytes 172040 | tf_op jit(solution)/shard_map/ppermute | solution.py:237
  43.1 5.9 %collective-permute-start.10 = (bf16[112,256]{1,0:T(8,128)(2,1)S(1)}, bf16[112,256]{1,0:T(8,128)(2,1)S(1)}, u32[]{:S(2)}, u32[]{:S(2)}) collective-permute-start(bf16[112,256]{1,0:T(8,128)(2,1)S(1)} %get-tuple-element.36), channel_id=1, source_target_pairs={{0,16},{2,18},{4,20},{6,22},{8,24},{10,26},{12,28},{14,30},{16,0},... | collective-permute-start | bytes 172040 | tf_op jit(solution)/shard_map/ppermute | solution.py:237
  45.9 6.0 %collective-permute-start.11 = (bf16[112,256]{1,0:T(8,128)(2,1)S(1)}, bf16[112,256]{1,0:T(8,128)(2,1)S(1)}, u32[]{:S(2)}, u32[]{:S(2)}) collective-permute-start(bf16[112,256]{1,0:T(8,128)(2,1)S(1)} %get-tuple-element.37), channel_id=1, source_target_pairs={{0,24},{2,26},{4,28},{6,30},{8,16},{10,18},{12,20},{14,22},{16,8},... | collective-permute-start | bytes 172040 | tf_op jit(solution)/shard_map/ppermute | solution.py:237
  51.9 1.0 %copy-start.6 = (f32[256,256]{1,0:T(8,128)S(1)}, f32[256,256]{1,0:T(8,128)}, u32[]{:S(2)}) copy-start(f32[256,256]{1,0:T(8,128)} %refs_4_.4) | copy-start | bytes 786436
  52.8 19.9 %copy-start.3 = (bf16[2,256,768]{2,1,0:T(8,128)(2,1)S(1)}, bf16[2,256,768]{2,1,0:T(8,128)(2,1)}, u32[]{:S(2)}) copy-start(bf16[2,256,768]{2,1,0:T(8,128)(2,1)} %refs_4_.5) | copy-start | bytes 2359300
  54.5 4.5 %collective-permute-start.12 = (bf16[96,256]{1,0:T(8,128)(2,1)S(1)}, bf16[96,256]{1,0:T(8,128)(2,1)S(1)}, u32[]{:S(2)}, u32[]{:S(2)}) collective-permute-start(bf16[96,256]{1,0:T(8,128)(2,1)S(1)} %get-tuple-element.39), channel_id=1, source_target_pairs={{0,8},{2,10},{4,12},{6,14},{8,0},{10,2},{12,4},{14,6},{16,24},{18,... | collective-permute-start | bytes 147464 | tf_op jit(solution)/shard_map/ppermute | solution.py:237
  54.6 5.1 %collective-permute-start.13 = (bf16[96,256]{1,0:T(8,128)(2,1)S(1)}, bf16[96,256]{1,0:T(8,128)(2,1)S(1)}, u32[]{:S(2)}, u32[]{:S(2)}) collective-permute-start(bf16[96,256]{1,0:T(8,128)(2,1)S(1)} %get-tuple-element.40), channel_id=1, source_target_pairs={{0,16},{2,18},{4,20},{6,22},{8,24},{10,26},{12,28},{14,30},{16,0},... | collective-permute-start | bytes 147464 | tf_op jit(solution)/shard_map/ppermute | solution.py:237
  56.7 5.9 %collective-permute-start.14 = (bf16[96,256]{1,0:T(8,128)(2,1)S(1)}, bf16[96,256]{1,0:T(8,128)(2,1)S(1)}, u32[]{:S(2)}, u32[]{:S(2)}) collective-permute-start(bf16[96,256]{1,0:T(8,128)(2,1)S(1)} %get-tuple-element.41), channel_id=1, source_target_pairs={{0,24},{2,26},{4,28},{6,30},{8,16},{10,18},{12,20},{14,22},{16,8},... | collective-permute-start | bytes 147464 | tf_op jit(solution)/shard_map/ppermute | solution.py:237
  63.3 6.7 %collective-permute-start.17 = (bf16[384,256]{1,0:T(8,128)(2,1)S(1)}, bf16[384,256]{1,0:T(8,128)(2,1)S(1)}, u32[]{:S(2)}, u32[]{:S(2)}) collective-permute-start(bf16[384,256]{1,0:T(8,128)(2,1)S(1)} %shard_map.77.refs_0_), channel_id=1, source_target_pairs={{0,6},{2,4},{4,2},{6,0},{8,14},{10,12},{12,10},{14,8},{16,22},{18,... | collective-permute-start | bytes 589832 | tf_op jit(solution)/shard_map/ppermute | solution.py:237
  65.0 7.0 %collective-permute-start.16 = (bf16[384,256]{1,0:T(8,128)(2,1)S(1)}, bf16[384,256]{1,0:T(8,128)(2,1)S(1)}, u32[]{:S(2)}, u32[]{:S(2)}) collective-permute-start(bf16[384,256]{1,0:T(8,128)(2,1)S(1)} %shard_map.77.refs_0_), channel_id=1, source_target_pairs={{0,4},{2,6},{4,0},{6,2},{8,12},{10,14},{12,8},{14,10},{16,20},{18,... | collective-permute-start | bytes 589832 | tf_op jit(solution)/shard_map/ppermute | solution.py:237
  66.4 6.4 %collective-permute-start.15 = (bf16[384,256]{1,0:T(8,128)(2,1)S(1)}, bf16[384,256]{1,0:T(8,128)(2,1)S(1)}, u32[]{:S(2)}, u32[]{:S(2)}) collective-permute-start(bf16[384,256]{1,0:T(8,128)(2,1)S(1)} %shard_map.77.refs_0_), channel_id=1, source_target_pairs={{0,2},{2,0},{4,6},{6,4},{8,10},{10,8},{12,14},{14,12},{16,18},{18,... | collective-permute-start | bytes 589832 | tf_op jit(solution)/shard_map/ppermute | solution.py:237
  84.1 4.5 %collective-permute-start.18 = (bf16[96,256]{1,0:T(8,128)(2,1)S(1)}, bf16[96,256]{1,0:T(8,128)(2,1)S(1)}, u32[]{:S(2)}, u32[]{:S(2)}) collective-permute-start(bf16[96,256]{1,0:T(8,128)(2,1)S(1)} %get-tuple-element.43), channel_id=1, source_target_pairs={{0,8},{2,10},{4,12},{6,14},{8,0},{10,2},{12,4},{14,6},{16,24},{18,... | collective-permute-start | bytes 147464 | tf_op jit(solution)/shard_map/ppermute | solution.py:237
  84.1 5.1 %collective-permute-start.19 = (bf16[96,256]{1,0:T(8,128)(2,1)S(1)}, bf16[96,256]{1,0:T(8,128)(2,1)S(1)}, u32[]{:S(2)}, u32[]{:S(2)}) collective-permute-start(bf16[96,256]{1,0:T(8,128)(2,1)S(1)} %get-tuple-element.44), channel_id=1, source_target_pairs={{0,16},{2,18},{4,20},{6,22},{8,24},{10,26},{12,28},{14,30},{16,0},... | collective-permute-start | bytes 147464 | tf_op jit(solution)/shard_map/ppermute | solution.py:237
  86.3 5.9 %collective-permute-start.20 = (bf16[96,256]{1,0:T(8,128)(2,1)S(1)}, bf16[96,256]{1,0:T(8,128)(2,1)S(1)}, u32[]{:S(2)}, u32[]{:S(2)}) collective-permute-start(bf16[96,256]{1,0:T(8,128)(2,1)S(1)} %get-tuple-element.45), channel_id=1, source_target_pairs={{0,24},{2,26},{4,28},{6,30},{8,16},{10,18},{12,20},{14,22},{16,8},... | collective-permute-start | bytes 147464 | tf_op jit(solution)/shard_map/ppermute | solution.py:237

commit v2 on v1

--- a/solution.py
+++ b/solution.py
@@ -9,6 +9,7 @@
 
 HEADS = 16
 PATCH = 1024
+TALL = 32
 BF16, F32, I32 = jnp.bfloat16, jnp.float32, jnp.int32
 NT = (((1,), (1,)), ((), ()))
 TN = (((0,), (0,)), ((), ()))
@@ -145,49 +146,77 @@
     packed_ref[...] = room[0 : plan.held]
 
 
+def query_body(plan, b, row_ref, weight_ref, query_ref):
+    head_size = plan.width // HEADS
+    projected = matmul(row_ref[...], weight_ref[b, :, : plan.width]).astype(BF16)
+    query_ref[0 : plan.held] = (projected * (head_size**-0.5)).astype(BF16)
+    query_ref[plan.held :] = jnp.zeros((2 * TALL, plan.width), BF16)
+
+
 def attend_body(plan, b, with_notes, count_ref, *refs):
     group, lines, held, cap, width = plan.group, plan.lines, plan.held, plan.cap, plan.width
-    part_refs, weight_ref = refs[:group], refs[group]
-    refs = refs[group + 1 :]
+    part_refs, weight_ref, query_ref = refs[:group], refs[group], refs[group + 1]
+    refs = refs[group + 2 :]
     if with_notes:
         member_ref, refs = refs[0], refs[1:]
-    out_refs, (all_rows, keys, values, queries, mixed) = refs[:lines], refs[lines:]
-    head_size = width // HEADS
+    out_refs, (all_rows, keys, values, mixed, scores) = refs[:lines], refs[lines:]
+    half = width // 2
+    half_heads = HEADS // 2
     offset = 0
     for k in range(group):
         all_rows[pl.ds(pl.multiple_of(offset, 16), held), :] = part_refs[k][...]
         for j in range(lines):
             offset = offset + count_ref[k * lines + j, 64 * b]
     patch_rows = all_rows[0:PATCH]
-    keys[...] = matmul(patch_rows, weight_ref[b, :, width : 2 * width]).astype(BF16)
-    values[...] = matmul(patch_rows, weight_ref[b, :, 2 * width :]).astype(BF16)
-    scaled = matmul(part_refs[0][...], weight_ref[b, :, :width]).astype(BF16) * (head_size**-0.5)
-    queries[...] = scaled.astype(BF16)
+    keys[...] = matmul(
+        weight_ref[b, :, width : 2 * width], patch_rows, (((0,), (1,)), ((), ()))
+    ).astype(BF16)
+    projected = matmul(patch_rows, weight_ref[b, :, 2 * width :]).astype(BF16)
+    ones = jnp.ones((PATCH, half), BF16)
+    for g in range(2):
+        values[g] = jnp.concatenate([projected[:, g * half : (g + 1) * half], ones], axis=1)
     mixed[...] = jnp.zeros(mixed.shape, mixed.dtype)
     own = 0
     offsets = []
     for j in range(lines):
         offsets.append(own)
         own = own + count_ref[j, 64 * b]
-    head_mask = iota((HEADS, 1, width), 0) == iota((HEADS, 1, width), 2) // head_size
-
-    def sixteen(start):
-        block = queries[pl.ds(start, 16), :]
-        spread = jnp.where(head_mask, block[None], jnp.zeros((), BF16)).reshape(HEADS * 16, width)
-        scores = matmul(spread, keys[...], NT)
-        weights = jnp.exp(scores - jnp.max(scores, axis=1, keepdims=True))
-        total = jnp.sum(weights, axis=1, keepdims=True)
-        summed = matmul(weights.astype(BF16), values[...]) / total
-        kept = jnp.where(head_mask, summed.reshape(HEADS, 16, width), 0.0)
-        mixed[pl.ds(start, 16), :] = jnp.sum(kept, axis=0).astype(BF16)
+    shape = (half_heads, 1, half)
+    head_mask = iota(shape, 0) == iota(shape, 2) // (width // HEADS)
+
+    def scored(slot, start, g):
+        block = query_ref[pl.ds(start, TALL), g * half : (g + 1) * half]
+        spread = jnp.where(head_mask, block[None], jnp.zeros((), BF16))
+        scores[slot] = matmul(
+            spread.reshape(half_heads * TALL, half), keys[g * half : (g + 1) * half]
+        )
+
+    def averaged(slot, start, g):
+        table = scores[slot]
+        weights = jnp.exp(table - jnp.max(table, axis=1, keepdims=True)).astype(BF16)
+        summed = matmul(weights, values[g])
+        summed = summed[:, :half] / summed[:, half:]
+        kept = jnp.where(head_mask, summed.reshape(half_heads, TALL, half), 0.0)
+        mixed[pl.ds(start, TALL), g * half : (g + 1) * half] = jnp.sum(kept, axis=0).astype(BF16)
+
+    scored(0, 0, 0)
+    scored(1, 0, 1)
 
     def step(i, carry):
-        start = pl.multiple_of(i * 32, 32)
-        sixteen(start)
-        sixteen(pl.multiple_of(start + 16, 16))
+        first = pl.multiple_of(i * 2 * TALL, 2 * TALL)
+        second = pl.multiple_of(first + TALL, TALL)
+        third = pl.multiple_of(second + TALL, TALL)
+        scored(2, second, 0)
+        averaged(0, first, 0)
+        scored(3, second, 1)
+        averaged(1, first, 1)
+        scored(0, third, 0)
+        averaged(2, second, 0)
+        scored(1, third, 1)
+        averaged(3, second, 1)
         return carry
 
-    lax.fori_loop(0, (own + 31) // 32, step, 0)
+    lax.fori_loop(0, (own + 2 * TALL - 1) // (2 * TALL), step, 0)
     for j in range(lines):
         out_refs[j][0:cap, :] = mixed[pl.ds(pl.multiple_of(offsets[j], 16), cap), :]
         if with_notes:
@@ -272,19 +301,24 @@
         last = b == blocks - 1
         tall = cap if b else cap + 16
         parts = in_group(packed)
+        (queries,) = kernel_call(
+            functools.partial(query_body, plan, b),
+            [struct((held + 2 * TALL, width), BF16)],
+            [whole(), whole()],
+        )(packed, qkv_weight)
         extra = [] if b else [members]
         mixed = kernel_call(
             functools.partial(attend_body, plan, b, b == 0),
             [struct((tall, width), BF16)] * lines,
-            [scalars()] + [whole()] * (group + 1 + len(extra)),
+            [scalars()] + [whole()] * (group + 2 + len(extra)),
             [
                 pltpu.VMEM((PATCH + held, width), BF16),
-                pltpu.VMEM((PATCH, width), BF16),
-                pltpu.VMEM((PATCH, width), BF16),
-                pltpu.VMEM((held, width), BF16),
+                pltpu.VMEM((width, PATCH), BF16),
+                pltpu.VMEM((2, PATCH, width), BF16),
                 pltpu.VMEM((held + cap, width), BF16),
+                pltpu.VMEM((4, HEADS // 2 * TALL, PATCH), F32),
             ],
-        )(counts, *parts, qkv_weight, *extra)
+        )(counts, *parts, qkv_weight, queries, *extra)
         pieces = along_line(mixed)
         if b == 0:
             kept = pieces

time: 94.4 us -> 83.7 us (0.89)
  Pallas kernels: 28.4 us -> 19.4 us
  local copies, waits for them, and re-layouts: 3.66 us -> 2.4 us
    pallas_call x2, Pallas kernels: 22.6 us -> 13.3 us  [by_lines(): kernel_call(functools.partial(attend_body, plan, b, b == 0), [struct((tal...]
    unnamed x18, local copies, waits for them, and re-layouts: 3.66 us -> 2.4 us
where the time goes in v2:
time: 83.7 us; the launch traced here: 83.5 us
  starting transfers between devices  31.9 us (38%)
  waiting for transfers between devices  29.5 us (35%)
  Pallas kernels  19.4 us (23%)
  local copies, waits for them, and re-layouts  2.4 us (3%)
    ppermute x21, starting transfers between devices, flip(): return lax.ppermute(block, 'pts', [(i, i ^ bit) for i in range(count)])  31.9 us
    ppermute x21, waiting for transfers between devices, flip(): return lax.ppermute(block, 'pts', [(i, i ^ bit) for i in range(count)])  29.5 us
    pallas_call x2, Pallas kernels, by_lines(): kernel_call(functools.partial(attend_body, plan, b, b == 0), [struct((tal...  13.3 us
    pallas_call x2, Pallas kernels, by_lines(): kernel_call(functools.partial(store_body, plan, b, last), outs, [whole()]...  3.63 us
    unnamed x18, local copies, waits for them, and re-layouts  2.4 us
  transfers between devices with their start and end apart: 21, of which 15 were waited for; matrix products, arithmetic and copies ran while one was open for 0% of the time, Pallas kernels for 0%

profile of v2, /device:TPU:0, one launch (start us, length us, event | category | flops | bytes accessed | tf_op | source)
XLA Modules:
  0.0 83.5 jit_solution(11267348819018149936)
XLA Ops:
  0.0 0.0 copy-start
  0.0 0.1 pad_add_fusion.place
  0.1 1.0 %copy-done.4 = f32[256,256]{1,0:T(8,128)S(1)} copy-done((f32[256,256]{1,0:T(8,128)S(1)}, f32[256,256]{1,0:T(8,128)}, u32[]{:S(2)}) %copy-start.4) | copy-done | bytes 262168
  1.1 0.7 copy-done.6
  1.8 0.7 copy-done.8
  2.5 0.9 %shard_map.73 = (bf16[256,256]{1,0:T(8,128)(2,1)S(1)}, bf16[32,256]{1,0:T(8,128)(2,1)S(1)}, bf16[32,256]{1,0:T(8,128)(2,1)S(1)}, bf16[32,256]{1,0:T(8,128)(2,1)S(1)}, bf16[32,256]{1,0:T(8,128)(2,1)S(1)}) custom-call(s32[2]{0:T(128)S(1)} %pad_add_fusion.place, f32[256,256]{1,0:T(8,128)S(1)} %copy-done.4, s32[2,256]{1,0:T(2,128)S(1)} %copy-done.8, ...), custom_call_target="tpu_custom_call" | custom-call | tf_op jit(solution)/shard_map/pallas_call | solution.py:286
  3.3 5.1 %collective-permute-start.2 = (bf16[256,256]{1,0:T(8,128)(2,1)S(1)}, bf16[256,256]{1,0:T(8,128)(2,1)S(1)}, u32[]{:S(2)}, u32[]{:S(2)}) collective-permute-start(bf16[256,256]{1,0:T(8,128)(2,1)S(1)} %get-tuple-element.26.refs_0_), channel_id=1, source_target_pairs={{0,24},{2,26},{4,28},{6,30},{8,16},{10,18},{12,20},{14,22},{16,8},... | collective-permute-start | bytes 393224 | tf_op jit(solution)/shard_map/ppermute | solution.py:266
  8.5 0.0 collective-permute-start.1
  8.5 0.6 collective-permute-start
  9.1 1.6 %collective-permute-start.3 = (bf16[32,256]{1,0:T(8,128)(2,1)S(1)}, bf16[32,256]{1,0:T(8,128)(2,1)S(1)}, u32[]{:S(2)}, u32[]{:S(2)}) collective-permute-start(bf16[32,256]{1,0:T(8,128)(2,1)S(1)} %get-tuple-element.28), channel_id=1, source_target_pairs={{0,2},{2,0},{4,6},{6,4},{8,10},{10,8},{12,14},{14,12},{16,18},{18,... | collective-permute-start | bytes 49160 | tf_op jit(solution)/shard_map/ppermute | solution.py:266
  10.7 1.5 %collective-permute-start.4 = (bf16[32,256]{1,0:T(8,128)(2,1)S(1)}, bf16[32,256]{1,0:T(8,128)(2,1)S(1)}, u32[]{:S(2)}, u32[]{:S(2)}) collective-permute-start(bf16[32,256]{1,0:T(8,128)(2,1)S(1)} %get-tuple-element.29), channel_id=1, source_target_pairs={{0,4},{2,6},{4,0},{6,2},{8,12},{10,14},{12,8},{14,10},{16,20},{18,... | collective-permute-start | bytes 49160 | tf_op jit(solution)/shard_map/ppermute | solution.py:266
  12.3 0.6 collective-permute-done.3.refs_5_
  12.8 2.6 %collective-permute-start.5 = (bf16[32,256]{1,0:T(8,128)(2,1)S(1)}, bf16[32,256]{1,0:T(8,128)(2,1)S(1)}, u32[]{:S(2)}, u32[]{:S(2)}) collective-permute-start(bf16[32,256]{1,0:T(8,128)(2,1)S(1)} %get-tuple-element.30), channel_id=1, source_target_pairs={{0,6},{2,4},{4,2},{6,0},{8,14},{10,12},{12,10},{14,8},{16,22},{18,... | collective-permute-start | bytes 49160 | tf_op jit(solution)/shard_map/ppermute | solution.py:266
  15.4 0.0 collective-permute-done.4.refs_6_
  15.4 2.0 %collective-permute-done.5.refs_7_ = bf16[32,256]{1,0:T(8,128)(2,1)S(1)} collective-permute-done((bf16[32,256]{1,0:T(8,128)(2,1)S(1)}, bf16[32,256]{1,0:T(8,128)(2,1)S(1)}, u32[]{:S(2)}, u32[]{:S(2)}) %collective-permute-start.5) | collective-permute-done | bytes 16416 | tf_op jit(solution)/shard_map/ppermute | solution.py:266
  17.5 0.0 collective-permute-done.2.refs_3_
  17.5 2.0 %collective-permute-done.1.refs_2_ = bf16[256,256]{1,0:T(8,128)(2,1)S(1)} collective-permute-done((bf16[256,256]{1,0:T(8,128)(2,1)S(1)}, bf16[256,256]{1,0:T(8,128)(2,1)S(1)}, u32[]{:S(2)}, u32[]{:S(2)}) %collective-permute-start.1) | collective-permute-done | bytes 131104 | tf_op jit(solution)/shard_map/ppermute | solution.py:266
  19.5 0.0 collective-permute-done.refs_1_
  19.5 0.5 shard_map.74
  20.1 2.5 %collective-permute-start.8 = (bf16[384,256]{1,0:T(8,128)(2,1)S(1)}, bf16[384,256]{1,0:T(8,128)(2,1)S(1)}, u32[]{:S(2)}, u32[]{:S(2)}) collective-permute-start(bf16[384,256]{1,0:T(8,128)(2,1)S(1)} %get-tuple-element.32.row_ref.refs_0_), channel_id=1, source_target_pairs={{0,6},{2,4},{4,2},{6,0},{8,14},{10,12},{12,10},{14,8},{16,22},{18,... | collective-permute-start | bytes 589832 | tf_op jit(solution)/shard_map/ppermute | solution.py:266
  22.6 0.5 collective-permute-start.7
  23.1 0.5 collective-permute-start.6
  23.6 0.0 copy-done
  23.6 0.2 shard_map.75.refs_5_
  23.8 0.0 copy-start.1
  23.9 4.9 %collective-permute-done.8.refs_3_ = bf16[384,256]{1,0:T(8,128)(2,1)S(1)} collective-permute-done((bf16[384,256]{1,0:T(8,128)(2,1)S(1)}, bf16[384,256]{1,0:T(8,128)(2,1)S(1)}, u32[]{:S(2)}, u32[]{:S(2)}) %collective-permute-start.8) | collective-permute-done | bytes 196640 | tf_op jit(solution)/shard_map/ppermute | solution.py:266
  28.8 2.5 %collective-permute-done.7.refs_2_ = bf16[384,256]{1,0:T(8,128)(2,1)S(1)} collective-permute-done((bf16[384,256]{1,0:T(8,128)(2,1)S(1)}, bf16[384,256]{1,0:T(8,128)(2,1)S(1)}, u32[]{:S(2)}, u32[]{:S(2)}) %collective-permute-start.7) | collective-permute-done | bytes 196640 | tf_op jit(solution)/shard_map/ppermute | solution.py:266
  31.2 0.1 collective-permute-done.6.refs_1_
  31.3 6.6 %shard_map.76 = (bf16[112,256]{1,0:T(8,128)(2,1)S(1)}, bf16[112,256]{1,0:T(8,128)(2,1)S(1)}, bf16[112,256]{1,0:T(8,128)(2,1)S(1)}, bf16[112,256]{1,0:T(8,128)(2,1)S(1)}) custom-call(s32[16,128]{1,0:T(8,128)S(1)} %get-tuple-element.31.count_ref, bf16[384,256]{1,0:T(8,128)(2,1)S(1)} %get-tuple-element.32.row_ref.refs_0_, ...), custom_call_target="tpu_custom_call" | custom-call | tf_op jit(solution)/shard_map/pallas_call | solution.py:310
  38.0 0.0 copy-start.7
  38.0 0.1 collective-permute-start.9
  38.1 2.8 %collective-permute-start.10 = (bf16[112,256]{1,0:T(8,128)(2,1)S(1)}, bf16[112,256]{1,0:T(8,128)(2,1)S(1)}, u32[]{:S(2)}, u32[]{:S(2)}) collective-permute-start(bf16[112,256]{1,0:T(8,128)(2,1)S(1)} %get-tuple-element.36), channel_id=1, source_target_pairs={{0,16},{2,18},{4,20},{6,22},{8,24},{10,26},{12,28},{14,30},{16,0},... | collective-permute-start | bytes 172040 | tf_op jit(solution)/shard_map/ppermute | solution.py:266
  40.9 1.5 %collective-permute-start.11 = (bf16[112,256]{1,0:T(8,128)(2,1)S(1)}, bf16[112,256]{1,0:T(8,128)(2,1)S(1)}, u32[]{:S(2)}, u32[]{:S(2)}) collective-permute-start(bf16[112,256]{1,0:T(8,128)(2,1)S(1)} %get-tuple-element.37), channel_id=1, source_target_pairs={{0,24},{2,26},{4,28},{6,30},{8,16},{10,18},{12,20},{14,22},{16,8},... | collective-permute-start | bytes 172040 | tf_op jit(solution)/shard_map/ppermute | solution.py:266
  42.4 0.0 collective-permute-done.9.refs_1_.refs_5_
  42.4 1.5 %collective-permute-done.10.refs_2_.refs_6_ = bf16[112,256]{1,0:T(8,128)(2,1)S(1)} collective-permute-done((bf16[112,256]{1,0:T(8,128)(2,1)S(1)}, bf16[112,256]{1,0:T(8,128)(2,1)S(1)}, u32[]{:S(2)}, u32[]{:S(2)}) %collective-permute-start.10) | collective-permute-done | bytes 57376 | tf_op jit(solution)/shard_map/ppermute | solution.py:266
  44.0 2.9 %collective-permute-done.11.refs_3_.refs_7_ = bf16[112,256]{1,0:T(8,128)(2,1)S(1)} collective-permute-done((bf16[112,256]{1,0:T(8,128)(2,1)S(1)}, bf16[112,256]{1,0:T(8,128)(2,1)S(1)}, u32[]{:S(2)}, u32[]{:S(2)}) %collective-permute-start.11) | collective-permute-done | bytes 57376 | tf_op jit(solution)/shard_map/ppermute | solution.py:266
  46.9 0.0 copy-done.2
  46.9 0.0 copy-done.1
  46.9 0.0 copy-done.3
  46.9 0.0 copy-done.5
  46.9 0.0 copy-done.7
  46.9 1.7 %shard_map.77 = (f32[256,256]{1,0:T(8,128)S(1)}, bf16[96,256]{1,0:T(8,128)(2,1)S(1)}, bf16[96,256]{1,0:T(8,128)(2,1)S(1)}, bf16[96,256]{1,0:T(8,128)(2,1)S(1)}, bf16[96,256]{1,0:T(8,128)(2,1)S(1)}) custom-call(bf16[112,256]{1,0:T(8,128)(2,1)S(1)} %get-tuple-element.34.refs_0_.refs_4_, bf16[112,256]{1,0:T(8,128)(2,1)S(1)} %collective-permute-done.9.refs_1_.refs_5_, ...), custom_call_target="tpu_custom_call" | custom-call | tf_op jit(solution)/shard_map/pallas_call | solution.py:328
  48.6 0.1 collective-permute-start.12
  48.7 2.1 %collective-permute-start.13 = (bf16[96,256]{1,0:T(8,128)(2,1)S(1)}, bf16[96,256]{1,0:T(8,128)(2,1)S(1)}, u32[]{:S(2)}, u32[]{:S(2)}) collective-permute-start(bf16[96,256]{1,0:T(8,128)(2,1)S(1)} %get-tuple-element.40), channel_id=1, source_target_pairs={{0,16},{2,18},{4,20},{6,22},{8,24},{10,26},{12,28},{14,30},{16,0},... | collective-permute-start | bytes 147464 | tf_op jit(solution)/shard_map/ppermute | solution.py:266
  50.8 2.3 %collective-permute-start.14 = (bf16[96,256]{1,0:T(8,128)(2,1)S(1)}, bf16[96,256]{1,0:T(8,128)(2,1)S(1)}, u32[]{:S(2)}, u32[]{:S(2)}) collective-permute-start(bf16[96,256]{1,0:T(8,128)(2,1)S(1)} %get-tuple-element.41), channel_id=1, source_target_pairs={{0,24},{2,26},{4,28},{6,30},{8,16},{10,18},{12,20},{14,22},{16,8},... | collective-permute-start | bytes 147464 | tf_op jit(solution)/shard_map/ppermute | solution.py:266
  53.1 0.0 collective-permute-done.12.refs_1_
  53.1 0.8 collective-permute-done.13.refs_2_
  53.8 2.8 %collective-permute-done.14.refs_3_ = bf16[96,256]{1,0:T(8,128)(2,1)S(1)} collective-permute-done((bf16[96,256]{1,0:T(8,128)(2,1)S(1)}, bf16[96,256]{1,0:T(8,128)(2,1)S(1)}, u32[]{:S(2)}, u32[]{:S(2)}) %collective-permute-start.14) | collective-permute-done | bytes 49184 | tf_op jit(solution)/shard_map/ppermute | solution.py:266
  56.7 0.7 shard_map.78.row_ref.refs_0_
  57.4 1.7 %collective-permute-start.17 = (bf16[384,256]{1,0:T(8,128)(2,1)S(1)}, bf16[384,256]{1,0:T(8,128)(2,1)S(1)}, u32[]{:S(2)}, u32[]{:S(2)}) collective-permute-start(bf16[384,256]{1,0:T(8,128)(2,1)S(1)} %shard_map.78.row_ref.refs_0_), channel_id=1, source_target_pairs={{0,6},{2,4},{4,2},{6,0},{8,14},{10,12},{12,10},{14,8},{16,22},{18,... | collective-permute-start | bytes 589832 | tf_op jit(solution)/shard_map/ppermute | solution.py:266
  59.1 1.4 %collective-permute-start.16 = (bf16[384,256]{1,0:T(8,128)(2,1)S(1)}, bf16[384,256]{1,0:T(8,128)(2,1)S(1)}, u32[]{:S(2)}, u32[]{:S(2)}) collective-permute-start(bf16[384,256]{1,0:T(8,128)(2,1)S(1)} %shard_map.78.row_ref.refs_0_), channel_id=1, source_target_pairs={{0,4},{2,6},{4,0},{6,2},{8,12},{10,14},{12,8},{14,10},{16,20},{18,... | collective-permute-start | bytes 589832 | tf_op jit(solution)/shard_map/ppermute | solution.py:266
  60.4 0.5 collective-permute-start.15
  60.9 0.2 shard_map.79.refs_5_
  61.1 3.0 %collective-permute-done.17.refs_3_ = bf16[384,256]{1,0:T(8,128)(2,1)S(1)} collective-permute-done((bf16[384,256]{1,0:T(8,128)(2,1)S(1)}, bf16[384,256]{1,0:T(8,128)(2,1)S(1)}, u32[]{:S(2)}, u32[]{:S(2)}) %collective-permute-start.17) | collective-permute-done | bytes 196640 | tf_op jit(solution)/shard_map/ppermute | solution.py:266
  64.1 2.0 %collective-permute-done.16.refs_2_ = bf16[384,256]{1,0:T(8,128)(2,1)S(1)} collective-permute-done((bf16[384,256]{1,0:T(8,128)(2,1)S(1)}, bf16[384,256]{1,0:T(8,128)(2,1)S(1)}, u32[]{:S(2)}, u32[]{:S(2)}) %collective-permute-start.16) | collective-permute-done | bytes 196640 | tf_op jit(solution)/shard_map/ppermute | solution.py:266
  66.1 0.7 collective-permute-done.15.refs_1_
  66.8 6.6 %shard_map.80 = (bf16[96,256]{1,0:T(8,128)(2,1)S(1)}, bf16[96,256]{1,0:T(8,128)(2,1)S(1)}, bf16[96,256]{1,0:T(8,128)(2,1)S(1)}, bf16[96,256]{1,0:T(8,128)(2,1)S(1)}) custom-call(s32[16,128]{1,0:T(8,128)S(1)} %get-tuple-element.31.count_ref, bf16[384,256]{1,0:T(8,128)(2,1)S(1)} %shard_map.78.row_ref.refs_0_, ...), custom_call_target="tpu_custom_call" | custom-call | tf_op jit(solution)/shard_map/pallas_call | solution.py:310
  73.5 0.1 collective-permute-start.18
  73.5 2.2 %collective-permute-start.19 = (bf16[96,256]{1,0:T(8,128)(2,1)S(1)}, bf16[96,256]{1,0:T(8,128)(2,1)S(1)}, u32[]{:S(2)}, u32[]{:S(2)}) collective-permute-start(bf16[96,256]{1,0:T(8,128)(2,1)S(1)} %get-tuple-element.44), channel_id=1, source_target_pairs={{0,16},{2,18},{4,20},{6,22},{8,24},{10,26},{12,28},{14,30},{16,0},... | collective-permute-start | bytes 147464 | tf_op jit(solution)/shard_map/ppermute | solution.py:266
  75.7 2.2 %collective-permute-start.20 = (bf16[96,256]{1,0:T(8,128)(2,1)S(1)}, bf16[96,256]{1,0:T(8,128)(2,1)S(1)}, u32[]{:S(2)}, u32[]{:S(2)}) collective-permute-start(bf16[96,256]{1,0:T(8,128)(2,1)S(1)} %get-tuple-element.45), channel_id=1, source_target_pairs={{0,24},{2,26},{4,28},{6,30},{8,16},{10,18},{12,20},{14,22},{16,8},... | collective-permute-start | bytes 147464 | tf_op jit(solution)/shard_map/ppermute | solution.py:266
  77.9 0.0 collective-permute-done.18.refs_1_
  77.9 0.7 collective-permute-done.19.refs_2_
  78.6 3.0 %collective-permute-done.20.refs_3_ = bf16[96,256]{1,0:T(8,128)(2,1)S(1)} collective-permute-done((bf16[96,256]{1,0:T(8,128)(2,1)S(1)}, bf16[96,256]{1,0:T(8,128)(2,1)S(1)}, u32[]{:S(2)}, u32[]{:S(2)}) %collective-permute-start.20) | collective-permute-done | bytes 49184 | tf_op jit(solution)/shard_map/ppermute | solution.py:266
  81.6 1.9 %shard_map.81 = f32[256,256]{1,0:T(8,128)} custom-call(bf16[96,256]{1,0:T(8,128)(2,1)S(1)} %get-tuple-element.42.refs_0_, bf16[96,256]{1,0:T(8,128)(2,1)S(1)} %collective-permute-done.18.refs_1_, bf16[96,256]{1,0:T(8,128)(2,1)S(1)} %collective-permute-done.19.refs_2_, bf16[96,256]{1,0:T(8,128)(2,1)S(1)} %collective-permute-done.20.refs_3_, ...), custom_call_target="tpu_custom_call" | custom-call | tf_op jit(solution)/shard_map/pallas_call | solution.py:328
  (6 shorter events, 0.0 us)
Async XLA Ops:
  0.0 23.6 %copy-start = (bf16[2,256,768]{2,1,0:T(8,128)(2,1)S(1)}, bf16[2,256,768]{2,1,0:T(8,128)(2,1)}, u32[]{:S(2)}) copy-start(bf16[2,256,768]{2,1,0:T(8,128)(2,1)} %refs_4_.5) | copy-start | bytes 2359300
  0.1 1.0 %copy-start.4 = (f32[256,256]{1,0:T(8,128)S(1)}, f32[256,256]{1,0:T(8,128)}, u32[]{:S(2)}) copy-start(f32[256,256]{1,0:T(8,128)} %refs_4_.4) | copy-start | bytes 786436
  1.1 0.7 copy-start.6
  1.8 0.7 copy-start.8
  3.3 14.1 %collective-permute-start.2 = (bf16[256,256]{1,0:T(8,128)(2,1)S(1)}, bf16[256,256]{1,0:T(8,128)(2,1)S(1)}, u32[]{:S(2)}, u32[]{:S(2)}) collective-permute-start(bf16[256,256]{1,0:T(8,128)(2,1)S(1)} %get-tuple-element.26.refs_0_), channel_id=1, source_target_pairs={{0,24},{2,26},{4,28},{6,30},{8,16},{10,18},{12,20},{14,22},{16,8},... | collective-permute-start | bytes 393224 | tf_op jit(solution)/shard_map/ppermute | solution.py:266
  8.5 11.1 %collective-permute-start.1 = (bf16[256,256]{1,0:T(8,128)(2,1)S(1)}, bf16[256,256]{1,0:T(8,128)(2,1)S(1)}, u32[]{:S(2)}, u32[]{:S(2)}) collective-permute-start(bf16[256,256]{1,0:T(8,128)(2,1)S(1)} %get-tuple-element.26.refs_0_), channel_id=1, source_target_pairs={{0,16},{2,18},{4,20},{6,22},{8,24},{10,26},{12,28},{14,30},{16,0},... | collective-permute-start | bytes 393224 | tf_op jit(solution)/shard_map/ppermute | solution.py:266
  8.5 11.1 %collective-permute-start = (bf16[256,256]{1,0:T(8,128)(2,1)S(1)}, bf16[256,256]{1,0:T(8,128)(2,1)S(1)}, u32[]{:S(2)}, u32[]{:S(2)}) collective-permute-start(bf16[256,256]{1,0:T(8,128)(2,1)S(1)} %get-tuple-element.26.refs_0_), channel_id=1, source_target_pairs={{0,8},{2,10},{4,12},{6,14},{8,0},{10,2},{12,4},{14,6},{16,24},{18,... | collective-permute-start | bytes 393224 | tf_op jit(solution)/shard_map/ppermute | solution.py:266
  9.1 3.7 %collective-permute-start.3 = (bf16[32,256]{1,0:T(8,128)(2,1)S(1)}, bf16[32,256]{1,0:T(8,128)(2,1)S(1)}, u32[]{:S(2)}, u32[]{:S(2)}) collective-permute-start(bf16[32,256]{1,0:T(8,128)(2,1)S(1)} %get-tuple-element.28), channel_id=1, source_target_pairs={{0,2},{2,0},{4,6},{6,4},{8,10},{10,8},{12,14},{14,12},{16,18},{18,... | collective-permute-start | bytes 49160 | tf_op jit(solution)/shard_map/ppermute | solution.py:266
  10.7 4.7 %collective-permute-start.4 = (bf16[32,256]{1,0:T(8,128)(2,1)S(1)}, bf16[32,256]{1,0:T(8,128)(2,1)S(1)}, u32[]{:S(2)}, u32[]{:S(2)}) collective-permute-start(bf16[32,256]{1,0:T(8,128)(2,1)S(1)} %get-tuple-element.29), channel_id=1, source_target_pairs={{0,4},{2,6},{4,0},{6,2},{8,12},{10,14},{12,8},{14,10},{16,20},{18,... | collective-permute-start | bytes 49160 | tf_op jit(solution)/shard_map/ppermute | solution.py:266
  12.8 4.6 %collective-permute-start.5 = (bf16[32,256]{1,0:T(8,128)(2,1)S(1)}, bf16[32,256]{1,0:T(8,128)(2,1)S(1)}, u32[]{:S(2)}, u32[]{:S(2)}) collective-permute-start(bf16[32,256]{1,0:T(8,128)(2,1)S(1)} %get-tuple-element.30), channel_id=1, source_target_pairs={{0,6},{2,4},{4,2},{6,0},{8,14},{10,12},{12,10},{14,8},{16,22},{18,... | collective-permute-start | bytes 49160 | tf_op jit(solution)/shard_map/ppermute | solution.py:266
  20.1 8.7 %collective-permute-start.8 = (bf16[384,256]{1,0:T(8,128)(2,1)S(1)}, bf16[384,256]{1,0:T(8,128)(2,1)S(1)}, u32[]{:S(2)}, u32[]{:S(2)}) collective-permute-start(bf16[384,256]{1,0:T(8,128)(2,1)S(1)} %get-tuple-element.32.row_ref.refs_0_), channel_id=1, source_target_pairs={{0,6},{2,4},{4,2},{6,0},{8,14},{10,12},{12,10},{14,8},{16,22},{18,... | collective-permute-start | bytes 589832 | tf_op jit(solution)/shard_map/ppermute | solution.py:266
  22.6 8.6 %collective-permute-start.7 = (bf16[384,256]{1,0:T(8,128)(2,1)S(1)}, bf16[384,256]{1,0:T(8,128)(2,1)S(1)}, u32[]{:S(2)}, u32[]{:S(2)}) collective-permute-start(bf16[384,256]{1,0:T(8,128)(2,1)S(1)} %get-tuple-element.32.row_ref.refs_0_), channel_id=1, source_target_pairs={{0,4},{2,6},{4,0},{6,2},{8,12},{10,14},{12,8},{14,10},{16,20},{18,... | collective-permute-start | bytes 589832 | tf_op jit(solution)/shard_map/ppermute | solution.py:266
  23.1 8.2 %collective-permute-start.6 = (bf16[384,256]{1,0:T(8,128)(2,1)S(1)}, bf16[384,256]{1,0:T(8,128)(2,1)S(1)}, u32[]{:S(2)}, u32[]{:S(2)}) collective-permute-start(bf16[384,256]{1,0:T(8,128)(2,1)S(1)} %get-tuple-element.32.row_ref.refs_0_), channel_id=1, source_target_pairs={{0,2},{2,0},{4,6},{6,4},{8,10},{10,8},{12,14},{14,12},{16,18},{18,... | collective-permute-start | bytes 589832 | tf_op jit(solution)/shard_map/ppermute | solution.py:266
  23.6 23.2 %copy-start.2 = (bf16[2,1024,256]{2,1,0:T(8,128)(2,1)S(1)}, bf16[2,1024,256]{2,1,0:T(8,128)(2,1)}, u32[]{:S(2)}) copy-start(bf16[2,1024,256]{2,1,0:T(8,128)(2,1)} %refs_12_.1) | copy-start | bytes 3145732
  23.8 23.0 %copy-start.1 = (bf16[2,256,1024]{2,1,0:T(8,128)(2,1)S(1)}, bf16[2,256,1024]{2,1,0:T(8,128)(2,1)}, u32[]{:S(2)}) copy-start(bf16[2,256,1024]{2,1,0:T(8,128)(2,1)} %refs_11_.1) | copy-start | bytes 3145732
  31.3 15.6 %copy-start.3 = (bf16[2,256,256]{2,1,0:T(8,128)(2,1)S(1)}, bf16[2,256,256]{2,1,0:T(8,128)(2,1)}, u32[]{:S(2)}) copy-start(bf16[2,256,256]{2,1,0:T(8,128)(2,1)} %refs_10_.1) | copy-start | bytes 786436
  31.3 15.6 %copy-start.5 = (f32[256,256]{1,0:T(8,128)S(1)}, f32[256,256]{1,0:T(8,128)}, u32[]{:S(2)}) copy-start(f32[256,256]{1,0:T(8,128)} %refs_4_.4) | copy-start | bytes 786436
  38.0 8.9 %copy-start.7 = (f32[2,2,256]{2,1,0:T(2,128)S(1)}, f32[2,2,256]{2,1,0:T(2,128)}, u32[]{:S(2)}) copy-start(f32[2,2,256]{2,1,0:T(2,128)} %refs_9_.1) | copy-start | bytes 12292
  38.0 4.5 %collective-permute-start.9 = (bf16[112,256]{1,0:T(8,128)(2,1)S(1)}, bf16[112,256]{1,0:T(8,128)(2,1)S(1)}, u32[]{:S(2)}, u32[]{:S(2)}) collective-permute-start(bf16[112,256]{1,0:T(8,128)(2,1)S(1)} %get-tuple-element.35), channel_id=1, source_target_pairs={{0,8},{2,10},{4,12},{6,14},{8,0},{10,2},{12,4},{14,6},{16,24},{18,... | collective-permute-start | bytes 172040 | tf_op jit(solution)/shard_map/ppermute | solution.py:266
  38.1 5.9 %collective-permute-start.10 = (bf16[112,256]{1,0:T(8,128)(2,1)S(1)}, bf16[112,256]{1,0:T(8,128)(2,1)S(1)}, u32[]{:S(2)}, u32[]{:S(2)}) collective-permute-start(bf16[112,256]{1,0:T(8,128)(2,1)S(1)} %get-tuple-element.36), channel_id=1, source_target_pairs={{0,16},{2,18},{4,20},{6,22},{8,24},{10,26},{12,28},{14,30},{16,0},... | collective-permute-start | bytes 172040 | tf_op jit(solution)/shard_map/ppermute | solution.py:266
  40.9 6.0 %collective-permute-start.11 = (bf16[112,256]{1,0:T(8,128)(2,1)S(1)}, bf16[112,256]{1,0:T(8,128)(2,1)S(1)}, u32[]{:S(2)}, u32[]{:S(2)}) collective-permute-start(bf16[112,256]{1,0:T(8,128)(2,1)S(1)} %get-tuple-element.37), channel_id=1, source_target_pairs={{0,24},{2,26},{4,28},{6,30},{8,16},{10,18},{12,20},{14,22},{16,8},... | collective-permute-start | bytes 172040 | tf_op jit(solution)/shard_map/ppermute | solution.py:266
  48.6 4.5 %collective-permute-start.12 = (bf16[96,256]{1,0:T(8,128)(2,1)S(1)}, bf16[96,256]{1,0:T(8,128)(2,1)S(1)}, u32[]{:S(2)}, u32[]{:S(2)}) collective-permute-start(bf16[96,256]{1,0:T(8,128)(2,1)S(1)} %get-tuple-element.39), channel_id=1, source_target_pairs={{0,8},{2,10},{4,12},{6,14},{8,0},{10,2},{12,4},{14,6},{16,24},{18,... | collective-permute-start | bytes 147464 | tf_op jit(solution)/shard_map/ppermute | solution.py:266
  48.7 5.1 %collective-permute-start.13 = (bf16[96,256]{1,0:T(8,128)(2,1)S(1)}, bf16[96,256]{1,0:T(8,128)(2,1)S(1)}, u32[]{:S(2)}, u32[]{:S(2)}) collective-permute-start(bf16[96,256]{1,0:T(8,128)(2,1)S(1)} %get-tuple-element.40), channel_id=1, source_target_pairs={{0,16},{2,18},{4,20},{6,22},{8,24},{10,26},{12,28},{14,30},{16,0},... | collective-permute-start | bytes 147464 | tf_op jit(solution)/shard_map/ppermute | solution.py:266
  50.8 5.9 %collective-permute-start.14 = (bf16[96,256]{1,0:T(8,128)(2,1)S(1)}, bf16[96,256]{1,0:T(8,128)(2,1)S(1)}, u32[]{:S(2)}, u32[]{:S(2)}) collective-permute-start(bf16[96,256]{1,0:T(8,128)(2,1)S(1)} %get-tuple-element.41), channel_id=1, source_target_pairs={{0,24},{2,26},{4,28},{6,30},{8,16},{10,18},{12,20},{14,22},{16,8},... | collective-permute-start | bytes 147464 | tf_op jit(solution)/shard_map/ppermute | solution.py:266
  57.4 6.7 %collective-permute-start.17 = (bf16[384,256]{1,0:T(8,128)(2,1)S(1)}, bf16[384,256]{1,0:T(8,128)(2,1)S(1)}, u32[]{:S(2)}, u32[]{:S(2)}) collective-permute-start(bf16[384,256]{1,0:T(8,128)(2,1)S(1)} %shard_map.78.row_ref.refs_0_), channel_id=1, source_target_pairs={{0,6},{2,4},{4,2},{6,0},{8,14},{10,12},{12,10},{14,8},{16,22},{18,... | collective-permute-start | bytes 589832 | tf_op jit(solution)/shard_map/ppermute | solution.py:266
  59.1 7.0 %collective-permute-start.16 = (bf16[384,256]{1,0:T(8,128)(2,1)S(1)}, bf16[384,256]{1,0:T(8,128)(2,1)S(1)}, u32[]{:S(2)}, u32[]{:S(2)}) collective-permute-start(bf16[384,256]{1,0:T(8,128)(2,1)S(1)} %shard_map.78.row_ref.refs_0_), channel_id=1, source_target_pairs={{0,4},{2,6},{4,0},{6,2},{8,12},{10,14},{12,8},{14,10},{16,20},{18,... | collective-permute-start | bytes 589832 | tf_op jit(solution)/shard_map/ppermute | solution.py:266
  60.4 6.4 %collective-permute-start.15 = (bf16[384,256]{1,0:T(8,128)(2,1)S(1)}, bf16[384,256]{1,0:T(8,128)(2,1)S(1)}, u32[]{:S(2)}, u32[]{:S(2)}) collective-permute-start(bf16[384,256]{1,0:T(8,128)(2,1)S(1)} %shard_map.78.row_ref.refs_0_), channel_id=1, source_target_pairs={{0,2},{2,0},{4,6},{6,4},{8,10},{10,8},{12,14},{14,12},{16,18},{18,... | collective-permute-start | bytes 589832 | tf_op jit(solution)/shard_map/ppermute | solution.py:266
  73.5 4.5 %collective-permute-start.18 = (bf16[96,256]{1,0:T(8,128)(2,1)S(1)}, bf16[96,256]{1,0:T(8,128)(2,1)S(1)}, u32[]{:S(2)}, u32[]{:S(2)}) collective-permute-start(bf16[96,256]{1,0:T(8,128)(2,1)S(1)} %get-tuple-element.43), channel_id=1, source_target_pairs={{0,8},{2,10},{4,12},{6,14},{8,0},{10,2},{12,4},{14,6},{16,24},{18,... | collective-permute-start | bytes 147464 | tf_op jit(solution)/shard_map/ppermute | solution.py:266
  73.5 5.1 %collective-permute-start.19 = (bf16[96,256]{1,0:T(8,128)(2,1)S(1)}, bf16[96,256]{1,0:T(8,128)(2,1)S(1)}, u32[]{:S(2)}, u32[]{:S(2)}) collective-permute-start(bf16[96,256]{1,0:T(8,128)(2,1)S(1)} %get-tuple-element.44), channel_id=1, source_target_pairs={{0,16},{2,18},{4,20},{6,22},{8,24},{10,26},{12,28},{14,30},{16,0},... | collective-permute-start | bytes 147464 | tf_op jit(solution)/shard_map/ppermute | solution.py:266
  75.7 5.9 %collective-permute-start.20 = (bf16[96,256]{1,0:T(8,128)(2,1)S(1)}, bf16[96,256]{1,0:T(8,128)(2,1)S(1)}, u32[]{:S(2)}, u32[]{:S(2)}) collective-permute-start(bf16[96,256]{1,0:T(8,128)(2,1)S(1)} %get-tuple-element.45), channel_id=1, source_target_pairs={{0,24},{2,26},{4,28},{6,30},{8,16},{10,18},{12,20},{14,22},{16,8},... | collective-permute-start | bytes 147464 | tf_op jit(solution)/shard_map/ppermute | solution.py:266

commit v3 on v2

--- a/solution.py
+++ b/solution.py
@@ -84,14 +84,20 @@
     return pl.BlockSpec(memory_space=SMEM)
 
 
-def open_body(plan, place, feature_ref, order_ref, gain_ref, normed_ref, *note_refs):
+def norm_body(feature_ref, gain_ref, order_ref, normed_ref, passed_ref):
+    passed_ref[...] = order_ref[...]
     normed_ref[...] = layer_norm(feature_ref[...], gain_ref[0, 0:1, :]).astype(BF16)
-    line, column = place[0], place[1]
+
+
+def note_body(plan, place, row_ref, order_ref, turned_ref, passed_ref, kept_ref, sent_ref):
+    passed_ref[...] = row_ref[...]
+    line, column, line_step, column_step, slab = (place[i] for i in range(5))
+    order = jnp.where(slab == 0, order_ref[...], turned_ref[...])
     bits = plan.rows.bit_length() - 1
     entry = iota((32, 1), 0)
-    notes = [None] * plan.group
-    for b in range(order_ref.shape[0]):
-        order_row = order_ref[b : b + 1, :]
+    notes = None
+    for b in range(order.shape[0]):
+        order_row = order[b : b + 1, :]
         owner = order_row >> bits
         within = order_row & (plan.rows - 1)
         inside = ones_where(iota((plan.rows, 1), 0) == within)
@@ -100,10 +106,12 @@
             target = column ^ k
             member = entry - 8 * b
             stored = jnp.where(
-                (member >= 0) & (member < plan.lines), (member ^ line) * plan.group + target, -1
+                (member >= 0) & (member < plan.lines),
+                (member ^ line) * line_step + target * column_step,
+                -1,
             )
             other = entry - 16
-            counted = ((other & 3) ^ line) * plan.group + (target ^ (other >> 2))
+            counted = ((other & 3) ^ line) * line_step + (target ^ (other >> 2)) * column_step
             picks.append(ones_where(owner == jnp.where(other >= 0, counted, stored)))
         pick = jnp.concatenate(picks, axis=0)
         found = matmul(pick, inside, NT)
@@ -112,14 +120,21 @@
         rowid = iota((32 * plan.group, 1), 0) & 31
         mine = (lane >= 128 * b) & (lane < 128 * (b + 1))
         part = jnp.where(rowid < 16, found, jnp.where(mine, counts, 0.0))
-        notes = part if b == 0 else notes + part
+        notes = part if notes is None else notes + part
     for k in range(plan.group):
-        note_refs[k][...] = notes[32 * k : 32 * (k + 1)].astype(BF16)
+        half = (kept_ref, sent_ref)[k & 1]
+        half[32 * (k >> 1) : 32 * (k >> 1) + 32] = notes[32 * k : 32 * (k + 1)].astype(BF16)
+
+
+def join_body(kept_ref, got_ref, mine_ref, sent_ref):
+    total = (kept_ref[...].astype(F32) + got_ref[...].astype(F32)).astype(BF16)
+    mine_ref[...] = total[:32]
+    sent_ref[...] = total[32:]
 
 
 def first_pack_body(plan, *refs):
-    row_refs, note_refs = refs[:4], refs[4:8]
-    packed_ref, count_ref, member_ref = refs[8:]
+    row_refs, note_refs = refs[:4], refs[4:6]
+    packed_ref, count_ref, member_ref = refs[6:]
     total = sum(r[...].astype(F32) for r in note_refs)
     members = total[:16]
     member_ref[...] = members.astype(BF16)
@@ -262,8 +277,15 @@
             send_refs[j][...] = matmul(places(j, b + 1), normed).astype(BF16)
 
 
-def flip(block, count, bit):
-    return lax.ppermute(block, "pts", [(i, i ^ bit) for i in range(count)])
+def move(block, peers, route):
+    slabs = len(route)
+    pairs = [
+        (slabs * i + s, slabs * route[s](i) + s)
+        for s in range(slabs)
+        if route[s]
+        for i in range(peers)
+    ]
+    return lax.ppermute(block, ("pts", "slab"), pairs)
 
 
 def struct(shape, dtype):
@@ -274,33 +296,50 @@
     rows, width, peers = plan.rows, plan.width, plan.peers
     group, lines, held, cap = plan.group, plan.lines, plan.held, plan.cap
     blocks = orders.shape[0]
-    me = lax.axis_index("pts")
-    place = jnp.stack([me // group, me % group]).astype(I32)
+    me = lax.axis_index("pts").astype(I32)
+    slab = lax.axis_index("slab").astype(I32)
+    shift = group.bit_length() - 1
+    high, low = me >> shift, me & (group - 1)
+    by_slab = lambda first, second: jnp.where(slab == 0, first, second)
+    place = jnp.stack(
+        [by_slab(high, low), by_slab(low, high), by_slab(group, 1), by_slab(1, group), slab]
+    ).astype(I32)
 
     def along_line(pieces):
-        return [pieces[0]] + [flip(pieces[j], peers, group * j) for j in range(1, lines)]
-
-    def in_group(piece):
-        return [piece] + [flip(piece, peers, k) for k in range(1, group)]
-
-    opened = kernel_call(
-        functools.partial(open_body, plan),
-        [struct((rows, width), BF16)] + [struct((32, width), BF16)] * group,
-        [scalars(), whole(), whole(), whole()],
-    )(place, features, orders, norm_gains)
-    normed, notes = opened[0], opened[1:]
+        def far(j):
+            return move(pieces[j], peers, [lambda i: i ^ (group * j), lambda i: i ^ j])
+
+        return [pieces[0]] + [far(j) for j in range(1, lines)]
+
+    def from_group(piece, k):
+        return move(piece, peers, [lambda i: i ^ k, lambda i: i ^ (group * k)])
+
+    turned = move(
+        orders, peers, [None, lambda i: (i & (group - 1)) * group + (i >> shift)]
+    )
+    normed, own_orders = kernel_call(
+        norm_body, [struct((rows, width), BF16), struct(orders.shape, I32)], [whole()] * 3
+    )(features, norm_gains, orders)
+    normed, kept, sent = kernel_call(
+        functools.partial(note_body, plan),
+        [struct((rows, width), BF16)] + [struct((64, width), BF16)] * 2,
+        [scalars()] + [whole()] * 3,
+    )(place, normed, own_orders, turned)
     line_rows = along_line([normed] * lines)
-    notes = [notes[0]] + [flip(notes[k], peers, k) for k in range(1, group)]
+    mine, sent = kernel_call(join_body, [struct((32, width), BF16)] * 2, [whole()] * 2)(
+        kept, from_group(sent, 1)
+    )
+    notes = [mine, from_group(sent, 2)]
     packed, counts, members = kernel_call(
         functools.partial(first_pack_body, plan),
         [struct((held, width), BF16), struct((16, 128), I32), struct((16, width), BF16)],
-        [whole()] * (lines + group),
+        [whole()] * (lines + 2),
     )(*line_rows, *notes)
     state = features
     for b in range(blocks):
         last = b == blocks - 1
         tall = cap if b else cap + 16
-        parts = in_group(packed)
+        parts = [packed] + [from_group(packed, k) for k in range(1, group)]
         (queries,) = kernel_call(
             functools.partial(query_body, plan, b),
             [struct((held + 2 * TALL, width), BF16)],

time: 83.7 us -> 81.4 us (0.973)
  starting transfers between devices: 31.9 us -> 30.3 us
  waiting for transfers between devices: 29.5 us -> 28.6 us
    ppermute x21, starting transfers between devices: 31.9 us -> 30.3 us  [move(): return lax.ppermute(block, ('pts', 'slab'), pairs)]
    ppermute x21, waiting for transfers between devices: 29.5 us -> 28.6 us  [move(): return lax.ppermute(block, ('pts', 'slab'), pairs)]
  transfers between devices with their start and end apart: 21 -> 21, of which waited for: 15 -> 13; matrix products, arithmetic and copies ran while one was open for 0% -> 0% of each run, Pallas kernels for 0% -> 1%
where the time goes in v3:
time: 81.4 us; the launch traced here: 81.2 us
  starting transfers between devices  30.3 us (37%)
  waiting for transfers between devices  28.6 us (35%)
  Pallas kernels  19.7 us (24%)
  local copies, waits for them, and re-layouts  2.43 us (3%)
    ppermute x21, starting transfers between devices, move(): return lax.ppermute(block, ('pts', 'slab'), pairs)  30.3 us
    ppermute x21, waiting for transfers between devices, move(): return lax.ppermute(block, ('pts', 'slab'), pairs)  28.6 us
    pallas_call x2, Pallas kernels, by_lines(): kernel_call(functools.partial(attend_body, plan, b, b == 0), [struct((tal...  13.3 us
    pallas_call x2, Pallas kernels, by_lines(): kernel_call(functools.partial(store_body, plan, b, last), outs, [whole()]...  3.64 us
    unnamed x18, local copies, waits for them, and re-layouts  2.34 us
  transfers between devices with their start and end apart: 21, of which 13 were waited for; matrix products, arithmetic and copies ran while one was open for 0% of the time, Pallas kernels for 1%

profile of v3, /device:TPU:0, one launch (start us, length us, event | category | flops | bytes accessed | tf_op | source)
XLA Modules:
  0.0 81.2 jit_solution(162783857184801711)
XLA Ops:
  0.0 0.8 collective-permute-start
  0.8 0.0 copy-start.4
  0.8 0.9 %copy-done.4 = f32[256,256]{1,0:T(8,128)S(1)} copy-done((f32[256,256]{1,0:T(8,128)S(1)}, f32[256,256]{1,0:T(8,128)}, u32[]{:S(2)}) %copy-start.4) | copy-done | bytes 262168
  1.8 0.7 copy-done.6
  2.5 0.7 copy-done.8
  3.1 0.2 shard_map.73
  3.3 0.1 stack.23.place
  3.4 0.0 collective-permute-done.turned_ref
  3.4 0.9 %shard_map.74 = (bf16[256,256]{1,0:T(8,128)(2,1)S(1)}, bf16[64,256]{1,0:T(8,128)(2,1)S(1)}, bf16[64,256]{1,0:T(8,128)(2,1)S(1)}) custom-call(s32[5]{0:T(128)S(1)} %stack.23.place, bf16[256,256]{1,0:T(8,128)(2,1)S(1)} %get-tuple-element.28.row_ref, s32[2,256]{1,0:T(2,128)S(1)} %get-tuple-element.29.order_ref, s32[2,256]{1,0:T(2,128)S(1)} %collective-permute-done.turned_ref), custom_call_target="tpu_custom_call" | custom-call | tf_op jit(solution)/shard_map/pallas_call | solution.py:323
  4.3 5.1 %collective-permute-start.3 = (bf16[256,256]{1,0:T(8,128)(2,1)S(1)}, bf16[256,256]{1,0:T(8,128)(2,1)S(1)}, u32[]{:S(2)}, u32[]{:S(2)}) collective-permute-start(bf16[256,256]{1,0:T(8,128)(2,1)S(1)} %get-tuple-element.30.refs_0_), channel_id=1, source_target_pairs={{0,24},{2,26},{4,28},{6,30},{8,16},{10,18},{12,20},{14,22},{16,8},... | collective-permute-start | bytes 393224 | tf_op jit(solution)/shard_map/ppermute | solution.py:288
  9.4 0.0 collective-permute-start.2
  9.4 0.6 collective-permute-start.1
  10.1 1.6 %collective-permute-start.4 = (bf16[64,256]{1,0:T(8,128)(2,1)S(1)}, bf16[64,256]{1,0:T(8,128)(2,1)S(1)}, u32[]{:S(2)}, u32[]{:S(2)}) collective-permute-start(bf16[64,256]{1,0:T(8,128)(2,1)S(1)} %get-tuple-element.32), channel_id=1, source_target_pairs={{0,2},{2,0},{4,6},{6,4},{8,10},{10,8},{12,14},{14,12},{16,18},{18,... | collective-permute-start | bytes 98312 | tf_op jit(solution)/shard_map/ppermute | solution.py:288
  11.7 2.6 %collective-permute-done.4.got_ref = bf16[64,256]{1,0:T(8,128)(2,1)S(1)} collective-permute-done((bf16[64,256]{1,0:T(8,128)(2,1)S(1)}, bf16[64,256]{1,0:T(8,128)(2,1)S(1)}, u32[]{:S(2)}, u32[]{:S(2)}) %collective-permute-start.4) | collective-permute-done | bytes 32800 | tf_op jit(solution)/shard_map/ppermute | solution.py:288
  14.3 1.7 %collective-permute-start.5 = (bf16[32,256]{1,0:T(8,128)(2,1)S(1)}, bf16[32,256]{1,0:T(8,128)(2,1)S(1)}, u32[]{:S(2)}, u32[]{:S(2)}) collective-permute-start(bf16[32,256]{1,0:T(8,128)(2,1)S(1)} %get-tuple-element.34), channel_id=1, source_target_pairs={{0,4},{2,6},{4,0},{6,2},{8,12},{10,14},{12,8},{14,10},{16,20},{18,... | collective-permute-start | bytes 49160 | tf_op jit(solution)/shard_map/ppermute | solution.py:288
  16.1 2.1 %collective-permute-done.5.refs_5_ = bf16[32,256]{1,0:T(8,128)(2,1)S(1)} collective-permute-done((bf16[32,256]{1,0:T(8,128)(2,1)S(1)}, bf16[32,256]{1,0:T(8,128)(2,1)S(1)}, u32[]{:S(2)}, u32[]{:S(2)}) %collective-permute-start.5) | collective-permute-done | bytes 16416 | tf_op jit(solution)/shard_map/ppermute | solution.py:288
  18.1 0.0 collective-permute-done.3.refs_3_
  18.1 0.0 collective-permute-done.2.refs_2_
  18.2 0.0 collective-permute-done.1.refs_1_
  18.2 0.5 shard_map.76
  18.7 2.3 %collective-permute-start.8 = (bf16[384,256]{1,0:T(8,128)(2,1)S(1)}, bf16[384,256]{1,0:T(8,128)(2,1)S(1)}, u32[]{:S(2)}, u32[]{:S(2)}) collective-permute-start(bf16[384,256]{1,0:T(8,128)(2,1)S(1)} %get-tuple-element.36.row_ref.refs_0_), channel_id=1, source_target_pairs={{0,6},{2,4},{4,2},{6,0},{8,14},{10,12},{12,10},{14,8},{16,22},{18,... | collective-permute-start | bytes 589832 | tf_op jit(solution)/shard_map/ppermute | solution.py:288
  21.0 0.6 collective-permute-start.7
  21.6 0.6 collective-permute-start.6
  22.3 0.0 copy-done
  22.3 0.2 shard_map.77.refs_5_
  22.5 0.0 copy-start.1
  22.5 2.9 %collective-permute-done.8.refs_3_ = bf16[384,256]{1,0:T(8,128)(2,1)S(1)} collective-permute-done((bf16[384,256]{1,0:T(8,128)(2,1)S(1)}, bf16[384,256]{1,0:T(8,128)(2,1)S(1)}, u32[]{:S(2)}, u32[]{:S(2)}) %collective-permute-start.8) | collective-permute-done | bytes 196640 | tf_op jit(solution)/shard_map/ppermute | solution.py:288
  25.4 2.0 %collective-permute-done.7.refs_2_ = bf16[384,256]{1,0:T(8,128)(2,1)S(1)} collective-permute-done((bf16[384,256]{1,0:T(8,128)(2,1)S(1)}, bf16[384,256]{1,0:T(8,128)(2,1)S(1)}, u32[]{:S(2)}, u32[]{:S(2)}) %collective-permute-start.7) | collective-permute-done | bytes 196640 | tf_op jit(solution)/shard_map/ppermute | solution.py:288
  27.4 0.2 collective-permute-done.6.refs_1_
  27.7 6.6 %shard_map.78 = (bf16[112,256]{1,0:T(8,128)(2,1)S(1)}, bf16[112,256]{1,0:T(8,128)(2,1)S(1)}, bf16[112,256]{1,0:T(8,128)(2,1)S(1)}, bf16[112,256]{1,0:T(8,128)(2,1)S(1)}) custom-call(s32[16,128]{1,0:T(8,128)S(1)} %get-tuple-element.35.count_ref, bf16[384,256]{1,0:T(8,128)(2,1)S(1)} %get-tuple-element.36.row_ref.refs_0_, ...), custom_call_target="tpu_custom_call" | custom-call | tf_op jit(solution)/shard_map/pallas_call | solution.py:349
  34.3 0.0 copy-start.7
  34.4 1.2 %collective-permute-start.9 = (bf16[112,256]{1,0:T(8,128)(2,1)S(1)}, bf16[112,256]{1,0:T(8,128)(2,1)S(1)}, u32[]{:S(2)}, u32[]{:S(2)}) collective-permute-start(bf16[112,256]{1,0:T(8,128)(2,1)S(1)} %get-tuple-element.39), channel_id=1, source_target_pairs={{0,8},{2,10},{4,12},{6,14},{8,0},{10,2},{12,4},{14,6},{16,24},{18,... | collective-permute-start | bytes 172040 | tf_op jit(solution)/shard_map/ppermute | solution.py:288
  35.6 3.0 %collective-permute-start.10 = (bf16[112,256]{1,0:T(8,128)(2,1)S(1)}, bf16[112,256]{1,0:T(8,128)(2,1)S(1)}, u32[]{:S(2)}, u32[]{:S(2)}) collective-permute-start(bf16[112,256]{1,0:T(8,128)(2,1)S(1)} %get-tuple-element.40), channel_id=1, source_target_pairs={{0,16},{2,18},{4,20},{6,22},{8,24},{10,26},{12,28},{14,30},{16,0},... | collective-permute-start | bytes 172040 | tf_op jit(solution)/shard_map/ppermute | solution.py:288
  38.6 0.2 collective-permute-start.11
  38.8 0.0 collective-permute-done.9.refs_1_.refs_5_
  38.8 2.5 %collective-permute-done.10.refs_2_.refs_6_ = bf16[112,256]{1,0:T(8,128)(2,1)S(1)} collective-permute-done((bf16[112,256]{1,0:T(8,128)(2,1)S(1)}, bf16[112,256]{1,0:T(8,128)(2,1)S(1)}, u32[]{:S(2)}, u32[]{:S(2)}) %collective-permute-start.10) | collective-permute-done | bytes 57376 | tf_op jit(solution)/shard_map/ppermute | solution.py:288
  41.3 3.2 %collective-permute-done.11.refs_3_.refs_7_ = bf16[112,256]{1,0:T(8,128)(2,1)S(1)} collective-permute-done((bf16[112,256]{1,0:T(8,128)(2,1)S(1)}, bf16[112,256]{1,0:T(8,128)(2,1)S(1)}, u32[]{:S(2)}, u32[]{:S(2)}) %collective-permute-start.11) | collective-permute-done | bytes 57376 | tf_op jit(solution)/shard_map/ppermute | solution.py:288
  44.5 0.0 copy-done.2
  44.5 0.0 copy-done.3
  44.6 0.0 copy-done.5
  44.6 0.0 copy-done.7
  44.6 1.7 %shard_map.79 = (f32[256,256]{1,0:T(8,128)S(1)}, bf16[96,256]{1,0:T(8,128)(2,1)S(1)}, bf16[96,256]{1,0:T(8,128)(2,1)S(1)}, bf16[96,256]{1,0:T(8,128)(2,1)S(1)}, bf16[96,256]{1,0:T(8,128)(2,1)S(1)}) custom-call(bf16[112,256]{1,0:T(8,128)(2,1)S(1)} %get-tuple-element.38.refs_0_.refs_4_, bf16[112,256]{1,0:T(8,128)(2,1)S(1)} %collective-permute-done.9.refs_1_.refs_5_, ...), custom_call_target="tpu_custom_call" | custom-call | tf_op jit(solution)/shard_map/pallas_call | solution.py:367
  46.3 0.1 collective-permute-start.12
  46.3 1.2 %collective-permute-start.13 = (bf16[96,256]{1,0:T(8,128)(2,1)S(1)}, bf16[96,256]{1,0:T(8,128)(2,1)S(1)}, u32[]{:S(2)}, u32[]{:S(2)}) collective-permute-start(bf16[96,256]{1,0:T(8,128)(2,1)S(1)} %get-tuple-element.44), channel_id=1, source_target_pairs={{0,16},{2,18},{4,20},{6,22},{8,24},{10,26},{12,28},{14,30},{16,0},... | collective-permute-start | bytes 147464 | tf_op jit(solution)/shard_map/ppermute | solution.py:288
  47.5 3.2 %collective-permute-start.14 = (bf16[96,256]{1,0:T(8,128)(2,1)S(1)}, bf16[96,256]{1,0:T(8,128)(2,1)S(1)}, u32[]{:S(2)}, u32[]{:S(2)}) collective-permute-start(bf16[96,256]{1,0:T(8,128)(2,1)S(1)} %get-tuple-element.45), channel_id=1, source_target_pairs={{0,24},{2,26},{4,28},{6,30},{8,16},{10,18},{12,20},{14,22},{16,8},... | collective-permute-start | bytes 147464 | tf_op jit(solution)/shard_map/ppermute | solution.py:288
  50.7 0.0 collective-permute-done.12.refs_1_
  50.7 0.7 collective-permute-done.13.refs_2_
  51.4 2.0 %collective-permute-done.14.refs_3_ = bf16[96,256]{1,0:T(8,128)(2,1)S(1)} collective-permute-done((bf16[96,256]{1,0:T(8,128)(2,1)S(1)}, bf16[96,256]{1,0:T(8,128)(2,1)S(1)}, u32[]{:S(2)}, u32[]{:S(2)}) %collective-permute-start.14) | collective-permute-done | bytes 49184 | tf_op jit(solution)/shard_map/ppermute | solution.py:288
  53.4 0.7 shard_map.80.row_ref.refs_0_
  54.1 1.7 %collective-permute-start.17 = (bf16[384,256]{1,0:T(8,128)(2,1)S(1)}, bf16[384,256]{1,0:T(8,128)(2,1)S(1)}, u32[]{:S(2)}, u32[]{:S(2)}) collective-permute-start(bf16[384,256]{1,0:T(8,128)(2,1)S(1)} %shard_map.80.row_ref.refs_0_), channel_id=1, source_target_pairs={{0,6},{2,4},{4,2},{6,0},{8,14},{10,12},{12,10},{14,8},{16,22},{18,... | collective-permute-start | bytes 589832 | tf_op jit(solution)/shard_map/ppermute | solution.py:288
  55.8 1.3 %collective-permute-start.16 = (bf16[384,256]{1,0:T(8,128)(2,1)S(1)}, bf16[384,256]{1,0:T(8,128)(2,1)S(1)}, u32[]{:S(2)}, u32[]{:S(2)}) collective-permute-start(bf16[384,256]{1,0:T(8,128)(2,1)S(1)} %shard_map.80.row_ref.refs_0_), channel_id=1, source_target_pairs={{0,4},{2,6},{4,0},{6,2},{8,12},{10,14},{12,8},{14,10},{16,20},{18,... | collective-permute-start | bytes 589832 | tf_op jit(solution)/shard_map/ppermute | solution.py:288
  57.1 0.6 collective-permute-start.15
  57.7 0.2 shard_map.81.refs_5_
  57.9 3.0 %collective-permute-done.17.refs_3_ = bf16[384,256]{1,0:T(8,128)(2,1)S(1)} collective-permute-done((bf16[384,256]{1,0:T(8,128)(2,1)S(1)}, bf16[384,256]{1,0:T(8,128)(2,1)S(1)}, u32[]{:S(2)}, u32[]{:S(2)}) %collective-permute-start.17) | collective-permute-done | bytes 196640 | tf_op jit(solution)/shard_map/ppermute | solution.py:288
  60.9 2.0 %collective-permute-done.16.refs_2_ = bf16[384,256]{1,0:T(8,128)(2,1)S(1)} collective-permute-done((bf16[384,256]{1,0:T(8,128)(2,1)S(1)}, bf16[384,256]{1,0:T(8,128)(2,1)S(1)}, u32[]{:S(2)}, u32[]{:S(2)}) %collective-permute-start.16) | collective-permute-done | bytes 196640 | tf_op jit(solution)/shard_map/ppermute | solution.py:288
  62.9 0.0 collective-permute-done.15.refs_1_
  62.9 6.6 %shard_map.82 = (bf16[96,256]{1,0:T(8,128)(2,1)S(1)}, bf16[96,256]{1,0:T(8,128)(2,1)S(1)}, bf16[96,256]{1,0:T(8,128)(2,1)S(1)}, bf16[96,256]{1,0:T(8,128)(2,1)S(1)}) custom-call(s32[16,128]{1,0:T(8,128)S(1)} %get-tuple-element.35.count_ref, bf16[384,256]{1,0:T(8,128)(2,1)S(1)} %shard_map.80.row_ref.refs_0_, ...), custom_call_target="tpu_custom_call" | custom-call | tf_op jit(solution)/shard_map/pallas_call | solution.py:349
  69.5 0.1 collective-permute-start.18
  69.6 3.8 %collective-permute-start.19 = (bf16[96,256]{1,0:T(8,128)(2,1)S(1)}, bf16[96,256]{1,0:T(8,128)(2,1)S(1)}, u32[]{:S(2)}, u32[]{:S(2)}) collective-permute-start(bf16[96,256]{1,0:T(8,128)(2,1)S(1)} %get-tuple-element.48), channel_id=1, source_target_pairs={{0,16},{2,18},{4,20},{6,22},{8,24},{10,26},{12,28},{14,30},{16,0},... | collective-permute-start | bytes 147464 | tf_op jit(solution)/shard_map/ppermute | solution.py:288
  73.3 0.6 collective-permute-start.20
  74.0 0.0 collective-permute-done.18.refs_1_
  74.0 1.4 %collective-permute-done.19.refs_2_ = bf16[96,256]{1,0:T(8,128)(2,1)S(1)} collective-permute-done((bf16[96,256]{1,0:T(8,128)(2,1)S(1)}, bf16[96,256]{1,0:T(8,128)(2,1)S(1)}, u32[]{:S(2)}, u32[]{:S(2)}) %collective-permute-start.19) | collective-permute-done | bytes 49184 | tf_op jit(solution)/shard_map/ppermute | solution.py:288
  75.4 3.8 %collective-permute-done.20.refs_3_ = bf16[96,256]{1,0:T(8,128)(2,1)S(1)} collective-permute-done((bf16[96,256]{1,0:T(8,128)(2,1)S(1)}, bf16[96,256]{1,0:T(8,128)(2,1)S(1)}, u32[]{:S(2)}, u32[]{:S(2)}) %collective-permute-start.20) | collective-permute-done | bytes 49184 | tf_op jit(solution)/shard_map/ppermute | solution.py:288
  79.2 2.0 %shard_map.83 = f32[256,256]{1,0:T(8,128)} custom-call(bf16[96,256]{1,0:T(8,128)(2,1)S(1)} %get-tuple-element.46.refs_0_, bf16[96,256]{1,0:T(8,128)(2,1)S(1)} %collective-permute-done.18.refs_1_, bf16[96,256]{1,0:T(8,128)(2,1)S(1)} %collective-permute-done.19.refs_2_, bf16[96,256]{1,0:T(8,128)(2,1)S(1)} %collective-permute-done.20.refs_3_, ...), custom_call_target="tpu_custom_call" | custom-call | tf_op jit(solution)/shard_map/pallas_call | solution.py:367
  (8 shorter events, 0.0 us)
Async XLA Ops:
  0.0 22.3 %copy-start = (bf16[2,256,768]{2,1,0:T(8,128)(2,1)S(1)}, bf16[2,256,768]{2,1,0:T(8,128)(2,1)}, u32[]{:S(2)}) copy-start(bf16[2,256,768]{2,1,0:T(8,128)(2,1)} %refs_4_.5) | copy-start | bytes 2359300
  0.0 3.4 %collective-permute-start = (s32[2,256]{1,0:T(2,128)}, s32[2,256]{1,0:T(2,128)S(1)}, u32[]{:S(2)}, u32[]{:S(2)}) collective-permute-start(s32[2,256]{1,0:T(2,128)} %order_ref.1), channel_id=1, source_target_pairs={{1,1},{3,9},{5,17},{7,25},{9,3},{11,11},{13,19},{15,27},{17,5},{19... | collective-permute-start | bytes 6152 | tf_op jit(solution)/shard_map/ppermute | solution.py:288
  0.8 1.0 %copy-start.4 = (f32[256,256]{1,0:T(8,128)S(1)}, f32[256,256]{1,0:T(8,128)}, u32[]{:S(2)}) copy-start(f32[256,256]{1,0:T(8,128)} %refs_4_.4) | copy-start | bytes 786436
  1.8 0.7 copy-start.6
  2.5 0.7 copy-start.8
  4.3 13.8 %collective-permute-start.3 = (bf16[256,256]{1,0:T(8,128)(2,1)S(1)}, bf16[256,256]{1,0:T(8,128)(2,1)S(1)}, u32[]{:S(2)}, u32[]{:S(2)}) collective-permute-start(bf16[256,256]{1,0:T(8,128)(2,1)S(1)} %get-tuple-element.30.refs_0_), channel_id=1, source_target_pairs={{0,24},{2,26},{4,28},{6,30},{8,16},{10,18},{12,20},{14,22},{16,8},... | collective-permute-start | bytes 393224 | tf_op jit(solution)/shard_map/ppermute | solution.py:288
  9.4 8.7 %collective-permute-start.2 = (bf16[256,256]{1,0:T(8,128)(2,1)S(1)}, bf16[256,256]{1,0:T(8,128)(2,1)S(1)}, u32[]{:S(2)}, u32[]{:S(2)}) collective-permute-start(bf16[256,256]{1,0:T(8,128)(2,1)S(1)} %get-tuple-element.30.refs_0_), channel_id=1, source_target_pairs={{0,16},{2,18},{4,20},{6,22},{8,24},{10,26},{12,28},{14,30},{16,0},... | collective-permute-start | bytes 393224 | tf_op jit(solution)/shard_map/ppermute | solution.py:288
  9.4 8.7 %collective-permute-start.1 = (bf16[256,256]{1,0:T(8,128)(2,1)S(1)}, bf16[256,256]{1,0:T(8,128)(2,1)S(1)}, u32[]{:S(2)}, u32[]{:S(2)}) collective-permute-start(bf16[256,256]{1,0:T(8,128)(2,1)S(1)} %get-tuple-element.30.refs_0_), channel_id=1, source_target_pairs={{0,8},{2,10},{4,12},{6,14},{8,0},{10,2},{12,4},{14,6},{16,24},{18,... | collective-permute-start | bytes 393224 | tf_op jit(solution)/shard_map/ppermute | solution.py:288
  10.1 4.3 %collective-permute-start.4 = (bf16[64,256]{1,0:T(8,128)(2,1)S(1)}, bf16[64,256]{1,0:T(8,128)(2,1)S(1)}, u32[]{:S(2)}, u32[]{:S(2)}) collective-permute-start(bf16[64,256]{1,0:T(8,128)(2,1)S(1)} %get-tuple-element.32), channel_id=1, source_target_pairs={{0,2},{2,0},{4,6},{6,4},{8,10},{10,8},{12,14},{14,12},{16,18},{18,... | collective-permute-start | bytes 98312 | tf_op jit(solution)/shard_map/ppermute | solution.py:288
  14.3 3.8 %collective-permute-start.5 = (bf16[32,256]{1,0:T(8,128)(2,1)S(1)}, bf16[32,256]{1,0:T(8,128)(2,1)S(1)}, u32[]{:S(2)}, u32[]{:S(2)}) collective-permute-start(bf16[32,256]{1,0:T(8,128)(2,1)S(1)} %get-tuple-element.34), channel_id=1, source_target_pairs={{0,4},{2,6},{4,0},{6,2},{8,12},{10,14},{12,8},{14,10},{16,20},{18,... | collective-permute-start | bytes 49160 | tf_op jit(solution)/shard_map/ppermute | solution.py:288
  18.7 6.7 %collective-permute-start.8 = (bf16[384,256]{1,0:T(8,128)(2,1)S(1)}, bf16[384,256]{1,0:T(8,128)(2,1)S(1)}, u32[]{:S(2)}, u32[]{:S(2)}) collective-permute-start(bf16[384,256]{1,0:T(8,128)(2,1)S(1)} %get-tuple-element.36.row_ref.refs_0_), channel_id=1, source_target_pairs={{0,6},{2,4},{4,2},{6,0},{8,14},{10,12},{12,10},{14,8},{16,22},{18,... | collective-permute-start | bytes 589832 | tf_op jit(solution)/shard_map/ppermute | solution.py:288
  21.0 6.4 %collective-permute-start.7 = (bf16[384,256]{1,0:T(8,128)(2,1)S(1)}, bf16[384,256]{1,0:T(8,128)(2,1)S(1)}, u32[]{:S(2)}, u32[]{:S(2)}) collective-permute-start(bf16[384,256]{1,0:T(8,128)(2,1)S(1)} %get-tuple-element.36.row_ref.refs_0_), channel_id=1, source_target_pairs={{0,4},{2,6},{4,0},{6,2},{8,12},{10,14},{12,8},{14,10},{16,20},{18,... | collective-permute-start | bytes 589832 | tf_op jit(solution)/shard_map/ppermute | solution.py:288
  21.6 6.1 %collective-permute-start.6 = (bf16[384,256]{1,0:T(8,128)(2,1)S(1)}, bf16[384,256]{1,0:T(8,128)(2,1)S(1)}, u32[]{:S(2)}, u32[]{:S(2)}) collective-permute-start(bf16[384,256]{1,0:T(8,128)(2,1)S(1)} %get-tuple-element.36.row_ref.refs_0_), channel_id=1, source_target_pairs={{0,2},{2,0},{4,6},{6,4},{8,10},{10,8},{12,14},{14,12},{16,18},{18,... | collective-permute-start | bytes 589832 | tf_op jit(solution)/shard_map/ppermute | solution.py:288
  22.3 22.3 %copy-start.2 = (bf16[2,1024,256]{2,1,0:T(8,128)(2,1)S(1)}, bf16[2,1024,256]{2,1,0:T(8,128)(2,1)}, u32[]{:S(2)}) copy-start(bf16[2,1024,256]{2,1,0:T(8,128)(2,1)} %refs_12_.1) | copy-start | bytes 3145732
  22.5 22.1 %copy-start.1 = (bf16[2,256,1024]{2,1,0:T(8,128)(2,1)S(1)}, bf16[2,256,1024]{2,1,0:T(8,128)(2,1)}, u32[]{:S(2)}) copy-start(bf16[2,256,1024]{2,1,0:T(8,128)(2,1)} %refs_11_.1) | copy-start | bytes 3145732
  27.7 16.9 %copy-start.3 = (bf16[2,256,256]{2,1,0:T(8,128)(2,1)S(1)}, bf16[2,256,256]{2,1,0:T(8,128)(2,1)}, u32[]{:S(2)}) copy-start(bf16[2,256,256]{2,1,0:T(8,128)(2,1)} %refs_10_.1) | copy-start | bytes 786436
  27.7 16.9 %copy-start.5 = (f32[256,256]{1,0:T(8,128)S(1)}, f32[256,256]{1,0:T(8,128)}, u32[]{:S(2)}) copy-start(f32[256,256]{1,0:T(8,128)} %refs_4_.4) | copy-start | bytes 786436
  34.3 10.2 %copy-start.7 = (f32[2,2,256]{2,1,0:T(2,128)S(1)}, f32[2,2,256]{2,1,0:T(2,128)}, u32[]{:S(2)}) copy-start(f32[2,2,256]{2,1,0:T(2,128)} %refs_9_.1) | copy-start | bytes 12292
  34.4 4.5 %collective-permute-start.9 = (bf16[112,256]{1,0:T(8,128)(2,1)S(1)}, bf16[112,256]{1,0:T(8,128)(2,1)S(1)}, u32[]{:S(2)}, u32[]{:S(2)}) collective-permute-start(bf16[112,256]{1,0:T(8,128)(2,1)S(1)} %get-tuple-element.39), channel_id=1, source_target_pairs={{0,8},{2,10},{4,12},{6,14},{8,0},{10,2},{12,4},{14,6},{16,24},{18,... | collective-permute-start | bytes 172040 | tf_op jit(solution)/shard_map/ppermute | solution.py:288
  35.6 5.8 %collective-permute-start.10 = (bf16[112,256]{1,0:T(8,128)(2,1)S(1)}, bf16[112,256]{1,0:T(8,128)(2,1)S(1)}, u32[]{:S(2)}, u32[]{:S(2)}) collective-permute-start(bf16[112,256]{1,0:T(8,128)(2,1)S(1)} %get-tuple-element.40), channel_id=1, source_target_pairs={{0,16},{2,18},{4,20},{6,22},{8,24},{10,26},{12,28},{14,30},{16,0},... | collective-permute-start | bytes 172040 | tf_op jit(solution)/shard_map/ppermute | solution.py:288
  38.6 6.0 %collective-permute-start.11 = (bf16[112,256]{1,0:T(8,128)(2,1)S(1)}, bf16[112,256]{1,0:T(8,128)(2,1)S(1)}, u32[]{:S(2)}, u32[]{:S(2)}) collective-permute-start(bf16[112,256]{1,0:T(8,128)(2,1)S(1)} %get-tuple-element.41), channel_id=1, source_target_pairs={{0,24},{2,26},{4,28},{6,30},{8,16},{10,18},{12,20},{14,22},{16,8},... | collective-permute-start | bytes 172040 | tf_op jit(solution)/shard_map/ppermute | solution.py:288
  46.3 4.5 %collective-permute-start.12 = (bf16[96,256]{1,0:T(8,128)(2,1)S(1)}, bf16[96,256]{1,0:T(8,128)(2,1)S(1)}, u32[]{:S(2)}, u32[]{:S(2)}) collective-permute-start(bf16[96,256]{1,0:T(8,128)(2,1)S(1)} %get-tuple-element.43), channel_id=1, source_target_pairs={{0,8},{2,10},{4,12},{6,14},{8,0},{10,2},{12,4},{14,6},{16,24},{18,... | collective-permute-start | bytes 147464 | tf_op jit(solution)/shard_map/ppermute | solution.py:288
  46.3 5.1 %collective-permute-start.13 = (bf16[96,256]{1,0:T(8,128)(2,1)S(1)}, bf16[96,256]{1,0:T(8,128)(2,1)S(1)}, u32[]{:S(2)}, u32[]{:S(2)}) collective-permute-start(bf16[96,256]{1,0:T(8,128)(2,1)S(1)} %get-tuple-element.44), channel_id=1, source_target_pairs={{0,16},{2,18},{4,20},{6,22},{8,24},{10,26},{12,28},{14,30},{16,0},... | collective-permute-start | bytes 147464 | tf_op jit(solution)/shard_map/ppermute | solution.py:288
  47.5 5.9 %collective-permute-start.14 = (bf16[96,256]{1,0:T(8,128)(2,1)S(1)}, bf16[96,256]{1,0:T(8,128)(2,1)S(1)}, u32[]{:S(2)}, u32[]{:S(2)}) collective-permute-start(bf16[96,256]{1,0:T(8,128)(2,1)S(1)} %get-tuple-element.45), channel_id=1, source_target_pairs={{0,24},{2,26},{4,28},{6,30},{8,16},{10,18},{12,20},{14,22},{16,8},... | collective-permute-start | bytes 147464 | tf_op jit(solution)/shard_map/ppermute | solution.py:288
  54.1 6.7 %collective-permute-start.17 = (bf16[384,256]{1,0:T(8,128)(2,1)S(1)}, bf16[384,256]{1,0:T(8,128)(2,1)S(1)}, u32[]{:S(2)}, u32[]{:S(2)}) collective-permute-start(bf16[384,256]{1,0:T(8,128)(2,1)S(1)} %shard_map.80.row_ref.refs_0_), channel_id=1, source_target_pairs={{0,6},{2,4},{4,2},{6,0},{8,14},{10,12},{12,10},{14,8},{16,22},{18,... | collective-permute-start | bytes 589832 | tf_op jit(solution)/shard_map/ppermute | solution.py:288
  55.8 7.0 %collective-permute-start.16 = (bf16[384,256]{1,0:T(8,128)(2,1)S(1)}, bf16[384,256]{1,0:T(8,128)(2,1)S(1)}, u32[]{:S(2)}, u32[]{:S(2)}) collective-permute-start(bf16[384,256]{1,0:T(8,128)(2,1)S(1)} %shard_map.80.row_ref.refs_0_), channel_id=1, source_target_pairs={{0,4},{2,6},{4,0},{6,2},{8,12},{10,14},{12,8},{14,10},{16,20},{18,... | collective-permute-start | bytes 589832 | tf_op jit(solution)/shard_map/ppermute | solution.py:288
  57.1 5.8 %collective-permute-start.15 = (bf16[384,256]{1,0:T(8,128)(2,1)S(1)}, bf16[384,256]{1,0:T(8,128)(2,1)S(1)}, u32[]{:S(2)}, u32[]{:S(2)}) collective-permute-start(bf16[384,256]{1,0:T(8,128)(2,1)S(1)} %shard_map.80.row_ref.refs_0_), channel_id=1, source_target_pairs={{0,2},{2,0},{4,6},{6,4},{8,10},{10,8},{12,14},{14,12},{16,18},{18,... | collective-permute-start | bytes 589832 | tf_op jit(solution)/shard_map/ppermute | solution.py:288
  69.5 4.5 %collective-permute-start.18 = (bf16[96,256]{1,0:T(8,128)(2,1)S(1)}, bf16[96,256]{1,0:T(8,128)(2,1)S(1)}, u32[]{:S(2)}, u32[]{:S(2)}) collective-permute-start(bf16[96,256]{1,0:T(8,128)(2,1)S(1)} %get-tuple-element.47), channel_id=1, source_target_pairs={{0,8},{2,10},{4,12},{6,14},{8,0},{10,2},{12,4},{14,6},{16,24},{18,... | collective-permute-start | bytes 147464 | tf_op jit(solution)/shard_map/ppermute | solution.py:288
  69.6 5.8 %collective-permute-start.19 = (bf16[96,256]{1,0:T(8,128)(2,1)S(1)}, bf16[96,256]{1,0:T(8,128)(2,1)S(1)}, u32[]{:S(2)}, u32[]{:S(2)}) collective-permute-start(bf16[96,256]{1,0:T(8,128)(2,1)S(1)} %get-tuple-element.48), channel_id=1, source_target_pairs={{0,16},{2,18},{4,20},{6,22},{8,24},{10,26},{12,28},{14,30},{16,0},... | collective-permute-start | bytes 147464 | tf_op jit(solution)/shard_map/ppermute | solution.py:288
  73.3 5.9 %collective-permute-start.20 = (bf16[96,256]{1,0:T(8,128)(2,1)S(1)}, bf16[96,256]{1,0:T(8,128)(2,1)S(1)}, u32[]{:S(2)}, u32[]{:S(2)}) collective-permute-start(bf16[96,256]{1,0:T(8,128)(2,1)S(1)} %get-tuple-element.49), channel_id=1, source_target_pairs={{0,24},{2,26},{4,28},{6,30},{8,16},{10,18},{12,20},{14,22},{16,8},... | collective-permute-start | bytes 147464 | tf_op jit(solution)/shard_map/ppermute | solution.py:288

commit v4 on v3

--- a/solution.py
+++ b/solution.py
@@ -14,7 +14,6 @@
 NT = (((1,), (1,)), ((), ()))
 TN = (((0,), (0,)), ((), ()))
 VMEM = pltpu.VMEM
-SMEM = pltpu.SMEM
 
 
 def layer_norm(values, gain_row):
@@ -80,10 +79,6 @@
     return pl.BlockSpec(memory_space=VMEM)
 
 
-def scalars():
-    return pl.BlockSpec(memory_space=SMEM)
-
-
 def norm_body(feature_ref, gain_ref, order_ref, normed_ref, passed_ref):
     passed_ref[...] = order_ref[...]
     normed_ref[...] = layer_norm(feature_ref[...], gain_ref[0, 0:1, :]).astype(BF16)
@@ -91,7 +86,7 @@
 
 def note_body(plan, place, row_ref, order_ref, turned_ref, passed_ref, kept_ref, sent_ref):
     passed_ref[...] = row_ref[...]
-    line, column, line_step, column_step, slab = (place[i] for i in range(5))
+    line, column, line_step, column_step, slab = (place[0, i] for i in range(5))
     order = jnp.where(slab == 0, order_ref[...], turned_ref[...])
     bits = plan.rows.bit_length() - 1
     entry = iota((32, 1), 0)
@@ -126,7 +121,8 @@
         half[32 * (k >> 1) : 32 * (k >> 1) + 32] = notes[32 * k : 32 * (k + 1)].astype(BF16)
 
 
-def join_body(kept_ref, got_ref, mine_ref, sent_ref):
+def join_body(kept_ref, got_ref, row_ref, mine_ref, sent_ref, passed_ref):
+    passed_ref[...] = row_ref[...]
     total = (kept_ref[...].astype(F32) + got_ref[...].astype(F32)).astype(BF16)
     mine_ref[...] = total[:32]
     sent_ref[...] = total[32:]
@@ -151,20 +147,29 @@
     packed_ref[...] = out.astype(BF16)
 
 
-def pack_body(plan, b, count_ref, *refs):
-    piece_refs, packed_ref, room = refs[:4], refs[4], refs[5]
+def lay_body(plan, *refs):
+    piece_refs, laid_ref = refs[:-1], refs[-1]
+    for j in range(plan.lines):
+        laid_ref[j * plan.cap : (j + 1) * plan.cap] = piece_refs[j][...]
+
+
+def pack_rows(plan, packed, offset, counts, piece_ref, room):
+    if packed:
+        room[pl.ds(pl.multiple_of(offset, 16), plan.held), :] = piece_ref[...]
+    for j in range(plan.lines):
+        if not packed:
+            piece = piece_ref[j * plan.cap : (j + 1) * plan.cap, :]
+            room[pl.ds(pl.multiple_of(offset, 16), plan.cap), :] = piece
+        offset = offset + counts[j]
+    return offset
+
+
+def query_body(plan, b, count_ref, row_ref, weight_ref, query_ref, room):
+    counts = [count_ref[j, 64 * b] for j in range(plan.lines)]
     room[...] = jnp.zeros(room.shape, room.dtype)
-    offset = 0
-    for j in range(plan.lines):
-        room[pl.ds(pl.multiple_of(offset, 16), plan.cap), :] = piece_refs[j][...]
-        offset = offset + count_ref[j, 64 * b]
-    packed_ref[...] = room[0 : plan.held]
-
-
-def query_body(plan, b, row_ref, weight_ref, query_ref):
-    head_size = plan.width // HEADS
-    projected = matmul(row_ref[...], weight_ref[b, :, : plan.width]).astype(BF16)
-    query_ref[0 : plan.held] = (projected * (head_size**-0.5)).astype(BF16)
+    pack_rows(plan, b == 0, 0, counts, row_ref, room)
+    projected = matmul(room[0 : plan.held], weight_ref[b, :, : plan.width]).astype(BF16)
+    query_ref[0 : plan.held] = (projected * ((plan.width // HEADS) ** -0.5)).astype(BF16)
     query_ref[plan.held :] = jnp.zeros((2 * TALL, plan.width), BF16)
 
 
@@ -179,9 +184,8 @@
     half_heads = HEADS // 2
     offset = 0
     for k in range(group):
-        all_rows[pl.ds(pl.multiple_of(offset, 16), held), :] = part_refs[k][...]
-        for j in range(lines):
-            offset = offset + count_ref[k * lines + j, 64 * b]
+        counts = [count_ref[k * lines + j, 64 * b] for j in range(lines)]
+        offset = pack_rows(plan, b == 0, offset, counts, part_refs[k], all_rows)
     patch_rows = all_rows[0:PATCH]
     keys[...] = matmul(
         weight_ref[b, :, width : 2 * width], patch_rows, (((0,), (1,)), ((), ()))
@@ -303,7 +307,7 @@
     by_slab = lambda first, second: jnp.where(slab == 0, first, second)
     place = jnp.stack(
         [by_slab(high, low), by_slab(low, high), by_slab(group, 1), by_slab(1, group), slab]
-    ).astype(I32)
+    ).astype(I32)[None]
 
     def along_line(pieces):
         def far(j):
@@ -323,12 +327,12 @@
     normed, kept, sent = kernel_call(
         functools.partial(note_body, plan),
         [struct((rows, width), BF16)] + [struct((64, width), BF16)] * 2,
-        [scalars()] + [whole()] * 3,
+        [whole()] * 4,
     )(place, normed, own_orders, turned)
-    line_rows = along_line([normed] * lines)
-    mine, sent = kernel_call(join_body, [struct((32, width), BF16)] * 2, [whole()] * 2)(
-        kept, from_group(sent, 1)
-    )
+    mine, sent, near = kernel_call(
+        join_body, [struct((32, width), BF16)] * 2 + [struct((rows, width), BF16)], [whole()] * 3
+    )(kept, from_group(sent, 1), normed)
+    line_rows = along_line([normed, near] + [normed] * (lines - 2))
     notes = [mine, from_group(sent, 2)]
     packed, counts, members = kernel_call(
         functools.partial(first_pack_body, plan),
@@ -343,13 +347,14 @@
         (queries,) = kernel_call(
             functools.partial(query_body, plan, b),
             [struct((held + 2 * TALL, width), BF16)],
-            [whole(), whole()],
-        )(packed, qkv_weight)
+            [whole()] * 3,
+            [pltpu.VMEM((held + cap, width), BF16)],
+        )(counts, packed, qkv_weight)
         extra = [] if b else [members]
         mixed = kernel_call(
             functools.partial(attend_body, plan, b, b == 0),
             [struct((tall, width), BF16)] * lines,
-            [scalars()] + [whole()] * (group + 2 + len(extra)),
+            [whole()] * (group + 3 + len(extra)),
             [
                 pltpu.VMEM((PATCH + held, width), BF16),
                 pltpu.VMEM((width, PATCH), BF16),
@@ -381,11 +386,8 @@
         if not last:
             arrived = along_line(stored[1:])
             (packed,) = kernel_call(
-                functools.partial(pack_body, plan, b + 1),
-                [struct((held, width), BF16)],
-                [scalars()] + [whole()] * lines,
-                [pltpu.VMEM((held + cap, width), BF16)],
-            )(counts, *arrived)
+                functools.partial(lay_body, plan), [struct((held, width), BF16)], [whole()] * lines
+            )(*arrived)
     return state
 
 

time: 81.4 us -> 77.4 us (0.951)
  Pallas kernels: 19.7 us -> 17.4 us
  waiting for transfers between devices: 28.6 us -> 27 us
    ppermute x21, waiting for transfers between devices: 28.6 us -> 27 us  [move(): return lax.ppermute(block, ('pts', 'slab'), pairs)]
    pallas_call x2, Pallas kernels: 13.3 us -> 12.1 us  [by_lines(): kernel_call(functools.partial(attend_body, plan, b, b == 0), [struct((tal...]
where the time goes in v4:
time: 77.4 us; the launch traced here: 77.2 us
  starting transfers between devices  30.2 us (39%)
  waiting for transfers between devices  27 us (35%)
  Pallas kernels  17.4 us (22%)
  local copies, waits for them, and re-layouts  2.43 us (3%)
    ppermute x21, starting transfers between devices, move(): return lax.ppermute(block, ('pts', 'slab'), pairs)  30.2 us
    ppermute x21, waiting for transfers between devices, move(): return lax.ppermute(block, ('pts', 'slab'), pairs)  27 us
    pallas_call x2, Pallas kernels, by_lines(): kernel_call(functools.partial(attend_body, plan, b, b == 0), [struct((tal...  12.1 us
    pallas_call x2, Pallas kernels, by_lines(): kernel_call(functools.partial(store_body, plan, b, last), outs, [whole()]...  3.64 us
    unnamed x18, local copies, waits for them, and re-layouts  2.34 us
  transfers between devices with their start and end apart: 21, of which 13 were waited for; matrix products, arithmetic and copies ran while one was open for 0% of the time, Pallas kernels for 1%

profile of v4, /device:TPU:0, one launch (start us, length us, event | category | flops | bytes accessed | tf_op | source)
XLA Modules:
  0.0 77.2 jit_solution(15077311167394644349)
XLA Ops:
  0.0 0.8 %collective-permute-start = (s32[2,256]{1,0:T(2,128)}, s32[2,256]{1,0:T(2,128)S(1)}, u32[]{:S(2)}, u32[]{:S(2)}) collective-permute-start(s32[2,256]{1,0:T(2,128)} %order_ref.1), channel_id=1, source_target_pairs={{1,1},{3,9},{5,17},{7,25},{9,3},{11,11},{13,19},{15,27},{17,5},{19... | collective-permute-start | bytes 6152 | tf_op jit(solution)/shard_map/ppermute | solution.py:292
  0.8 0.0 copy-start.4
  0.8 0.9 %copy-done.4 = f32[256,256]{1,0:T(8,128)S(1)} copy-done((f32[256,256]{1,0:T(8,128)S(1)}, f32[256,256]{1,0:T(8,128)}, u32[]{:S(2)}) %copy-start.4) | copy-done | bytes 262168
  1.8 0.7 copy-done.6
  2.5 0.7 copy-done.8
  3.1 0.2 shard_map.73
  3.3 0.1 stack.23
  3.4 0.0 collective-permute-done.turned_ref
  3.4 0.4 shard_map.74
  3.9 3.0 %collective-permute-start.1 = (bf16[64,256]{1,0:T(8,128)(2,1)S(1)}, bf16[64,256]{1,0:T(8,128)(2,1)S(1)}, u32[]{:S(2)}, u32[]{:S(2)}) collective-permute-start(bf16[64,256]{1,0:T(8,128)(2,1)S(1)} %get-tuple-element.33), channel_id=1, source_target_pairs={{0,2},{2,0},{4,6},{6,4},{8,10},{10,8},{12,14},{14,12},{16,18},{18,... | collective-permute-start | bytes 98312 | tf_op jit(solution)/shard_map/ppermute | solution.py:292
  6.9 3.6 %collective-permute-start.4 = (bf16[256,256]{1,0:T(8,128)(2,1)S(1)}, bf16[256,256]{1,0:T(8,128)(2,1)S(1)}, u32[]{:S(2)}, u32[]{:S(2)}) collective-permute-start(bf16[256,256]{1,0:T(8,128)(2,1)S(1)} %get-tuple-element.31.row_ref.refs_0_), channel_id=1, source_target_pairs={{0,24},{2,26},{4,28},{6,30},{8,16},{10,18},{12,20},{14,22},{16,8},... | collective-permute-start | bytes 393224 | tf_op jit(solution)/shard_map/ppermute | solution.py:292
  10.5 0.0 collective-permute-start.3
  10.5 0.0 collective-permute-done.1.got_ref
  10.5 0.8 %collective-permute-start.2 = (bf16[256,256]{1,0:T(8,128)(2,1)S(1)}, bf16[256,256]{1,0:T(8,128)(2,1)S(1)}, u32[]{:S(2)}, u32[]{:S(2)}) collective-permute-start(bf16[256,256]{1,0:T(8,128)(2,1)S(1)} %get-tuple-element.34), channel_id=1, source_target_pairs={{0,8},{2,10},{4,12},{6,14},{8,0},{10,2},{12,4},{14,6},{16,24},{18,... | collective-permute-start | bytes 393224 | tf_op jit(solution)/shard_map/ppermute | solution.py:292
  11.3 1.5 %collective-permute-start.5 = (bf16[32,256]{1,0:T(8,128)(2,1)S(1)}, bf16[32,256]{1,0:T(8,128)(2,1)S(1)}, u32[]{:S(2)}, u32[]{:S(2)}) collective-permute-start(bf16[32,256]{1,0:T(8,128)(2,1)S(1)} %get-tuple-element.36), channel_id=1, source_target_pairs={{0,4},{2,6},{4,0},{6,2},{8,12},{10,14},{12,8},{14,10},{16,20},{18,... | collective-permute-start | bytes 49160 | tf_op jit(solution)/shard_map/ppermute | solution.py:292
  12.9 2.4 %collective-permute-done.5.refs_5_ = bf16[32,256]{1,0:T(8,128)(2,1)S(1)} collective-permute-done((bf16[32,256]{1,0:T(8,128)(2,1)S(1)}, bf16[32,256]{1,0:T(8,128)(2,1)S(1)}, u32[]{:S(2)}, u32[]{:S(2)}) %collective-permute-start.5) | collective-permute-done | bytes 16416 | tf_op jit(solution)/shard_map/ppermute | solution.py:292
  15.2 0.0 collective-permute-done.4.refs_3_
  15.3 1.8 %collective-permute-done.3.refs_2_ = bf16[256,256]{1,0:T(8,128)(2,1)S(1)} collective-permute-done((bf16[256,256]{1,0:T(8,128)(2,1)S(1)}, bf16[256,256]{1,0:T(8,128)(2,1)S(1)}, u32[]{:S(2)}, u32[]{:S(2)}) %collective-permute-start.3) | collective-permute-done | bytes 131104 | tf_op jit(solution)/shard_map/ppermute | solution.py:292
  17.0 0.0 collective-permute-done.2.refs_1_
  17.1 0.5 shard_map.76
  17.6 1.6 %collective-permute-start.8 = (bf16[384,256]{1,0:T(8,128)(2,1)S(1)}, bf16[384,256]{1,0:T(8,128)(2,1)S(1)}, u32[]{:S(2)}, u32[]{:S(2)}) collective-permute-start(bf16[384,256]{1,0:T(8,128)(2,1)S(1)} %get-tuple-element.38.row_ref.refs_0_), channel_id=1, source_target_pairs={{0,6},{2,4},{4,2},{6,0},{8,14},{10,12},{12,10},{14,8},{16,22},{18,... | collective-permute-start | bytes 589832 | tf_op jit(solution)/shard_map/ppermute | solution.py:292
  19.2 0.5 collective-permute-start.7
  19.7 1.5 %collective-permute-start.6 = (bf16[384,256]{1,0:T(8,128)(2,1)S(1)}, bf16[384,256]{1,0:T(8,128)(2,1)S(1)}, u32[]{:S(2)}, u32[]{:S(2)}) collective-permute-start(bf16[384,256]{1,0:T(8,128)(2,1)S(1)} %get-tuple-element.38.row_ref.refs_0_), channel_id=1, source_target_pairs={{0,2},{2,0},{4,6},{6,4},{8,10},{10,8},{12,14},{14,12},{16,18},{18,... | collective-permute-start | bytes 589832 | tf_op jit(solution)/shard_map/ppermute | solution.py:292
  21.2 0.0 copy-done
  21.2 0.2 shard_map.77.refs_5_
  21.4 0.0 copy-start.1
  21.4 3.0 %collective-permute-done.8.refs_3_ = bf16[384,256]{1,0:T(8,128)(2,1)S(1)} collective-permute-done((bf16[384,256]{1,0:T(8,128)(2,1)S(1)}, bf16[384,256]{1,0:T(8,128)(2,1)S(1)}, u32[]{:S(2)}, u32[]{:S(2)}) %collective-permute-start.8) | collective-permute-done | bytes 196640 | tf_op jit(solution)/shard_map/ppermute | solution.py:292
  24.3 2.0 %collective-permute-done.7.refs_2_ = bf16[384,256]{1,0:T(8,128)(2,1)S(1)} collective-permute-done((bf16[384,256]{1,0:T(8,128)(2,1)S(1)}, bf16[384,256]{1,0:T(8,128)(2,1)S(1)}, u32[]{:S(2)}, u32[]{:S(2)}) %collective-permute-start.7) | collective-permute-done | bytes 196640 | tf_op jit(solution)/shard_map/ppermute | solution.py:292
  26.3 0.1 collective-permute-done.6.refs_1_
  26.5 6.0 %shard_map.78 = (bf16[112,256]{1,0:T(8,128)(2,1)S(1)}, bf16[112,256]{1,0:T(8,128)(2,1)S(1)}, bf16[112,256]{1,0:T(8,128)(2,1)S(1)}, bf16[112,256]{1,0:T(8,128)(2,1)S(1)}) custom-call(s32[16,128]{1,0:T(8,128)S(1)} %get-tuple-element.37.count_ref, bf16[384,256]{1,0:T(8,128)(2,1)S(1)} %get-tuple-element.38.row_ref.refs_0_, ...), custom_call_target="tpu_custom_call" | custom-call | tf_op jit(solution)/shard_map/pallas_call | solution.py:354
  32.5 0.0 copy-start.7
  32.5 1.5 %collective-permute-start.9 = (bf16[112,256]{1,0:T(8,128)(2,1)S(1)}, bf16[112,256]{1,0:T(8,128)(2,1)S(1)}, u32[]{:S(2)}, u32[]{:S(2)}) collective-permute-start(bf16[112,256]{1,0:T(8,128)(2,1)S(1)} %get-tuple-element.41), channel_id=1, source_target_pairs={{0,8},{2,10},{4,12},{6,14},{8,0},{10,2},{12,4},{14,6},{16,24},{18,... | collective-permute-start | bytes 172040 | tf_op jit(solution)/shard_map/ppermute | solution.py:292
  33.9 1.9 %collective-permute-start.10 = (bf16[112,256]{1,0:T(8,128)(2,1)S(1)}, bf16[112,256]{1,0:T(8,128)(2,1)S(1)}, u32[]{:S(2)}, u32[]{:S(2)}) collective-permute-start(bf16[112,256]{1,0:T(8,128)(2,1)S(1)} %get-tuple-element.42), channel_id=1, source_target_pairs={{0,16},{2,18},{4,20},{6,22},{8,24},{10,26},{12,28},{14,30},{16,0},... | collective-permute-start | bytes 172040 | tf_op jit(solution)/shard_map/ppermute | solution.py:292
  35.8 1.1 %collective-permute-start.11 = (bf16[112,256]{1,0:T(8,128)(2,1)S(1)}, bf16[112,256]{1,0:T(8,128)(2,1)S(1)}, u32[]{:S(2)}, u32[]{:S(2)}) collective-permute-start(bf16[112,256]{1,0:T(8,128)(2,1)S(1)} %get-tuple-element.43), channel_id=1, source_target_pairs={{0,24},{2,26},{4,28},{6,30},{8,16},{10,18},{12,20},{14,22},{16,8},... | collective-permute-start | bytes 172040 | tf_op jit(solution)/shard_map/ppermute | solution.py:292
  36.9 0.0 collective-permute-done.9.refs_1_.refs_5_
  36.9 2.7 %collective-permute-done.10.refs_2_.refs_6_ = bf16[112,256]{1,0:T(8,128)(2,1)S(1)} collective-permute-done((bf16[112,256]{1,0:T(8,128)(2,1)S(1)}, bf16[112,256]{1,0:T(8,128)(2,1)S(1)}, u32[]{:S(2)}, u32[]{:S(2)}) %collective-permute-start.10) | collective-permute-done | bytes 57376 | tf_op jit(solution)/shard_map/ppermute | solution.py:292
  39.6 2.2 %collective-permute-done.11.refs_3_.refs_7_ = bf16[112,256]{1,0:T(8,128)(2,1)S(1)} collective-permute-done((bf16[112,256]{1,0:T(8,128)(2,1)S(1)}, bf16[112,256]{1,0:T(8,128)(2,1)S(1)}, u32[]{:S(2)}, u32[]{:S(2)}) %collective-permute-start.11) | collective-permute-done | bytes 57376 | tf_op jit(solution)/shard_map/ppermute | solution.py:292
  41.8 0.0 copy-done.2
  41.8 0.0 copy-done.1
  41.8 0.0 copy-done.3
  41.8 0.0 copy-done.5
  41.8 0.0 copy-done.7
  41.8 1.7 %shard_map.79 = (f32[256,256]{1,0:T(8,128)S(1)}, bf16[96,256]{1,0:T(8,128)(2,1)S(1)}, bf16[96,256]{1,0:T(8,128)(2,1)S(1)}, bf16[96,256]{1,0:T(8,128)(2,1)S(1)}, bf16[96,256]{1,0:T(8,128)(2,1)S(1)}) custom-call(bf16[112,256]{1,0:T(8,128)(2,1)S(1)} %get-tuple-element.40.refs_0_.refs_4_, bf16[112,256]{1,0:T(8,128)(2,1)S(1)} %collective-permute-done.9.refs_1_.refs_5_, ...), custom_call_target="tpu_custom_call" | custom-call | tf_op jit(solution)/shard_map/pallas_call | solution.py:372
  43.5 0.1 collective-permute-start.12
  43.6 1.7 %collective-permute-start.13 = (bf16[96,256]{1,0:T(8,128)(2,1)S(1)}, bf16[96,256]{1,0:T(8,128)(2,1)S(1)}, u32[]{:S(2)}, u32[]{:S(2)}) collective-permute-start(bf16[96,256]{1,0:T(8,128)(2,1)S(1)} %get-tuple-element.46), channel_id=1, source_target_pairs={{0,16},{2,18},{4,20},{6,22},{8,24},{10,26},{12,28},{14,30},{16,0},... | collective-permute-start | bytes 147464 | tf_op jit(solution)/shard_map/ppermute | solution.py:292
  45.3 2.7 %collective-permute-start.14 = (bf16[96,256]{1,0:T(8,128)(2,1)S(1)}, bf16[96,256]{1,0:T(8,128)(2,1)S(1)}, u32[]{:S(2)}, u32[]{:S(2)}) collective-permute-start(bf16[96,256]{1,0:T(8,128)(2,1)S(1)} %get-tuple-element.47), channel_id=1, source_target_pairs={{0,24},{2,26},{4,28},{6,30},{8,16},{10,18},{12,20},{14,22},{16,8},... | collective-permute-start | bytes 147464 | tf_op jit(solution)/shard_map/ppermute | solution.py:292
  48.0 0.0 collective-permute-done.12.refs_1_
  48.0 0.7 collective-permute-done.13.refs_2_
  48.7 2.5 %collective-permute-done.14.refs_3_ = bf16[96,256]{1,0:T(8,128)(2,1)S(1)} collective-permute-done((bf16[96,256]{1,0:T(8,128)(2,1)S(1)}, bf16[96,256]{1,0:T(8,128)(2,1)S(1)}, u32[]{:S(2)}, u32[]{:S(2)}) %collective-permute-start.14) | collective-permute-done | bytes 49184 | tf_op jit(solution)/shard_map/ppermute | solution.py:292
  51.2 1.4 %collective-permute-start.17 = (bf16[384,256]{1,0:T(8,128)(2,1)S(1)}, bf16[384,256]{1,0:T(8,128)(2,1)S(1)}, u32[]{:S(2)}, u32[]{:S(2)}) collective-permute-start(bf16[384,256]{1,0:T(8,128)(2,1)S(1)} %shard_map.80.row_ref.refs_0_), channel_id=1, source_target_pairs={{0,6},{2,4},{4,2},{6,0},{8,14},{10,12},{12,10},{14,8},{16,22},{18,... | collective-permute-start | bytes 589832 | tf_op jit(solution)/shard_map/ppermute | solution.py:292
  52.7 0.6 collective-permute-start.16
  53.3 1.5 %collective-permute-start.15 = (bf16[384,256]{1,0:T(8,128)(2,1)S(1)}, bf16[384,256]{1,0:T(8,128)(2,1)S(1)}, u32[]{:S(2)}, u32[]{:S(2)}) collective-permute-start(bf16[384,256]{1,0:T(8,128)(2,1)S(1)} %shard_map.80.row_ref.refs_0_), channel_id=1, source_target_pairs={{0,2},{2,0},{4,6},{6,4},{8,10},{10,8},{12,14},{14,12},{16,18},{18,... | collective-permute-start | bytes 589832 | tf_op jit(solution)/shard_map/ppermute | solution.py:292
  54.8 0.3 shard_map.81.refs_5_
  55.1 2.9 %collective-permute-done.17.refs_3_ = bf16[384,256]{1,0:T(8,128)(2,1)S(1)} collective-permute-done((bf16[384,256]{1,0:T(8,128)(2,1)S(1)}, bf16[384,256]{1,0:T(8,128)(2,1)S(1)}, u32[]{:S(2)}, u32[]{:S(2)}) %collective-permute-start.17) | collective-permute-done | bytes 196640 | tf_op jit(solution)/shard_map/ppermute | solution.py:292
  58.0 2.0 %collective-permute-done.16.refs_2_ = bf16[384,256]{1,0:T(8,128)(2,1)S(1)} collective-permute-done((bf16[384,256]{1,0:T(8,128)(2,1)S(1)}, bf16[384,256]{1,0:T(8,128)(2,1)S(1)}, u32[]{:S(2)}, u32[]{:S(2)}) %collective-permute-start.16) | collective-permute-done | bytes 196640 | tf_op jit(solution)/shard_map/ppermute | solution.py:292
  60.0 0.0 collective-permute-done.15.refs_1_
  60.0 6.1 %shard_map.82 = (bf16[96,256]{1,0:T(8,128)(2,1)S(1)}, bf16[96,256]{1,0:T(8,128)(2,1)S(1)}, bf16[96,256]{1,0:T(8,128)(2,1)S(1)}, bf16[96,256]{1,0:T(8,128)(2,1)S(1)}) custom-call(s32[16,128]{1,0:T(8,128)S(1)} %get-tuple-element.37.count_ref, bf16[384,256]{1,0:T(8,128)(2,1)S(1)} %shard_map.80.row_ref.refs_0_, ...), custom_call_target="tpu_custom_call" | custom-call | tf_op jit(solution)/shard_map/pallas_call | solution.py:354
  66.1 0.1 collective-permute-start.18
  66.1 3.2 %collective-permute-start.19 = (bf16[96,256]{1,0:T(8,128)(2,1)S(1)}, bf16[96,256]{1,0:T(8,128)(2,1)S(1)}, u32[]{:S(2)}, u32[]{:S(2)}) collective-permute-start(bf16[96,256]{1,0:T(8,128)(2,1)S(1)} %get-tuple-element.50), channel_id=1, source_target_pairs={{0,16},{2,18},{4,20},{6,22},{8,24},{10,26},{12,28},{14,30},{16,0},... | collective-permute-start | bytes 147464 | tf_op jit(solution)/shard_map/ppermute | solution.py:292
  69.4 1.2 %collective-permute-start.20 = (bf16[96,256]{1,0:T(8,128)(2,1)S(1)}, bf16[96,256]{1,0:T(8,128)(2,1)S(1)}, u32[]{:S(2)}, u32[]{:S(2)}) collective-permute-start(bf16[96,256]{1,0:T(8,128)(2,1)S(1)} %get-tuple-element.51), channel_id=1, source_target_pairs={{0,24},{2,26},{4,28},{6,30},{8,16},{10,18},{12,20},{14,22},{16,8},... | collective-permute-start | bytes 147464 | tf_op jit(solution)/shard_map/ppermute | solution.py:292
  70.5 0.0 collective-permute-done.18.refs_1_
  70.5 0.9 %collective-permute-done.19.refs_2_ = bf16[96,256]{1,0:T(8,128)(2,1)S(1)} collective-permute-done((bf16[96,256]{1,0:T(8,128)(2,1)S(1)}, bf16[96,256]{1,0:T(8,128)(2,1)S(1)}, u32[]{:S(2)}, u32[]{:S(2)}) %collective-permute-start.19) | collective-permute-done | bytes 49184 | tf_op jit(solution)/shard_map/ppermute | solution.py:292
  71.4 3.8 %collective-permute-done.20.refs_3_ = bf16[96,256]{1,0:T(8,128)(2,1)S(1)} collective-permute-done((bf16[96,256]{1,0:T(8,128)(2,1)S(1)}, bf16[96,256]{1,0:T(8,128)(2,1)S(1)}, u32[]{:S(2)}, u32[]{:S(2)}) %collective-permute-start.20) | collective-permute-done | bytes 49184 | tf_op jit(solution)/shard_map/ppermute | solution.py:292
  75.2 1.9 %shard_map.83 = f32[256,256]{1,0:T(8,128)} custom-call(bf16[96,256]{1,0:T(8,128)(2,1)S(1)} %get-tuple-element.48.refs_0_, bf16[96,256]{1,0:T(8,128)(2,1)S(1)} %collective-permute-done.18.refs_1_, bf16[96,256]{1,0:T(8,128)(2,1)S(1)} %collective-permute-done.19.refs_2_, bf16[96,256]{1,0:T(8,128)(2,1)S(1)} %collective-permute-done.20.refs_3_, ...), custom_call_target="tpu_custom_call" | custom-call | tf_op jit(solution)/shard_map/pallas_call | solution.py:372
  (8 shorter events, 0.0 us)
Async XLA Ops:
  0.0 21.2 %copy-start = (bf16[2,256,768]{2,1,0:T(8,128)(2,1)S(1)}, bf16[2,256,768]{2,1,0:T(8,128)(2,1)}, u32[]{:S(2)}) copy-start(bf16[2,256,768]{2,1,0:T(8,128)(2,1)} %refs_4_.5) | copy-start | bytes 2359300
  0.0 3.4 %collective-permute-start = (s32[2,256]{1,0:T(2,128)}, s32[2,256]{1,0:T(2,128)S(1)}, u32[]{:S(2)}, u32[]{:S(2)}) collective-permute-start(s32[2,256]{1,0:T(2,128)} %order_ref.1), channel_id=1, source_target_pairs={{1,1},{3,9},{5,17},{7,25},{9,3},{11,11},{13,19},{15,27},{17,5},{19... | collective-permute-start | bytes 6152 | tf_op jit(solution)/shard_map/ppermute | solution.py:292
  0.8 1.0 %copy-start.4 = (f32[256,256]{1,0:T(8,128)S(1)}, f32[256,256]{1,0:T(8,128)}, u32[]{:S(2)}) copy-start(f32[256,256]{1,0:T(8,128)} %refs_4_.4) | copy-start | bytes 786436
  1.8 0.7 copy-start.6
  2.5 0.7 copy-start.8
  3.9 6.6 %collective-permute-start.1 = (bf16[64,256]{1,0:T(8,128)(2,1)S(1)}, bf16[64,256]{1,0:T(8,128)(2,1)S(1)}, u32[]{:S(2)}, u32[]{:S(2)}) collective-permute-start(bf16[64,256]{1,0:T(8,128)(2,1)S(1)} %get-tuple-element.33), channel_id=1, source_target_pairs={{0,2},{2,0},{4,6},{6,4},{8,10},{10,8},{12,14},{14,12},{16,18},{18,... | collective-permute-start | bytes 98312 | tf_op jit(solution)/shard_map/ppermute | solution.py:292
  6.9 8.4 %collective-permute-start.4 = (bf16[256,256]{1,0:T(8,128)(2,1)S(1)}, bf16[256,256]{1,0:T(8,128)(2,1)S(1)}, u32[]{:S(2)}, u32[]{:S(2)}) collective-permute-start(bf16[256,256]{1,0:T(8,128)(2,1)S(1)} %get-tuple-element.31.row_ref.refs_0_), channel_id=1, source_target_pairs={{0,24},{2,26},{4,28},{6,30},{8,16},{10,18},{12,20},{14,22},{16,8},... | collective-permute-start | bytes 393224 | tf_op jit(solution)/shard_map/ppermute | solution.py:292
  10.5 6.6 %collective-permute-start.3 = (bf16[256,256]{1,0:T(8,128)(2,1)S(1)}, bf16[256,256]{1,0:T(8,128)(2,1)S(1)}, u32[]{:S(2)}, u32[]{:S(2)}) collective-permute-start(bf16[256,256]{1,0:T(8,128)(2,1)S(1)} %get-tuple-element.31.row_ref.refs_0_), channel_id=1, source_target_pairs={{0,16},{2,18},{4,20},{6,22},{8,24},{10,26},{12,28},{14,30},{16,0},... | collective-permute-start | bytes 393224 | tf_op jit(solution)/shard_map/ppermute | solution.py:292
  10.5 6.6 %collective-permute-start.2 = (bf16[256,256]{1,0:T(8,128)(2,1)S(1)}, bf16[256,256]{1,0:T(8,128)(2,1)S(1)}, u32[]{:S(2)}, u32[]{:S(2)}) collective-permute-start(bf16[256,256]{1,0:T(8,128)(2,1)S(1)} %get-tuple-element.34), channel_id=1, source_target_pairs={{0,8},{2,10},{4,12},{6,14},{8,0},{10,2},{12,4},{14,6},{16,24},{18,... | collective-permute-start | bytes 393224 | tf_op jit(solution)/shard_map/ppermute | solution.py:292
  11.3 3.9 %collective-permute-start.5 = (bf16[32,256]{1,0:T(8,128)(2,1)S(1)}, bf16[32,256]{1,0:T(8,128)(2,1)S(1)}, u32[]{:S(2)}, u32[]{:S(2)}) collective-permute-start(bf16[32,256]{1,0:T(8,128)(2,1)S(1)} %get-tuple-element.36), channel_id=1, source_target_pairs={{0,4},{2,6},{4,0},{6,2},{8,12},{10,14},{12,8},{14,10},{16,20},{18,... | collective-permute-start | bytes 49160 | tf_op jit(solution)/shard_map/ppermute | solution.py:292
  17.6 6.7 %collective-permute-start.8 = (bf16[384,256]{1,0:T(8,128)(2,1)S(1)}, bf16[384,256]{1,0:T(8,128)(2,1)S(1)}, u32[]{:S(2)}, u32[]{:S(2)}) collective-permute-start(bf16[384,256]{1,0:T(8,128)(2,1)S(1)} %get-tuple-element.38.row_ref.refs_0_), channel_id=1, source_target_pairs={{0,6},{2,4},{4,2},{6,0},{8,14},{10,12},{12,10},{14,8},{16,22},{18,... | collective-permute-start | bytes 589832 | tf_op jit(solution)/shard_map/ppermute | solution.py:292
  19.2 7.2 %collective-permute-start.7 = (bf16[384,256]{1,0:T(8,128)(2,1)S(1)}, bf16[384,256]{1,0:T(8,128)(2,1)S(1)}, u32[]{:S(2)}, u32[]{:S(2)}) collective-permute-start(bf16[384,256]{1,0:T(8,128)(2,1)S(1)} %get-tuple-element.38.row_ref.refs_0_), channel_id=1, source_target_pairs={{0,4},{2,6},{4,0},{6,2},{8,12},{10,14},{12,8},{14,10},{16,20},{18,... | collective-permute-start | bytes 589832 | tf_op jit(solution)/shard_map/ppermute | solution.py:292
  19.7 6.8 %collective-permute-start.6 = (bf16[384,256]{1,0:T(8,128)(2,1)S(1)}, bf16[384,256]{1,0:T(8,128)(2,1)S(1)}, u32[]{:S(2)}, u32[]{:S(2)}) collective-permute-start(bf16[384,256]{1,0:T(8,128)(2,1)S(1)} %get-tuple-element.38.row_ref.refs_0_), channel_id=1, source_target_pairs={{0,2},{2,0},{4,6},{6,4},{8,10},{10,8},{12,14},{14,12},{16,18},{18,... | collective-permute-start | bytes 589832 | tf_op jit(solution)/shard_map/ppermute | solution.py:292
  21.2 20.6 %copy-start.2 = (bf16[2,1024,256]{2,1,0:T(8,128)(2,1)S(1)}, bf16[2,1024,256]{2,1,0:T(8,128)(2,1)}, u32[]{:S(2)}) copy-start(bf16[2,1024,256]{2,1,0:T(8,128)(2,1)} %refs_12_.1) | copy-start | bytes 3145732
  21.4 20.4 %copy-start.1 = (bf16[2,256,1024]{2,1,0:T(8,128)(2,1)S(1)}, bf16[2,256,1024]{2,1,0:T(8,128)(2,1)}, u32[]{:S(2)}) copy-start(bf16[2,256,1024]{2,1,0:T(8,128)(2,1)} %refs_11_.1) | copy-start | bytes 3145732
  26.4 15.4 %copy-start.3 = (bf16[2,256,256]{2,1,0:T(8,128)(2,1)S(1)}, bf16[2,256,256]{2,1,0:T(8,128)(2,1)}, u32[]{:S(2)}) copy-start(bf16[2,256,256]{2,1,0:T(8,128)(2,1)} %refs_10_.1) | copy-start | bytes 786436
  26.4 15.4 %copy-start.5 = (f32[256,256]{1,0:T(8,128)S(1)}, f32[256,256]{1,0:T(8,128)}, u32[]{:S(2)}) copy-start(f32[256,256]{1,0:T(8,128)} %refs_4_.4) | copy-start | bytes 786436
  32.5 9.4 %copy-start.7 = (f32[2,2,256]{2,1,0:T(2,128)S(1)}, f32[2,2,256]{2,1,0:T(2,128)}, u32[]{:S(2)}) copy-start(f32[2,2,256]{2,1,0:T(2,128)} %refs_9_.1) | copy-start | bytes 12292
  32.5 4.5 %collective-permute-start.9 = (bf16[112,256]{1,0:T(8,128)(2,1)S(1)}, bf16[112,256]{1,0:T(8,128)(2,1)S(1)}, u32[]{:S(2)}, u32[]{:S(2)}) collective-permute-start(bf16[112,256]{1,0:T(8,128)(2,1)S(1)} %get-tuple-element.41), channel_id=1, source_target_pairs={{0,8},{2,10},{4,12},{6,14},{8,0},{10,2},{12,4},{14,6},{16,24},{18,... | collective-permute-start | bytes 172040 | tf_op jit(solution)/shard_map/ppermute | solution.py:292
  33.9 5.7 %collective-permute-start.10 = (bf16[112,256]{1,0:T(8,128)(2,1)S(1)}, bf16[112,256]{1,0:T(8,128)(2,1)S(1)}, u32[]{:S(2)}, u32[]{:S(2)}) collective-permute-start(bf16[112,256]{1,0:T(8,128)(2,1)S(1)} %get-tuple-element.42), channel_id=1, source_target_pairs={{0,16},{2,18},{4,20},{6,22},{8,24},{10,26},{12,28},{14,30},{16,0},... | collective-permute-start | bytes 172040 | tf_op jit(solution)/shard_map/ppermute | solution.py:292
  35.8 6.0 %collective-permute-start.11 = (bf16[112,256]{1,0:T(8,128)(2,1)S(1)}, bf16[112,256]{1,0:T(8,128)(2,1)S(1)}, u32[]{:S(2)}, u32[]{:S(2)}) collective-permute-start(bf16[112,256]{1,0:T(8,128)(2,1)S(1)} %get-tuple-element.43), channel_id=1, source_target_pairs={{0,24},{2,26},{4,28},{6,30},{8,16},{10,18},{12,20},{14,22},{16,8},... | collective-permute-start | bytes 172040 | tf_op jit(solution)/shard_map/ppermute | solution.py:292
  43.5 4.5 %collective-permute-start.12 = (bf16[96,256]{1,0:T(8,128)(2,1)S(1)}, bf16[96,256]{1,0:T(8,128)(2,1)S(1)}, u32[]{:S(2)}, u32[]{:S(2)}) collective-permute-start(bf16[96,256]{1,0:T(8,128)(2,1)S(1)} %get-tuple-element.45), channel_id=1, source_target_pairs={{0,8},{2,10},{4,12},{6,14},{8,0},{10,2},{12,4},{14,6},{16,24},{18,... | collective-permute-start | bytes 147464 | tf_op jit(solution)/shard_map/ppermute | solution.py:292
  43.6 5.1 %collective-permute-start.13 = (bf16[96,256]{1,0:T(8,128)(2,1)S(1)}, bf16[96,256]{1,0:T(8,128)(2,1)S(1)}, u32[]{:S(2)}, u32[]{:S(2)}) collective-permute-start(bf16[96,256]{1,0:T(8,128)(2,1)S(1)} %get-tuple-element.46), channel_id=1, source_target_pairs={{0,16},{2,18},{4,20},{6,22},{8,24},{10,26},{12,28},{14,30},{16,0},... | collective-permute-start | bytes 147464 | tf_op jit(solution)/shard_map/ppermute | solution.py:292
  45.3 5.9 %collective-permute-start.14 = (bf16[96,256]{1,0:T(8,128)(2,1)S(1)}, bf16[96,256]{1,0:T(8,128)(2,1)S(1)}, u32[]{:S(2)}, u32[]{:S(2)}) collective-permute-start(bf16[96,256]{1,0:T(8,128)(2,1)S(1)} %get-tuple-element.47), channel_id=1, source_target_pairs={{0,24},{2,26},{4,28},{6,30},{8,16},{10,18},{12,20},{14,22},{16,8},... | collective-permute-start | bytes 147464 | tf_op jit(solution)/shard_map/ppermute | solution.py:292
  51.2 6.7 %collective-permute-start.17 = (bf16[384,256]{1,0:T(8,128)(2,1)S(1)}, bf16[384,256]{1,0:T(8,128)(2,1)S(1)}, u32[]{:S(2)}, u32[]{:S(2)}) collective-permute-start(bf16[384,256]{1,0:T(8,128)(2,1)S(1)} %shard_map.80.row_ref.refs_0_), channel_id=1, source_target_pairs={{0,6},{2,4},{4,2},{6,0},{8,14},{10,12},{12,10},{14,8},{16,22},{18,... | collective-permute-start | bytes 589832 | tf_op jit(solution)/shard_map/ppermute | solution.py:292
  52.7 7.3 %collective-permute-start.16 = (bf16[384,256]{1,0:T(8,128)(2,1)S(1)}, bf16[384,256]{1,0:T(8,128)(2,1)S(1)}, u32[]{:S(2)}, u32[]{:S(2)}) collective-permute-start(bf16[384,256]{1,0:T(8,128)(2,1)S(1)} %shard_map.80.row_ref.refs_0_), channel_id=1, source_target_pairs={{0,4},{2,6},{4,0},{6,2},{8,12},{10,14},{12,8},{14,10},{16,20},{18,... | collective-permute-start | bytes 589832 | tf_op jit(solution)/shard_map/ppermute | solution.py:292
  53.3 6.7 %collective-permute-start.15 = (bf16[384,256]{1,0:T(8,128)(2,1)S(1)}, bf16[384,256]{1,0:T(8,128)(2,1)S(1)}, u32[]{:S(2)}, u32[]{:S(2)}) collective-permute-start(bf16[384,256]{1,0:T(8,128)(2,1)S(1)} %shard_map.80.row_ref.refs_0_), channel_id=1, source_target_pairs={{0,2},{2,0},{4,6},{6,4},{8,10},{10,8},{12,14},{14,12},{16,18},{18,... | collective-permute-start | bytes 589832 | tf_op jit(solution)/shard_map/ppermute | solution.py:292
  66.1 4.5 %collective-permute-start.18 = (bf16[96,256]{1,0:T(8,128)(2,1)S(1)}, bf16[96,256]{1,0:T(8,128)(2,1)S(1)}, u32[]{:S(2)}, u32[]{:S(2)}) collective-permute-start(bf16[96,256]{1,0:T(8,128)(2,1)S(1)} %get-tuple-element.49), channel_id=1, source_target_pairs={{0,8},{2,10},{4,12},{6,14},{8,0},{10,2},{12,4},{14,6},{16,24},{18,... | collective-permute-start | bytes 147464 | tf_op jit(solution)/shard_map/ppermute | solution.py:292
  66.1 5.3 %collective-permute-start.19 = (bf16[96,256]{1,0:T(8,128)(2,1)S(1)}, bf16[96,256]{1,0:T(8,128)(2,1)S(1)}, u32[]{:S(2)}, u32[]{:S(2)}) collective-permute-start(bf16[96,256]{1,0:T(8,128)(2,1)S(1)} %get-tuple-element.50), channel_id=1, source_target_pairs={{0,16},{2,18},{4,20},{6,22},{8,24},{10,26},{12,28},{14,30},{16,0},... | collective-permute-start | bytes 147464 | tf_op jit(solution)/shard_map/ppermute | solution.py:292
  69.4 5.9 %collective-permute-start.20 = (bf16[96,256]{1,0:T(8,128)(2,1)S(1)}, bf16[96,256]{1,0:T(8,128)(2,1)S(1)}, u32[]{:S(2)}, u32[]{:S(2)}) collective-permute-start(bf16[96,256]{1,0:T(8,128)(2,1)S(1)} %get-tuple-element.51), channel_id=1, source_target_pairs={{0,24},{2,26},{4,28},{6,30},{8,16},{10,18},{12,20},{14,22},{16,8},... | collective-permute-start | bytes 147464 | tf_op jit(solution)/shard_map/ppermute | solution.py:292

commit v5 on v4

--- a/solution.py
+++ b/solution.py
@@ -164,59 +164,43 @@
     return offset
 
 
-def query_body(plan, b, count_ref, row_ref, weight_ref, query_ref, room):
-    counts = [count_ref[j, 64 * b] for j in range(plan.lines)]
-    room[...] = jnp.zeros(room.shape, room.dtype)
-    pack_rows(plan, b == 0, 0, counts, row_ref, room)
-    projected = matmul(room[0 : plan.held], weight_ref[b, :, : plan.width]).astype(BF16)
-    query_ref[0 : plan.held] = (projected * ((plan.width // HEADS) ** -0.5)).astype(BF16)
-    query_ref[plan.held :] = jnp.zeros((2 * TALL, plan.width), BF16)
-
-
-def attend_body(plan, b, with_notes, count_ref, *refs):
-    group, lines, held, cap, width = plan.group, plan.lines, plan.held, plan.cap, plan.width
-    part_refs, weight_ref, query_ref = refs[:group], refs[group], refs[group + 1]
-    refs = refs[group + 2 :]
-    if with_notes:
-        member_ref, refs = refs[0], refs[1:]
-    out_refs, (all_rows, keys, values, mixed, scores) = refs[:lines], refs[lines:]
+def project_pair(plan, b, rows, weight_ref, at, keys, values):
+    width = plan.width
+    half = width // 2
+    keys[:, at] = matmul(
+        weight_ref[b, :, width : 2 * width], rows, (((0,), (1,)), ((), ()))
+    ).astype(BF16)
+    projected = matmul(rows, weight_ref[b, :, 2 * width :]).astype(BF16)
+    ones = jnp.ones((rows.shape[0], half), BF16)
+    for g in range(2):
+        values[g, at] = jnp.concatenate([projected[:, g * half : (g + 1) * half], ones], axis=1)
+
+
+def attention(plan, own, query_ref, keys, values, at, scores, finish):
+    width = plan.width
     half = width // 2
     half_heads = HEADS // 2
-    offset = 0
-    for k in range(group):
-        counts = [count_ref[k * lines + j, 64 * b] for j in range(lines)]
-        offset = pack_rows(plan, b == 0, offset, counts, part_refs[k], all_rows)
-    patch_rows = all_rows[0:PATCH]
-    keys[...] = matmul(
-        weight_ref[b, :, width : 2 * width], patch_rows, (((0,), (1,)), ((), ()))
-    ).astype(BF16)
-    projected = matmul(patch_rows, weight_ref[b, :, 2 * width :]).astype(BF16)
-    ones = jnp.ones((PATCH, half), BF16)
-    for g in range(2):
-        values[g] = jnp.concatenate([projected[:, g * half : (g + 1) * half], ones], axis=1)
-    mixed[...] = jnp.zeros(mixed.shape, mixed.dtype)
-    own = 0
-    offsets = []
-    for j in range(lines):
-        offsets.append(own)
-        own = own + count_ref[j, 64 * b]
     shape = (half_heads, 1, half)
     head_mask = iota(shape, 0) == iota(shape, 2) // (width // HEADS)
+    count = at.stop - at.start
+
+    def own_head(table):
+        kept = jnp.where(head_mask, table.reshape(half_heads, TALL, half), 0.0)
+        return jnp.sum(kept, axis=0)
 
     def scored(slot, start, g):
         block = query_ref[pl.ds(start, TALL), g * half : (g + 1) * half]
         spread = jnp.where(head_mask, block[None], jnp.zeros((), BF16))
-        scores[slot] = matmul(
-            spread.reshape(half_heads * TALL, half), keys[g * half : (g + 1) * half]
+        scores[slot, :, 0:count] = matmul(
+            spread.reshape(half_heads * TALL, half), keys[g * half : (g + 1) * half, at]
         )
 
     def averaged(slot, start, g):
-        table = scores[slot]
-        weights = jnp.exp(table - jnp.max(table, axis=1, keepdims=True)).astype(BF16)
-        summed = matmul(weights, values[g])
-        summed = summed[:, :half] / summed[:, half:]
-        kept = jnp.where(head_mask, summed.reshape(half_heads, TALL, half), 0.0)
-        mixed[pl.ds(start, TALL), g * half : (g + 1) * half] = jnp.sum(kept, axis=0).astype(BF16)
+        table = scores[slot, :, 0:count]
+        peak = jnp.max(table, axis=1, keepdims=True)
+        weights = jnp.exp(table - peak).astype(BF16)
+        summed = matmul(weights, values[g, at])
+        finish(pl.ds(start, TALL), slice(g * half, (g + 1) * half), summed, peak, own_head)
 
     scored(0, 0, 0)
     scored(1, 0, 1)
@@ -236,6 +220,72 @@
         return carry
 
     lax.fori_loop(0, (own + 2 * TALL - 1) // (2 * TALL), step, 0)
+
+
+def early_body(plan, b, count_ref, row_ref, weight_ref, *refs):
+    query_ref, sum_ref, total_ref, peak_ref, room, keys, values, scores = refs
+    rows, half = plan.rows, plan.width // 2
+    counts = [count_ref[j, 64 * b] for j in range(plan.lines)]
+    room[...] = jnp.zeros(room.shape, room.dtype)
+    own = pack_rows(plan, b == 0, 0, counts, row_ref, room)
+    projected = matmul(room[0 : plan.held], weight_ref[b, :, : plan.width]).astype(BF16)
+    query_ref[0 : plan.held] = (projected * ((plan.width // HEADS) ** -0.5)).astype(BF16)
+    query_ref[plan.held :] = jnp.zeros((2 * TALL, plan.width), BF16)
+
+    def finish(at, lanes, summed, peak, own_head):
+        sum_ref[at, lanes] = own_head(summed[:, :half])
+        total_ref[at, lanes] = own_head(summed[:, half:])
+        peak_ref[at, lanes] = own_head(jnp.broadcast_to(peak, (peak.shape[0], half)))
+
+    @pl.when(own >= rows)
+    def _():
+        some = slice(0, rows)
+        project_pair(plan, b, room[some], weight_ref, some, keys, values)
+        attention(plan, own, query_ref, keys, values, some, scores, finish)
+
+
+def attend_body(plan, b, with_notes, count_ref, *refs):
+    group, lines, held, cap, width = plan.group, plan.lines, plan.held, plan.cap, plan.width
+    rows, half = plan.rows, width // 2
+    part_refs, weight_ref, query_ref = refs[:group], refs[group], refs[group + 1]
+    sum_ref, total_ref, peak_ref = refs[group + 2 : group + 5]
+    refs = refs[group + 5 :]
+    if with_notes:
+        member_ref, refs = refs[0], refs[1:]
+    out_refs, (all_rows, keys, values, mixed, scores) = refs[:lines], refs[lines:]
+    offset = 0
+    for k in range(group):
+        counts = [count_ref[k * lines + j, 64 * b] for j in range(lines)]
+        offset = pack_rows(plan, b == 0, offset, counts, part_refs[k], all_rows)
+    mixed[...] = jnp.zeros(mixed.shape, mixed.dtype)
+    own = 0
+    offsets = []
+    for j in range(lines):
+        offsets.append(own)
+        own = own + count_ref[j, 64 * b]
+    first, others = slice(0, rows), slice(rows, PATCH)
+    project_pair(plan, b, all_rows[others], weight_ref, others, keys, values)
+
+    def joined(at, lanes, summed, peak, own_head):
+        peak = own_head(jnp.broadcast_to(peak, (peak.shape[0], half)))
+        most = jnp.maximum(peak, peak_ref[at, lanes])
+        here, early = jnp.exp(peak - most), jnp.exp(peak_ref[at, lanes] - most)
+        over = own_head(summed[:, :half]) * here + sum_ref[at, lanes] * early
+        under = own_head(summed[:, half:]) * here + total_ref[at, lanes] * early
+        mixed[at, lanes] = (over / under).astype(BF16)
+
+    def alone(at, lanes, summed, peak, own_head):
+        mixed[at, lanes] = own_head(summed[:, :half] / summed[:, half:]).astype(BF16)
+
+    @pl.when(own >= rows)
+    def _():
+        attention(plan, own, query_ref, keys, values, others, scores, joined)
+
+    @pl.when(own < rows)
+    def _():
+        project_pair(plan, b, all_rows[first], weight_ref, first, keys, values)
+        attention(plan, own, query_ref, keys, values, slice(0, PATCH), scores, alone)
+
     for j in range(lines):
         out_refs[j][0:cap, :] = mixed[pl.ds(pl.multiple_of(offsets[j], 16), cap), :]
         if with_notes:
@@ -271,9 +321,13 @@
     mixed = matmul(where_from, pieces, TN).astype(BF16)
     attended = state_ref[...] + matmul(mixed, proj_ref[b])
     normed_two = layer_norm(attended, gain_ref[b, 1:2, :]).astype(BF16)
-    hidden = matmul(normed_two, fc1_ref[b])
-    expanded = (0.5 * hidden * (1.0 + lax.erf(hidden * (0.5**0.5)))).astype(BF16)
-    state = attended + matmul(expanded, fc2_ref[b])
+    state = attended
+    units = fc1_ref.shape[2]
+    for start in range(0, units, units // 4):
+        at = slice(start, start + units // 4)
+        hidden = matmul(normed_two, fc1_ref[b, :, at])
+        expanded = (0.5 * hidden * (1.0 + lax.erf(hidden * (0.5**0.5)))).astype(BF16)
+        state = state + matmul(expanded, fc2_ref[b, at, :])
     state_out[...] = state
     if not last:
         normed = layer_norm(state, gain_ref[b + 1, 0:1, :]).astype(BF16)
@@ -344,25 +398,31 @@
         last = b == blocks - 1
         tall = cap if b else cap + 16
         parts = [packed] + [from_group(packed, k) for k in range(1, group)]
-        (queries,) = kernel_call(
-            functools.partial(query_body, plan, b),
-            [struct((held + 2 * TALL, width), BF16)],
+        table = HEADS // 2 * TALL
+        early = kernel_call(
+            functools.partial(early_body, plan, b),
+            [struct((held + 2 * TALL, width), BF16)] + [struct((held, width), F32)] * 3,
             [whole()] * 3,
-            [pltpu.VMEM((held + cap, width), BF16)],
+            [
+                pltpu.VMEM((held + cap, width), BF16),
+                pltpu.VMEM((width, rows), BF16),
+                pltpu.VMEM((2, rows, width), BF16),
+                pltpu.VMEM((4, table, rows), F32),
+            ],
         )(counts, packed, qkv_weight)
         extra = [] if b else [members]
         mixed = kernel_call(
             functools.partial(attend_body, plan, b, b == 0),
             [struct((tall, width), BF16)] * lines,
-            [whole()] * (group + 3 + len(extra)),
+            [whole()] * (group + 6 + len(extra)),
             [
                 pltpu.VMEM((PATCH + held, width), BF16),
                 pltpu.VMEM((width, PATCH), BF16),
                 pltpu.VMEM((2, PATCH, width), BF16),
                 pltpu.VMEM((held + cap, width), BF16),
-                pltpu.VMEM((4, HEADS // 2 * TALL, PATCH), F32),
+                pltpu.VMEM((4, table, PATCH), F32),
             ],
-        )(counts, *parts, qkv_weight, queries, *extra)
+        )(counts, *parts, qkv_weight, *early, *extra)
         pieces = along_line(mixed)
         if b == 0:
             kept = pieces

time: 77.4 us -> 75.4 us (0.974)
  waiting for transfers between devices: 27 us -> 22.3 us
  Pallas kernels: 17.4 us -> 20 us
    pallas_call x2, Pallas kernels: 0.5 us -> 5.2 us  [by_lines(): kernel_call(functools.partial(early_body, plan, b), [struct((held + 2 * T...]
    ppermute x21, waiting for transfers between devices: 27 us -> 22.3 us  [move(): return lax.ppermute(block, ('pts', 'slab'), pairs)]
    pallas_call x2, Pallas kernels: 12.1 us -> 10.1 us  [by_lines(): kernel_call(functools.partial(attend_body, plan, b, b == 0), [struct((tal...]
  transfers between devices with their start and end apart: 21 -> 21, of which waited for: 13 -> 13; matrix products, arithmetic and copies ran while one was open for 0% -> 0% of each run, Pallas kernels for 1% -> 7%
where the time goes in v5:
time: 75.4 us; the launch traced here: 75.2 us
  starting transfers between devices  30.2 us (40%)
  waiting for transfers between devices  22.3 us (30%)
  Pallas kernels  20 us (27%)
  local copies, waits for them, and re-layouts  2.43 us (3%)
    ppermute x21, starting transfers between devices, move(): return lax.ppermute(block, ('pts', 'slab'), pairs)  30.2 us
    ppermute x21, waiting for transfers between devices, move(): return lax.ppermute(block, ('pts', 'slab'), pairs)  22.3 us
    pallas_call x2, Pallas kernels, by_lines(): kernel_call(functools.partial(attend_body, plan, b, b == 0), [struct((tal...  10.1 us
    pallas_call x2, Pallas kernels, by_lines(): kernel_call(functools.partial(early_body, plan, b), [struct((held + 2 * T...  5.2 us
    pallas_call x2, Pallas kernels, by_lines(): kernel_call(functools.partial(store_body, plan, b, last), outs, [whole()]...  3.52 us
    unnamed x18, local copies, waits for them, and re-layouts  2.34 us
  transfers between devices with their start and end apart: 21, of which 13 were waited for; matrix products, arithmetic and copies ran while one was open for 0% of the time, Pallas kernels for 7%

profile of v5, /device:TPU:0, one launch (start us, length us, event | category | flops | bytes accessed | tf_op | source)
XLA Modules:
  0.0 75.2 jit_solution(14836449315644234805)
XLA Ops:
  0.0 0.8 %collective-permute-start = (s32[2,256]{1,0:T(2,128)}, s32[2,256]{1,0:T(2,128)S(1)}, u32[]{:S(2)}, u32[]{:S(2)}) collective-permute-start(s32[2,256]{1,0:T(2,128)} %order_ref.1), channel_id=1, source_target_pairs={{1,1},{3,9},{5,17},{7,25},{9,3},{11,11},{13,19},{15,27},{17,5},{19... | collective-permute-start | bytes 6152 | tf_op jit(solution)/shard_map/ppermute | solution.py:346
  0.8 0.0 copy-start.4
  0.8 0.9 %copy-done.4 = f32[256,256]{1,0:T(8,128)S(1)} copy-done((f32[256,256]{1,0:T(8,128)S(1)}, f32[256,256]{1,0:T(8,128)}, u32[]{:S(2)}) %copy-start.4) | copy-done | bytes 262168
  1.8 0.0 copy-start.6
  1.8 0.7 copy-done.6
  2.5 0.7 copy-done.8
  3.1 0.2 shard_map.73
  3.3 0.1 stack.23
  3.4 0.0 collective-permute-done.turned_ref
  3.4 0.4 shard_map.74
  3.9 3.0 %collective-permute-start.1 = (bf16[64,256]{1,0:T(8,128)(2,1)S(1)}, bf16[64,256]{1,0:T(8,128)(2,1)S(1)}, u32[]{:S(2)}, u32[]{:S(2)}) collective-permute-start(bf16[64,256]{1,0:T(8,128)(2,1)S(1)} %get-tuple-element.41), channel_id=1, source_target_pairs={{0,2},{2,0},{4,6},{6,4},{8,10},{10,8},{12,14},{14,12},{16,18},{18,... | collective-permute-start | bytes 98312 | tf_op jit(solution)/shard_map/ppermute | solution.py:346
  6.9 3.6 %collective-permute-start.4 = (bf16[256,256]{1,0:T(8,128)(2,1)S(1)}, bf16[256,256]{1,0:T(8,128)(2,1)S(1)}, u32[]{:S(2)}, u32[]{:S(2)}) collective-permute-start(bf16[256,256]{1,0:T(8,128)(2,1)S(1)} %get-tuple-element.39.row_ref.refs_0_), channel_id=1, source_target_pairs={{0,24},{2,26},{4,28},{6,30},{8,16},{10,18},{12,20},{14,22},{16,8},... | collective-permute-start | bytes 393224 | tf_op jit(solution)/shard_map/ppermute | solution.py:346
  10.5 0.0 collective-permute-start.3
  10.5 0.0 collective-permute-done.1.got_ref
  10.5 0.8 %collective-permute-start.2 = (bf16[256,256]{1,0:T(8,128)(2,1)S(1)}, bf16[256,256]{1,0:T(8,128)(2,1)S(1)}, u32[]{:S(2)}, u32[]{:S(2)}) collective-permute-start(bf16[256,256]{1,0:T(8,128)(2,1)S(1)} %get-tuple-element.42), channel_id=1, source_target_pairs={{0,8},{2,10},{4,12},{6,14},{8,0},{10,2},{12,4},{14,6},{16,24},{18,... | collective-permute-start | bytes 393224 | tf_op jit(solution)/shard_map/ppermute | solution.py:346
  11.3 1.5 %collective-permute-start.5 = (bf16[32,256]{1,0:T(8,128)(2,1)S(1)}, bf16[32,256]{1,0:T(8,128)(2,1)S(1)}, u32[]{:S(2)}, u32[]{:S(2)}) collective-permute-start(bf16[32,256]{1,0:T(8,128)(2,1)S(1)} %get-tuple-element.44), channel_id=1, source_target_pairs={{0,4},{2,6},{4,0},{6,2},{8,12},{10,14},{12,8},{14,10},{16,20},{18,... | collective-permute-start | bytes 49160 | tf_op jit(solution)/shard_map/ppermute | solution.py:346
  12.9 2.4 %collective-permute-done.5.refs_5_ = bf16[32,256]{1,0:T(8,128)(2,1)S(1)} collective-permute-done((bf16[32,256]{1,0:T(8,128)(2,1)S(1)}, bf16[32,256]{1,0:T(8,128)(2,1)S(1)}, u32[]{:S(2)}, u32[]{:S(2)}) %collective-permute-start.5) | collective-permute-done | bytes 16416 | tf_op jit(solution)/shard_map/ppermute | solution.py:346
  15.2 0.0 collective-permute-done.4.refs_3_
  15.3 1.8 %collective-permute-done.3.refs_2_ = bf16[256,256]{1,0:T(8,128)(2,1)S(1)} collective-permute-done((bf16[256,256]{1,0:T(8,128)(2,1)S(1)}, bf16[256,256]{1,0:T(8,128)(2,1)S(1)}, u32[]{:S(2)}, u32[]{:S(2)}) %collective-permute-start.3) | collective-permute-done | bytes 131104 | tf_op jit(solution)/shard_map/ppermute | solution.py:346
  17.0 0.0 collective-permute-done.2.refs_1_
  17.1 0.5 shard_map.76
  17.6 1.6 %collective-permute-start.8 = (bf16[384,256]{1,0:T(8,128)(2,1)S(1)}, bf16[384,256]{1,0:T(8,128)(2,1)S(1)}, u32[]{:S(2)}, u32[]{:S(2)}) collective-permute-start(bf16[384,256]{1,0:T(8,128)(2,1)S(1)} %get-tuple-element.46.row_ref.refs_0_), channel_id=1, source_target_pairs={{0,6},{2,4},{4,2},{6,0},{8,14},{10,12},{12,10},{14,8},{16,22},{18,... | collective-permute-start | bytes 589832 | tf_op jit(solution)/shard_map/ppermute | solution.py:346
  19.2 0.5 collective-permute-start.7
  19.7 1.5 %collective-permute-start.6 = (bf16[384,256]{1,0:T(8,128)(2,1)S(1)}, bf16[384,256]{1,0:T(8,128)(2,1)S(1)}, u32[]{:S(2)}, u32[]{:S(2)}) collective-permute-start(bf16[384,256]{1,0:T(8,128)(2,1)S(1)} %get-tuple-element.46.row_ref.refs_0_), channel_id=1, source_target_pairs={{0,2},{2,0},{4,6},{6,4},{8,10},{10,8},{12,14},{14,12},{16,18},{18,... | collective-permute-start | bytes 589832 | tf_op jit(solution)/shard_map/ppermute | solution.py:346
  21.2 0.0 copy-done
  21.2 2.6 %shard_map.77 = (bf16[448,256]{1,0:T(8,128)(2,1)S(1)}, f32[384,256]{1,0:T(8,128)S(1)}, f32[384,256]{1,0:T(8,128)S(1)}, f32[384,256]{1,0:T(8,128)S(1)}) custom-call(s32[16,128]{1,0:T(8,128)S(1)} %get-tuple-element.45.count_ref, bf16[384,256]{1,0:T(8,128)(2,1)S(1)} %get-tuple-element.46.row_ref.refs_0_, bf16[2,256,768]{2,1,0:T(8,128)(2,1)S(1)} %copy-done), custom_call_target="tpu_custom_call" | custom-call | tf_op jit(solution)/shard_map/pallas_call | solution.py:402
  23.7 0.6 collective-permute-done.8.refs_3_
  24.3 2.0 %collective-permute-done.7.refs_2_ = bf16[384,256]{1,0:T(8,128)(2,1)S(1)} collective-permute-done((bf16[384,256]{1,0:T(8,128)(2,1)S(1)}, bf16[384,256]{1,0:T(8,128)(2,1)S(1)}, u32[]{:S(2)}, u32[]{:S(2)}) %collective-permute-start.7) | collective-permute-done | bytes 196640 | tf_op jit(solution)/shard_map/ppermute | solution.py:346
  26.3 0.1 collective-permute-done.6.refs_1_
  26.5 5.0 %shard_map.78 = (bf16[112,256]{1,0:T(8,128)(2,1)S(1)}, bf16[112,256]{1,0:T(8,128)(2,1)S(1)}, bf16[112,256]{1,0:T(8,128)(2,1)S(1)}, bf16[112,256]{1,0:T(8,128)(2,1)S(1)}) custom-call(s32[16,128]{1,0:T(8,128)S(1)} %get-tuple-element.45.count_ref, bf16[384,256]{1,0:T(8,128)(2,1)S(1)} %get-tuple-element.46.row_ref.refs_0_, ...), custom_call_target="tpu_custom_call" | custom-call | tf_op jit(solution)/shard_map/pallas_call | solution.py:414
  31.5 0.0 copy-start.7
  31.5 1.5 %collective-permute-start.9 = (bf16[112,256]{1,0:T(8,128)(2,1)S(1)}, bf16[112,256]{1,0:T(8,128)(2,1)S(1)}, u32[]{:S(2)}, u32[]{:S(2)}) collective-permute-start(bf16[112,256]{1,0:T(8,128)(2,1)S(1)} %get-tuple-element.53), channel_id=1, source_target_pairs={{0,8},{2,10},{4,12},{6,14},{8,0},{10,2},{12,4},{14,6},{16,24},{18,... | collective-permute-start | bytes 172040 | tf_op jit(solution)/shard_map/ppermute | solution.py:346
  33.0 1.9 %collective-permute-start.10 = (bf16[112,256]{1,0:T(8,128)(2,1)S(1)}, bf16[112,256]{1,0:T(8,128)(2,1)S(1)}, u32[]{:S(2)}, u32[]{:S(2)}) collective-permute-start(bf16[112,256]{1,0:T(8,128)(2,1)S(1)} %get-tuple-element.54), channel_id=1, source_target_pairs={{0,16},{2,18},{4,20},{6,22},{8,24},{10,26},{12,28},{14,30},{16,0},... | collective-permute-start | bytes 172040 | tf_op jit(solution)/shard_map/ppermute | solution.py:346
  34.9 1.1 %collective-permute-start.11 = (bf16[112,256]{1,0:T(8,128)(2,1)S(1)}, bf16[112,256]{1,0:T(8,128)(2,1)S(1)}, u32[]{:S(2)}, u32[]{:S(2)}) collective-permute-start(bf16[112,256]{1,0:T(8,128)(2,1)S(1)} %get-tuple-element.55), channel_id=1, source_target_pairs={{0,24},{2,26},{4,28},{6,30},{8,16},{10,18},{12,20},{14,22},{16,8},... | collective-permute-start | bytes 172040 | tf_op jit(solution)/shard_map/ppermute | solution.py:346
  35.9 0.0 collective-permute-done.9.refs_1_.refs_5_
  35.9 2.7 %collective-permute-done.10.refs_2_.refs_6_ = bf16[112,256]{1,0:T(8,128)(2,1)S(1)} collective-permute-done((bf16[112,256]{1,0:T(8,128)(2,1)S(1)}, bf16[112,256]{1,0:T(8,128)(2,1)S(1)}, u32[]{:S(2)}, u32[]{:S(2)}) %collective-permute-start.10) | collective-permute-done | bytes 57376 | tf_op jit(solution)/shard_map/ppermute | solution.py:346
  38.7 2.2 %collective-permute-done.11.refs_3_.refs_7_ = bf16[112,256]{1,0:T(8,128)(2,1)S(1)} collective-permute-done((bf16[112,256]{1,0:T(8,128)(2,1)S(1)}, bf16[112,256]{1,0:T(8,128)(2,1)S(1)}, u32[]{:S(2)}, u32[]{:S(2)}) %collective-permute-start.11) | collective-permute-done | bytes 57376 | tf_op jit(solution)/shard_map/ppermute | solution.py:346
  40.8 0.0 copy-done.1
  40.8 0.0 copy-done.2
  40.9 0.0 copy-done.3
  40.9 0.0 copy-done.5
  40.9 0.0 copy-done.7
  40.9 1.6 %shard_map.79 = (f32[256,256]{1,0:T(8,128)S(1)}, bf16[96,256]{1,0:T(8,128)(2,1)S(1)}, bf16[96,256]{1,0:T(8,128)(2,1)S(1)}, bf16[96,256]{1,0:T(8,128)(2,1)S(1)}, bf16[96,256]{1,0:T(8,128)(2,1)S(1)}) custom-call(bf16[112,256]{1,0:T(8,128)(2,1)S(1)} %get-tuple-element.52.refs_0_.refs_4_, bf16[112,256]{1,0:T(8,128)(2,1)S(1)} %collective-permute-done.9.refs_1_.refs_5_, ...), custom_call_target="tpu_custom_call" | custom-call | tf_op jit(solution)/shard_map/pallas_call | solution.py:432
  42.5 0.1 collective-permute-start.12
  42.6 1.7 %collective-permute-start.13 = (bf16[96,256]{1,0:T(8,128)(2,1)S(1)}, bf16[96,256]{1,0:T(8,128)(2,1)S(1)}, u32[]{:S(2)}, u32[]{:S(2)}) collective-permute-start(bf16[96,256]{1,0:T(8,128)(2,1)S(1)} %get-tuple-element.58), channel_id=1, source_target_pairs={{0,16},{2,18},{4,20},{6,22},{8,24},{10,26},{12,28},{14,30},{16,0},... | collective-permute-start | bytes 147464 | tf_op jit(solution)/shard_map/ppermute | solution.py:346
  44.2 2.7 %collective-permute-start.14 = (bf16[96,256]{1,0:T(8,128)(2,1)S(1)}, bf16[96,256]{1,0:T(8,128)(2,1)S(1)}, u32[]{:S(2)}, u32[]{:S(2)}) collective-permute-start(bf16[96,256]{1,0:T(8,128)(2,1)S(1)} %get-tuple-element.59), channel_id=1, source_target_pairs={{0,24},{2,26},{4,28},{6,30},{8,16},{10,18},{12,20},{14,22},{16,8},... | collective-permute-start | bytes 147464 | tf_op jit(solution)/shard_map/ppermute | solution.py:346
  46.9 0.0 collective-permute-done.12.refs_1_
  46.9 0.7 collective-permute-done.13.refs_2_
  47.6 2.5 %collective-permute-done.14.refs_3_ = bf16[96,256]{1,0:T(8,128)(2,1)S(1)} collective-permute-done((bf16[96,256]{1,0:T(8,128)(2,1)S(1)}, bf16[96,256]{1,0:T(8,128)(2,1)S(1)}, u32[]{:S(2)}, u32[]{:S(2)}) %collective-permute-start.14) | collective-permute-done | bytes 49184 | tf_op jit(solution)/shard_map/ppermute | solution.py:346
  50.2 1.5 %collective-permute-start.17 = (bf16[384,256]{1,0:T(8,128)(2,1)S(1)}, bf16[384,256]{1,0:T(8,128)(2,1)S(1)}, u32[]{:S(2)}, u32[]{:S(2)}) collective-permute-start(bf16[384,256]{1,0:T(8,128)(2,1)S(1)} %shard_map.80.row_ref.refs_0_), channel_id=1, source_target_pairs={{0,6},{2,4},{4,2},{6,0},{8,14},{10,12},{12,10},{14,8},{16,22},{18,... | collective-permute-start | bytes 589832 | tf_op jit(solution)/shard_map/ppermute | solution.py:346
  51.6 0.6 collective-permute-start.16
  52.2 1.5 %collective-permute-start.15 = (bf16[384,256]{1,0:T(8,128)(2,1)S(1)}, bf16[384,256]{1,0:T(8,128)(2,1)S(1)}, u32[]{:S(2)}, u32[]{:S(2)}) collective-permute-start(bf16[384,256]{1,0:T(8,128)(2,1)S(1)} %shard_map.80.row_ref.refs_0_), channel_id=1, source_target_pairs={{0,2},{2,0},{4,6},{6,4},{8,10},{10,8},{12,14},{14,12},{16,18},{18,... | collective-permute-start | bytes 589832 | tf_op jit(solution)/shard_map/ppermute | solution.py:346
  53.7 2.6 %shard_map.81 = (bf16[448,256]{1,0:T(8,128)(2,1)S(1)}, f32[384,256]{1,0:T(8,128)S(1)}, f32[384,256]{1,0:T(8,128)S(1)}, f32[384,256]{1,0:T(8,128)S(1)}) custom-call(s32[16,128]{1,0:T(8,128)S(1)} %get-tuple-element.45.count_ref, bf16[384,256]{1,0:T(8,128)(2,1)S(1)} %shard_map.80.row_ref.refs_0_, bf16[2,256,768]{2,1,0:T(8,128)(2,1)S(1)} %copy-done), custom_call_target="tpu_custom_call" | custom-call | tf_op jit(solution)/shard_map/pallas_call | solution.py:402
  56.4 0.5 collective-permute-done.17.refs_3_
  56.9 2.0 %collective-permute-done.16.refs_2_ = bf16[384,256]{1,0:T(8,128)(2,1)S(1)} collective-permute-done((bf16[384,256]{1,0:T(8,128)(2,1)S(1)}, bf16[384,256]{1,0:T(8,128)(2,1)S(1)}, u32[]{:S(2)}, u32[]{:S(2)}) %collective-permute-start.16) | collective-permute-done | bytes 196640 | tf_op jit(solution)/shard_map/ppermute | solution.py:346
  58.9 0.0 collective-permute-done.15.refs_1_
  58.9 5.1 %shard_map.82 = (bf16[96,256]{1,0:T(8,128)(2,1)S(1)}, bf16[96,256]{1,0:T(8,128)(2,1)S(1)}, bf16[96,256]{1,0:T(8,128)(2,1)S(1)}, bf16[96,256]{1,0:T(8,128)(2,1)S(1)}) custom-call(s32[16,128]{1,0:T(8,128)S(1)} %get-tuple-element.45.count_ref, bf16[384,256]{1,0:T(8,128)(2,1)S(1)} %shard_map.80.row_ref.refs_0_, ...), custom_call_target="tpu_custom_call" | custom-call | tf_op jit(solution)/shard_map/pallas_call | solution.py:414
  64.0 0.1 collective-permute-start.18
  64.1 3.3 %collective-permute-start.19 = (bf16[96,256]{1,0:T(8,128)(2,1)S(1)}, bf16[96,256]{1,0:T(8,128)(2,1)S(1)}, u32[]{:S(2)}, u32[]{:S(2)}) collective-permute-start(bf16[96,256]{1,0:T(8,128)(2,1)S(1)} %get-tuple-element.66), channel_id=1, source_target_pairs={{0,16},{2,18},{4,20},{6,22},{8,24},{10,26},{12,28},{14,30},{16,0},... | collective-permute-start | bytes 147464 | tf_op jit(solution)/shard_map/ppermute | solution.py:346
  67.4 1.1 %collective-permute-start.20 = (bf16[96,256]{1,0:T(8,128)(2,1)S(1)}, bf16[96,256]{1,0:T(8,128)(2,1)S(1)}, u32[]{:S(2)}, u32[]{:S(2)}) collective-permute-start(bf16[96,256]{1,0:T(8,128)(2,1)S(1)} %get-tuple-element.67), channel_id=1, source_target_pairs={{0,24},{2,26},{4,28},{6,30},{8,16},{10,18},{12,20},{14,22},{16,8},... | collective-permute-start | bytes 147464 | tf_op jit(solution)/shard_map/ppermute | solution.py:346
  68.5 0.0 collective-permute-done.18.refs_1_
  68.5 0.9 %collective-permute-done.19.refs_2_ = bf16[96,256]{1,0:T(8,128)(2,1)S(1)} collective-permute-done((bf16[96,256]{1,0:T(8,128)(2,1)S(1)}, bf16[96,256]{1,0:T(8,128)(2,1)S(1)}, u32[]{:S(2)}, u32[]{:S(2)}) %collective-permute-start.19) | collective-permute-done | bytes 49184 | tf_op jit(solution)/shard_map/ppermute | solution.py:346
  69.4 3.8 %collective-permute-done.20.refs_3_ = bf16[96,256]{1,0:T(8,128)(2,1)S(1)} collective-permute-done((bf16[96,256]{1,0:T(8,128)(2,1)S(1)}, bf16[96,256]{1,0:T(8,128)(2,1)S(1)}, u32[]{:S(2)}, u32[]{:S(2)}) %collective-permute-start.20) | collective-permute-done | bytes 49184 | tf_op jit(solution)/shard_map/ppermute | solution.py:346
  73.2 1.9 %shard_map.83 = f32[256,256]{1,0:T(8,128)} custom-call(bf16[96,256]{1,0:T(8,128)(2,1)S(1)} %get-tuple-element.64.refs_0_, bf16[96,256]{1,0:T(8,128)(2,1)S(1)} %collective-permute-done.18.refs_1_, bf16[96,256]{1,0:T(8,128)(2,1)S(1)} %collective-permute-done.19.refs_2_, bf16[96,256]{1,0:T(8,128)(2,1)S(1)} %collective-permute-done.20.refs_3_, ...), custom_call_target="tpu_custom_call" | custom-call | tf_op jit(solution)/shard_map/pallas_call | solution.py:432
  (8 shorter events, 0.0 us)
Async XLA Ops:
  0.0 21.2 %copy-start = (bf16[2,256,768]{2,1,0:T(8,128)(2,1)S(1)}, bf16[2,256,768]{2,1,0:T(8,128)(2,1)}, u32[]{:S(2)}) copy-start(bf16[2,256,768]{2,1,0:T(8,128)(2,1)} %refs_4_.5) | copy-start | bytes 2359300
  0.0 3.4 %collective-permute-start = (s32[2,256]{1,0:T(2,128)}, s32[2,256]{1,0:T(2,128)S(1)}, u32[]{:S(2)}, u32[]{:S(2)}) collective-permute-start(s32[2,256]{1,0:T(2,128)} %order_ref.1), channel_id=1, source_target_pairs={{1,1},{3,9},{5,17},{7,25},{9,3},{11,11},{13,19},{15,27},{17,5},{19... | collective-permute-start | bytes 6152 | tf_op jit(solution)/shard_map/ppermute | solution.py:346
  0.8 1.0 %copy-start.4 = (f32[256,256]{1,0:T(8,128)S(1)}, f32[256,256]{1,0:T(8,128)}, u32[]{:S(2)}) copy-start(f32[256,256]{1,0:T(8,128)} %refs_4_.4) | copy-start | bytes 786436
  1.8 0.7 copy-start.6
  2.5 0.7 copy-start.8
  3.9 6.6 %collective-permute-start.1 = (bf16[64,256]{1,0:T(8,128)(2,1)S(1)}, bf16[64,256]{1,0:T(8,128)(2,1)S(1)}, u32[]{:S(2)}, u32[]{:S(2)}) collective-permute-start(bf16[64,256]{1,0:T(8,128)(2,1)S(1)} %get-tuple-element.41), channel_id=1, source_target_pairs={{0,2},{2,0},{4,6},{6,4},{8,10},{10,8},{12,14},{14,12},{16,18},{18,... | collective-permute-start | bytes 98312 | tf_op jit(solution)/shard_map/ppermute | solution.py:346
  6.9 8.4 %collective-permute-start.4 = (bf16[256,256]{1,0:T(8,128)(2,1)S(1)}, bf16[256,256]{1,0:T(8,128)(2,1)S(1)}, u32[]{:S(2)}, u32[]{:S(2)}) collective-permute-start(bf16[256,256]{1,0:T(8,128)(2,1)S(1)} %get-tuple-element.39.row_ref.refs_0_), channel_id=1, source_target_pairs={{0,24},{2,26},{4,28},{6,30},{8,16},{10,18},{12,20},{14,22},{16,8},... | collective-permute-start | bytes 393224 | tf_op jit(solution)/shard_map/ppermute | solution.py:346
  10.5 6.6 %collective-permute-start.3 = (bf16[256,256]{1,0:T(8,128)(2,1)S(1)}, bf16[256,256]{1,0:T(8,128)(2,1)S(1)}, u32[]{:S(2)}, u32[]{:S(2)}) collective-permute-start(bf16[256,256]{1,0:T(8,128)(2,1)S(1)} %get-tuple-element.39.row_ref.refs_0_), channel_id=1, source_target_pairs={{0,16},{2,18},{4,20},{6,22},{8,24},{10,26},{12,28},{14,30},{16,0},... | collective-permute-start | bytes 393224 | tf_op jit(solution)/shard_map/ppermute | solution.py:346
  10.5 6.6 %collective-permute-start.2 = (bf16[256,256]{1,0:T(8,128)(2,1)S(1)}, bf16[256,256]{1,0:T(8,128)(2,1)S(1)}, u32[]{:S(2)}, u32[]{:S(2)}) collective-permute-start(bf16[256,256]{1,0:T(8,128)(2,1)S(1)} %get-tuple-element.42), channel_id=1, source_target_pairs={{0,8},{2,10},{4,12},{6,14},{8,0},{10,2},{12,4},{14,6},{16,24},{18,... | collective-permute-start | bytes 393224 | tf_op jit(solution)/shard_map/ppermute | solution.py:346
  11.3 3.9 %collective-permute-start.5 = (bf16[32,256]{1,0:T(8,128)(2,1)S(1)}, bf16[32,256]{1,0:T(8,128)(2,1)S(1)}, u32[]{:S(2)}, u32[]{:S(2)}) collective-permute-start(bf16[32,256]{1,0:T(8,128)(2,1)S(1)} %get-tuple-element.44), channel_id=1, source_target_pairs={{0,4},{2,6},{4,0},{6,2},{8,12},{10,14},{12,8},{14,10},{16,20},{18,... | collective-permute-start | bytes 49160 | tf_op jit(solution)/shard_map/ppermute | solution.py:346
  17.6 6.7 %collective-permute-start.8 = (bf16[384,256]{1,0:T(8,128)(2,1)S(1)}, bf16[384,256]{1,0:T(8,128)(2,1)S(1)}, u32[]{:S(2)}, u32[]{:S(2)}) collective-permute-start(bf16[384,256]{1,0:T(8,128)(2,1)S(1)} %get-tuple-element.46.row_ref.refs_0_), channel_id=1, source_target_pairs={{0,6},{2,4},{4,2},{6,0},{8,14},{10,12},{12,10},{14,8},{16,22},{18,... | collective-permute-start | bytes 589832 | tf_op jit(solution)/shard_map/ppermute | solution.py:346
  19.2 7.2 %collective-permute-start.7 = (bf16[384,256]{1,0:T(8,128)(2,1)S(1)}, bf16[384,256]{1,0:T(8,128)(2,1)S(1)}, u32[]{:S(2)}, u32[]{:S(2)}) collective-permute-start(bf16[384,256]{1,0:T(8,128)(2,1)S(1)} %get-tuple-element.46.row_ref.refs_0_), channel_id=1, source_target_pairs={{0,4},{2,6},{4,0},{6,2},{8,12},{10,14},{12,8},{14,10},{16,20},{18,... | collective-permute-start | bytes 589832 | tf_op jit(solution)/shard_map/ppermute | solution.py:346
  19.7 6.8 %collective-permute-start.6 = (bf16[384,256]{1,0:T(8,128)(2,1)S(1)}, bf16[384,256]{1,0:T(8,128)(2,1)S(1)}, u32[]{:S(2)}, u32[]{:S(2)}) collective-permute-start(bf16[384,256]{1,0:T(8,128)(2,1)S(1)} %get-tuple-element.46.row_ref.refs_0_), channel_id=1, source_target_pairs={{0,2},{2,0},{4,6},{6,4},{8,10},{10,8},{12,14},{14,12},{16,18},{18,... | collective-permute-start | bytes 589832 | tf_op jit(solution)/shard_map/ppermute | solution.py:346
  26.4 14.4 %copy-start.1 = (bf16[2,256,1024]{2,1,0:T(8,128)(2,1)S(1)}, bf16[2,256,1024]{2,1,0:T(8,128)(2,1)}, u32[]{:S(2)}) copy-start(bf16[2,256,1024]{2,1,0:T(8,128)(2,1)} %refs_11_.1) | copy-start | bytes 3145732
  26.4 14.4 %copy-start.2 = (bf16[2,1024,256]{2,1,0:T(8,128)(2,1)S(1)}, bf16[2,1024,256]{2,1,0:T(8,128)(2,1)}, u32[]{:S(2)}) copy-start(bf16[2,1024,256]{2,1,0:T(8,128)(2,1)} %refs_12_.1) | copy-start | bytes 3145732
  26.5 14.4 %copy-start.3 = (bf16[2,256,256]{2,1,0:T(8,128)(2,1)S(1)}, bf16[2,256,256]{2,1,0:T(8,128)(2,1)}, u32[]{:S(2)}) copy-start(bf16[2,256,256]{2,1,0:T(8,128)(2,1)} %refs_10_.1) | copy-start | bytes 786436
  26.5 14.4 %copy-start.5 = (f32[256,256]{1,0:T(8,128)S(1)}, f32[256,256]{1,0:T(8,128)}, u32[]{:S(2)}) copy-start(f32[256,256]{1,0:T(8,128)} %refs_4_.4) | copy-start | bytes 786436
  31.5 9.4 %copy-start.7 = (f32[2,2,256]{2,1,0:T(2,128)S(1)}, f32[2,2,256]{2,1,0:T(2,128)}, u32[]{:S(2)}) copy-start(f32[2,2,256]{2,1,0:T(2,128)} %refs_9_.1) | copy-start | bytes 12292
  31.5 4.5 %collective-permute-start.9 = (bf16[112,256]{1,0:T(8,128)(2,1)S(1)}, bf16[112,256]{1,0:T(8,128)(2,1)S(1)}, u32[]{:S(2)}, u32[]{:S(2)}) collective-permute-start(bf16[112,256]{1,0:T(8,128)(2,1)S(1)} %get-tuple-element.53), channel_id=1, source_target_pairs={{0,8},{2,10},{4,12},{6,14},{8,0},{10,2},{12,4},{14,6},{16,24},{18,... | collective-permute-start | bytes 172040 | tf_op jit(solution)/shard_map/ppermute | solution.py:346
  33.0 5.7 %collective-permute-start.10 = (bf16[112,256]{1,0:T(8,128)(2,1)S(1)}, bf16[112,256]{1,0:T(8,128)(2,1)S(1)}, u32[]{:S(2)}, u32[]{:S(2)}) collective-permute-start(bf16[112,256]{1,0:T(8,128)(2,1)S(1)} %get-tuple-element.54), channel_id=1, source_target_pairs={{0,16},{2,18},{4,20},{6,22},{8,24},{10,26},{12,28},{14,30},{16,0},... | collective-permute-start | bytes 172040 | tf_op jit(solution)/shard_map/ppermute | solution.py:346
  34.9 6.0 %collective-permute-start.11 = (bf16[112,256]{1,0:T(8,128)(2,1)S(1)}, bf16[112,256]{1,0:T(8,128)(2,1)S(1)}, u32[]{:S(2)}, u32[]{:S(2)}) collective-permute-start(bf16[112,256]{1,0:T(8,128)(2,1)S(1)} %get-tuple-element.55), channel_id=1, source_target_pairs={{0,24},{2,26},{4,28},{6,30},{8,16},{10,18},{12,20},{14,22},{16,8},... | collective-permute-start | bytes 172040 | tf_op jit(solution)/shard_map/ppermute | solution.py:346
  42.5 4.5 %collective-permute-start.12 = (bf16[96,256]{1,0:T(8,128)(2,1)S(1)}, bf16[96,256]{1,0:T(8,128)(2,1)S(1)}, u32[]{:S(2)}, u32[]{:S(2)}) collective-permute-start(bf16[96,256]{1,0:T(8,128)(2,1)S(1)} %get-tuple-element.57), channel_id=1, source_target_pairs={{0,8},{2,10},{4,12},{6,14},{8,0},{10,2},{12,4},{14,6},{16,24},{18,... | collective-permute-start | bytes 147464 | tf_op jit(solution)/shard_map/ppermute | solution.py:346
  42.6 5.1 %collective-permute-start.13 = (bf16[96,256]{1,0:T(8,128)(2,1)S(1)}, bf16[96,256]{1,0:T(8,128)(2,1)S(1)}, u32[]{:S(2)}, u32[]{:S(2)}) collective-permute-start(bf16[96,256]{1,0:T(8,128)(2,1)S(1)} %get-tuple-element.58), channel_id=1, source_target_pairs={{0,16},{2,18},{4,20},{6,22},{8,24},{10,26},{12,28},{14,30},{16,0},... | collective-permute-start | bytes 147464 | tf_op jit(solution)/shard_map/ppermute | solution.py:346
  44.2 5.9 %collective-permute-start.14 = (bf16[96,256]{1,0:T(8,128)(2,1)S(1)}, bf16[96,256]{1,0:T(8,128)(2,1)S(1)}, u32[]{:S(2)}, u32[]{:S(2)}) collective-permute-start(bf16[96,256]{1,0:T(8,128)(2,1)S(1)} %get-tuple-element.59), channel_id=1, source_target_pairs={{0,24},{2,26},{4,28},{6,30},{8,16},{10,18},{12,20},{14,22},{16,8},... | collective-permute-start | bytes 147464 | tf_op jit(solution)/shard_map/ppermute | solution.py:346
  50.2 6.7 %collective-permute-start.17 = (bf16[384,256]{1,0:T(8,128)(2,1)S(1)}, bf16[384,256]{1,0:T(8,128)(2,1)S(1)}, u32[]{:S(2)}, u32[]{:S(2)}) collective-permute-start(bf16[384,256]{1,0:T(8,128)(2,1)S(1)} %shard_map.80.row_ref.refs_0_), channel_id=1, source_target_pairs={{0,6},{2,4},{4,2},{6,0},{8,14},{10,12},{12,10},{14,8},{16,22},{18,... | collective-permute-start | bytes 589832 | tf_op jit(solution)/shard_map/ppermute | solution.py:346
  51.6 7.3 %collective-permute-start.16 = (bf16[384,256]{1,0:T(8,128)(2,1)S(1)}, bf16[384,256]{1,0:T(8,128)(2,1)S(1)}, u32[]{:S(2)}, u32[]{:S(2)}) collective-permute-start(bf16[384,256]{1,0:T(8,128)(2,1)S(1)} %shard_map.80.row_ref.refs_0_), channel_id=1, source_target_pairs={{0,4},{2,6},{4,0},{6,2},{8,12},{10,14},{12,8},{14,10},{16,20},{18,... | collective-permute-start | bytes 589832 | tf_op jit(solution)/shard_map/ppermute | solution.py:346
  52.2 6.7 %collective-permute-start.15 = (bf16[384,256]{1,0:T(8,128)(2,1)S(1)}, bf16[384,256]{1,0:T(8,128)(2,1)S(1)}, u32[]{:S(2)}, u32[]{:S(2)}) collective-permute-start(bf16[384,256]{1,0:T(8,128)(2,1)S(1)} %shard_map.80.row_ref.refs_0_), channel_id=1, source_target_pairs={{0,2},{2,0},{4,6},{6,4},{8,10},{10,8},{12,14},{14,12},{16,18},{18,... | collective-permute-start | bytes 589832 | tf_op jit(solution)/shard_map/ppermute | solution.py:346
  64.0 4.5 %collective-permute-start.18 = (bf16[96,256]{1,0:T(8,128)(2,1)S(1)}, bf16[96,256]{1,0:T(8,128)(2,1)S(1)}, u32[]{:S(2)}, u32[]{:S(2)}) collective-permute-start(bf16[96,256]{1,0:T(8,128)(2,1)S(1)} %get-tuple-element.65), channel_id=1, source_target_pairs={{0,8},{2,10},{4,12},{6,14},{8,0},{10,2},{12,4},{14,6},{16,24},{18,... | collective-permute-start | bytes 147464 | tf_op jit(solution)/shard_map/ppermute | solution.py:346
  64.1 5.3 %collective-permute-start.19 = (bf16[96,256]{1,0:T(8,128)(2,1)S(1)}, bf16[96,256]{1,0:T(8,128)(2,1)S(1)}, u32[]{:S(2)}, u32[]{:S(2)}) collective-permute-start(bf16[96,256]{1,0:T(8,128)(2,1)S(1)} %get-tuple-element.66), channel_id=1, source_target_pairs={{0,16},{2,18},{4,20},{6,22},{8,24},{10,26},{12,28},{14,30},{16,0},... | collective-permute-start | bytes 147464 | tf_op jit(solution)/shard_map/ppermute | solution.py:346
  67.4 5.9 %collective-permute-start.20 = (bf16[96,256]{1,0:T(8,128)(2,1)S(1)}, bf16[96,256]{1,0:T(8,128)(2,1)S(1)}, u32[]{:S(2)}, u32[]{:S(2)}) collective-permute-start(bf16[96,256]{1,0:T(8,128)(2,1)S(1)} %get-tuple-element.67), channel_id=1, source_target_pairs={{0,24},{2,26},{4,28},{6,30},{8,16},{10,18},{12,20},{14,22},{16,8},... | collective-permute-start | bytes 147464 | tf_op jit(solution)/shard_map/ppermute | solution.py:346

commit v6 on v5

--- a/solution.py
+++ b/solution.py
@@ -219,7 +219,25 @@
         averaged(3, second, 1)
         return carry
 
-    lax.fori_loop(0, (own + 2 * TALL - 1) // (2 * TALL), step, 0)
+    full = own // (2 * TALL)
+    lax.fori_loop(0, full, step, 0)
+    rest = own - full * 2 * TALL
+    first = pl.multiple_of(full * 2 * TALL, 2 * TALL)
+    second = pl.multiple_of(first + TALL, TALL)
+
+    @pl.when((rest > 0) & (rest <= TALL))
+    def _():
+        averaged(0, first, 0)
+        averaged(1, first, 1)
+
+    @pl.when(rest > TALL)
+    def _():
+        scored(2, second, 0)
+        averaged(0, first, 0)
+        scored(3, second, 1)
+        averaged(1, first, 1)
+        averaged(2, second, 0)
+        averaged(3, second, 1)
 
 
 def early_body(plan, b, count_ref, row_ref, weight_ref, *refs):
@@ -296,19 +314,11 @@
             out_refs[j][cap : cap + 16, :] = note.astype(BF16)
 
 
-def store_body(plan, b, last, *refs):
-    lines, cap, rows = plan.lines, plan.cap, plan.rows
-    piece_refs, refs = refs[:lines], refs[lines:]
-    if b:
-        note_refs, refs = refs[:lines], refs[lines:]
-    else:
-        note_refs = piece_refs
-    state_ref, gain_ref, proj_ref, fc1_ref, fc2_ref = refs[:5]
-    refs = refs[5:]
-    state_out, send_refs = refs[0], refs[1:]
+def slots_of(plan, note_refs):
+    cap = plan.cap
     notes = [r[cap : cap + 16, :].astype(F32) for r in note_refs]
     members = jnp.concatenate(notes, axis=0)
-    ranks = matmul(members.astype(BF16), earlier_mask(rows))
+    ranks = matmul(members.astype(BF16), earlier_mask(plan.rows))
     slot = iota((cap, 1), 0).astype(F32)
 
     def places(j, block):
@@ -316,9 +326,36 @@
         where = jnp.where(members[at : at + 1] > 0.5, ranks[at : at + 1], -1.0)
         return ones_where(slot == where)
 
-    where_from = jnp.concatenate([places(j, b) for j in range(lines)], axis=0)
+    return places
+
+
+def place_body(plan, b, *refs):
+    note_refs, where_ref = refs[:-1], refs[-1]
+    places = slots_of(plan, note_refs)
+    found = jnp.concatenate([places(j, b) for j in range(plan.lines)], axis=0)
+    same = ones_where(iota((plan.rows, plan.rows), 0) == iota((plan.rows, plan.rows), 1))
+    where_ref[...] = matmul(same, found, NT).astype(BF16)
+
+
+def store_body(plan, b, last, *refs):
+    lines, cap, rows = plan.lines, plan.cap, plan.rows
+    piece_refs, refs = refs[:lines], refs[lines:]
+    note_refs = piece_refs
+    if b:
+        where_ref, refs = refs[0], refs[1:]
+        if not last:
+            note_refs, refs = refs[:lines], refs[lines:]
+    state_ref, gain_ref, proj_ref, fc1_ref, fc2_ref = refs[:5]
+    refs = refs[5:]
+    state_out, send_refs = refs[0], refs[1:]
+    if not b or not last:
+        places = slots_of(plan, note_refs)
     pieces = jnp.concatenate([r[0:cap, :] for r in piece_refs], axis=0)
-    mixed = matmul(where_from, pieces, TN).astype(BF16)
+    if b:
+        mixed = matmul(where_ref[...], pieces).astype(BF16)
+    else:
+        where_from = jnp.concatenate([places(j, b) for j in range(lines)], axis=0)
+        mixed = matmul(where_from, pieces, TN).astype(BF16)
     attended = state_ref[...] + matmul(mixed, proj_ref[b])
     normed_two = layer_norm(attended, gain_ref[b, 1:2, :]).astype(BF16)
     state = attended
@@ -425,23 +462,20 @@
         )(counts, *parts, qkv_weight, *early, *extra)
         pieces = along_line(mixed)
         if b == 0:
-            kept = pieces
+            kept_notes, told = pieces, []
+        else:
+            told = kernel_call(
+                functools.partial(place_body, plan, b),
+                [struct((rows, held), BF16)],
+                [whole()] * lines,
+            )(*kept_notes)
+            told = list(told) + ([] if last else kept_notes)
         outs = [struct((rows, width), F32)]
         if not last:
             outs += [struct((cap, width), BF16)] * lines
         stored = kernel_call(
-            functools.partial(store_body, plan, b, last),
-            outs,
-            [whole()] * (lines * (2 if b else 1) + 5),
-        )(
-            *pieces,
-            *(kept if b else []),
-            state,
-            norm_gains,
-            proj_weight,
-            fc1_weight,
-            fc2_weight,
-        )
+            functools.partial(store_body, plan, b, last), outs, [whole()] * (lines + len(told) + 5)
+        )(*pieces, *told, state, norm_gains, proj_weight, fc1_weight, fc2_weight)
         state = stored[0]
         if not last:
             arrived = along_line(stored[1:])

time: 75.4 us -> 75.2 us (level)
  transfers between devices with their start and end apart: 21 -> 21, of which waited for: 13 -> 13; matrix products, arithmetic and copies ran while one was open for 0% -> 0% of each run, Pallas kernels for 7% -> 8%
where the time goes in v6:
time: 75.2 us; the launch traced here: 75 us
  starting transfers between devices  30.2 us (40%)
  waiting for transfers between devices  21.7 us (29%)
  Pallas kernels  20.5 us (27%)
  local copies, waits for them, and re-layouts  2.43 us (3%)
    ppermute x21, starting transfers between devices, move(): return lax.ppermute(block, ('pts', 'slab'), pairs)  30.2 us
    ppermute x21, waiting for transfers between devices, move(): return lax.ppermute(block, ('pts', 'slab'), pairs)  21.7 us
    pallas_call x2, Pallas kernels, by_lines(): kernel_call(functools.partial(attend_body, plan, b, b == 0), [struct((tal...  10.2 us
    pallas_call x2, Pallas kernels, by_lines(): kernel_call(functools.partial(early_body, plan, b), [struct((held + 2 * T...  5.39 us
    pallas_call x2, Pallas kernels, by_lines(): kernel_call(functools.partial(store_body, plan, b, last), outs, [whole()]...  3.36 us
    unnamed x18, local copies, waits for them, and re-layouts  2.34 us
  transfers between devices with their start and end apart: 21, of which 13 were waited for; matrix products, arithmetic and copies ran while one was open for 0% of the time, Pallas kernels for 8%

profile of v6, /device:TPU:0, one launch (start us, length us, event | category | flops | bytes accessed | tf_op | source)
XLA Modules:
  0.0 75.0 jit_solution(13311678705409753026)
XLA Ops:
  0.0 0.8 %collective-permute-start = (s32[2,256]{1,0:T(2,128)}, s32[2,256]{1,0:T(2,128)S(1)}, u32[]{:S(2)}, u32[]{:S(2)}) collective-permute-start(s32[2,256]{1,0:T(2,128)} %order_ref.1), channel_id=1, source_target_pairs={{1,1},{3,9},{5,17},{7,25},{9,3},{11,11},{13,19},{15,27},{17,5},{19... | collective-permute-start | bytes 6152 | tf_op jit(solution)/shard_map/ppermute | solution.py:383
  0.8 0.0 copy-start.4
  0.8 0.9 %copy-done.4 = f32[256,256]{1,0:T(8,128)S(1)} copy-done((f32[256,256]{1,0:T(8,128)S(1)}, f32[256,256]{1,0:T(8,128)}, u32[]{:S(2)}) %copy-start.4) | copy-done | bytes 262168
  1.8 0.7 copy-done.6
  2.5 0.7 copy-done.8
  3.1 0.2 shard_map.73
  3.3 0.1 stack.23
  3.4 0.0 collective-permute-done.turned_ref
  3.4 0.4 shard_map.74
  3.9 3.0 %collective-permute-start.1 = (bf16[64,256]{1,0:T(8,128)(2,1)S(1)}, bf16[64,256]{1,0:T(8,128)(2,1)S(1)}, u32[]{:S(2)}, u32[]{:S(2)}) collective-permute-start(bf16[64,256]{1,0:T(8,128)(2,1)S(1)} %get-tuple-element.41), channel_id=1, source_target_pairs={{0,2},{2,0},{4,6},{6,4},{8,10},{10,8},{12,14},{14,12},{16,18},{18,... | collective-permute-start | bytes 98312 | tf_op jit(solution)/shard_map/ppermute | solution.py:383
  6.9 3.6 %collective-permute-start.4 = (bf16[256,256]{1,0:T(8,128)(2,1)S(1)}, bf16[256,256]{1,0:T(8,128)(2,1)S(1)}, u32[]{:S(2)}, u32[]{:S(2)}) collective-permute-start(bf16[256,256]{1,0:T(8,128)(2,1)S(1)} %get-tuple-element.39.row_ref.refs_0_), channel_id=1, source_target_pairs={{0,24},{2,26},{4,28},{6,30},{8,16},{10,18},{12,20},{14,22},{16,8},... | collective-permute-start | bytes 393224 | tf_op jit(solution)/shard_map/ppermute | solution.py:383
  10.5 0.0 collective-permute-start.3
  10.5 0.0 collective-permute-done.1.got_ref
  10.5 0.8 %collective-permute-start.2 = (bf16[256,256]{1,0:T(8,128)(2,1)S(1)}, bf16[256,256]{1,0:T(8,128)(2,1)S(1)}, u32[]{:S(2)}, u32[]{:S(2)}) collective-permute-start(bf16[256,256]{1,0:T(8,128)(2,1)S(1)} %get-tuple-element.42), channel_id=1, source_target_pairs={{0,8},{2,10},{4,12},{6,14},{8,0},{10,2},{12,4},{14,6},{16,24},{18,... | collective-permute-start | bytes 393224 | tf_op jit(solution)/shard_map/ppermute | solution.py:383
  11.3 1.5 %collective-permute-start.5 = (bf16[32,256]{1,0:T(8,128)(2,1)S(1)}, bf16[32,256]{1,0:T(8,128)(2,1)S(1)}, u32[]{:S(2)}, u32[]{:S(2)}) collective-permute-start(bf16[32,256]{1,0:T(8,128)(2,1)S(1)} %get-tuple-element.44), channel_id=1, source_target_pairs={{0,4},{2,6},{4,0},{6,2},{8,12},{10,14},{12,8},{14,10},{16,20},{18,... | collective-permute-start | bytes 49160 | tf_op jit(solution)/shard_map/ppermute | solution.py:383
  12.9 2.4 %collective-permute-done.5.refs_5_ = bf16[32,256]{1,0:T(8,128)(2,1)S(1)} collective-permute-done((bf16[32,256]{1,0:T(8,128)(2,1)S(1)}, bf16[32,256]{1,0:T(8,128)(2,1)S(1)}, u32[]{:S(2)}, u32[]{:S(2)}) %collective-permute-start.5) | collective-permute-done | bytes 16416 | tf_op jit(solution)/shard_map/ppermute | solution.py:383
  15.2 0.0 collective-permute-done.4.refs_3_
  15.3 1.8 %collective-permute-done.3.refs_2_ = bf16[256,256]{1,0:T(8,128)(2,1)S(1)} collective-permute-done((bf16[256,256]{1,0:T(8,128)(2,1)S(1)}, bf16[256,256]{1,0:T(8,128)(2,1)S(1)}, u32[]{:S(2)}, u32[]{:S(2)}) %collective-permute-start.3) | collective-permute-done | bytes 131104 | tf_op jit(solution)/shard_map/ppermute | solution.py:383
  17.0 0.0 collective-permute-done.2.refs_1_
  17.1 0.5 shard_map.76
  17.6 1.6 %collective-permute-start.8 = (bf16[384,256]{1,0:T(8,128)(2,1)S(1)}, bf16[384,256]{1,0:T(8,128)(2,1)S(1)}, u32[]{:S(2)}, u32[]{:S(2)}) collective-permute-start(bf16[384,256]{1,0:T(8,128)(2,1)S(1)} %get-tuple-element.46.row_ref.refs_0_), channel_id=1, source_target_pairs={{0,6},{2,4},{4,2},{6,0},{8,14},{10,12},{12,10},{14,8},{16,22},{18,... | collective-permute-start | bytes 589832 | tf_op jit(solution)/shard_map/ppermute | solution.py:383
  19.2 0.5 collective-permute-start.7
  19.7 1.5 %collective-permute-start.6 = (bf16[384,256]{1,0:T(8,128)(2,1)S(1)}, bf16[384,256]{1,0:T(8,128)(2,1)S(1)}, u32[]{:S(2)}, u32[]{:S(2)}) collective-permute-start(bf16[384,256]{1,0:T(8,128)(2,1)S(1)} %get-tuple-element.46.row_ref.refs_0_), channel_id=1, source_target_pairs={{0,2},{2,0},{4,6},{6,4},{8,10},{10,8},{12,14},{14,12},{16,18},{18,... | collective-permute-start | bytes 589832 | tf_op jit(solution)/shard_map/ppermute | solution.py:383
  21.2 0.0 copy-done
  21.2 2.6 %shard_map.77 = (bf16[448,256]{1,0:T(8,128)(2,1)S(1)}, f32[384,256]{1,0:T(8,128)S(1)}, f32[384,256]{1,0:T(8,128)S(1)}, f32[384,256]{1,0:T(8,128)S(1)}) custom-call(s32[16,128]{1,0:T(8,128)S(1)} %get-tuple-element.45.count_ref, bf16[384,256]{1,0:T(8,128)(2,1)S(1)} %get-tuple-element.46.row_ref.refs_0_, bf16[2,256,768]{2,1,0:T(8,128)(2,1)S(1)} %copy-done), custom_call_target="tpu_custom_call" | custom-call | tf_op jit(solution)/shard_map/pallas_call | solution.py:439
  23.7 0.6 collective-permute-done.8.refs_3_
  24.3 2.0 %collective-permute-done.7.refs_2_ = bf16[384,256]{1,0:T(8,128)(2,1)S(1)} collective-permute-done((bf16[384,256]{1,0:T(8,128)(2,1)S(1)}, bf16[384,256]{1,0:T(8,128)(2,1)S(1)}, u32[]{:S(2)}, u32[]{:S(2)}) %collective-permute-start.7) | collective-permute-done | bytes 196640 | tf_op jit(solution)/shard_map/ppermute | solution.py:383
  26.3 0.1 collective-permute-done.6.refs_1_
  26.5 5.0 %shard_map.78 = (bf16[112,256]{1,0:T(8,128)(2,1)S(1)}, bf16[112,256]{1,0:T(8,128)(2,1)S(1)}, bf16[112,256]{1,0:T(8,128)(2,1)S(1)}, bf16[112,256]{1,0:T(8,128)(2,1)S(1)}) custom-call(s32[16,128]{1,0:T(8,128)S(1)} %get-tuple-element.45.count_ref, bf16[384,256]{1,0:T(8,128)(2,1)S(1)} %get-tuple-element.46.row_ref.refs_0_, ...), custom_call_target="tpu_custom_call" | custom-call | tf_op jit(solution)/shard_map/pallas_call | solution.py:451
  31.5 0.0 copy-start.7
  31.5 1.5 %collective-permute-start.9 = (bf16[112,256]{1,0:T(8,128)(2,1)S(1)}, bf16[112,256]{1,0:T(8,128)(2,1)S(1)}, u32[]{:S(2)}, u32[]{:S(2)}) collective-permute-start(bf16[112,256]{1,0:T(8,128)(2,1)S(1)} %get-tuple-element.53), channel_id=1, source_target_pairs={{0,8},{2,10},{4,12},{6,14},{8,0},{10,2},{12,4},{14,6},{16,24},{18,... | collective-permute-start | bytes 172040 | tf_op jit(solution)/shard_map/ppermute | solution.py:383
  33.0 1.9 %collective-permute-start.10 = (bf16[112,256]{1,0:T(8,128)(2,1)S(1)}, bf16[112,256]{1,0:T(8,128)(2,1)S(1)}, u32[]{:S(2)}, u32[]{:S(2)}) collective-permute-start(bf16[112,256]{1,0:T(8,128)(2,1)S(1)} %get-tuple-element.54), channel_id=1, source_target_pairs={{0,16},{2,18},{4,20},{6,22},{8,24},{10,26},{12,28},{14,30},{16,0},... | collective-permute-start | bytes 172040 | tf_op jit(solution)/shard_map/ppermute | solution.py:383
  34.9 1.1 %collective-permute-start.11 = (bf16[112,256]{1,0:T(8,128)(2,1)S(1)}, bf16[112,256]{1,0:T(8,128)(2,1)S(1)}, u32[]{:S(2)}, u32[]{:S(2)}) collective-permute-start(bf16[112,256]{1,0:T(8,128)(2,1)S(1)} %get-tuple-element.55), channel_id=1, source_target_pairs={{0,24},{2,26},{4,28},{6,30},{8,16},{10,18},{12,20},{14,22},{16,8},... | collective-permute-start | bytes 172040 | tf_op jit(solution)/shard_map/ppermute | solution.py:383
  36.0 0.0 collective-permute-done.9.refs_1_
  36.0 2.7 %collective-permute-done.10.refs_2_ = bf16[112,256]{1,0:T(8,128)(2,1)S(1)} collective-permute-done((bf16[112,256]{1,0:T(8,128)(2,1)S(1)}, bf16[112,256]{1,0:T(8,128)(2,1)S(1)}, u32[]{:S(2)}, u32[]{:S(2)}) %collective-permute-start.10) | collective-permute-done | bytes 57376 | tf_op jit(solution)/shard_map/ppermute | solution.py:383
  38.7 2.2 %collective-permute-done.11.refs_3_ = bf16[112,256]{1,0:T(8,128)(2,1)S(1)} collective-permute-done((bf16[112,256]{1,0:T(8,128)(2,1)S(1)}, bf16[112,256]{1,0:T(8,128)(2,1)S(1)}, u32[]{:S(2)}, u32[]{:S(2)}) %collective-permute-start.11) | collective-permute-done | bytes 57376 | tf_op jit(solution)/shard_map/ppermute | solution.py:383
  40.9 0.0 copy-done.1
  40.9 0.0 copy-done.2
  40.9 0.0 copy-done.3
  40.9 0.0 copy-done.5
  40.9 0.0 copy-done.7
  40.9 1.6 %shard_map.79 = (f32[256,256]{1,0:T(8,128)S(1)}, bf16[96,256]{1,0:T(8,128)(2,1)S(1)}, bf16[96,256]{1,0:T(8,128)(2,1)S(1)}, bf16[96,256]{1,0:T(8,128)(2,1)S(1)}, bf16[96,256]{1,0:T(8,128)(2,1)S(1)}) custom-call(bf16[112,256]{1,0:T(8,128)(2,1)S(1)} %get-tuple-element.52.refs_0_, bf16[112,256]{1,0:T(8,128)(2,1)S(1)} %collective-permute-done.9.refs_1_, ...), custom_call_target="tpu_custom_call" | custom-call | tf_op jit(solution)/shard_map/pallas_call | solution.py:476
  42.5 0.1 collective-permute-start.12
  42.6 1.7 %collective-permute-start.13 = (bf16[96,256]{1,0:T(8,128)(2,1)S(1)}, bf16[96,256]{1,0:T(8,128)(2,1)S(1)}, u32[]{:S(2)}, u32[]{:S(2)}) collective-permute-start(bf16[96,256]{1,0:T(8,128)(2,1)S(1)} %get-tuple-element.58), channel_id=1, source_target_pairs={{0,16},{2,18},{4,20},{6,22},{8,24},{10,26},{12,28},{14,30},{16,0},... | collective-permute-start | bytes 147464 | tf_op jit(solution)/shard_map/ppermute | solution.py:383
  44.3 2.7 %collective-permute-start.14 = (bf16[96,256]{1,0:T(8,128)(2,1)S(1)}, bf16[96,256]{1,0:T(8,128)(2,1)S(1)}, u32[]{:S(2)}, u32[]{:S(2)}) collective-permute-start(bf16[96,256]{1,0:T(8,128)(2,1)S(1)} %get-tuple-element.59), channel_id=1, source_target_pairs={{0,24},{2,26},{4,28},{6,30},{8,16},{10,18},{12,20},{14,22},{16,8},... | collective-permute-start | bytes 147464 | tf_op jit(solution)/shard_map/ppermute | solution.py:383
  46.9 0.0 collective-permute-done.12.refs_1_
  47.0 0.7 collective-permute-done.13.refs_2_
  47.6 2.5 %collective-permute-done.14.refs_3_ = bf16[96,256]{1,0:T(8,128)(2,1)S(1)} collective-permute-done((bf16[96,256]{1,0:T(8,128)(2,1)S(1)}, bf16[96,256]{1,0:T(8,128)(2,1)S(1)}, u32[]{:S(2)}, u32[]{:S(2)}) %collective-permute-start.14) | collective-permute-done | bytes 49184 | tf_op jit(solution)/shard_map/ppermute | solution.py:383
  50.2 1.5 %collective-permute-start.17 = (bf16[384,256]{1,0:T(8,128)(2,1)S(1)}, bf16[384,256]{1,0:T(8,128)(2,1)S(1)}, u32[]{:S(2)}, u32[]{:S(2)}) collective-permute-start(bf16[384,256]{1,0:T(8,128)(2,1)S(1)} %shard_map.80.row_ref.refs_0_), channel_id=1, source_target_pairs={{0,6},{2,4},{4,2},{6,0},{8,14},{10,12},{12,10},{14,8},{16,22},{18,... | collective-permute-start | bytes 589832 | tf_op jit(solution)/shard_map/ppermute | solution.py:383
  51.7 0.6 collective-permute-start.16
  52.2 1.5 %collective-permute-start.15 = (bf16[384,256]{1,0:T(8,128)(2,1)S(1)}, bf16[384,256]{1,0:T(8,128)(2,1)S(1)}, u32[]{:S(2)}, u32[]{:S(2)}) collective-permute-start(bf16[384,256]{1,0:T(8,128)(2,1)S(1)} %shard_map.80.row_ref.refs_0_), channel_id=1, source_target_pairs={{0,2},{2,0},{4,6},{6,4},{8,10},{10,8},{12,14},{14,12},{16,18},{18,... | collective-permute-start | bytes 589832 | tf_op jit(solution)/shard_map/ppermute | solution.py:383
  53.7 2.8 %shard_map.81 = (bf16[448,256]{1,0:T(8,128)(2,1)S(1)}, f32[384,256]{1,0:T(8,128)S(1)}, f32[384,256]{1,0:T(8,128)S(1)}, f32[384,256]{1,0:T(8,128)S(1)}) custom-call(s32[16,128]{1,0:T(8,128)S(1)} %get-tuple-element.45.count_ref, bf16[384,256]{1,0:T(8,128)(2,1)S(1)} %shard_map.80.row_ref.refs_0_, bf16[2,256,768]{2,1,0:T(8,128)(2,1)S(1)} %copy-done), custom_call_target="tpu_custom_call" | custom-call | tf_op jit(solution)/shard_map/pallas_call | solution.py:439
  56.6 0.3 collective-permute-done.17.refs_3_
  56.9 2.0 %collective-permute-done.16.refs_2_ = bf16[384,256]{1,0:T(8,128)(2,1)S(1)} collective-permute-done((bf16[384,256]{1,0:T(8,128)(2,1)S(1)}, bf16[384,256]{1,0:T(8,128)(2,1)S(1)}, u32[]{:S(2)}, u32[]{:S(2)}) %collective-permute-start.16) | collective-permute-done | bytes 196640 | tf_op jit(solution)/shard_map/ppermute | solution.py:383
  58.9 0.0 collective-permute-done.15.refs_1_
  58.9 5.1 %shard_map.82 = (bf16[96,256]{1,0:T(8,128)(2,1)S(1)}, bf16[96,256]{1,0:T(8,128)(2,1)S(1)}, bf16[96,256]{1,0:T(8,128)(2,1)S(1)}, bf16[96,256]{1,0:T(8,128)(2,1)S(1)}) custom-call(s32[16,128]{1,0:T(8,128)S(1)} %get-tuple-element.45.count_ref, bf16[384,256]{1,0:T(8,128)(2,1)S(1)} %shard_map.80.row_ref.refs_0_, ...), custom_call_target="tpu_custom_call" | custom-call | tf_op jit(solution)/shard_map/pallas_call | solution.py:451
  64.1 0.1 collective-permute-start.18
  64.1 3.2 %collective-permute-start.19 = (bf16[96,256]{1,0:T(8,128)(2,1)S(1)}, bf16[96,256]{1,0:T(8,128)(2,1)S(1)}, u32[]{:S(2)}, u32[]{:S(2)}) collective-permute-start(bf16[96,256]{1,0:T(8,128)(2,1)S(1)} %get-tuple-element.66), channel_id=1, source_target_pairs={{0,16},{2,18},{4,20},{6,22},{8,24},{10,26},{12,28},{14,30},{16,0},... | collective-permute-start | bytes 147464 | tf_op jit(solution)/shard_map/ppermute | solution.py:383
  67.4 1.1 %collective-permute-start.20 = (bf16[96,256]{1,0:T(8,128)(2,1)S(1)}, bf16[96,256]{1,0:T(8,128)(2,1)S(1)}, u32[]{:S(2)}, u32[]{:S(2)}) collective-permute-start(bf16[96,256]{1,0:T(8,128)(2,1)S(1)} %get-tuple-element.67), channel_id=1, source_target_pairs={{0,24},{2,26},{4,28},{6,30},{8,16},{10,18},{12,20},{14,22},{16,8},... | collective-permute-start | bytes 147464 | tf_op jit(solution)/shard_map/ppermute | solution.py:383
  68.5 0.4 shard_map.83.refs_4_
  68.9 0.0 collective-permute-done.18.refs_1_
  68.9 0.5 collective-permute-done.19.refs_2_
  69.4 3.8 %collective-permute-done.20.refs_3_ = bf16[96,256]{1,0:T(8,128)(2,1)S(1)} collective-permute-done((bf16[96,256]{1,0:T(8,128)(2,1)S(1)}, bf16[96,256]{1,0:T(8,128)(2,1)S(1)}, u32[]{:S(2)}, u32[]{:S(2)}) %collective-permute-start.20) | collective-permute-done | bytes 49184 | tf_op jit(solution)/shard_map/ppermute | solution.py:383
  73.3 1.7 %shard_map.84 = f32[256,256]{1,0:T(8,128)} custom-call(bf16[96,256]{1,0:T(8,128)(2,1)S(1)} %get-tuple-element.64.refs_0_, bf16[96,256]{1,0:T(8,128)(2,1)S(1)} %collective-permute-done.18.refs_1_, bf16[96,256]{1,0:T(8,128)(2,1)S(1)} %collective-permute-done.19.refs_2_, bf16[96,256]{1,0:T(8,128)(2,1)S(1)} %collective-permute-done.20.refs_3_, ...), custom_call_target="tpu_custom_call" | custom-call | tf_op jit(solution)/shard_map/pallas_call | solution.py:476
  (9 shorter events, 0.0 us)
Async XLA Ops:
  0.0 21.2 %copy-start = (bf16[2,256,768]{2,1,0:T(8,128)(2,1)S(1)}, bf16[2,256,768]{2,1,0:T(8,128)(2,1)}, u32[]{:S(2)}) copy-start(bf16[2,256,768]{2,1,0:T(8,128)(2,1)} %refs_4_.5) | copy-start | bytes 2359300
  0.0 3.4 %collective-permute-start = (s32[2,256]{1,0:T(2,128)}, s32[2,256]{1,0:T(2,128)S(1)}, u32[]{:S(2)}, u32[]{:S(2)}) collective-permute-start(s32[2,256]{1,0:T(2,128)} %order_ref.1), channel_id=1, source_target_pairs={{1,1},{3,9},{5,17},{7,25},{9,3},{11,11},{13,19},{15,27},{17,5},{19... | collective-permute-start | bytes 6152 | tf_op jit(solution)/shard_map/ppermute | solution.py:383
  0.8 1.0 %copy-start.4 = (f32[256,256]{1,0:T(8,128)S(1)}, f32[256,256]{1,0:T(8,128)}, u32[]{:S(2)}) copy-start(f32[256,256]{1,0:T(8,128)} %refs_4_.4) | copy-start | bytes 786436
  1.8 0.7 copy-start.6
  2.5 0.7 copy-start.8
  3.9 6.6 %collective-permute-start.1 = (bf16[64,256]{1,0:T(8,128)(2,1)S(1)}, bf16[64,256]{1,0:T(8,128)(2,1)S(1)}, u32[]{:S(2)}, u32[]{:S(2)}) collective-permute-start(bf16[64,256]{1,0:T(8,128)(2,1)S(1)} %get-tuple-element.41), channel_id=1, source_target_pairs={{0,2},{2,0},{4,6},{6,4},{8,10},{10,8},{12,14},{14,12},{16,18},{18,... | collective-permute-start | bytes 98312 | tf_op jit(solution)/shard_map/ppermute | solution.py:383
  6.9 8.4 %collective-permute-start.4 = (bf16[256,256]{1,0:T(8,128)(2,1)S(1)}, bf16[256,256]{1,0:T(8,128)(2,1)S(1)}, u32[]{:S(2)}, u32[]{:S(2)}) collective-permute-start(bf16[256,256]{1,0:T(8,128)(2,1)S(1)} %get-tuple-element.39.row_ref.refs_0_), channel_id=1, source_target_pairs={{0,24},{2,26},{4,28},{6,30},{8,16},{10,18},{12,20},{14,22},{16,8},... | collective-permute-start | bytes 393224 | tf_op jit(solution)/shard_map/ppermute | solution.py:383
  10.5 6.6 %collective-permute-start.3 = (bf16[256,256]{1,0:T(8,128)(2,1)S(1)}, bf16[256,256]{1,0:T(8,128)(2,1)S(1)}, u32[]{:S(2)}, u32[]{:S(2)}) collective-permute-start(bf16[256,256]{1,0:T(8,128)(2,1)S(1)} %get-tuple-element.39.row_ref.refs_0_), channel_id=1, source_target_pairs={{0,16},{2,18},{4,20},{6,22},{8,24},{10,26},{12,28},{14,30},{16,0},... | collective-permute-start | bytes 393224 | tf_op jit(solution)/shard_map/ppermute | solution.py:383
  10.5 6.6 %collective-permute-start.2 = (bf16[256,256]{1,0:T(8,128)(2,1)S(1)}, bf16[256,256]{1,0:T(8,128)(2,1)S(1)}, u32[]{:S(2)}, u32[]{:S(2)}) collective-permute-start(bf16[256,256]{1,0:T(8,128)(2,1)S(1)} %get-tuple-element.42), channel_id=1, source_target_pairs={{0,8},{2,10},{4,12},{6,14},{8,0},{10,2},{12,4},{14,6},{16,24},{18,... | collective-permute-start | bytes 393224 | tf_op jit(solution)/shard_map/ppermute | solution.py:383
  11.3 3.9 %collective-permute-start.5 = (bf16[32,256]{1,0:T(8,128)(2,1)S(1)}, bf16[32,256]{1,0:T(8,128)(2,1)S(1)}, u32[]{:S(2)}, u32[]{:S(2)}) collective-permute-start(bf16[32,256]{1,0:T(8,128)(2,1)S(1)} %get-tuple-element.44), channel_id=1, source_target_pairs={{0,4},{2,6},{4,0},{6,2},{8,12},{10,14},{12,8},{14,10},{16,20},{18,... | collective-permute-start | bytes 49160 | tf_op jit(solution)/shard_map/ppermute | solution.py:383
  17.6 6.7 %collective-permute-start.8 = (bf16[384,256]{1,0:T(8,128)(2,1)S(1)}, bf16[384,256]{1,0:T(8,128)(2,1)S(1)}, u32[]{:S(2)}, u32[]{:S(2)}) collective-permute-start(bf16[384,256]{1,0:T(8,128)(2,1)S(1)} %get-tuple-element.46.row_ref.refs_0_), channel_id=1, source_target_pairs={{0,6},{2,4},{4,2},{6,0},{8,14},{10,12},{12,10},{14,8},{16,22},{18,... | collective-permute-start | bytes 589832 | tf_op jit(solution)/shard_map/ppermute | solution.py:383
  19.2 7.2 %collective-permute-start.7 = (bf16[384,256]{1,0:T(8,128)(2,1)S(1)}, bf16[384,256]{1,0:T(8,128)(2,1)S(1)}, u32[]{:S(2)}, u32[]{:S(2)}) collective-permute-start(bf16[384,256]{1,0:T(8,128)(2,1)S(1)} %get-tuple-element.46.row_ref.refs_0_), channel_id=1, source_target_pairs={{0,4},{2,6},{4,0},{6,2},{8,12},{10,14},{12,8},{14,10},{16,20},{18,... | collective-permute-start | bytes 589832 | tf_op jit(solution)/shard_map/ppermute | solution.py:383
  19.7 6.8 %collective-permute-start.6 = (bf16[384,256]{1,0:T(8,128)(2,1)S(1)}, bf16[384,256]{1,0:T(8,128)(2,1)S(1)}, u32[]{:S(2)}, u32[]{:S(2)}) collective-permute-start(bf16[384,256]{1,0:T(8,128)(2,1)S(1)} %get-tuple-element.46.row_ref.refs_0_), channel_id=1, source_target_pairs={{0,2},{2,0},{4,6},{6,4},{8,10},{10,8},{12,14},{14,12},{16,18},{18,... | collective-permute-start | bytes 589832 | tf_op jit(solution)/shard_map/ppermute | solution.py:383
  26.4 14.4 %copy-start.1 = (bf16[2,256,1024]{2,1,0:T(8,128)(2,1)S(1)}, bf16[2,256,1024]{2,1,0:T(8,128)(2,1)}, u32[]{:S(2)}) copy-start(bf16[2,256,1024]{2,1,0:T(8,128)(2,1)} %refs_8_.3) | copy-start | bytes 3145732
  26.4 14.4 %copy-start.2 = (bf16[2,1024,256]{2,1,0:T(8,128)(2,1)S(1)}, bf16[2,1024,256]{2,1,0:T(8,128)(2,1)}, u32[]{:S(2)}) copy-start(bf16[2,1024,256]{2,1,0:T(8,128)(2,1)} %refs_9_.1) | copy-start | bytes 3145732
  26.4 14.4 %copy-start.3 = (bf16[2,256,256]{2,1,0:T(8,128)(2,1)S(1)}, bf16[2,256,256]{2,1,0:T(8,128)(2,1)}, u32[]{:S(2)}) copy-start(bf16[2,256,256]{2,1,0:T(8,128)(2,1)} %refs_7_.3) | copy-start | bytes 786436
  26.4 14.4 %copy-start.5 = (f32[256,256]{1,0:T(8,128)S(1)}, f32[256,256]{1,0:T(8,128)}, u32[]{:S(2)}) copy-start(f32[256,256]{1,0:T(8,128)} %refs_4_.4) | copy-start | bytes 786436
  31.5 9.4 %copy-start.7 = (f32[2,2,256]{2,1,0:T(2,128)S(1)}, f32[2,2,256]{2,1,0:T(2,128)}, u32[]{:S(2)}) copy-start(f32[2,2,256]{2,1,0:T(2,128)} %refs_6_.3) | copy-start | bytes 12292
  31.5 4.5 %collective-permute-start.9 = (bf16[112,256]{1,0:T(8,128)(2,1)S(1)}, bf16[112,256]{1,0:T(8,128)(2,1)S(1)}, u32[]{:S(2)}, u32[]{:S(2)}) collective-permute-start(bf16[112,256]{1,0:T(8,128)(2,1)S(1)} %get-tuple-element.53), channel_id=1, source_target_pairs={{0,8},{2,10},{4,12},{6,14},{8,0},{10,2},{12,4},{14,6},{16,24},{18,... | collective-permute-start | bytes 172040 | tf_op jit(solution)/shard_map/ppermute | solution.py:383
  33.0 5.7 %collective-permute-start.10 = (bf16[112,256]{1,0:T(8,128)(2,1)S(1)}, bf16[112,256]{1,0:T(8,128)(2,1)S(1)}, u32[]{:S(2)}, u32[]{:S(2)}) collective-permute-start(bf16[112,256]{1,0:T(8,128)(2,1)S(1)} %get-tuple-element.54), channel_id=1, source_target_pairs={{0,16},{2,18},{4,20},{6,22},{8,24},{10,26},{12,28},{14,30},{16,0},... | collective-permute-start | bytes 172040 | tf_op jit(solution)/shard_map/ppermute | solution.py:383
  34.9 6.0 %collective-permute-start.11 = (bf16[112,256]{1,0:T(8,128)(2,1)S(1)}, bf16[112,256]{1,0:T(8,128)(2,1)S(1)}, u32[]{:S(2)}, u32[]{:S(2)}) collective-permute-start(bf16[112,256]{1,0:T(8,128)(2,1)S(1)} %get-tuple-element.55), channel_id=1, source_target_pairs={{0,24},{2,26},{4,28},{6,30},{8,16},{10,18},{12,20},{14,22},{16,8},... | collective-permute-start | bytes 172040 | tf_op jit(solution)/shard_map/ppermute | solution.py:383
  42.5 4.5 %collective-permute-start.12 = (bf16[96,256]{1,0:T(8,128)(2,1)S(1)}, bf16[96,256]{1,0:T(8,128)(2,1)S(1)}, u32[]{:S(2)}, u32[]{:S(2)}) collective-permute-start(bf16[96,256]{1,0:T(8,128)(2,1)S(1)} %get-tuple-element.57), channel_id=1, source_target_pairs={{0,8},{2,10},{4,12},{6,14},{8,0},{10,2},{12,4},{14,6},{16,24},{18,... | collective-permute-start | bytes 147464 | tf_op jit(solution)/shard_map/ppermute | solution.py:383
  42.6 5.1 %collective-permute-start.13 = (bf16[96,256]{1,0:T(8,128)(2,1)S(1)}, bf16[96,256]{1,0:T(8,128)(2,1)S(1)}, u32[]{:S(2)}, u32[]{:S(2)}) collective-permute-start(bf16[96,256]{1,0:T(8,128)(2,1)S(1)} %get-tuple-element.58), channel_id=1, source_target_pairs={{0,16},{2,18},{4,20},{6,22},{8,24},{10,26},{12,28},{14,30},{16,0},... | collective-permute-start | bytes 147464 | tf_op jit(solution)/shard_map/ppermute | solution.py:383
  44.3 5.9 %collective-permute-start.14 = (bf16[96,256]{1,0:T(8,128)(2,1)S(1)}, bf16[96,256]{1,0:T(8,128)(2,1)S(1)}, u32[]{:S(2)}, u32[]{:S(2)}) collective-permute-start(bf16[96,256]{1,0:T(8,128)(2,1)S(1)} %get-tuple-element.59), channel_id=1, source_target_pairs={{0,24},{2,26},{4,28},{6,30},{8,16},{10,18},{12,20},{14,22},{16,8},... | collective-permute-start | bytes 147464 | tf_op jit(solution)/shard_map/ppermute | solution.py:383
  50.2 6.7 %collective-permute-start.17 = (bf16[384,256]{1,0:T(8,128)(2,1)S(1)}, bf16[384,256]{1,0:T(8,128)(2,1)S(1)}, u32[]{:S(2)}, u32[]{:S(2)}) collective-permute-start(bf16[384,256]{1,0:T(8,128)(2,1)S(1)} %shard_map.80.row_ref.refs_0_), channel_id=1, source_target_pairs={{0,6},{2,4},{4,2},{6,0},{8,14},{10,12},{12,10},{14,8},{16,22},{18,... | collective-permute-start | bytes 589832 | tf_op jit(solution)/shard_map/ppermute | solution.py:383
  51.7 7.3 %collective-permute-start.16 = (bf16[384,256]{1,0:T(8,128)(2,1)S(1)}, bf16[384,256]{1,0:T(8,128)(2,1)S(1)}, u32[]{:S(2)}, u32[]{:S(2)}) collective-permute-start(bf16[384,256]{1,0:T(8,128)(2,1)S(1)} %shard_map.80.row_ref.refs_0_), channel_id=1, source_target_pairs={{0,4},{2,6},{4,0},{6,2},{8,12},{10,14},{12,8},{14,10},{16,20},{18,... | collective-permute-start | bytes 589832 | tf_op jit(solution)/shard_map/ppermute | solution.py:383
  52.2 6.7 %collective-permute-start.15 = (bf16[384,256]{1,0:T(8,128)(2,1)S(1)}, bf16[384,256]{1,0:T(8,128)(2,1)S(1)}, u32[]{:S(2)}, u32[]{:S(2)}) collective-permute-start(bf16[384,256]{1,0:T(8,128)(2,1)S(1)} %shard_map.80.row_ref.refs_0_), channel_id=1, source_target_pairs={{0,2},{2,0},{4,6},{6,4},{8,10},{10,8},{12,14},{14,12},{16,18},{18,... | collective-permute-start | bytes 589832 | tf_op jit(solution)/shard_map/ppermute | solution.py:383
  64.1 4.9 %collective-permute-start.18 = (bf16[96,256]{1,0:T(8,128)(2,1)S(1)}, bf16[96,256]{1,0:T(8,128)(2,1)S(1)}, u32[]{:S(2)}, u32[]{:S(2)}) collective-permute-start(bf16[96,256]{1,0:T(8,128)(2,1)S(1)} %get-tuple-element.65), channel_id=1, source_target_pairs={{0,8},{2,10},{4,12},{6,14},{8,0},{10,2},{12,4},{14,6},{16,24},{18,... | collective-permute-start | bytes 147464 | tf_op jit(solution)/shard_map/ppermute | solution.py:383
  64.1 5.3 %collective-permute-start.19 = (bf16[96,256]{1,0:T(8,128)(2,1)S(1)}, bf16[96,256]{1,0:T(8,128)(2,1)S(1)}, u32[]{:S(2)}, u32[]{:S(2)}) collective-permute-start(bf16[96,256]{1,0:T(8,128)(2,1)S(1)} %get-tuple-element.66), channel_id=1, source_target_pairs={{0,16},{2,18},{4,20},{6,22},{8,24},{10,26},{12,28},{14,30},{16,0},... | collective-permute-start | bytes 147464 | tf_op jit(solution)/shard_map/ppermute | solution.py:383
  67.4 5.9 %collective-permute-start.20 = (bf16[96,256]{1,0:T(8,128)(2,1)S(1)}, bf16[96,256]{1,0:T(8,128)(2,1)S(1)}, u32[]{:S(2)}, u32[]{:S(2)}) collective-permute-start(bf16[96,256]{1,0:T(8,128)(2,1)S(1)} %get-tuple-element.67), channel_id=1, source_target_pairs={{0,24},{2,26},{4,28},{6,30},{8,16},{10,18},{12,20},{14,22},{16,8},... | collective-permute-start | bytes 147464 | tf_op jit(solution)/shard_map/ppermute | solution.py:383

commit v7 on v6

--- a/solution.py
+++ b/solution.py
@@ -147,8 +147,12 @@
     packed_ref[...] = out.astype(BF16)
 
 
+def far_first(pieces):
+    return list(pieces[:1]) + list(pieces[:0:-1])
+
+
 def lay_body(plan, *refs):
-    piece_refs, laid_ref = refs[:-1], refs[-1]
+    piece_refs, laid_ref = far_first(refs[:-1]), refs[-1]
     for j in range(plan.lines):
         laid_ref[j * plan.cap : (j + 1) * plan.cap] = piece_refs[j][...]
 
@@ -339,7 +343,7 @@
 
 def store_body(plan, b, last, *refs):
     lines, cap, rows = plan.lines, plan.cap, plan.rows
-    piece_refs, refs = refs[:lines], refs[lines:]
+    piece_refs, refs = far_first(refs[:lines]), refs[lines:]
     note_refs = piece_refs
     if b:
         where_ref, refs = refs[0], refs[1:]
@@ -475,13 +479,13 @@
             outs += [struct((cap, width), BF16)] * lines
         stored = kernel_call(
             functools.partial(store_body, plan, b, last), outs, [whole()] * (lines + len(told) + 5)
-        )(*pieces, *told, state, norm_gains, proj_weight, fc1_weight, fc2_weight)
+        )(*far_first(pieces), *told, state, norm_gains, proj_weight, fc1_weight, fc2_weight)
         state = stored[0]
         if not last:
             arrived = along_line(stored[1:])
             (packed,) = kernel_call(
                 functools.partial(lay_body, plan), [struct((held, width), BF16)], [whole()] * lines
-            )(*arrived)
+            )(*far_first(arrived))
     return state
 
 

time: 75.2 us -> 72.2 us (0.960)
  waiting for transfers between devices: 21.7 us -> 18.1 us
    ppermute x21, waiting for transfers between devices: 21.7 us -> 18.1 us  [move(): return lax.ppermute(block, ('pts', 'slab'), pairs)]
where the time goes in v7:
time: 72.2 us; the launch traced here: 71.5 us
  starting transfers between devices  30.2 us (42%)
  Pallas kernels  20.5 us (28%)
  waiting for transfers between devices  18.1 us (25%)
  local copies, waits for them, and re-layouts  2.43 us (3%)
    ppermute x21, starting transfers between devices, move(): return lax.ppermute(block, ('pts', 'slab'), pairs)  30.2 us
    ppermute x21, waiting for transfers between devices, move(): return lax.ppermute(block, ('pts', 'slab'), pairs)  18.1 us
    pallas_call x2, Pallas kernels, by_lines(): kernel_call(functools.partial(attend_body, plan, b, b == 0), [struct((tal...  10.2 us
    pallas_call x2, Pallas kernels, by_lines(): kernel_call(functools.partial(early_body, plan, b), [struct((held + 2 * T...  5.39 us
    pallas_call x2, Pallas kernels, by_lines(): kernel_call(functools.partial(store_body, plan, b, last), outs, [whole()]...  3.36 us
    unnamed x18, local copies, waits for them, and re-layouts  2.34 us
  transfers between devices with their start and end apart: 21, of which 13 were waited for; matrix products, arithmetic and copies ran while one was open for 0% of the time, Pallas kernels for 8%

profile of v7, /device:TPU:0, one launch (start us, length us, event | category | flops | bytes accessed | tf_op | source)
XLA Modules:
  0.0 71.5 jit_solution(14787159342157698516)
XLA Ops:
  0.0 0.8 %collective-permute-start = (s32[2,256]{1,0:T(2,128)}, s32[2,256]{1,0:T(2,128)S(1)}, u32[]{:S(2)}, u32[]{:S(2)}) collective-permute-start(s32[2,256]{1,0:T(2,128)} %order_ref.1), channel_id=1, source_target_pairs={{1,1},{3,9},{5,17},{7,25},{9,3},{11,11},{13,19},{15,27},{17,5},{19... | collective-permute-start | bytes 6152 | tf_op jit(solution)/shard_map/ppermute | solution.py:387
  0.8 0.0 copy-start.4
  0.8 0.9 %copy-done.4 = f32[256,256]{1,0:T(8,128)S(1)} copy-done((f32[256,256]{1,0:T(8,128)S(1)}, f32[256,256]{1,0:T(8,128)}, u32[]{:S(2)}) %copy-start.4) | copy-done | bytes 262168
  1.8 0.7 copy-done.6
  2.5 0.7 copy-done.8
  3.1 0.2 shard_map.73
  3.3 0.1 stack.23
  3.4 0.0 collective-permute-done.turned_ref
  3.4 0.4 shard_map.74
  3.9 3.0 %collective-permute-start.1 = (bf16[64,256]{1,0:T(8,128)(2,1)S(1)}, bf16[64,256]{1,0:T(8,128)(2,1)S(1)}, u32[]{:S(2)}, u32[]{:S(2)}) collective-permute-start(bf16[64,256]{1,0:T(8,128)(2,1)S(1)} %get-tuple-element.41), channel_id=1, source_target_pairs={{0,2},{2,0},{4,6},{6,4},{8,10},{10,8},{12,14},{14,12},{16,18},{18,... | collective-permute-start | bytes 98312 | tf_op jit(solution)/shard_map/ppermute | solution.py:387
  6.9 3.6 %collective-permute-start.4 = (bf16[256,256]{1,0:T(8,128)(2,1)S(1)}, bf16[256,256]{1,0:T(8,128)(2,1)S(1)}, u32[]{:S(2)}, u32[]{:S(2)}) collective-permute-start(bf16[256,256]{1,0:T(8,128)(2,1)S(1)} %get-tuple-element.39.row_ref.refs_0_), channel_id=1, source_target_pairs={{0,24},{2,26},{4,28},{6,30},{8,16},{10,18},{12,20},{14,22},{16,8},... | collective-permute-start | bytes 393224 | tf_op jit(solution)/shard_map/ppermute | solution.py:387
  10.5 0.0 collective-permute-start.3
  10.5 0.0 collective-permute-done.1.got_ref
  10.5 0.8 %collective-permute-start.2 = (bf16[256,256]{1,0:T(8,128)(2,1)S(1)}, bf16[256,256]{1,0:T(8,128)(2,1)S(1)}, u32[]{:S(2)}, u32[]{:S(2)}) collective-permute-start(bf16[256,256]{1,0:T(8,128)(2,1)S(1)} %get-tuple-element.42), channel_id=1, source_target_pairs={{0,8},{2,10},{4,12},{6,14},{8,0},{10,2},{12,4},{14,6},{16,24},{18,... | collective-permute-start | bytes 393224 | tf_op jit(solution)/shard_map/ppermute | solution.py:387
  11.3 1.5 %collective-permute-start.5 = (bf16[32,256]{1,0:T(8,128)(2,1)S(1)}, bf16[32,256]{1,0:T(8,128)(2,1)S(1)}, u32[]{:S(2)}, u32[]{:S(2)}) collective-permute-start(bf16[32,256]{1,0:T(8,128)(2,1)S(1)} %get-tuple-element.44), channel_id=1, source_target_pairs={{0,4},{2,6},{4,0},{6,2},{8,12},{10,14},{12,8},{14,10},{16,20},{18,... | collective-permute-start | bytes 49160 | tf_op jit(solution)/shard_map/ppermute | solution.py:387
  12.9 2.4 %collective-permute-done.5.refs_5_ = bf16[32,256]{1,0:T(8,128)(2,1)S(1)} collective-permute-done((bf16[32,256]{1,0:T(8,128)(2,1)S(1)}, bf16[32,256]{1,0:T(8,128)(2,1)S(1)}, u32[]{:S(2)}, u32[]{:S(2)}) %collective-permute-start.5) | collective-permute-done | bytes 16416 | tf_op jit(solution)/shard_map/ppermute | solution.py:387
  15.2 0.0 collective-permute-done.4.refs_3_
  15.3 1.8 %collective-permute-done.3.refs_2_ = bf16[256,256]{1,0:T(8,128)(2,1)S(1)} collective-permute-done((bf16[256,256]{1,0:T(8,128)(2,1)S(1)}, bf16[256,256]{1,0:T(8,128)(2,1)S(1)}, u32[]{:S(2)}, u32[]{:S(2)}) %collective-permute-start.3) | collective-permute-done | bytes 131104 | tf_op jit(solution)/shard_map/ppermute | solution.py:387
  17.0 0.0 collective-permute-done.2.refs_1_
  17.1 0.5 shard_map.76
  17.6 1.6 %collective-permute-start.8 = (bf16[384,256]{1,0:T(8,128)(2,1)S(1)}, bf16[384,256]{1,0:T(8,128)(2,1)S(1)}, u32[]{:S(2)}, u32[]{:S(2)}) collective-permute-start(bf16[384,256]{1,0:T(8,128)(2,1)S(1)} %get-tuple-element.46.row_ref.refs_0_), channel_id=1, source_target_pairs={{0,6},{2,4},{4,2},{6,0},{8,14},{10,12},{12,10},{14,8},{16,22},{18,... | collective-permute-start | bytes 589832 | tf_op jit(solution)/shard_map/ppermute | solution.py:387
  19.2 0.5 collective-permute-start.7
  19.7 1.5 %collective-permute-start.6 = (bf16[384,256]{1,0:T(8,128)(2,1)S(1)}, bf16[384,256]{1,0:T(8,128)(2,1)S(1)}, u32[]{:S(2)}, u32[]{:S(2)}) collective-permute-start(bf16[384,256]{1,0:T(8,128)(2,1)S(1)} %get-tuple-element.46.row_ref.refs_0_), channel_id=1, source_target_pairs={{0,2},{2,0},{4,6},{6,4},{8,10},{10,8},{12,14},{14,12},{16,18},{18,... | collective-permute-start | bytes 589832 | tf_op jit(solution)/shard_map/ppermute | solution.py:387
  21.2 0.0 copy-done
  21.2 2.6 %shard_map.77 = (bf16[448,256]{1,0:T(8,128)(2,1)S(1)}, f32[384,256]{1,0:T(8,128)S(1)}, f32[384,256]{1,0:T(8,128)S(1)}, f32[384,256]{1,0:T(8,128)S(1)}) custom-call(s32[16,128]{1,0:T(8,128)S(1)} %get-tuple-element.45.count_ref, bf16[384,256]{1,0:T(8,128)(2,1)S(1)} %get-tuple-element.46.row_ref.refs_0_, bf16[2,256,768]{2,1,0:T(8,128)(2,1)S(1)} %copy-done), custom_call_target="tpu_custom_call" | custom-call | tf_op jit(solution)/shard_map/pallas_call | solution.py:443
  23.7 0.6 collective-permute-done.8.refs_3_
  24.3 2.0 %collective-permute-done.7.refs_2_ = bf16[384,256]{1,0:T(8,128)(2,1)S(1)} collective-permute-done((bf16[384,256]{1,0:T(8,128)(2,1)S(1)}, bf16[384,256]{1,0:T(8,128)(2,1)S(1)}, u32[]{:S(2)}, u32[]{:S(2)}) %collective-permute-start.7) | collective-permute-done | bytes 196640 | tf_op jit(solution)/shard_map/ppermute | solution.py:387
  26.3 0.1 collective-permute-done.6.refs_1_
  26.5 5.0 %shard_map.78 = (bf16[112,256]{1,0:T(8,128)(2,1)S(1)}, bf16[112,256]{1,0:T(8,128)(2,1)S(1)}, bf16[112,256]{1,0:T(8,128)(2,1)S(1)}, bf16[112,256]{1,0:T(8,128)(2,1)S(1)}) custom-call(s32[16,128]{1,0:T(8,128)S(1)} %get-tuple-element.45.count_ref, bf16[384,256]{1,0:T(8,128)(2,1)S(1)} %get-tuple-element.46.row_ref.refs_0_, ...), custom_call_target="tpu_custom_call" | custom-call | tf_op jit(solution)/shard_map/pallas_call | solution.py:455
  31.5 0.0 copy-start.7
  31.5 2.8 %collective-permute-start.9 = (bf16[112,256]{1,0:T(8,128)(2,1)S(1)}, bf16[112,256]{1,0:T(8,128)(2,1)S(1)}, u32[]{:S(2)}, u32[]{:S(2)}) collective-permute-start(bf16[112,256]{1,0:T(8,128)(2,1)S(1)} %get-tuple-element.53), channel_id=1, source_target_pairs={{0,24},{2,26},{4,28},{6,30},{8,16},{10,18},{12,20},{14,22},{16,8},... | collective-permute-start | bytes 172040 | tf_op jit(solution)/shard_map/ppermute | solution.py:387
  34.3 0.1 collective-permute-start.10
  34.4 1.5 %collective-permute-start.11 = (bf16[112,256]{1,0:T(8,128)(2,1)S(1)}, bf16[112,256]{1,0:T(8,128)(2,1)S(1)}, u32[]{:S(2)}, u32[]{:S(2)}) collective-permute-start(bf16[112,256]{1,0:T(8,128)(2,1)S(1)} %get-tuple-element.55), channel_id=1, source_target_pairs={{0,8},{2,10},{4,12},{6,14},{8,0},{10,2},{12,4},{14,6},{16,24},{18,... | collective-permute-start | bytes 172040 | tf_op jit(solution)/shard_map/ppermute | solution.py:387
  36.0 1.6 %collective-permute-done.9.refs_1_.refs_3_ = bf16[112,256]{1,0:T(8,128)(2,1)S(1)} collective-permute-done((bf16[112,256]{1,0:T(8,128)(2,1)S(1)}, bf16[112,256]{1,0:T(8,128)(2,1)S(1)}, u32[]{:S(2)}, u32[]{:S(2)}) %collective-permute-start.9) | collective-permute-done | bytes 57376 | tf_op jit(solution)/shard_map/ppermute | solution.py:387
  37.5 1.8 %collective-permute-done.10.refs_2_ = bf16[112,256]{1,0:T(8,128)(2,1)S(1)} collective-permute-done((bf16[112,256]{1,0:T(8,128)(2,1)S(1)}, bf16[112,256]{1,0:T(8,128)(2,1)S(1)}, u32[]{:S(2)}, u32[]{:S(2)}) %collective-permute-start.10) | collective-permute-done | bytes 57376 | tf_op jit(solution)/shard_map/ppermute | solution.py:387
  39.4 0.0 collective-permute-done.11.refs_3_.refs_1_
  39.4 0.0 copy-done.1
  39.4 0.0 copy-done.2
  39.4 0.0 copy-done.3
  39.4 0.0 copy-done.5
  39.4 0.0 copy-done.7
  39.4 1.6 %shard_map.79 = (f32[256,256]{1,0:T(8,128)S(1)}, bf16[96,256]{1,0:T(8,128)(2,1)S(1)}, bf16[96,256]{1,0:T(8,128)(2,1)S(1)}, bf16[96,256]{1,0:T(8,128)(2,1)S(1)}, bf16[96,256]{1,0:T(8,128)(2,1)S(1)}) custom-call(bf16[112,256]{1,0:T(8,128)(2,1)S(1)} %get-tuple-element.52.refs_0_, bf16[112,256]{1,0:T(8,128)(2,1)S(1)} %collective-permute-done.9.refs_1_.refs_3_, ...), custom_call_target="tpu_custom_call" | custom-call | tf_op jit(solution)/shard_map/pallas_call | solution.py:480
  41.0 2.2 %collective-permute-start.12 = (bf16[96,256]{1,0:T(8,128)(2,1)S(1)}, bf16[96,256]{1,0:T(8,128)(2,1)S(1)}, u32[]{:S(2)}, u32[]{:S(2)}) collective-permute-start(bf16[96,256]{1,0:T(8,128)(2,1)S(1)} %get-tuple-element.57), channel_id=1, source_target_pairs={{0,24},{2,26},{4,28},{6,30},{8,16},{10,18},{12,20},{14,22},{16,8},... | collective-permute-start | bytes 147464 | tf_op jit(solution)/shard_map/ppermute | solution.py:387
  43.2 0.1 collective-permute-start.13
  43.3 2.2 %collective-permute-start.14 = (bf16[96,256]{1,0:T(8,128)(2,1)S(1)}, bf16[96,256]{1,0:T(8,128)(2,1)S(1)}, u32[]{:S(2)}, u32[]{:S(2)}) collective-permute-start(bf16[96,256]{1,0:T(8,128)(2,1)S(1)} %get-tuple-element.59), channel_id=1, source_target_pairs={{0,8},{2,10},{4,12},{6,14},{8,0},{10,2},{12,4},{14,6},{16,24},{18,... | collective-permute-start | bytes 147464 | tf_op jit(solution)/shard_map/ppermute | solution.py:387
  45.5 1.5 %collective-permute-done.12.refs_1_ = bf16[96,256]{1,0:T(8,128)(2,1)S(1)} collective-permute-done((bf16[96,256]{1,0:T(8,128)(2,1)S(1)}, bf16[96,256]{1,0:T(8,128)(2,1)S(1)}, u32[]{:S(2)}, u32[]{:S(2)}) %collective-permute-start.12) | collective-permute-done | bytes 49184 | tf_op jit(solution)/shard_map/ppermute | solution.py:387
  47.0 1.6 %collective-permute-done.13.refs_2_ = bf16[96,256]{1,0:T(8,128)(2,1)S(1)} collective-permute-done((bf16[96,256]{1,0:T(8,128)(2,1)S(1)}, bf16[96,256]{1,0:T(8,128)(2,1)S(1)}, u32[]{:S(2)}, u32[]{:S(2)}) %collective-permute-start.13) | collective-permute-done | bytes 49184 | tf_op jit(solution)/shard_map/ppermute | solution.py:387
  48.6 0.0 collective-permute-done.14.refs_3_
  48.7 1.4 %collective-permute-start.17 = (bf16[384,256]{1,0:T(8,128)(2,1)S(1)}, bf16[384,256]{1,0:T(8,128)(2,1)S(1)}, u32[]{:S(2)}, u32[]{:S(2)}) collective-permute-start(bf16[384,256]{1,0:T(8,128)(2,1)S(1)} %shard_map.80.row_ref.refs_0_), channel_id=1, source_target_pairs={{0,6},{2,4},{4,2},{6,0},{8,14},{10,12},{12,10},{14,8},{16,22},{18,... | collective-permute-start | bytes 589832 | tf_op jit(solution)/shard_map/ppermute | solution.py:387
  50.1 0.7 collective-permute-start.16
  50.7 1.5 %collective-permute-start.15 = (bf16[384,256]{1,0:T(8,128)(2,1)S(1)}, bf16[384,256]{1,0:T(8,128)(2,1)S(1)}, u32[]{:S(2)}, u32[]{:S(2)}) collective-permute-start(bf16[384,256]{1,0:T(8,128)(2,1)S(1)} %shard_map.80.row_ref.refs_0_), channel_id=1, source_target_pairs={{0,2},{2,0},{4,6},{6,4},{8,10},{10,8},{12,14},{14,12},{16,18},{18,... | collective-permute-start | bytes 589832 | tf_op jit(solution)/shard_map/ppermute | solution.py:387
  52.2 2.8 %shard_map.81 = (bf16[448,256]{1,0:T(8,128)(2,1)S(1)}, f32[384,256]{1,0:T(8,128)S(1)}, f32[384,256]{1,0:T(8,128)S(1)}, f32[384,256]{1,0:T(8,128)S(1)}) custom-call(s32[16,128]{1,0:T(8,128)S(1)} %get-tuple-element.45.count_ref, bf16[384,256]{1,0:T(8,128)(2,1)S(1)} %shard_map.80.row_ref.refs_0_, bf16[2,256,768]{2,1,0:T(8,128)(2,1)S(1)} %copy-done), custom_call_target="tpu_custom_call" | custom-call | tf_op jit(solution)/shard_map/pallas_call | solution.py:443
  55.1 0.3 collective-permute-done.17.refs_3_
  55.4 2.0 %collective-permute-done.16.refs_2_ = bf16[384,256]{1,0:T(8,128)(2,1)S(1)} collective-permute-done((bf16[384,256]{1,0:T(8,128)(2,1)S(1)}, bf16[384,256]{1,0:T(8,128)(2,1)S(1)}, u32[]{:S(2)}, u32[]{:S(2)}) %collective-permute-start.16) | collective-permute-done | bytes 196640 | tf_op jit(solution)/shard_map/ppermute | solution.py:387
  57.4 0.0 collective-permute-done.15.refs_1_
  57.4 5.1 %shard_map.82 = (bf16[96,256]{1,0:T(8,128)(2,1)S(1)}, bf16[96,256]{1,0:T(8,128)(2,1)S(1)}, bf16[96,256]{1,0:T(8,128)(2,1)S(1)}, bf16[96,256]{1,0:T(8,128)(2,1)S(1)}) custom-call(s32[16,128]{1,0:T(8,128)S(1)} %get-tuple-element.45.count_ref, bf16[384,256]{1,0:T(8,128)(2,1)S(1)} %shard_map.80.row_ref.refs_0_, ...), custom_call_target="tpu_custom_call" | custom-call | tf_op jit(solution)/shard_map/pallas_call | solution.py:455
  62.6 2.1 %collective-permute-start.18 = (bf16[96,256]{1,0:T(8,128)(2,1)S(1)}, bf16[96,256]{1,0:T(8,128)(2,1)S(1)}, u32[]{:S(2)}, u32[]{:S(2)}) collective-permute-start(bf16[96,256]{1,0:T(8,128)(2,1)S(1)} %get-tuple-element.65), channel_id=1, source_target_pairs={{0,24},{2,26},{4,28},{6,30},{8,16},{10,18},{12,20},{14,22},{16,8},... | collective-permute-start | bytes 147464 | tf_op jit(solution)/shard_map/ppermute | solution.py:387
  64.6 0.4 collective-permute-start.19
  65.0 2.0 %collective-permute-start.20 = (bf16[96,256]{1,0:T(8,128)(2,1)S(1)}, bf16[96,256]{1,0:T(8,128)(2,1)S(1)}, u32[]{:S(2)}, u32[]{:S(2)}) collective-permute-start(bf16[96,256]{1,0:T(8,128)(2,1)S(1)} %get-tuple-element.67), channel_id=1, source_target_pairs={{0,8},{2,10},{4,12},{6,14},{8,0},{10,2},{12,4},{14,6},{16,24},{18,... | collective-permute-start | bytes 147464 | tf_op jit(solution)/shard_map/ppermute | solution.py:387
  67.0 0.4 shard_map.83.refs_4_
  67.4 1.1 %collective-permute-done.18.refs_1_ = bf16[96,256]{1,0:T(8,128)(2,1)S(1)} collective-permute-done((bf16[96,256]{1,0:T(8,128)(2,1)S(1)}, bf16[96,256]{1,0:T(8,128)(2,1)S(1)}, u32[]{:S(2)}, u32[]{:S(2)}) %collective-permute-start.18) | collective-permute-done | bytes 49184 | tf_op jit(solution)/shard_map/ppermute | solution.py:387
  68.5 1.2 %collective-permute-done.19.refs_2_ = bf16[96,256]{1,0:T(8,128)(2,1)S(1)} collective-permute-done((bf16[96,256]{1,0:T(8,128)(2,1)S(1)}, bf16[96,256]{1,0:T(8,128)(2,1)S(1)}, u32[]{:S(2)}, u32[]{:S(2)}) %collective-permute-start.19) | collective-permute-done | bytes 49184 | tf_op jit(solution)/shard_map/ppermute | solution.py:387
  69.7 0.0 collective-permute-done.20.refs_3_
  69.7 1.7 %shard_map.84 = f32[256,256]{1,0:T(8,128)} custom-call(bf16[96,256]{1,0:T(8,128)(2,1)S(1)} %get-tuple-element.64.refs_0_, bf16[96,256]{1,0:T(8,128)(2,1)S(1)} %collective-permute-done.18.refs_1_, bf16[96,256]{1,0:T(8,128)(2,1)S(1)} %collective-permute-done.19.refs_2_, bf16[96,256]{1,0:T(8,128)(2,1)S(1)} %collective-permute-done.20.refs_3_, ...), custom_call_target="tpu_custom_call" | custom-call | tf_op jit(solution)/shard_map/pallas_call | solution.py:480
  (9 shorter events, 0.0 us)
Async XLA Ops:
  0.0 21.2 %copy-start = (bf16[2,256,768]{2,1,0:T(8,128)(2,1)S(1)}, bf16[2,256,768]{2,1,0:T(8,128)(2,1)}, u32[]{:S(2)}) copy-start(bf16[2,256,768]{2,1,0:T(8,128)(2,1)} %refs_4_.5) | copy-start | bytes 2359300
  0.0 3.4 %collective-permute-start = (s32[2,256]{1,0:T(2,128)}, s32[2,256]{1,0:T(2,128)S(1)}, u32[]{:S(2)}, u32[]{:S(2)}) collective-permute-start(s32[2,256]{1,0:T(2,128)} %order_ref.1), channel_id=1, source_target_pairs={{1,1},{3,9},{5,17},{7,25},{9,3},{11,11},{13,19},{15,27},{17,5},{19... | collective-permute-start | bytes 6152 | tf_op jit(solution)/shard_map/ppermute | solution.py:387
  0.8 1.0 %copy-start.4 = (f32[256,256]{1,0:T(8,128)S(1)}, f32[256,256]{1,0:T(8,128)}, u32[]{:S(2)}) copy-start(f32[256,256]{1,0:T(8,128)} %refs_4_.4) | copy-start | bytes 786436
  1.8 0.7 copy-start.6
  2.5 0.7 copy-start.8
  3.9 6.6 %collective-permute-start.1 = (bf16[64,256]{1,0:T(8,128)(2,1)S(1)}, bf16[64,256]{1,0:T(8,128)(2,1)S(1)}, u32[]{:S(2)}, u32[]{:S(2)}) collective-permute-start(bf16[64,256]{1,0:T(8,128)(2,1)S(1)} %get-tuple-element.41), channel_id=1, source_target_pairs={{0,2},{2,0},{4,6},{6,4},{8,10},{10,8},{12,14},{14,12},{16,18},{18,... | collective-permute-start | bytes 98312 | tf_op jit(solution)/shard_map/ppermute | solution.py:387
  6.9 8.4 %collective-permute-start.4 = (bf16[256,256]{1,0:T(8,128)(2,1)S(1)}, bf16[256,256]{1,0:T(8,128)(2,1)S(1)}, u32[]{:S(2)}, u32[]{:S(2)}) collective-permute-start(bf16[256,256]{1,0:T(8,128)(2,1)S(1)} %get-tuple-element.39.row_ref.refs_0_), channel_id=1, source_target_pairs={{0,24},{2,26},{4,28},{6,30},{8,16},{10,18},{12,20},{14,22},{16,8},... | collective-permute-start | bytes 393224 | tf_op jit(solution)/shard_map/ppermute | solution.py:387
  10.5 6.6 %collective-permute-start.3 = (bf16[256,256]{1,0:T(8,128)(2,1)S(1)}, bf16[256,256]{1,0:T(8,128)(2,1)S(1)}, u32[]{:S(2)}, u32[]{:S(2)}) collective-permute-start(bf16[256,256]{1,0:T(8,128)(2,1)S(1)} %get-tuple-element.39.row_ref.refs_0_), channel_id=1, source_target_pairs={{0,16},{2,18},{4,20},{6,22},{8,24},{10,26},{12,28},{14,30},{16,0},... | collective-permute-start | bytes 393224 | tf_op jit(solution)/shard_map/ppermute | solution.py:387
  10.5 6.6 %collective-permute-start.2 = (bf16[256,256]{1,0:T(8,128)(2,1)S(1)}, bf16[256,256]{1,0:T(8,128)(2,1)S(1)}, u32[]{:S(2)}, u32[]{:S(2)}) collective-permute-start(bf16[256,256]{1,0:T(8,128)(2,1)S(1)} %get-tuple-element.42), channel_id=1, source_target_pairs={{0,8},{2,10},{4,12},{6,14},{8,0},{10,2},{12,4},{14,6},{16,24},{18,... | collective-permute-start | bytes 393224 | tf_op jit(solution)/shard_map/ppermute | solution.py:387
  11.3 3.9 %collective-permute-start.5 = (bf16[32,256]{1,0:T(8,128)(2,1)S(1)}, bf16[32,256]{1,0:T(8,128)(2,1)S(1)}, u32[]{:S(2)}, u32[]{:S(2)}) collective-permute-start(bf16[32,256]{1,0:T(8,128)(2,1)S(1)} %get-tuple-element.44), channel_id=1, source_target_pairs={{0,4},{2,6},{4,0},{6,2},{8,12},{10,14},{12,8},{14,10},{16,20},{18,... | collective-permute-start | bytes 49160 | tf_op jit(solution)/shard_map/ppermute | solution.py:387
  17.6 6.7 %collective-permute-start.8 = (bf16[384,256]{1,0:T(8,128)(2,1)S(1)}, bf16[384,256]{1,0:T(8,128)(2,1)S(1)}, u32[]{:S(2)}, u32[]{:S(2)}) collective-permute-start(bf16[384,256]{1,0:T(8,128)(2,1)S(1)} %get-tuple-element.46.row_ref.refs_0_), channel_id=1, source_target_pairs={{0,6},{2,4},{4,2},{6,0},{8,14},{10,12},{12,10},{14,8},{16,22},{18,... | collective-permute-start | bytes 589832 | tf_op jit(solution)/shard_map/ppermute | solution.py:387
  19.2 7.2 %collective-permute-start.7 = (bf16[384,256]{1,0:T(8,128)(2,1)S(1)}, bf16[384,256]{1,0:T(8,128)(2,1)S(1)}, u32[]{:S(2)}, u32[]{:S(2)}) collective-permute-start(bf16[384,256]{1,0:T(8,128)(2,1)S(1)} %get-tuple-element.46.row_ref.refs_0_), channel_id=1, source_target_pairs={{0,4},{2,6},{4,0},{6,2},{8,12},{10,14},{12,8},{14,10},{16,20},{18,... | collective-permute-start | bytes 589832 | tf_op jit(solution)/shard_map/ppermute | solution.py:387
  19.7 6.8 %collective-permute-start.6 = (bf16[384,256]{1,0:T(8,128)(2,1)S(1)}, bf16[384,256]{1,0:T(8,128)(2,1)S(1)}, u32[]{:S(2)}, u32[]{:S(2)}) collective-permute-start(bf16[384,256]{1,0:T(8,128)(2,1)S(1)} %get-tuple-element.46.row_ref.refs_0_), channel_id=1, source_target_pairs={{0,2},{2,0},{4,6},{6,4},{8,10},{10,8},{12,14},{14,12},{16,18},{18,... | collective-permute-start | bytes 589832 | tf_op jit(solution)/shard_map/ppermute | solution.py:387
  26.4 13.0 %copy-start.1 = (bf16[2,256,1024]{2,1,0:T(8,128)(2,1)S(1)}, bf16[2,256,1024]{2,1,0:T(8,128)(2,1)}, u32[]{:S(2)}) copy-start(bf16[2,256,1024]{2,1,0:T(8,128)(2,1)} %refs_8_.3) | copy-start | bytes 3145732
  26.4 13.0 %copy-start.2 = (bf16[2,1024,256]{2,1,0:T(8,128)(2,1)S(1)}, bf16[2,1024,256]{2,1,0:T(8,128)(2,1)}, u32[]{:S(2)}) copy-start(bf16[2,1024,256]{2,1,0:T(8,128)(2,1)} %refs_9_.1) | copy-start | bytes 3145732
  26.4 13.0 %copy-start.3 = (bf16[2,256,256]{2,1,0:T(8,128)(2,1)S(1)}, bf16[2,256,256]{2,1,0:T(8,128)(2,1)}, u32[]{:S(2)}) copy-start(bf16[2,256,256]{2,1,0:T(8,128)(2,1)} %refs_7_.3) | copy-start | bytes 786436
  26.4 13.0 %copy-start.5 = (f32[256,256]{1,0:T(8,128)S(1)}, f32[256,256]{1,0:T(8,128)}, u32[]{:S(2)}) copy-start(f32[256,256]{1,0:T(8,128)} %refs_4_.4) | copy-start | bytes 786436
  31.5 7.9 %copy-start.7 = (f32[2,2,256]{2,1,0:T(2,128)S(1)}, f32[2,2,256]{2,1,0:T(2,128)}, u32[]{:S(2)}) copy-start(f32[2,2,256]{2,1,0:T(2,128)} %refs_6_.3) | copy-start | bytes 12292
  31.5 6.0 %collective-permute-start.9 = (bf16[112,256]{1,0:T(8,128)(2,1)S(1)}, bf16[112,256]{1,0:T(8,128)(2,1)S(1)}, u32[]{:S(2)}, u32[]{:S(2)}) collective-permute-start(bf16[112,256]{1,0:T(8,128)(2,1)S(1)} %get-tuple-element.53), channel_id=1, source_target_pairs={{0,24},{2,26},{4,28},{6,30},{8,16},{10,18},{12,20},{14,22},{16,8},... | collective-permute-start | bytes 172040 | tf_op jit(solution)/shard_map/ppermute | solution.py:387
  34.3 5.1 %collective-permute-start.10 = (bf16[112,256]{1,0:T(8,128)(2,1)S(1)}, bf16[112,256]{1,0:T(8,128)(2,1)S(1)}, u32[]{:S(2)}, u32[]{:S(2)}) collective-permute-start(bf16[112,256]{1,0:T(8,128)(2,1)S(1)} %get-tuple-element.54), channel_id=1, source_target_pairs={{0,16},{2,18},{4,20},{6,22},{8,24},{10,26},{12,28},{14,30},{16,0},... | collective-permute-start | bytes 172040 | tf_op jit(solution)/shard_map/ppermute | solution.py:387
  34.4 5.0 %collective-permute-start.11 = (bf16[112,256]{1,0:T(8,128)(2,1)S(1)}, bf16[112,256]{1,0:T(8,128)(2,1)S(1)}, u32[]{:S(2)}, u32[]{:S(2)}) collective-permute-start(bf16[112,256]{1,0:T(8,128)(2,1)S(1)} %get-tuple-element.55), channel_id=1, source_target_pairs={{0,8},{2,10},{4,12},{6,14},{8,0},{10,2},{12,4},{14,6},{16,24},{18,... | collective-permute-start | bytes 172040 | tf_op jit(solution)/shard_map/ppermute | solution.py:387
  41.0 6.0 %collective-permute-start.12 = (bf16[96,256]{1,0:T(8,128)(2,1)S(1)}, bf16[96,256]{1,0:T(8,128)(2,1)S(1)}, u32[]{:S(2)}, u32[]{:S(2)}) collective-permute-start(bf16[96,256]{1,0:T(8,128)(2,1)S(1)} %get-tuple-element.57), channel_id=1, source_target_pairs={{0,24},{2,26},{4,28},{6,30},{8,16},{10,18},{12,20},{14,22},{16,8},... | collective-permute-start | bytes 147464 | tf_op jit(solution)/shard_map/ppermute | solution.py:387
  43.2 5.4 %collective-permute-start.13 = (bf16[96,256]{1,0:T(8,128)(2,1)S(1)}, bf16[96,256]{1,0:T(8,128)(2,1)S(1)}, u32[]{:S(2)}, u32[]{:S(2)}) collective-permute-start(bf16[96,256]{1,0:T(8,128)(2,1)S(1)} %get-tuple-element.58), channel_id=1, source_target_pairs={{0,16},{2,18},{4,20},{6,22},{8,24},{10,26},{12,28},{14,30},{16,0},... | collective-permute-start | bytes 147464 | tf_op jit(solution)/shard_map/ppermute | solution.py:387
  43.3 5.3 %collective-permute-start.14 = (bf16[96,256]{1,0:T(8,128)(2,1)S(1)}, bf16[96,256]{1,0:T(8,128)(2,1)S(1)}, u32[]{:S(2)}, u32[]{:S(2)}) collective-permute-start(bf16[96,256]{1,0:T(8,128)(2,1)S(1)} %get-tuple-element.59), channel_id=1, source_target_pairs={{0,8},{2,10},{4,12},{6,14},{8,0},{10,2},{12,4},{14,6},{16,24},{18,... | collective-permute-start | bytes 147464 | tf_op jit(solution)/shard_map/ppermute | solution.py:387
  48.7 6.7 %collective-permute-start.17 = (bf16[384,256]{1,0:T(8,128)(2,1)S(1)}, bf16[384,256]{1,0:T(8,128)(2,1)S(1)}, u32[]{:S(2)}, u32[]{:S(2)}) collective-permute-start(bf16[384,256]{1,0:T(8,128)(2,1)S(1)} %shard_map.80.row_ref.refs_0_), channel_id=1, source_target_pairs={{0,6},{2,4},{4,2},{6,0},{8,14},{10,12},{12,10},{14,8},{16,22},{18,... | collective-permute-start | bytes 589832 | tf_op jit(solution)/shard_map/ppermute | solution.py:387
  50.1 7.4 %collective-permute-start.16 = (bf16[384,256]{1,0:T(8,128)(2,1)S(1)}, bf16[384,256]{1,0:T(8,128)(2,1)S(1)}, u32[]{:S(2)}, u32[]{:S(2)}) collective-permute-start(bf16[384,256]{1,0:T(8,128)(2,1)S(1)} %shard_map.80.row_ref.refs_0_), channel_id=1, source_target_pairs={{0,4},{2,6},{4,0},{6,2},{8,12},{10,14},{12,8},{14,10},{16,20},{18,... | collective-permute-start | bytes 589832 | tf_op jit(solution)/shard_map/ppermute | solution.py:387
  50.7 6.7 %collective-permute-start.15 = (bf16[384,256]{1,0:T(8,128)(2,1)S(1)}, bf16[384,256]{1,0:T(8,128)(2,1)S(1)}, u32[]{:S(2)}, u32[]{:S(2)}) collective-permute-start(bf16[384,256]{1,0:T(8,128)(2,1)S(1)} %shard_map.80.row_ref.refs_0_), channel_id=1, source_target_pairs={{0,2},{2,0},{4,6},{6,4},{8,10},{10,8},{12,14},{14,12},{16,18},{18,... | collective-permute-start | bytes 589832 | tf_op jit(solution)/shard_map/ppermute | solution.py:387
  62.6 6.0 %collective-permute-start.18 = (bf16[96,256]{1,0:T(8,128)(2,1)S(1)}, bf16[96,256]{1,0:T(8,128)(2,1)S(1)}, u32[]{:S(2)}, u32[]{:S(2)}) collective-permute-start(bf16[96,256]{1,0:T(8,128)(2,1)S(1)} %get-tuple-element.65), channel_id=1, source_target_pairs={{0,24},{2,26},{4,28},{6,30},{8,16},{10,18},{12,20},{14,22},{16,8},... | collective-permute-start | bytes 147464 | tf_op jit(solution)/shard_map/ppermute | solution.py:387
  64.6 5.1 %collective-permute-start.19 = (bf16[96,256]{1,0:T(8,128)(2,1)S(1)}, bf16[96,256]{1,0:T(8,128)(2,1)S(1)}, u32[]{:S(2)}, u32[]{:S(2)}) collective-permute-start(bf16[96,256]{1,0:T(8,128)(2,1)S(1)} %get-tuple-element.66), channel_id=1, source_target_pairs={{0,16},{2,18},{4,20},{6,22},{8,24},{10,26},{12,28},{14,30},{16,0},... | collective-permute-start | bytes 147464 | tf_op jit(solution)/shard_map/ppermute | solution.py:387
  65.0 4.7 %collective-permute-start.20 = (bf16[96,256]{1,0:T(8,128)(2,1)S(1)}, bf16[96,256]{1,0:T(8,128)(2,1)S(1)}, u32[]{:S(2)}, u32[]{:S(2)}) collective-permute-start(bf16[96,256]{1,0:T(8,128)(2,1)S(1)} %get-tuple-element.67), channel_id=1, source_target_pairs={{0,8},{2,10},{4,12},{6,14},{8,0},{10,2},{12,4},{14,6},{16,24},{18,... | collective-permute-start | bytes 147464 | tf_op jit(solution)/shard_map/ppermute | solution.py:387

commit v8 on v7

--- a/solution.py
+++ b/solution.py
@@ -308,12 +308,13 @@
         project_pair(plan, b, all_rows[first], weight_ref, first, keys, values)
         attention(plan, own, query_ref, keys, values, slice(0, PATCH), scores, alone)
 
+    if with_notes:
+        members = member_ref[...].astype(F32)
     for j in range(lines):
         out_refs[j][0:cap, :] = mixed[pl.ds(pl.multiple_of(offsets[j], 16), cap), :]
         if with_notes:
             entry = iota((16, 1), 0)
-            now = member_ref[j : j + 1, :].astype(F32)
-            later = member_ref[8 + j : 9 + j, :].astype(F32)
+            now, later = members[j : j + 1], members[8 + j : 9 + j]
             note = jnp.where(entry == 0, now, jnp.where(entry == 1, later, 0.0))
             out_refs[j][cap : cap + 16, :] = note.astype(BF16)
 

time: 72.2 us -> 71.7 us (level)
  no operation moved by 1% of the time
where the time goes in v8:
time: 71.7 us; the launch traced here: 71.5 us
  starting transfers between devices  30.2 us (42%)
  Pallas kernels  20.5 us (29%)
  waiting for transfers between devices  18.1 us (25%)
  local copies, waits for them, and re-layouts  2.43 us (3%)
    ppermute x21, starting transfers between devices, move(): return lax.ppermute(block, ('pts', 'slab'), pairs)  30.2 us
    ppermute x21, waiting for transfers between devices, move(): return lax.ppermute(block, ('pts', 'slab'), pairs)  18.1 us
    pallas_call x2, Pallas kernels, by_lines(): kernel_call(functools.partial(attend_body, plan, b, b == 0), [struct((tal...  10.2 us
    pallas_call x2, Pallas kernels, by_lines(): kernel_call(functools.partial(early_body, plan, b), [struct((held + 2 * T...  5.39 us
    pallas_call x2, Pallas kernels, by_lines(): kernel_call(functools.partial(store_body, plan, b, last), outs, [whole()]...  3.37 us
    unnamed x18, local copies, waits for them, and re-layouts  2.34 us
  transfers between devices with their start and end apart: 21, of which 13 were waited for; matrix products, arithmetic and copies ran while one was open for 0% of the time, Pallas kernels for 8%

profile of v8, /device:TPU:0, one launch (start us, length us, event | category | flops | bytes accessed | tf_op | source)
XLA Modules:
  0.0 71.5 jit_solution(11771923025921071672)
XLA Ops:
  0.0 0.8 %collective-permute-start = (s32[2,256]{1,0:T(2,128)}, s32[2,256]{1,0:T(2,128)S(1)}, u32[]{:S(2)}, u32[]{:S(2)}) collective-permute-start(s32[2,256]{1,0:T(2,128)} %order_ref.1), channel_id=1, source_target_pairs={{1,1},{3,9},{5,17},{7,25},{9,3},{11,11},{13,19},{15,27},{17,5},{19... | collective-permute-start | bytes 6152 | tf_op jit(solution)/shard_map/ppermute | solution.py:388
  0.8 0.0 copy-start.4
  0.8 0.9 %copy-done.4 = f32[256,256]{1,0:T(8,128)S(1)} copy-done((f32[256,256]{1,0:T(8,128)S(1)}, f32[256,256]{1,0:T(8,128)}, u32[]{:S(2)}) %copy-start.4) | copy-done | bytes 262168
  1.8 0.7 copy-done.6
  2.5 0.7 copy-done.8
  3.1 0.2 shard_map.73
  3.3 0.1 stack.23
  3.4 0.0 collective-permute-done.turned_ref
  3.4 0.4 shard_map.74
  3.9 3.0 %collective-permute-start.1 = (bf16[64,256]{1,0:T(8,128)(2,1)S(1)}, bf16[64,256]{1,0:T(8,128)(2,1)S(1)}, u32[]{:S(2)}, u32[]{:S(2)}) collective-permute-start(bf16[64,256]{1,0:T(8,128)(2,1)S(1)} %get-tuple-element.41), channel_id=1, source_target_pairs={{0,2},{2,0},{4,6},{6,4},{8,10},{10,8},{12,14},{14,12},{16,18},{18,... | collective-permute-start | bytes 98312 | tf_op jit(solution)/shard_map/ppermute | solution.py:388
  6.9 3.6 %collective-permute-start.4 = (bf16[256,256]{1,0:T(8,128)(2,1)S(1)}, bf16[256,256]{1,0:T(8,128)(2,1)S(1)}, u32[]{:S(2)}, u32[]{:S(2)}) collective-permute-start(bf16[256,256]{1,0:T(8,128)(2,1)S(1)} %get-tuple-element.39.row_ref.refs_0_), channel_id=1, source_target_pairs={{0,24},{2,26},{4,28},{6,30},{8,16},{10,18},{12,20},{14,22},{16,8},... | collective-permute-start | bytes 393224 | tf_op jit(solution)/shard_map/ppermute | solution.py:388
  10.5 0.0 collective-permute-start.3
  10.5 0.0 collective-permute-done.1.got_ref
  10.5 0.8 %collective-permute-start.2 = (bf16[256,256]{1,0:T(8,128)(2,1)S(1)}, bf16[256,256]{1,0:T(8,128)(2,1)S(1)}, u32[]{:S(2)}, u32[]{:S(2)}) collective-permute-start(bf16[256,256]{1,0:T(8,128)(2,1)S(1)} %get-tuple-element.42), channel_id=1, source_target_pairs={{0,8},{2,10},{4,12},{6,14},{8,0},{10,2},{12,4},{14,6},{16,24},{18,... | collective-permute-start | bytes 393224 | tf_op jit(solution)/shard_map/ppermute | solution.py:388
  11.3 1.5 %collective-permute-start.5 = (bf16[32,256]{1,0:T(8,128)(2,1)S(1)}, bf16[32,256]{1,0:T(8,128)(2,1)S(1)}, u32[]{:S(2)}, u32[]{:S(2)}) collective-permute-start(bf16[32,256]{1,0:T(8,128)(2,1)S(1)} %get-tuple-element.44), channel_id=1, source_target_pairs={{0,4},{2,6},{4,0},{6,2},{8,12},{10,14},{12,8},{14,10},{16,20},{18,... | collective-permute-start | bytes 49160 | tf_op jit(solution)/shard_map/ppermute | solution.py:388
  12.9 2.4 %collective-permute-done.5.refs_5_ = bf16[32,256]{1,0:T(8,128)(2,1)S(1)} collective-permute-done((bf16[32,256]{1,0:T(8,128)(2,1)S(1)}, bf16[32,256]{1,0:T(8,128)(2,1)S(1)}, u32[]{:S(2)}, u32[]{:S(2)}) %collective-permute-start.5) | collective-permute-done | bytes 16416 | tf_op jit(solution)/shard_map/ppermute | solution.py:388
  15.2 0.0 collective-permute-done.4.refs_3_
  15.3 1.8 %collective-permute-done.3.refs_2_ = bf16[256,256]{1,0:T(8,128)(2,1)S(1)} collective-permute-done((bf16[256,256]{1,0:T(8,128)(2,1)S(1)}, bf16[256,256]{1,0:T(8,128)(2,1)S(1)}, u32[]{:S(2)}, u32[]{:S(2)}) %collective-permute-start.3) | collective-permute-done | bytes 131104 | tf_op jit(solution)/shard_map/ppermute | solution.py:388
  17.0 0.0 collective-permute-done.2.refs_1_
  17.1 0.5 shard_map.76
  17.6 1.6 %collective-permute-start.8 = (bf16[384,256]{1,0:T(8,128)(2,1)S(1)}, bf16[384,256]{1,0:T(8,128)(2,1)S(1)}, u32[]{:S(2)}, u32[]{:S(2)}) collective-permute-start(bf16[384,256]{1,0:T(8,128)(2,1)S(1)} %get-tuple-element.46.row_ref.refs_0_), channel_id=1, source_target_pairs={{0,6},{2,4},{4,2},{6,0},{8,14},{10,12},{12,10},{14,8},{16,22},{18,... | collective-permute-start | bytes 589832 | tf_op jit(solution)/shard_map/ppermute | solution.py:388
  19.2 0.5 collective-permute-start.7
  19.7 1.5 %collective-permute-start.6 = (bf16[384,256]{1,0:T(8,128)(2,1)S(1)}, bf16[384,256]{1,0:T(8,128)(2,1)S(1)}, u32[]{:S(2)}, u32[]{:S(2)}) collective-permute-start(bf16[384,256]{1,0:T(8,128)(2,1)S(1)} %get-tuple-element.46.row_ref.refs_0_), channel_id=1, source_target_pairs={{0,2},{2,0},{4,6},{6,4},{8,10},{10,8},{12,14},{14,12},{16,18},{18,... | collective-permute-start | bytes 589832 | tf_op jit(solution)/shard_map/ppermute | solution.py:388
  21.2 0.0 copy-done
  21.2 2.6 %shard_map.77 = (bf16[448,256]{1,0:T(8,128)(2,1)S(1)}, f32[384,256]{1,0:T(8,128)S(1)}, f32[384,256]{1,0:T(8,128)S(1)}, f32[384,256]{1,0:T(8,128)S(1)}) custom-call(s32[16,128]{1,0:T(8,128)S(1)} %get-tuple-element.45.count_ref, bf16[384,256]{1,0:T(8,128)(2,1)S(1)} %get-tuple-element.46.row_ref.refs_0_, bf16[2,256,768]{2,1,0:T(8,128)(2,1)S(1)} %copy-done), custom_call_target="tpu_custom_call" | custom-call | tf_op jit(solution)/shard_map/pallas_call | solution.py:444
  23.7 0.6 collective-permute-done.8.refs_3_
  24.3 2.0 %collective-permute-done.7.refs_2_ = bf16[384,256]{1,0:T(8,128)(2,1)S(1)} collective-permute-done((bf16[384,256]{1,0:T(8,128)(2,1)S(1)}, bf16[384,256]{1,0:T(8,128)(2,1)S(1)}, u32[]{:S(2)}, u32[]{:S(2)}) %collective-permute-start.7) | collective-permute-done | bytes 196640 | tf_op jit(solution)/shard_map/ppermute | solution.py:388
  26.3 0.1 collective-permute-done.6.refs_1_
  26.5 5.0 %shard_map.78 = (bf16[112,256]{1,0:T(8,128)(2,1)S(1)}, bf16[112,256]{1,0:T(8,128)(2,1)S(1)}, bf16[112,256]{1,0:T(8,128)(2,1)S(1)}, bf16[112,256]{1,0:T(8,128)(2,1)S(1)}) custom-call(s32[16,128]{1,0:T(8,128)S(1)} %get-tuple-element.45.count_ref, bf16[384,256]{1,0:T(8,128)(2,1)S(1)} %get-tuple-element.46.row_ref.refs_0_, ...), custom_call_target="tpu_custom_call" | custom-call | tf_op jit(solution)/shard_map/pallas_call | solution.py:456
  31.5 0.0 copy-start.7
  31.5 2.8 %collective-permute-start.9 = (bf16[112,256]{1,0:T(8,128)(2,1)S(1)}, bf16[112,256]{1,0:T(8,128)(2,1)S(1)}, u32[]{:S(2)}, u32[]{:S(2)}) collective-permute-start(bf16[112,256]{1,0:T(8,128)(2,1)S(1)} %get-tuple-element.53), channel_id=1, source_target_pairs={{0,24},{2,26},{4,28},{6,30},{8,16},{10,18},{12,20},{14,22},{16,8},... | collective-permute-start | bytes 172040 | tf_op jit(solution)/shard_map/ppermute | solution.py:388
  34.3 0.1 collective-permute-start.10
  34.4 1.5 %collective-permute-start.11 = (bf16[112,256]{1,0:T(8,128)(2,1)S(1)}, bf16[112,256]{1,0:T(8,128)(2,1)S(1)}, u32[]{:S(2)}, u32[]{:S(2)}) collective-permute-start(bf16[112,256]{1,0:T(8,128)(2,1)S(1)} %get-tuple-element.55), channel_id=1, source_target_pairs={{0,8},{2,10},{4,12},{6,14},{8,0},{10,2},{12,4},{14,6},{16,24},{18,... | collective-permute-start | bytes 172040 | tf_op jit(solution)/shard_map/ppermute | solution.py:388
  36.0 1.6 %collective-permute-done.9.refs_1_.refs_3_ = bf16[112,256]{1,0:T(8,128)(2,1)S(1)} collective-permute-done((bf16[112,256]{1,0:T(8,128)(2,1)S(1)}, bf16[112,256]{1,0:T(8,128)(2,1)S(1)}, u32[]{:S(2)}, u32[]{:S(2)}) %collective-permute-start.9) | collective-permute-done | bytes 57376 | tf_op jit(solution)/shard_map/ppermute | solution.py:388
  37.5 1.8 %collective-permute-done.10.refs_2_ = bf16[112,256]{1,0:T(8,128)(2,1)S(1)} collective-permute-done((bf16[112,256]{1,0:T(8,128)(2,1)S(1)}, bf16[112,256]{1,0:T(8,128)(2,1)S(1)}, u32[]{:S(2)}, u32[]{:S(2)}) %collective-permute-start.10) | collective-permute-done | bytes 57376 | tf_op jit(solution)/shard_map/ppermute | solution.py:388
  39.4 0.0 collective-permute-done.11.refs_3_.refs_1_
  39.4 0.0 copy-done.1
  39.4 0.0 copy-done.2
  39.4 0.0 copy-done.3
  39.4 0.0 copy-done.5
  39.4 0.0 copy-done.7
  39.4 1.6 %shard_map.79 = (f32[256,256]{1,0:T(8,128)S(1)}, bf16[96,256]{1,0:T(8,128)(2,1)S(1)}, bf16[96,256]{1,0:T(8,128)(2,1)S(1)}, bf16[96,256]{1,0:T(8,128)(2,1)S(1)}, bf16[96,256]{1,0:T(8,128)(2,1)S(1)}) custom-call(bf16[112,256]{1,0:T(8,128)(2,1)S(1)} %get-tuple-element.52.refs_0_, bf16[112,256]{1,0:T(8,128)(2,1)S(1)} %collective-permute-done.9.refs_1_.refs_3_, ...), custom_call_target="tpu_custom_call" | custom-call | tf_op jit(solution)/shard_map/pallas_call | solution.py:481
  41.0 2.2 %collective-permute-start.12 = (bf16[96,256]{1,0:T(8,128)(2,1)S(1)}, bf16[96,256]{1,0:T(8,128)(2,1)S(1)}, u32[]{:S(2)}, u32[]{:S(2)}) collective-permute-start(bf16[96,256]{1,0:T(8,128)(2,1)S(1)} %get-tuple-element.57), channel_id=1, source_target_pairs={{0,24},{2,26},{4,28},{6,30},{8,16},{10,18},{12,20},{14,22},{16,8},... | collective-permute-start | bytes 147464 | tf_op jit(solution)/shard_map/ppermute | solution.py:388
  43.2 0.1 collective-permute-start.13
  43.3 2.2 %collective-permute-start.14 = (bf16[96,256]{1,0:T(8,128)(2,1)S(1)}, bf16[96,256]{1,0:T(8,128)(2,1)S(1)}, u32[]{:S(2)}, u32[]{:S(2)}) collective-permute-start(bf16[96,256]{1,0:T(8,128)(2,1)S(1)} %get-tuple-element.59), channel_id=1, source_target_pairs={{0,8},{2,10},{4,12},{6,14},{8,0},{10,2},{12,4},{14,6},{16,24},{18,... | collective-permute-start | bytes 147464 | tf_op jit(solution)/shard_map/ppermute | solution.py:388
  45.5 1.5 %collective-permute-done.12.refs_1_ = bf16[96,256]{1,0:T(8,128)(2,1)S(1)} collective-permute-done((bf16[96,256]{1,0:T(8,128)(2,1)S(1)}, bf16[96,256]{1,0:T(8,128)(2,1)S(1)}, u32[]{:S(2)}, u32[]{:S(2)}) %collective-permute-start.12) | collective-permute-done | bytes 49184 | tf_op jit(solution)/shard_map/ppermute | solution.py:388
  47.0 1.6 %collective-permute-done.13.refs_2_ = bf16[96,256]{1,0:T(8,128)(2,1)S(1)} collective-permute-done((bf16[96,256]{1,0:T(8,128)(2,1)S(1)}, bf16[96,256]{1,0:T(8,128)(2,1)S(1)}, u32[]{:S(2)}, u32[]{:S(2)}) %collective-permute-start.13) | collective-permute-done | bytes 49184 | tf_op jit(solution)/shard_map/ppermute | solution.py:388
  48.6 0.0 collective-permute-done.14.refs_3_
  48.7 1.4 %collective-permute-start.17 = (bf16[384,256]{1,0:T(8,128)(2,1)S(1)}, bf16[384,256]{1,0:T(8,128)(2,1)S(1)}, u32[]{:S(2)}, u32[]{:S(2)}) collective-permute-start(bf16[384,256]{1,0:T(8,128)(2,1)S(1)} %shard_map.80.row_ref.refs_0_), channel_id=1, source_target_pairs={{0,6},{2,4},{4,2},{6,0},{8,14},{10,12},{12,10},{14,8},{16,22},{18,... | collective-permute-start | bytes 589832 | tf_op jit(solution)/shard_map/ppermute | solution.py:388
  50.0 0.7 collective-permute-start.16
  50.7 1.5 %collective-permute-start.15 = (bf16[384,256]{1,0:T(8,128)(2,1)S(1)}, bf16[384,256]{1,0:T(8,128)(2,1)S(1)}, u32[]{:S(2)}, u32[]{:S(2)}) collective-permute-start(bf16[384,256]{1,0:T(8,128)(2,1)S(1)} %shard_map.80.row_ref.refs_0_), channel_id=1, source_target_pairs={{0,2},{2,0},{4,6},{6,4},{8,10},{10,8},{12,14},{14,12},{16,18},{18,... | collective-permute-start | bytes 589832 | tf_op jit(solution)/shard_map/ppermute | solution.py:388
  52.2 2.8 %shard_map.81 = (bf16[448,256]{1,0:T(8,128)(2,1)S(1)}, f32[384,256]{1,0:T(8,128)S(1)}, f32[384,256]{1,0:T(8,128)S(1)}, f32[384,256]{1,0:T(8,128)S(1)}) custom-call(s32[16,128]{1,0:T(8,128)S(1)} %get-tuple-element.45.count_ref, bf16[384,256]{1,0:T(8,128)(2,1)S(1)} %shard_map.80.row_ref.refs_0_, bf16[2,256,768]{2,1,0:T(8,128)(2,1)S(1)} %copy-done), custom_call_target="tpu_custom_call" | custom-call | tf_op jit(solution)/shard_map/pallas_call | solution.py:444
  55.1 0.3 collective-permute-done.17.refs_3_
  55.4 2.0 %collective-permute-done.16.refs_2_ = bf16[384,256]{1,0:T(8,128)(2,1)S(1)} collective-permute-done((bf16[384,256]{1,0:T(8,128)(2,1)S(1)}, bf16[384,256]{1,0:T(8,128)(2,1)S(1)}, u32[]{:S(2)}, u32[]{:S(2)}) %collective-permute-start.16) | collective-permute-done | bytes 196640 | tf_op jit(solution)/shard_map/ppermute | solution.py:388
  57.4 0.0 collective-permute-done.15.refs_1_
  57.4 5.1 %shard_map.82 = (bf16[96,256]{1,0:T(8,128)(2,1)S(1)}, bf16[96,256]{1,0:T(8,128)(2,1)S(1)}, bf16[96,256]{1,0:T(8,128)(2,1)S(1)}, bf16[96,256]{1,0:T(8,128)(2,1)S(1)}) custom-call(s32[16,128]{1,0:T(8,128)S(1)} %get-tuple-element.45.count_ref, bf16[384,256]{1,0:T(8,128)(2,1)S(1)} %shard_map.80.row_ref.refs_0_, ...), custom_call_target="tpu_custom_call" | custom-call | tf_op jit(solution)/shard_map/pallas_call | solution.py:456
  62.6 2.1 %collective-permute-start.18 = (bf16[96,256]{1,0:T(8,128)(2,1)S(1)}, bf16[96,256]{1,0:T(8,128)(2,1)S(1)}, u32[]{:S(2)}, u32[]{:S(2)}) collective-permute-start(bf16[96,256]{1,0:T(8,128)(2,1)S(1)} %get-tuple-element.65), channel_id=1, source_target_pairs={{0,24},{2,26},{4,28},{6,30},{8,16},{10,18},{12,20},{14,22},{16,8},... | collective-permute-start | bytes 147464 | tf_op jit(solution)/shard_map/ppermute | solution.py:388
  64.6 0.4 collective-permute-start.19
  65.0 2.0 %collective-permute-start.20 = (bf16[96,256]{1,0:T(8,128)(2,1)S(1)}, bf16[96,256]{1,0:T(8,128)(2,1)S(1)}, u32[]{:S(2)}, u32[]{:S(2)}) collective-permute-start(bf16[96,256]{1,0:T(8,128)(2,1)S(1)} %get-tuple-element.67), channel_id=1, source_target_pairs={{0,8},{2,10},{4,12},{6,14},{8,0},{10,2},{12,4},{14,6},{16,24},{18,... | collective-permute-start | bytes 147464 | tf_op jit(solution)/shard_map/ppermute | solution.py:388
  67.0 0.4 shard_map.83.refs_4_
  67.4 1.1 %collective-permute-done.18.refs_1_ = bf16[96,256]{1,0:T(8,128)(2,1)S(1)} collective-permute-done((bf16[96,256]{1,0:T(8,128)(2,1)S(1)}, bf16[96,256]{1,0:T(8,128)(2,1)S(1)}, u32[]{:S(2)}, u32[]{:S(2)}) %collective-permute-start.18) | collective-permute-done | bytes 49184 | tf_op jit(solution)/shard_map/ppermute | solution.py:388
  68.5 1.2 %collective-permute-done.19.refs_2_ = bf16[96,256]{1,0:T(8,128)(2,1)S(1)} collective-permute-done((bf16[96,256]{1,0:T(8,128)(2,1)S(1)}, bf16[96,256]{1,0:T(8,128)(2,1)S(1)}, u32[]{:S(2)}, u32[]{:S(2)}) %collective-permute-start.19) | collective-permute-done | bytes 49184 | tf_op jit(solution)/shard_map/ppermute | solution.py:388
  69.7 0.0 collective-permute-done.20.refs_3_
  69.7 1.7 %shard_map.84 = f32[256,256]{1,0:T(8,128)} custom-call(bf16[96,256]{1,0:T(8,128)(2,1)S(1)} %get-tuple-element.64.refs_0_, bf16[96,256]{1,0:T(8,128)(2,1)S(1)} %collective-permute-done.18.refs_1_, bf16[96,256]{1,0:T(8,128)(2,1)S(1)} %collective-permute-done.19.refs_2_, bf16[96,256]{1,0:T(8,128)(2,1)S(1)} %collective-permute-done.20.refs_3_, ...), custom_call_target="tpu_custom_call" | custom-call | tf_op jit(solution)/shard_map/pallas_call | solution.py:481
  (9 shorter events, 0.0 us)
Async XLA Ops:
  0.0 21.2 %copy-start = (bf16[2,256,768]{2,1,0:T(8,128)(2,1)S(1)}, bf16[2,256,768]{2,1,0:T(8,128)(2,1)}, u32[]{:S(2)}) copy-start(bf16[2,256,768]{2,1,0:T(8,128)(2,1)} %refs_4_.5) | copy-start | bytes 2359300
  0.0 3.4 %collective-permute-start = (s32[2,256]{1,0:T(2,128)}, s32[2,256]{1,0:T(2,128)S(1)}, u32[]{:S(2)}, u32[]{:S(2)}) collective-permute-start(s32[2,256]{1,0:T(2,128)} %order_ref.1), channel_id=1, source_target_pairs={{1,1},{3,9},{5,17},{7,25},{9,3},{11,11},{13,19},{15,27},{17,5},{19... | collective-permute-start | bytes 6152 | tf_op jit(solution)/shard_map/ppermute | solution.py:388
  0.8 1.0 %copy-start.4 = (f32[256,256]{1,0:T(8,128)S(1)}, f32[256,256]{1,0:T(8,128)}, u32[]{:S(2)}) copy-start(f32[256,256]{1,0:T(8,128)} %refs_4_.4) | copy-start | bytes 786436
  1.8 0.7 copy-start.6
  2.5 0.7 copy-start.8
  3.9 6.6 %collective-permute-start.1 = (bf16[64,256]{1,0:T(8,128)(2,1)S(1)}, bf16[64,256]{1,0:T(8,128)(2,1)S(1)}, u32[]{:S(2)}, u32[]{:S(2)}) collective-permute-start(bf16[64,256]{1,0:T(8,128)(2,1)S(1)} %get-tuple-element.41), channel_id=1, source_target_pairs={{0,2},{2,0},{4,6},{6,4},{8,10},{10,8},{12,14},{14,12},{16,18},{18,... | collective-permute-start | bytes 98312 | tf_op jit(solution)/shard_map/ppermute | solution.py:388
  6.9 8.4 %collective-permute-start.4 = (bf16[256,256]{1,0:T(8,128)(2,1)S(1)}, bf16[256,256]{1,0:T(8,128)(2,1)S(1)}, u32[]{:S(2)}, u32[]{:S(2)}) collective-permute-start(bf16[256,256]{1,0:T(8,128)(2,1)S(1)} %get-tuple-element.39.row_ref.refs_0_), channel_id=1, source_target_pairs={{0,24},{2,26},{4,28},{6,30},{8,16},{10,18},{12,20},{14,22},{16,8},... | collective-permute-start | bytes 393224 | tf_op jit(solution)/shard_map/ppermute | solution.py:388
  10.5 6.6 %collective-permute-start.3 = (bf16[256,256]{1,0:T(8,128)(2,1)S(1)}, bf16[256,256]{1,0:T(8,128)(2,1)S(1)}, u32[]{:S(2)}, u32[]{:S(2)}) collective-permute-start(bf16[256,256]{1,0:T(8,128)(2,1)S(1)} %get-tuple-element.39.row_ref.refs_0_), channel_id=1, source_target_pairs={{0,16},{2,18},{4,20},{6,22},{8,24},{10,26},{12,28},{14,30},{16,0},... | collective-permute-start | bytes 393224 | tf_op jit(solution)/shard_map/ppermute | solution.py:388
  10.5 6.6 %collective-permute-start.2 = (bf16[256,256]{1,0:T(8,128)(2,1)S(1)}, bf16[256,256]{1,0:T(8,128)(2,1)S(1)}, u32[]{:S(2)}, u32[]{:S(2)}) collective-permute-start(bf16[256,256]{1,0:T(8,128)(2,1)S(1)} %get-tuple-element.42), channel_id=1, source_target_pairs={{0,8},{2,10},{4,12},{6,14},{8,0},{10,2},{12,4},{14,6},{16,24},{18,... | collective-permute-start | bytes 393224 | tf_op jit(solution)/shard_map/ppermute | solution.py:388
  11.3 3.9 %collective-permute-start.5 = (bf16[32,256]{1,0:T(8,128)(2,1)S(1)}, bf16[32,256]{1,0:T(8,128)(2,1)S(1)}, u32[]{:S(2)}, u32[]{:S(2)}) collective-permute-start(bf16[32,256]{1,0:T(8,128)(2,1)S(1)} %get-tuple-element.44), channel_id=1, source_target_pairs={{0,4},{2,6},{4,0},{6,2},{8,12},{10,14},{12,8},{14,10},{16,20},{18,... | collective-permute-start | bytes 49160 | tf_op jit(solution)/shard_map/ppermute | solution.py:388
  17.6 6.7 %collective-permute-start.8 = (bf16[384,256]{1,0:T(8,128)(2,1)S(1)}, bf16[384,256]{1,0:T(8,128)(2,1)S(1)}, u32[]{:S(2)}, u32[]{:S(2)}) collective-permute-start(bf16[384,256]{1,0:T(8,128)(2,1)S(1)} %get-tuple-element.46.row_ref.refs_0_), channel_id=1, source_target_pairs={{0,6},{2,4},{4,2},{6,0},{8,14},{10,12},{12,10},{14,8},{16,22},{18,... | collective-permute-start | bytes 589832 | tf_op jit(solution)/shard_map/ppermute | solution.py:388
  19.2 7.2 %collective-permute-start.7 = (bf16[384,256]{1,0:T(8,128)(2,1)S(1)}, bf16[384,256]{1,0:T(8,128)(2,1)S(1)}, u32[]{:S(2)}, u32[]{:S(2)}) collective-permute-start(bf16[384,256]{1,0:T(8,128)(2,1)S(1)} %get-tuple-element.46.row_ref.refs_0_), channel_id=1, source_target_pairs={{0,4},{2,6},{4,0},{6,2},{8,12},{10,14},{12,8},{14,10},{16,20},{18,... | collective-permute-start | bytes 589832 | tf_op jit(solution)/shard_map/ppermute | solution.py:388
  19.7 6.8 %collective-permute-start.6 = (bf16[384,256]{1,0:T(8,128)(2,1)S(1)}, bf16[384,256]{1,0:T(8,128)(2,1)S(1)}, u32[]{:S(2)}, u32[]{:S(2)}) collective-permute-start(bf16[384,256]{1,0:T(8,128)(2,1)S(1)} %get-tuple-element.46.row_ref.refs_0_), channel_id=1, source_target_pairs={{0,2},{2,0},{4,6},{6,4},{8,10},{10,8},{12,14},{14,12},{16,18},{18,... | collective-permute-start | bytes 589832 | tf_op jit(solution)/shard_map/ppermute | solution.py:388
  26.4 13.0 %copy-start.1 = (bf16[2,256,1024]{2,1,0:T(8,128)(2,1)S(1)}, bf16[2,256,1024]{2,1,0:T(8,128)(2,1)}, u32[]{:S(2)}) copy-start(bf16[2,256,1024]{2,1,0:T(8,128)(2,1)} %refs_8_.3) | copy-start | bytes 3145732
  26.4 13.0 %copy-start.2 = (bf16[2,1024,256]{2,1,0:T(8,128)(2,1)S(1)}, bf16[2,1024,256]{2,1,0:T(8,128)(2,1)}, u32[]{:S(2)}) copy-start(bf16[2,1024,256]{2,1,0:T(8,128)(2,1)} %refs_9_.1) | copy-start | bytes 3145732
  26.4 13.0 %copy-start.3 = (bf16[2,256,256]{2,1,0:T(8,128)(2,1)S(1)}, bf16[2,256,256]{2,1,0:T(8,128)(2,1)}, u32[]{:S(2)}) copy-start(bf16[2,256,256]{2,1,0:T(8,128)(2,1)} %refs_7_.3) | copy-start | bytes 786436
  26.4 13.0 %copy-start.5 = (f32[256,256]{1,0:T(8,128)S(1)}, f32[256,256]{1,0:T(8,128)}, u32[]{:S(2)}) copy-start(f32[256,256]{1,0:T(8,128)} %refs_4_.4) | copy-start | bytes 786436
  31.5 7.9 %copy-start.7 = (f32[2,2,256]{2,1,0:T(2,128)S(1)}, f32[2,2,256]{2,1,0:T(2,128)}, u32[]{:S(2)}) copy-start(f32[2,2,256]{2,1,0:T(2,128)} %refs_6_.3) | copy-start | bytes 12292
  31.5 6.0 %collective-permute-start.9 = (bf16[112,256]{1,0:T(8,128)(2,1)S(1)}, bf16[112,256]{1,0:T(8,128)(2,1)S(1)}, u32[]{:S(2)}, u32[]{:S(2)}) collective-permute-start(bf16[112,256]{1,0:T(8,128)(2,1)S(1)} %get-tuple-element.53), channel_id=1, source_target_pairs={{0,24},{2,26},{4,28},{6,30},{8,16},{10,18},{12,20},{14,22},{16,8},... | collective-permute-start | bytes 172040 | tf_op jit(solution)/shard_map/ppermute | solution.py:388
  34.3 5.1 %collective-permute-start.10 = (bf16[112,256]{1,0:T(8,128)(2,1)S(1)}, bf16[112,256]{1,0:T(8,128)(2,1)S(1)}, u32[]{:S(2)}, u32[]{:S(2)}) collective-permute-start(bf16[112,256]{1,0:T(8,128)(2,1)S(1)} %get-tuple-element.54), channel_id=1, source_target_pairs={{0,16},{2,18},{4,20},{6,22},{8,24},{10,26},{12,28},{14,30},{16,0},... | collective-permute-start | bytes 172040 | tf_op jit(solution)/shard_map/ppermute | solution.py:388
  34.4 5.0 %collective-permute-start.11 = (bf16[112,256]{1,0:T(8,128)(2,1)S(1)}, bf16[112,256]{1,0:T(8,128)(2,1)S(1)}, u32[]{:S(2)}, u32[]{:S(2)}) collective-permute-start(bf16[112,256]{1,0:T(8,128)(2,1)S(1)} %get-tuple-element.55), channel_id=1, source_target_pairs={{0,8},{2,10},{4,12},{6,14},{8,0},{10,2},{12,4},{14,6},{16,24},{18,... | collective-permute-start | bytes 172040 | tf_op jit(solution)/shard_map/ppermute | solution.py:388
  41.0 6.0 %collective-permute-start.12 = (bf16[96,256]{1,0:T(8,128)(2,1)S(1)}, bf16[96,256]{1,0:T(8,128)(2,1)S(1)}, u32[]{:S(2)}, u32[]{:S(2)}) collective-permute-start(bf16[96,256]{1,0:T(8,128)(2,1)S(1)} %get-tuple-element.57), channel_id=1, source_target_pairs={{0,24},{2,26},{4,28},{6,30},{8,16},{10,18},{12,20},{14,22},{16,8},... | collective-permute-start | bytes 147464 | tf_op jit(solution)/shard_map/ppermute | solution.py:388
  43.2 5.4 %collective-permute-start.13 = (bf16[96,256]{1,0:T(8,128)(2,1)S(1)}, bf16[96,256]{1,0:T(8,128)(2,1)S(1)}, u32[]{:S(2)}, u32[]{:S(2)}) collective-permute-start(bf16[96,256]{1,0:T(8,128)(2,1)S(1)} %get-tuple-element.58), channel_id=1, source_target_pairs={{0,16},{2,18},{4,20},{6,22},{8,24},{10,26},{12,28},{14,30},{16,0},... | collective-permute-start | bytes 147464 | tf_op jit(solution)/shard_map/ppermute | solution.py:388
  43.3 5.3 %collective-permute-start.14 = (bf16[96,256]{1,0:T(8,128)(2,1)S(1)}, bf16[96,256]{1,0:T(8,128)(2,1)S(1)}, u32[]{:S(2)}, u32[]{:S(2)}) collective-permute-start(bf16[96,256]{1,0:T(8,128)(2,1)S(1)} %get-tuple-element.59), channel_id=1, source_target_pairs={{0,8},{2,10},{4,12},{6,14},{8,0},{10,2},{12,4},{14,6},{16,24},{18,... | collective-permute-start | bytes 147464 | tf_op jit(solution)/shard_map/ppermute | solution.py:388
  48.7 6.7 %collective-permute-start.17 = (bf16[384,256]{1,0:T(8,128)(2,1)S(1)}, bf16[384,256]{1,0:T(8,128)(2,1)S(1)}, u32[]{:S(2)}, u32[]{:S(2)}) collective-permute-start(bf16[384,256]{1,0:T(8,128)(2,1)S(1)} %shard_map.80.row_ref.refs_0_), channel_id=1, source_target_pairs={{0,6},{2,4},{4,2},{6,0},{8,14},{10,12},{12,10},{14,8},{16,22},{18,... | collective-permute-start | bytes 589832 | tf_op jit(solution)/shard_map/ppermute | solution.py:388
  50.0 7.4 %collective-permute-start.16 = (bf16[384,256]{1,0:T(8,128)(2,1)S(1)}, bf16[384,256]{1,0:T(8,128)(2,1)S(1)}, u32[]{:S(2)}, u32[]{:S(2)}) collective-permute-start(bf16[384,256]{1,0:T(8,128)(2,1)S(1)} %shard_map.80.row_ref.refs_0_), channel_id=1, source_target_pairs={{0,4},{2,6},{4,0},{6,2},{8,12},{10,14},{12,8},{14,10},{16,20},{18,... | collective-permute-start | bytes 589832 | tf_op jit(solution)/shard_map/ppermute | solution.py:388
  50.7 6.7 %collective-permute-start.15 = (bf16[384,256]{1,0:T(8,128)(2,1)S(1)}, bf16[384,256]{1,0:T(8,128)(2,1)S(1)}, u32[]{:S(2)}, u32[]{:S(2)}) collective-permute-start(bf16[384,256]{1,0:T(8,128)(2,1)S(1)} %shard_map.80.row_ref.refs_0_), channel_id=1, source_target_pairs={{0,2},{2,0},{4,6},{6,4},{8,10},{10,8},{12,14},{14,12},{16,18},{18,... | collective-permute-start | bytes 589832 | tf_op jit(solution)/shard_map/ppermute | solution.py:388
  62.6 6.0 %collective-permute-start.18 = (bf16[96,256]{1,0:T(8,128)(2,1)S(1)}, bf16[96,256]{1,0:T(8,128)(2,1)S(1)}, u32[]{:S(2)}, u32[]{:S(2)}) collective-permute-start(bf16[96,256]{1,0:T(8,128)(2,1)S(1)} %get-tuple-element.65), channel_id=1, source_target_pairs={{0,24},{2,26},{4,28},{6,30},{8,16},{10,18},{12,20},{14,22},{16,8},... | collective-permute-start | bytes 147464 | tf_op jit(solution)/shard_map/ppermute | solution.py:388
  64.6 5.1 %collective-permute-start.19 = (bf16[96,256]{1,0:T(8,128)(2,1)S(1)}, bf16[96,256]{1,0:T(8,128)(2,1)S(1)}, u32[]{:S(2)}, u32[]{:S(2)}) collective-permute-start(bf16[96,256]{1,0:T(8,128)(2,1)S(1)} %get-tuple-element.66), channel_id=1, source_target_pairs={{0,16},{2,18},{4,20},{6,22},{8,24},{10,26},{12,28},{14,30},{16,0},... | collective-permute-start | bytes 147464 | tf_op jit(solution)/shard_map/ppermute | solution.py:388
  65.0 4.7 %collective-permute-start.20 = (bf16[96,256]{1,0:T(8,128)(2,1)S(1)}, bf16[96,256]{1,0:T(8,128)(2,1)S(1)}, u32[]{:S(2)}, u32[]{:S(2)}) collective-permute-start(bf16[96,256]{1,0:T(8,128)(2,1)S(1)} %get-tuple-element.67), channel_id=1, source_target_pairs={{0,8},{2,10},{4,12},{6,14},{8,0},{10,2},{12,4},{14,6},{16,24},{18,... | collective-permute-start | bytes 147464 | tf_op jit(solution)/shard_map/ppermute | solution.py:388

commit v9 on v8

--- a/solution.py
+++ b/solution.py
@@ -79,15 +79,14 @@
     return pl.BlockSpec(memory_space=VMEM)
 
 
-def norm_body(feature_ref, gain_ref, order_ref, normed_ref, passed_ref):
-    passed_ref[...] = order_ref[...]
+def norm_body(feature_ref, gain_ref, normed_ref):
     normed_ref[...] = layer_norm(feature_ref[...], gain_ref[0, 0:1, :]).astype(BF16)
 
 
-def note_body(plan, place, row_ref, order_ref, turned_ref, passed_ref, kept_ref, sent_ref):
+def note_body(plan, place, row_ref, turned_ref, passed_ref, kept_ref, sent_ref):
     passed_ref[...] = row_ref[...]
-    line, column, line_step, column_step, slab = (place[0, i] for i in range(5))
-    order = jnp.where(slab == 0, order_ref[...], turned_ref[...])
+    line, column, line_step, column_step = (place[0, i] for i in range(4))
+    order = turned_ref[...]
     bits = plan.rows.bit_length() - 1
     entry = iota((32, 1), 0)
     notes = None
@@ -415,16 +414,16 @@
         return move(piece, peers, [lambda i: i ^ k, lambda i: i ^ (group * k)])
 
     turned = move(
-        orders, peers, [None, lambda i: (i & (group - 1)) * group + (i >> shift)]
+        orders, peers, [lambda i: i, lambda i: (i & (group - 1)) * group + (i >> shift)]
     )
-    normed, own_orders = kernel_call(
-        norm_body, [struct((rows, width), BF16), struct(orders.shape, I32)], [whole()] * 3
-    )(features, norm_gains, orders)
+    (normed,) = kernel_call(norm_body, [struct((rows, width), BF16)], [whole()] * 2)(
+        features, norm_gains
+    )
     normed, kept, sent = kernel_call(
         functools.partial(note_body, plan),
         [struct((rows, width), BF16)] + [struct((64, width), BF16)] * 2,
-        [whole()] * 4,
-    )(place, normed, own_orders, turned)
+        [whole()] * 3,
+    )(place, normed, turned)
     mine, sent, near = kernel_call(
         join_body, [struct((32, width), BF16)] * 2 + [struct((rows, width), BF16)], [whole()] * 3
     )(kept, from_group(sent, 1), normed)

time: 71.7 us -> 71.9 us (level)
    unnamed x18 -> x16, local copies, waits for them, and re-layouts: 2.34 us -> 1.66 us
where the time goes in v9:
time: 71.9 us; the launch traced here: 71.4 us
  starting transfers between devices  30.9 us (43%)
  Pallas kernels  20.5 us (29%)
  waiting for transfers between devices  18.2 us (25%)
  local copies, waits for them, and re-layouts  1.75 us (2%)
    ppermute x21, starting transfers between devices, move(): return lax.ppermute(block, ('pts', 'slab'), pairs)  30.9 us
    ppermute x21, waiting for transfers between devices, move(): return lax.ppermute(block, ('pts', 'slab'), pairs)  18.2 us
    pallas_call x2, Pallas kernels, by_lines(): kernel_call(functools.partial(attend_body, plan, b, b == 0), [struct((tal...  10.2 us
    pallas_call x2, Pallas kernels, by_lines(): kernel_call(functools.partial(early_body, plan, b), [struct((held + 2 * T...  5.4 us
    pallas_call x2, Pallas kernels, by_lines(): kernel_call(functools.partial(store_body, plan, b, last), outs, [whole()]...  3.37 us
    unnamed x16, local copies, waits for them, and re-layouts  1.66 us
  transfers between devices with their start and end apart: 21, of which 13 were waited for; matrix products, arithmetic and copies ran while one was open for 0% of the time, Pallas kernels for 8%

profile of v9, /device:TPU:0, one launch (start us, length us, event | category | flops | bytes accessed | tf_op | source)
XLA Modules:
  0.0 71.4 jit_solution(5794422206475413497)
XLA Ops:
  0.0 1.5 %collective-permute-start = (s32[2,256]{1,0:T(2,128)}, s32[2,256]{1,0:T(2,128)S(1)}, u32[]{:S(2)}, u32[]{:S(2)}) collective-permute-start(s32[2,256]{1,0:T(2,128)} %param.8), channel_id=1, source_target_pairs={{0,0},{2,2},{4,4},{6,6},{8,8},{10,10},{12,12},{14,14},{16,16},{18,... | collective-permute-start | bytes 6152 | tf_op jit(solution)/shard_map/ppermute | solution.py:387
  1.5 0.0 copy-start.4
  1.5 0.9 %copy-done.4 = f32[256,256]{1,0:T(8,128)S(1)} copy-done((f32[256,256]{1,0:T(8,128)S(1)}, f32[256,256]{1,0:T(8,128)}, u32[]{:S(2)}) %copy-start.4) | copy-done | bytes 262168
  2.4 0.0 copy-start.6
  2.4 0.7 copy-done.6
  3.1 0.2 shard_map.73.row_ref
  3.3 0.1 stack.23
  3.4 0.0 collective-permute-done.turned_ref
  3.4 0.3 shard_map.74
  3.8 3.0 %collective-permute-start.1 = (bf16[64,256]{1,0:T(8,128)(2,1)S(1)}, bf16[64,256]{1,0:T(8,128)(2,1)S(1)}, u32[]{:S(2)}, u32[]{:S(2)}) collective-permute-start(bf16[64,256]{1,0:T(8,128)(2,1)S(1)} %get-tuple-element.37), channel_id=1, source_target_pairs={{0,2},{2,0},{4,6},{6,4},{8,10},{10,8},{12,14},{14,12},{16,18},{18,... | collective-permute-start | bytes 98312 | tf_op jit(solution)/shard_map/ppermute | solution.py:387
  6.8 3.6 %collective-permute-start.4 = (bf16[256,256]{1,0:T(8,128)(2,1)S(1)}, bf16[256,256]{1,0:T(8,128)(2,1)S(1)}, u32[]{:S(2)}, u32[]{:S(2)}) collective-permute-start(bf16[256,256]{1,0:T(8,128)(2,1)S(1)} %get-tuple-element.35.row_ref.refs_0_), channel_id=1, source_target_pairs={{0,24},{2,26},{4,28},{6,30},{8,16},{10,18},{12,20},{14,22},{16,8},... | collective-permute-start | bytes 393224 | tf_op jit(solution)/shard_map/ppermute | solution.py:387
  10.4 0.0 collective-permute-start.3
  10.4 0.0 collective-permute-done.1.got_ref
  10.4 0.8 %collective-permute-start.2 = (bf16[256,256]{1,0:T(8,128)(2,1)S(1)}, bf16[256,256]{1,0:T(8,128)(2,1)S(1)}, u32[]{:S(2)}, u32[]{:S(2)}) collective-permute-start(bf16[256,256]{1,0:T(8,128)(2,1)S(1)} %get-tuple-element.38), channel_id=1, source_target_pairs={{0,8},{2,10},{4,12},{6,14},{8,0},{10,2},{12,4},{14,6},{16,24},{18,... | collective-permute-start | bytes 393224 | tf_op jit(solution)/shard_map/ppermute | solution.py:387
  11.2 1.5 %collective-permute-start.5 = (bf16[32,256]{1,0:T(8,128)(2,1)S(1)}, bf16[32,256]{1,0:T(8,128)(2,1)S(1)}, u32[]{:S(2)}, u32[]{:S(2)}) collective-permute-start(bf16[32,256]{1,0:T(8,128)(2,1)S(1)} %get-tuple-element.40), channel_id=1, source_target_pairs={{0,4},{2,6},{4,0},{6,2},{8,12},{10,14},{12,8},{14,10},{16,20},{18,... | collective-permute-start | bytes 49160 | tf_op jit(solution)/shard_map/ppermute | solution.py:387
  12.8 2.4 %collective-permute-done.5.refs_5_ = bf16[32,256]{1,0:T(8,128)(2,1)S(1)} collective-permute-done((bf16[32,256]{1,0:T(8,128)(2,1)S(1)}, bf16[32,256]{1,0:T(8,128)(2,1)S(1)}, u32[]{:S(2)}, u32[]{:S(2)}) %collective-permute-start.5) | collective-permute-done | bytes 16416 | tf_op jit(solution)/shard_map/ppermute | solution.py:387
  15.1 0.0 collective-permute-done.4.refs_3_
  15.1 1.8 %collective-permute-done.3.refs_2_ = bf16[256,256]{1,0:T(8,128)(2,1)S(1)} collective-permute-done((bf16[256,256]{1,0:T(8,128)(2,1)S(1)}, bf16[256,256]{1,0:T(8,128)(2,1)S(1)}, u32[]{:S(2)}, u32[]{:S(2)}) %collective-permute-start.3) | collective-permute-done | bytes 131104 | tf_op jit(solution)/shard_map/ppermute | solution.py:387
  17.0 0.0 collective-permute-done.2.refs_1_
  17.0 0.5 shard_map.76
  17.5 1.7 %collective-permute-start.8 = (bf16[384,256]{1,0:T(8,128)(2,1)S(1)}, bf16[384,256]{1,0:T(8,128)(2,1)S(1)}, u32[]{:S(2)}, u32[]{:S(2)}) collective-permute-start(bf16[384,256]{1,0:T(8,128)(2,1)S(1)} %get-tuple-element.42.row_ref.refs_0_), channel_id=1, source_target_pairs={{0,6},{2,4},{4,2},{6,0},{8,14},{10,12},{12,10},{14,8},{16,22},{18,... | collective-permute-start | bytes 589832 | tf_op jit(solution)/shard_map/ppermute | solution.py:387
  19.2 0.4 collective-permute-start.7
  19.6 1.5 %collective-permute-start.6 = (bf16[384,256]{1,0:T(8,128)(2,1)S(1)}, bf16[384,256]{1,0:T(8,128)(2,1)S(1)}, u32[]{:S(2)}, u32[]{:S(2)}) collective-permute-start(bf16[384,256]{1,0:T(8,128)(2,1)S(1)} %get-tuple-element.42.row_ref.refs_0_), channel_id=1, source_target_pairs={{0,2},{2,0},{4,6},{6,4},{8,10},{10,8},{12,14},{14,12},{16,18},{18,... | collective-permute-start | bytes 589832 | tf_op jit(solution)/shard_map/ppermute | solution.py:387
  21.1 0.0 copy-done
  21.1 2.6 %shard_map.77 = (bf16[448,256]{1,0:T(8,128)(2,1)S(1)}, f32[384,256]{1,0:T(8,128)S(1)}, f32[384,256]{1,0:T(8,128)S(1)}, f32[384,256]{1,0:T(8,128)S(1)}) custom-call(s32[16,128]{1,0:T(8,128)S(1)} %get-tuple-element.41.count_ref, bf16[384,256]{1,0:T(8,128)(2,1)S(1)} %get-tuple-element.42.row_ref.refs_0_, bf16[2,256,768]{2,1,0:T(8,128)(2,1)S(1)} %copy-done), custom_call_target="tpu_custom_call" | custom-call | tf_op jit(solution)/shard_map/pallas_call | solution.py:443
  23.6 0.6 collective-permute-done.8.refs_3_
  24.2 2.0 %collective-permute-done.7.refs_2_ = bf16[384,256]{1,0:T(8,128)(2,1)S(1)} collective-permute-done((bf16[384,256]{1,0:T(8,128)(2,1)S(1)}, bf16[384,256]{1,0:T(8,128)(2,1)S(1)}, u32[]{:S(2)}, u32[]{:S(2)}) %collective-permute-start.7) | collective-permute-done | bytes 196640 | tf_op jit(solution)/shard_map/ppermute | solution.py:387
  26.2 0.1 collective-permute-done.6.refs_1_
  26.4 5.0 %shard_map.78 = (bf16[112,256]{1,0:T(8,128)(2,1)S(1)}, bf16[112,256]{1,0:T(8,128)(2,1)S(1)}, bf16[112,256]{1,0:T(8,128)(2,1)S(1)}, bf16[112,256]{1,0:T(8,128)(2,1)S(1)}) custom-call(s32[16,128]{1,0:T(8,128)S(1)} %get-tuple-element.41.count_ref, bf16[384,256]{1,0:T(8,128)(2,1)S(1)} %get-tuple-element.42.row_ref.refs_0_, ...), custom_call_target="tpu_custom_call" | custom-call | tf_op jit(solution)/shard_map/pallas_call | solution.py:455
  31.4 0.0 copy-start.7
  31.4 2.8 %collective-permute-start.9 = (bf16[112,256]{1,0:T(8,128)(2,1)S(1)}, bf16[112,256]{1,0:T(8,128)(2,1)S(1)}, u32[]{:S(2)}, u32[]{:S(2)}) collective-permute-start(bf16[112,256]{1,0:T(8,128)(2,1)S(1)} %get-tuple-element.49), channel_id=1, source_target_pairs={{0,24},{2,26},{4,28},{6,30},{8,16},{10,18},{12,20},{14,22},{16,8},... | collective-permute-start | bytes 172040 | tf_op jit(solution)/shard_map/ppermute | solution.py:387
  34.2 0.1 collective-permute-start.10
  34.3 1.5 %collective-permute-start.11 = (bf16[112,256]{1,0:T(8,128)(2,1)S(1)}, bf16[112,256]{1,0:T(8,128)(2,1)S(1)}, u32[]{:S(2)}, u32[]{:S(2)}) collective-permute-start(bf16[112,256]{1,0:T(8,128)(2,1)S(1)} %get-tuple-element.51), channel_id=1, source_target_pairs={{0,8},{2,10},{4,12},{6,14},{8,0},{10,2},{12,4},{14,6},{16,24},{18,... | collective-permute-start | bytes 172040 | tf_op jit(solution)/shard_map/ppermute | solution.py:387
  35.9 1.6 %collective-permute-done.9.refs_1_.refs_3_ = bf16[112,256]{1,0:T(8,128)(2,1)S(1)} collective-permute-done((bf16[112,256]{1,0:T(8,128)(2,1)S(1)}, bf16[112,256]{1,0:T(8,128)(2,1)S(1)}, u32[]{:S(2)}, u32[]{:S(2)}) %collective-permute-start.9) | collective-permute-done | bytes 57376 | tf_op jit(solution)/shard_map/ppermute | solution.py:387
  37.5 1.8 %collective-permute-done.10.refs_2_ = bf16[112,256]{1,0:T(8,128)(2,1)S(1)} collective-permute-done((bf16[112,256]{1,0:T(8,128)(2,1)S(1)}, bf16[112,256]{1,0:T(8,128)(2,1)S(1)}, u32[]{:S(2)}, u32[]{:S(2)}) %collective-permute-start.10) | collective-permute-done | bytes 57376 | tf_op jit(solution)/shard_map/ppermute | solution.py:387
  39.3 0.0 collective-permute-done.11.refs_3_.refs_1_
  39.3 0.0 copy-done.1
  39.3 0.0 copy-done.2
  39.3 0.0 copy-done.3
  39.3 0.0 copy-done.5
  39.3 0.0 copy-done.7
  39.3 1.6 %shard_map.79 = (f32[256,256]{1,0:T(8,128)S(1)}, bf16[96,256]{1,0:T(8,128)(2,1)S(1)}, bf16[96,256]{1,0:T(8,128)(2,1)S(1)}, bf16[96,256]{1,0:T(8,128)(2,1)S(1)}, bf16[96,256]{1,0:T(8,128)(2,1)S(1)}) custom-call(bf16[112,256]{1,0:T(8,128)(2,1)S(1)} %get-tuple-element.48.refs_0_, bf16[112,256]{1,0:T(8,128)(2,1)S(1)} %collective-permute-done.9.refs_1_.refs_3_, ...), custom_call_target="tpu_custom_call" | custom-call | tf_op jit(solution)/shard_map/pallas_call | solution.py:480
  41.0 2.2 %collective-permute-start.12 = (bf16[96,256]{1,0:T(8,128)(2,1)S(1)}, bf16[96,256]{1,0:T(8,128)(2,1)S(1)}, u32[]{:S(2)}, u32[]{:S(2)}) collective-permute-start(bf16[96,256]{1,0:T(8,128)(2,1)S(1)} %get-tuple-element.53), channel_id=1, source_target_pairs={{0,24},{2,26},{4,28},{6,30},{8,16},{10,18},{12,20},{14,22},{16,8},... | collective-permute-start | bytes 147464 | tf_op jit(solution)/shard_map/ppermute | solution.py:387
  43.1 0.1 collective-permute-start.13
  43.2 2.2 %collective-permute-start.14 = (bf16[96,256]{1,0:T(8,128)(2,1)S(1)}, bf16[96,256]{1,0:T(8,128)(2,1)S(1)}, u32[]{:S(2)}, u32[]{:S(2)}) collective-permute-start(bf16[96,256]{1,0:T(8,128)(2,1)S(1)} %get-tuple-element.55), channel_id=1, source_target_pairs={{0,8},{2,10},{4,12},{6,14},{8,0},{10,2},{12,4},{14,6},{16,24},{18,... | collective-permute-start | bytes 147464 | tf_op jit(solution)/shard_map/ppermute | solution.py:387
  45.4 1.5 %collective-permute-done.12.refs_1_ = bf16[96,256]{1,0:T(8,128)(2,1)S(1)} collective-permute-done((bf16[96,256]{1,0:T(8,128)(2,1)S(1)}, bf16[96,256]{1,0:T(8,128)(2,1)S(1)}, u32[]{:S(2)}, u32[]{:S(2)}) %collective-permute-start.12) | collective-permute-done | bytes 49184 | tf_op jit(solution)/shard_map/ppermute | solution.py:387
  46.9 1.6 %collective-permute-done.13.refs_2_ = bf16[96,256]{1,0:T(8,128)(2,1)S(1)} collective-permute-done((bf16[96,256]{1,0:T(8,128)(2,1)S(1)}, bf16[96,256]{1,0:T(8,128)(2,1)S(1)}, u32[]{:S(2)}, u32[]{:S(2)}) %collective-permute-start.13) | collective-permute-done | bytes 49184 | tf_op jit(solution)/shard_map/ppermute | solution.py:387
  48.5 0.0 collective-permute-done.14.refs_3_
  48.6 1.4 %collective-permute-start.17 = (bf16[384,256]{1,0:T(8,128)(2,1)S(1)}, bf16[384,256]{1,0:T(8,128)(2,1)S(1)}, u32[]{:S(2)}, u32[]{:S(2)}) collective-permute-start(bf16[384,256]{1,0:T(8,128)(2,1)S(1)} %shard_map.80.row_ref.refs_0_), channel_id=1, source_target_pairs={{0,6},{2,4},{4,2},{6,0},{8,14},{10,12},{12,10},{14,8},{16,22},{18,... | collective-permute-start | bytes 589832 | tf_op jit(solution)/shard_map/ppermute | solution.py:387
  49.9 0.7 collective-permute-start.16
  50.6 1.5 %collective-permute-start.15 = (bf16[384,256]{1,0:T(8,128)(2,1)S(1)}, bf16[384,256]{1,0:T(8,128)(2,1)S(1)}, u32[]{:S(2)}, u32[]{:S(2)}) collective-permute-start(bf16[384,256]{1,0:T(8,128)(2,1)S(1)} %shard_map.80.row_ref.refs_0_), channel_id=1, source_target_pairs={{0,2},{2,0},{4,6},{6,4},{8,10},{10,8},{12,14},{14,12},{16,18},{18,... | collective-permute-start | bytes 589832 | tf_op jit(solution)/shard_map/ppermute | solution.py:387
  52.1 2.8 %shard_map.81 = (bf16[448,256]{1,0:T(8,128)(2,1)S(1)}, f32[384,256]{1,0:T(8,128)S(1)}, f32[384,256]{1,0:T(8,128)S(1)}, f32[384,256]{1,0:T(8,128)S(1)}) custom-call(s32[16,128]{1,0:T(8,128)S(1)} %get-tuple-element.41.count_ref, bf16[384,256]{1,0:T(8,128)(2,1)S(1)} %shard_map.80.row_ref.refs_0_, bf16[2,256,768]{2,1,0:T(8,128)(2,1)S(1)} %copy-done), custom_call_target="tpu_custom_call" | custom-call | tf_op jit(solution)/shard_map/pallas_call | solution.py:443
  55.0 0.3 collective-permute-done.17.refs_3_
  55.3 2.0 %collective-permute-done.16.refs_2_ = bf16[384,256]{1,0:T(8,128)(2,1)S(1)} collective-permute-done((bf16[384,256]{1,0:T(8,128)(2,1)S(1)}, bf16[384,256]{1,0:T(8,128)(2,1)S(1)}, u32[]{:S(2)}, u32[]{:S(2)}) %collective-permute-start.16) | collective-permute-done | bytes 196640 | tf_op jit(solution)/shard_map/ppermute | solution.py:387
  57.3 0.0 collective-permute-done.15.refs_1_
  57.3 5.1 %shard_map.82 = (bf16[96,256]{1,0:T(8,128)(2,1)S(1)}, bf16[96,256]{1,0:T(8,128)(2,1)S(1)}, bf16[96,256]{1,0:T(8,128)(2,1)S(1)}, bf16[96,256]{1,0:T(8,128)(2,1)S(1)}) custom-call(s32[16,128]{1,0:T(8,128)S(1)} %get-tuple-element.41.count_ref, bf16[384,256]{1,0:T(8,128)(2,1)S(1)} %shard_map.80.row_ref.refs_0_, ...), custom_call_target="tpu_custom_call" | custom-call | tf_op jit(solution)/shard_map/pallas_call | solution.py:455
  62.5 2.1 %collective-permute-start.18 = (bf16[96,256]{1,0:T(8,128)(2,1)S(1)}, bf16[96,256]{1,0:T(8,128)(2,1)S(1)}, u32[]{:S(2)}, u32[]{:S(2)}) collective-permute-start(bf16[96,256]{1,0:T(8,128)(2,1)S(1)} %get-tuple-element.61), channel_id=1, source_target_pairs={{0,24},{2,26},{4,28},{6,30},{8,16},{10,18},{12,20},{14,22},{16,8},... | collective-permute-start | bytes 147464 | tf_op jit(solution)/shard_map/ppermute | solution.py:387
  64.5 0.4 collective-permute-start.19
  64.9 2.0 %collective-permute-start.20 = (bf16[96,256]{1,0:T(8,128)(2,1)S(1)}, bf16[96,256]{1,0:T(8,128)(2,1)S(1)}, u32[]{:S(2)}, u32[]{:S(2)}) collective-permute-start(bf16[96,256]{1,0:T(8,128)(2,1)S(1)} %get-tuple-element.63), channel_id=1, source_target_pairs={{0,8},{2,10},{4,12},{6,14},{8,0},{10,2},{12,4},{14,6},{16,24},{18,... | collective-permute-start | bytes 147464 | tf_op jit(solution)/shard_map/ppermute | solution.py:387
  66.9 0.4 shard_map.83.refs_4_
  67.3 1.1 %collective-permute-done.18.refs_1_ = bf16[96,256]{1,0:T(8,128)(2,1)S(1)} collective-permute-done((bf16[96,256]{1,0:T(8,128)(2,1)S(1)}, bf16[96,256]{1,0:T(8,128)(2,1)S(1)}, u32[]{:S(2)}, u32[]{:S(2)}) %collective-permute-start.18) | collective-permute-done | bytes 49184 | tf_op jit(solution)/shard_map/ppermute | solution.py:387
  68.4 1.2 %collective-permute-done.19.refs_2_ = bf16[96,256]{1,0:T(8,128)(2,1)S(1)} collective-permute-done((bf16[96,256]{1,0:T(8,128)(2,1)S(1)}, bf16[96,256]{1,0:T(8,128)(2,1)S(1)}, u32[]{:S(2)}, u32[]{:S(2)}) %collective-permute-start.19) | collective-permute-done | bytes 49184 | tf_op jit(solution)/shard_map/ppermute | solution.py:387
  69.6 0.0 collective-permute-done.20.refs_3_
  69.6 1.7 %shard_map.84 = f32[256,256]{1,0:T(8,128)} custom-call(bf16[96,256]{1,0:T(8,128)(2,1)S(1)} %get-tuple-element.60.refs_0_, bf16[96,256]{1,0:T(8,128)(2,1)S(1)} %collective-permute-done.18.refs_1_, bf16[96,256]{1,0:T(8,128)(2,1)S(1)} %collective-permute-done.19.refs_2_, bf16[96,256]{1,0:T(8,128)(2,1)S(1)} %collective-permute-done.20.refs_3_, ...), custom_call_target="tpu_custom_call" | custom-call | tf_op jit(solution)/shard_map/pallas_call | solution.py:480
  (7 shorter events, 0.0 us)
Async XLA Ops:
  0.0 21.1 %copy-start = (bf16[2,256,768]{2,1,0:T(8,128)(2,1)S(1)}, bf16[2,256,768]{2,1,0:T(8,128)(2,1)}, u32[]{:S(2)}) copy-start(bf16[2,256,768]{2,1,0:T(8,128)(2,1)} %refs_4_.5) | copy-start | bytes 2359300
  0.0 3.4 %collective-permute-start = (s32[2,256]{1,0:T(2,128)}, s32[2,256]{1,0:T(2,128)S(1)}, u32[]{:S(2)}, u32[]{:S(2)}) collective-permute-start(s32[2,256]{1,0:T(2,128)} %param.8), channel_id=1, source_target_pairs={{0,0},{2,2},{4,4},{6,6},{8,8},{10,10},{12,12},{14,14},{16,16},{18,... | collective-permute-start | bytes 6152 | tf_op jit(solution)/shard_map/ppermute | solution.py:387
  1.5 0.9 %copy-start.4 = (f32[256,256]{1,0:T(8,128)S(1)}, f32[256,256]{1,0:T(8,128)}, u32[]{:S(2)}) copy-start(f32[256,256]{1,0:T(8,128)} %refs_4_.4) | copy-start | bytes 786436
  2.4 0.7 copy-start.6
  3.8 6.6 %collective-permute-start.1 = (bf16[64,256]{1,0:T(8,128)(2,1)S(1)}, bf16[64,256]{1,0:T(8,128)(2,1)S(1)}, u32[]{:S(2)}, u32[]{:S(2)}) collective-permute-start(bf16[64,256]{1,0:T(8,128)(2,1)S(1)} %get-tuple-element.37), channel_id=1, source_target_pairs={{0,2},{2,0},{4,6},{6,4},{8,10},{10,8},{12,14},{14,12},{16,18},{18,... | collective-permute-start | bytes 98312 | tf_op jit(solution)/shard_map/ppermute | solution.py:387
  6.8 8.4 %collective-permute-start.4 = (bf16[256,256]{1,0:T(8,128)(2,1)S(1)}, bf16[256,256]{1,0:T(8,128)(2,1)S(1)}, u32[]{:S(2)}, u32[]{:S(2)}) collective-permute-start(bf16[256,256]{1,0:T(8,128)(2,1)S(1)} %get-tuple-element.35.row_ref.refs_0_), channel_id=1, source_target_pairs={{0,24},{2,26},{4,28},{6,30},{8,16},{10,18},{12,20},{14,22},{16,8},... | collective-permute-start | bytes 393224 | tf_op jit(solution)/shard_map/ppermute | solution.py:387
  10.4 6.6 %collective-permute-start.3 = (bf16[256,256]{1,0:T(8,128)(2,1)S(1)}, bf16[256,256]{1,0:T(8,128)(2,1)S(1)}, u32[]{:S(2)}, u32[]{:S(2)}) collective-permute-start(bf16[256,256]{1,0:T(8,128)(2,1)S(1)} %get-tuple-element.35.row_ref.refs_0_), channel_id=1, source_target_pairs={{0,16},{2,18},{4,20},{6,22},{8,24},{10,26},{12,28},{14,30},{16,0},... | collective-permute-start | bytes 393224 | tf_op jit(solution)/shard_map/ppermute | solution.py:387
  10.4 6.6 %collective-permute-start.2 = (bf16[256,256]{1,0:T(8,128)(2,1)S(1)}, bf16[256,256]{1,0:T(8,128)(2,1)S(1)}, u32[]{:S(2)}, u32[]{:S(2)}) collective-permute-start(bf16[256,256]{1,0:T(8,128)(2,1)S(1)} %get-tuple-element.38), channel_id=1, source_target_pairs={{0,8},{2,10},{4,12},{6,14},{8,0},{10,2},{12,4},{14,6},{16,24},{18,... | collective-permute-start | bytes 393224 | tf_op jit(solution)/shard_map/ppermute | solution.py:387
  11.2 3.9 %collective-permute-start.5 = (bf16[32,256]{1,0:T(8,128)(2,1)S(1)}, bf16[32,256]{1,0:T(8,128)(2,1)S(1)}, u32[]{:S(2)}, u32[]{:S(2)}) collective-permute-start(bf16[32,256]{1,0:T(8,128)(2,1)S(1)} %get-tuple-element.40), channel_id=1, source_target_pairs={{0,4},{2,6},{4,0},{6,2},{8,12},{10,14},{12,8},{14,10},{16,20},{18,... | collective-permute-start | bytes 49160 | tf_op jit(solution)/shard_map/ppermute | solution.py:387
  17.5 6.7 %collective-permute-start.8 = (bf16[384,256]{1,0:T(8,128)(2,1)S(1)}, bf16[384,256]{1,0:T(8,128)(2,1)S(1)}, u32[]{:S(2)}, u32[]{:S(2)}) collective-permute-start(bf16[384,256]{1,0:T(8,128)(2,1)S(1)} %get-tuple-element.42.row_ref.refs_0_), channel_id=1, source_target_pairs={{0,6},{2,4},{4,2},{6,0},{8,14},{10,12},{12,10},{14,8},{16,22},{18,... | collective-permute-start | bytes 589832 | tf_op jit(solution)/shard_map/ppermute | solution.py:387
  19.2 7.1 %collective-permute-start.7 = (bf16[384,256]{1,0:T(8,128)(2,1)S(1)}, bf16[384,256]{1,0:T(8,128)(2,1)S(1)}, u32[]{:S(2)}, u32[]{:S(2)}) collective-permute-start(bf16[384,256]{1,0:T(8,128)(2,1)S(1)} %get-tuple-element.42.row_ref.refs_0_), channel_id=1, source_target_pairs={{0,4},{2,6},{4,0},{6,2},{8,12},{10,14},{12,8},{14,10},{16,20},{18,... | collective-permute-start | bytes 589832 | tf_op jit(solution)/shard_map/ppermute | solution.py:387
  19.6 6.8 %collective-permute-start.6 = (bf16[384,256]{1,0:T(8,128)(2,1)S(1)}, bf16[384,256]{1,0:T(8,128)(2,1)S(1)}, u32[]{:S(2)}, u32[]{:S(2)}) collective-permute-start(bf16[384,256]{1,0:T(8,128)(2,1)S(1)} %get-tuple-element.42.row_ref.refs_0_), channel_id=1, source_target_pairs={{0,2},{2,0},{4,6},{6,4},{8,10},{10,8},{12,14},{14,12},{16,18},{18,... | collective-permute-start | bytes 589832 | tf_op jit(solution)/shard_map/ppermute | solution.py:387
  26.3 13.0 %copy-start.1 = (bf16[2,256,1024]{2,1,0:T(8,128)(2,1)S(1)}, bf16[2,256,1024]{2,1,0:T(8,128)(2,1)}, u32[]{:S(2)}) copy-start(bf16[2,256,1024]{2,1,0:T(8,128)(2,1)} %refs_8_.3) | copy-start | bytes 3145732
  26.4 13.0 %copy-start.2 = (bf16[2,1024,256]{2,1,0:T(8,128)(2,1)S(1)}, bf16[2,1024,256]{2,1,0:T(8,128)(2,1)}, u32[]{:S(2)}) copy-start(bf16[2,1024,256]{2,1,0:T(8,128)(2,1)} %refs_9_.1) | copy-start | bytes 3145732
  26.4 13.0 %copy-start.3 = (bf16[2,256,256]{2,1,0:T(8,128)(2,1)S(1)}, bf16[2,256,256]{2,1,0:T(8,128)(2,1)}, u32[]{:S(2)}) copy-start(bf16[2,256,256]{2,1,0:T(8,128)(2,1)} %refs_7_.3) | copy-start | bytes 786436
  26.4 13.0 %copy-start.5 = (f32[256,256]{1,0:T(8,128)S(1)}, f32[256,256]{1,0:T(8,128)}, u32[]{:S(2)}) copy-start(f32[256,256]{1,0:T(8,128)} %refs_4_.4) | copy-start | bytes 786436
  31.4 7.9 %copy-start.7 = (f32[2,2,256]{2,1,0:T(2,128)S(1)}, f32[2,2,256]{2,1,0:T(2,128)}, u32[]{:S(2)}) copy-start(f32[2,2,256]{2,1,0:T(2,128)} %refs_6_.3) | copy-start | bytes 12292
  31.4 6.0 %collective-permute-start.9 = (bf16[112,256]{1,0:T(8,128)(2,1)S(1)}, bf16[112,256]{1,0:T(8,128)(2,1)S(1)}, u32[]{:S(2)}, u32[]{:S(2)}) collective-permute-start(bf16[112,256]{1,0:T(8,128)(2,1)S(1)} %get-tuple-element.49), channel_id=1, source_target_pairs={{0,24},{2,26},{4,28},{6,30},{8,16},{10,18},{12,20},{14,22},{16,8},... | collective-permute-start | bytes 172040 | tf_op jit(solution)/shard_map/ppermute | solution.py:387
  34.2 5.1 %collective-permute-start.10 = (bf16[112,256]{1,0:T(8,128)(2,1)S(1)}, bf16[112,256]{1,0:T(8,128)(2,1)S(1)}, u32[]{:S(2)}, u32[]{:S(2)}) collective-permute-start(bf16[112,256]{1,0:T(8,128)(2,1)S(1)} %get-tuple-element.50), channel_id=1, source_target_pairs={{0,16},{2,18},{4,20},{6,22},{8,24},{10,26},{12,28},{14,30},{16,0},... | collective-permute-start | bytes 172040 | tf_op jit(solution)/shard_map/ppermute | solution.py:387
  34.3 5.0 %collective-permute-start.11 = (bf16[112,256]{1,0:T(8,128)(2,1)S(1)}, bf16[112,256]{1,0:T(8,128)(2,1)S(1)}, u32[]{:S(2)}, u32[]{:S(2)}) collective-permute-start(bf16[112,256]{1,0:T(8,128)(2,1)S(1)} %get-tuple-element.51), channel_id=1, source_target_pairs={{0,8},{2,10},{4,12},{6,14},{8,0},{10,2},{12,4},{14,6},{16,24},{18,... | collective-permute-start | bytes 172040 | tf_op jit(solution)/shard_map/ppermute | solution.py:387
  41.0 6.0 %collective-permute-start.12 = (bf16[96,256]{1,0:T(8,128)(2,1)S(1)}, bf16[96,256]{1,0:T(8,128)(2,1)S(1)}, u32[]{:S(2)}, u32[]{:S(2)}) collective-permute-start(bf16[96,256]{1,0:T(8,128)(2,1)S(1)} %get-tuple-element.53), channel_id=1, source_target_pairs={{0,24},{2,26},{4,28},{6,30},{8,16},{10,18},{12,20},{14,22},{16,8},... | collective-permute-start | bytes 147464 | tf_op jit(solution)/shard_map/ppermute | solution.py:387
  43.1 5.4 %collective-permute-start.13 = (bf16[96,256]{1,0:T(8,128)(2,1)S(1)}, bf16[96,256]{1,0:T(8,128)(2,1)S(1)}, u32[]{:S(2)}, u32[]{:S(2)}) collective-permute-start(bf16[96,256]{1,0:T(8,128)(2,1)S(1)} %get-tuple-element.54), channel_id=1, source_target_pairs={{0,16},{2,18},{4,20},{6,22},{8,24},{10,26},{12,28},{14,30},{16,0},... | collective-permute-start | bytes 147464 | tf_op jit(solution)/shard_map/ppermute | solution.py:387
  43.2 5.3 %collective-permute-start.14 = (bf16[96,256]{1,0:T(8,128)(2,1)S(1)}, bf16[96,256]{1,0:T(8,128)(2,1)S(1)}, u32[]{:S(2)}, u32[]{:S(2)}) collective-permute-start(bf16[96,256]{1,0:T(8,128)(2,1)S(1)} %get-tuple-element.55), channel_id=1, source_target_pairs={{0,8},{2,10},{4,12},{6,14},{8,0},{10,2},{12,4},{14,6},{16,24},{18,... | collective-permute-start | bytes 147464 | tf_op jit(solution)/shard_map/ppermute | solution.py:387
  48.6 6.7 %collective-permute-start.17 = (bf16[384,256]{1,0:T(8,128)(2,1)S(1)}, bf16[384,256]{1,0:T(8,128)(2,1)S(1)}, u32[]{:S(2)}, u32[]{:S(2)}) collective-permute-start(bf16[384,256]{1,0:T(8,128)(2,1)S(1)} %shard_map.80.row_ref.refs_0_), channel_id=1, source_target_pairs={{0,6},{2,4},{4,2},{6,0},{8,14},{10,12},{12,10},{14,8},{16,22},{18,... | collective-permute-start | bytes 589832 | tf_op jit(solution)/shard_map/ppermute | solution.py:387
  49.9 7.4 %collective-permute-start.16 = (bf16[384,256]{1,0:T(8,128)(2,1)S(1)}, bf16[384,256]{1,0:T(8,128)(2,1)S(1)}, u32[]{:S(2)}, u32[]{:S(2)}) collective-permute-start(bf16[384,256]{1,0:T(8,128)(2,1)S(1)} %shard_map.80.row_ref.refs_0_), channel_id=1, source_target_pairs={{0,4},{2,6},{4,0},{6,2},{8,12},{10,14},{12,8},{14,10},{16,20},{18,... | collective-permute-start | bytes 589832 | tf_op jit(solution)/shard_map/ppermute | solution.py:387
  50.6 6.7 %collective-permute-start.15 = (bf16[384,256]{1,0:T(8,128)(2,1)S(1)}, bf16[384,256]{1,0:T(8,128)(2,1)S(1)}, u32[]{:S(2)}, u32[]{:S(2)}) collective-permute-start(bf16[384,256]{1,0:T(8,128)(2,1)S(1)} %shard_map.80.row_ref.refs_0_), channel_id=1, source_target_pairs={{0,2},{2,0},{4,6},{6,4},{8,10},{10,8},{12,14},{14,12},{16,18},{18,... | collective-permute-start | bytes 589832 | tf_op jit(solution)/shard_map/ppermute | solution.py:387
  62.5 6.0 %collective-permute-start.18 = (bf16[96,256]{1,0:T(8,128)(2,1)S(1)}, bf16[96,256]{1,0:T(8,128)(2,1)S(1)}, u32[]{:S(2)}, u32[]{:S(2)}) collective-permute-start(bf16[96,256]{1,0:T(8,128)(2,1)S(1)} %get-tuple-element.61), channel_id=1, source_target_pairs={{0,24},{2,26},{4,28},{6,30},{8,16},{10,18},{12,20},{14,22},{16,8},... | collective-permute-start | bytes 147464 | tf_op jit(solution)/shard_map/ppermute | solution.py:387
  64.5 5.1 %collective-permute-start.19 = (bf16[96,256]{1,0:T(8,128)(2,1)S(1)}, bf16[96,256]{1,0:T(8,128)(2,1)S(1)}, u32[]{:S(2)}, u32[]{:S(2)}) collective-permute-start(bf16[96,256]{1,0:T(8,128)(2,1)S(1)} %get-tuple-element.62), channel_id=1, source_target_pairs={{0,16},{2,18},{4,20},{6,22},{8,24},{10,26},{12,28},{14,30},{16,0},... | collective-permute-start | bytes 147464 | tf_op jit(solution)/shard_map/ppermute | solution.py:387
  64.9 4.7 %collective-permute-start.20 = (bf16[96,256]{1,0:T(8,128)(2,1)S(1)}, bf16[96,256]{1,0:T(8,128)(2,1)S(1)}, u32[]{:S(2)}, u32[]{:S(2)}) collective-permute-start(bf16[96,256]{1,0:T(8,128)(2,1)S(1)} %get-tuple-element.63), channel_id=1, source_target_pairs={{0,8},{2,10},{4,12},{6,14},{8,0},{10,2},{12,4},{14,6},{16,24},{18,... | collective-permute-start | bytes 147464 | tf_op jit(solution)/shard_map/ppermute | solution.py:387
